TPU v7x, 32 devices: a whole 2x2x4 slice. The times are simulated.
32 devices in a mesh: expert: 8 (over y, x, core), dp: 4 (over z).
Axes of the slice: x: 2, y: 2, z: 4, core: 2. Of those that a mesh axis runs over, the one named last changes fastest.
Arguments:
- tokens: bfloat16 [512, 2048], P(('expert', 'dp')), may hold values from -6 to 6
- cotangent: bfloat16 [512, 2048], P(('expert', 'dp')), may hold values from -6 to 6
- route_ids: int32 [512, 8], P(('expert', 'dp')), may hold values from 0 to 7, all different within a row; in each aligned block of 16 rows (0 to 15, 16 to 31, ...) at most 16 rows name the same one
- route_gates: bfloat16 [512, 8], P(('expert', 'dp')), may hold values from 0.019897461 to 0.5
- gate_up: bfloat16 [8, 2048, 1536], P('expert', 'dp'), may hold values from -0.125 to 0.125
- down: bfloat16 [8, 2048, 768], P('expert', 'dp'), may hold values from -6 to 6
- moment1: bfloat16 [8, 2048, 768], P('expert', 'dp'), may hold values from -4 to 4
- moment2: bfloat16 [8, 2048, 768], P('expert', 'dp'), may hold values from 0.049804688 to 0.5
- placement: int32 [8], replicated, may hold values from 0 to 7, each once
Outputs:
- rollout_down: bfloat16 [8, 2048, 768], P('expert', None, 'dp')
Inputs may be any that keep to these rules, and one draw needn't show every extreme that they name: `route_ids`: each row names 8 different experts; within the rows of one device no expert is named more than 16 times, a bound that some block reaches. `placement`: each expert exactly once.
All inputs are finite; a program needn't handle non-finite values.
Results may differ from a plain program's by a relative error of at most 0.003.
Values may be sent and summed in bfloat16 or wider, within the bound.
No kernel may reach another device: no remote copies, remote signals or barrier semaphores. Data moves between devices by JAX's collectives and lax.ppermute only.
A program may use at most 64 MiB of HBM per device.

v0:
```python
import jax
import jax.numpy as jnp
from jax import lax
from jax.sharding import PartitionSpec as P

OPT_STEP = 2


BETA_ONE = 0.9
BETA_TWO = 0.95
ADAM_EPS = 1e-08
LEARN_RATE = 0.25


def shards(tokens, cotangent, route_ids, route_gates, gate_up, down, moment1, moment2, placement):
    experts = lax.axis_size("expert")
    tok_rows = tokens.shape[0]
    width = tokens.shape[1]
    top_count = route_ids.shape[1]
    hidden_units = down.shape[2]
    capacity = min(tok_rows, 2 * tok_rows * top_count // experts)
    total_slots = experts * capacity
    route_hits = jnp.sum(
        (route_ids[:, :, None] == jnp.arange(experts, dtype=jnp.int32)).astype(jnp.int32), axis=1
    )
    earlier_hits = jnp.cumsum(route_hits, axis=0) - route_hits
    slot_index = jnp.take_along_axis(earlier_hits, route_ids, axis=1)
    target_slot = route_ids * capacity + slot_index
    matched = (target_slot[:, :, None] == jnp.arange(total_slots, dtype=jnp.int32)).astype(
        jnp.float32
    )
    picker = jnp.sum(matched, axis=1).astype(jnp.bfloat16)
    contract_rows = (((0,), (0,)), ((), ()))
    send_rows = lax.dot_general(picker, tokens, contract_rows, preferred_element_type=jnp.float32)
    send_rows = send_rows.astype(jnp.bfloat16).reshape(experts, capacity, width)
    send_grads = lax.dot_general(
        picker, cotangent, contract_rows, preferred_element_type=jnp.float32
    )
    send_grads = send_grads.astype(jnp.bfloat16).reshape(experts, capacity, width)
    send_gates = jnp.sum(matched * route_gates.astype(jnp.float32)[:, :, None], axis=(0, 1))
    send_gates = send_gates.astype(jnp.bfloat16).reshape(experts, capacity)
    rows_in, grads_in, gates_in = (
        lax.all_to_all(send_rows, "expert", split_axis=0, concat_axis=0, tiled=True),
        lax.all_to_all(send_grads, "expert", split_axis=0, concat_axis=0, tiled=True),
        lax.all_to_all(send_gates, "expert", split_axis=0, concat_axis=0, tiled=True),
    )
    rows_flat = rows_in.reshape(total_slots, width)
    pre_all = jnp.dot(
        rows_flat,
        lax.all_gather(gate_up, "dp", axis=1, tiled=True)[0],
        preferred_element_type=jnp.float32,
    )
    hidden = (jax.nn.silu(pre_all[:, :hidden_units]) * pre_all[:, hidden_units:]).astype(
        jnp.bfloat16
    )
    scaled = gates_in.reshape(total_slots, 1).astype(jnp.float32) * grads_in.reshape(
        total_slots, width
    ).astype(jnp.float32)
    scaled = scaled.astype(jnp.bfloat16)
    grad_share = lax.psum_scatter(
        lax.dot_general(scaled, hidden, contract_rows, preferred_element_type=jnp.float32).astype(
            jnp.bfloat16
        ),
        "dp",
        scatter_dimension=0,
        tiled=True,
    ).astype(jnp.float32)
    correct_one = 1.0 - BETA_ONE**OPT_STEP
    correct_two = 1.0 - BETA_TWO**OPT_STEP
    first = BETA_ONE * moment1[0].astype(jnp.float32) + (1.0 - BETA_ONE) * grad_share
    second = BETA_TWO * moment2[0].astype(jnp.float32) + (1.0 - BETA_TWO) * grad_share * grad_share
    direction = first / correct_one / (jnp.sqrt(second / correct_two) + ADAM_EPS)
    updated = (down[0].astype(jnp.float32) - LEARN_RATE * direction).astype(jnp.bfloat16)
    column_block = lax.all_to_all(updated, "dp", split_axis=1, concat_axis=0, tiled=True)
    block_cols = column_block.shape[1]
    piece_flat = column_block.reshape(experts, width * block_cols // experts)
    spread = lax.all_to_all(piece_flat, "expert", split_axis=0, concat_axis=0, tiled=True)
    picked = jnp.take(spread, placement, axis=0)
    landed = lax.all_to_all(picked, "expert", split_axis=0, concat_axis=0, tiled=True)
    return landed.reshape(1, width, block_cols)


def solution(mesh):
    placed = (
        P(("expert", "dp"), None),
        P(("expert", "dp"), None),
        P(("expert", "dp"), None),
        P(("expert", "dp"), None),
        P("expert", "dp", None),
        P("expert", "dp", None),
        P("expert", "dp", None),
        P("expert", "dp", None),
        P(),
    )
    return jax.shard_map(
        shards, mesh=mesh, in_specs=placed, out_specs=P("expert", None, "dp"), check_vma=False
    )
```

profile of v0, /device:TPU:0, one launch (start us, length us, event | category | flops | bytes accessed | tf_op | source)
XLA Modules:
  0.0 279.1 jit_solution(4406237694580856510)
XLA Ops:
  6.5 0.7 all-gather.2.cloned.1.call-update
  7.3 0.1 copy.47
  7.4 0.1 copy.49
  7.5 0.1 reshape.117
  7.6 0.0 copy-start.6
  7.6 1.3 gather_fusion.1
  8.9 0.0 copy-start.4
  8.9 0.1 reshape.120
  9.0 0.1 copy.50
  9.0 0.1 copy.51
  9.1 0.1 copy.52
  9.2 0.1 select_reduce_fusion
  9.3 0.7 convert_element_type.102
  10.0 5.2 %all-to-all-start = ((bf16[8,1,16]{2,1,0:T(2,128)(2,1)}), bf16[8,1,16]{2,1,0:T(2,128)(2,1)S(1)}, u32[]{:S(2)}, u32[]{:S(2)}) async-start(bf16[8,1,16]{2,1,0:T(2,128)(2,1)} %convert_element_type.102), calls=%async_computation | async-start | bytes 8192 | tf_op jit(solution)/shard_map/all_to_all | solution.py:45
  15.2 1.1 convolution_convert_fusion.1
  16.3 3.5 %all-to-all-done = bf16[8,1,16]{2,1,0:T(2,128)(2,1)S(1)} async-done(((bf16[8,1,16]{2,1,0:T(2,128)(2,1)}), bf16[8,1,16]{2,1,0:T(2,128)(2,1)S(1)}, u32[]{:S(2)}, u32[]{:S(2)}) %all-to-all-start) | async-done | bytes 288 | tf_op jit(solution)/shard_map/all_to_all | solution.py:45
  19.8 3.5 %all-to-all-start.2 = ((bf16[8,16,2048]{2,1,0:T(8,128)(2,1)}), bf16[8,16,2048]{2,1,0:T(8,128)(2,1)S(1)}, u32[]{:S(2)}, u32[]{:S(2)}) async-start(bf16[8,16,2048]{2,1,0:T(8,128)(2,1)} %bitcast.5), calls=%async_computation.2 | async-start | bytes 1048576 | tf_op jit(solution)/shard_map/all_to_all | solution.py:43
  23.3 1.1 convolution_convert_fusion.2
  24.4 8.6 %all-to-all-done.2 = bf16[8,16,2048]{2,1,0:T(8,128)(2,1)S(1)} async-done(((bf16[8,16,2048]{2,1,0:T(8,128)(2,1)}), bf16[8,16,2048]{2,1,0:T(8,128)(2,1)S(1)}, u32[]{:S(2)}, u32[]{:S(2)}) %all-to-all-start.2) | async-done | bytes 524320 | tf_op jit(solution)/shard_map/all_to_all | solution.py:43
  33.0 3.5 %all-to-all-start.1 = ((bf16[8,16,2048]{2,1,0:T(8,128)(2,1)}), bf16[8,16,2048]{2,1,0:T(8,128)(2,1)S(1)}, u32[]{:S(2)}, u32[]{:S(2)}) async-start(bf16[8,16,2048]{2,1,0:T(8,128)(2,1)} %bitcast.3), calls=%async_computation.1 | async-start | bytes 1048576 | tf_op jit(solution)/shard_map/all_to_all | solution.py:44
  36.5 0.0 reduce-scatter.2.cloned.1.call-start
  36.5 0.1 reshape.107
  36.6 90.4 %all-gather.2.cloned.1.call-done = bf16[1,2048,1536]{2,1,0:T(8,128)(2,1)} async-done(((bf16[1,512,1536]{2,1,0:T(8,128)(2,1)}), bf16[1,2048,1536]{2,1,0:T(8,128)(2,1)}) %all-gather.2.cloned.1.call-update) | async-done | bytes 6291472 | tf_op jit(solution)/shard_map/all_gather | solution.py:50
  127.0 3.8 %fusion = f32[128,1536]{1,0:T(8,128)S(1)} fusion(bf16[128,2048]{1,0:T(8,128)(2,1)S(1)} %bitcast.36, bf16[1,2048,1536]{2,1,0:T(8,128)(2,1)} %all-gather.2.cloned.1.call-done), kind=kOutput, calls=%fused_computation.2 | convolution fusion | flops 805306368 | bytes 7602176 | tf_op jit(solution)/shard_map/dot_general | solution.py:48
  130.8 2.8 convolution_convert_fusion
  133.6 0.0 reduce-scatter.2.cloned.1.call-update
  133.6 58.6 %reduce-scatter.2.cloned.1.call-done = bf16[512,768]{1,0:T(8,128)(2,1)} async-done(((bf16[2048,768]{1,0:T(8,128)(2,1)}), bf16[512,768]{1,0:T(8,128)(2,1)}) %reduce-scatter.2.cloned.1.call-update) | async-done | bytes 786448 | tf_op jit(solution)/shard_map/reduce_scatter | solution.py:60
  192.2 2.5 fusion.11
  194.7 0.3 copy.54
  195.0 23.7 %all_to_all.51 = bf16[512,4,192]{0,2,1:T(8,128)(2,1)S(1)} all-to-all(bf16[512,4,192]{0,2,1:T(8,128)(2,1)S(1)} %bitcast.38), channel_id=1, replica_groups=mesh['expert'=8,'dp'=4] {'dp'}, dimensions={1} | all-to-all | bytes 1572864 | tf_op jit(solution)/shard_map/all_to_all | solution.py:74
  218.7 0.5 copy.55
  219.2 1.4 all_to_all.44
  220.6 0.6 broadcast.80
  221.2 5.5 %reduce.5 = bf16[8,49152]{1,0:T(8,128)(2,1)S(1)} reduce(bf16[8,1,49152]{2,1,0:T(2,128)(2,1)S(1)} %all_to_all.44, bf16[]{:T(256)} %broadcast.80), dimensions={1}, to_apply=%all_to_all.44.reduce_sub_computation | reduce | bytes 1572866 | tf_op jit(solution)/shard_map/all_to_all | solution.py:77
  226.7 1.5 reshape.137
  228.2 3.7 %all-to-all-start.4 = ((bf16[8,2,24576]{2,1,0:T(2,128)(2,1)}), bf16[8,2,24576]{2,1,0:T(2,128)(2,1)S(1)}, u32[]{:S(2)}, u32[]{:S(2)}) async-start(bf16[8,2,24576]{2,1,0:T(2,128)(2,1)} %reshape.137), calls=%async_computation.5 | async-start | bytes 1572864 | tf_op jit(solution)/shard_map/all_to_all | solution.py:77
  232.0 12.5 %all-to-all-done.4 = bf16[8,2,24576]{2,1,0:T(2,128)(2,1)S(1)} async-done(((bf16[8,2,24576]{2,1,0:T(2,128)(2,1)}), bf16[8,2,24576]{2,1,0:T(2,128)(2,1)S(1)}, u32[]{:S(2)}, u32[]{:S(2)}) %all-to-all-start.4) | async-done | bytes 786464 | tf_op jit(solution)/shard_map/all_to_all | solution.py:77
  244.5 0.8 reshape.138
  245.3 0.9 copy.61
  246.2 1.1 gather_fusion
  247.2 0.1 bitcast_select_fusion
  247.4 1.3 reduce.6
  248.7 0.6 reshape.139
  249.3 15.0 %all_to_all.52 = bf16[8,2,24576]{2,1,0:T(2,128)(2,1)S(1)} all-to-all(bf16[8,2,24576]{2,1,0:T(2,128)(2,1)S(1)} %reshape.139), channel_id=1, replica_groups=mesh['expert'=8,'dp'=4] {'expert'}, dimensions={0} | all-to-all | bytes 1572864 | tf_op jit(solution)/shard_map/all_to_all | solution.py:79
  264.3 0.8 reshape.140
  265.1 4.8 %reduce.1 = bf16[8,49152]{1,0:T(8,128)(2,1)S(1)} reduce(bf16[8,1,49152]{2,1,0:T(2,128)(2,1)S(1)} %reshape.140, bf16[]{:T(256)} %constant.81), dimensions={1}, to_apply=%all_to_all.43.reduce_sub_computation | reduce | bytes 1572866 | tf_op jit(solution)/shard_map/all_to_all | solution.py:79
  269.9 1.2 reshape.105
  271.1 1.2 copy.58
  (25 shorter events, 0.1 us)
Async XLA Ops:
  6.5 8.7 %copy-start = (bf16[16,2048]{1,0:T(8,128)(2,1)S(1)}, bf16[16,2048]{1,0:T(8,128)(2,1)}, u32[]{:S(2)}) copy-start(bf16[16,2048]{1,0:T(8,128)(2,1)} %param.9) | copy-start | bytes 196612
  6.5 0.7 copy-start.5
  6.5 120.5 %all-gather.2.cloned.1.call-start = ((), (), s32[]{:S(2)}) async-start(), calls=%async_computation.7 | async-start | bytes 7864320 | tf_op jit(solution)/shard_map/all_gather | solution.py:50
  7.6 1.5 copy-start.6
  8.9 14.4 %copy-start.4 = (bf16[16,2048]{1,0:T(8,128)(2,1)S(1)}, bf16[16,2048]{1,0:T(8,128)(2,1)}, u32[]{:S(2)}) copy-start(bf16[16,2048]{1,0:T(8,128)(2,1)} %param.10) | copy-start | bytes 196612
  10.0 9.8 %all-to-all-start = ((bf16[8,1,16]{2,1,0:T(2,128)(2,1)}), bf16[8,1,16]{2,1,0:T(2,128)(2,1)S(1)}, u32[]{:S(2)}, u32[]{:S(2)}) async-start(bf16[8,1,16]{2,1,0:T(2,128)(2,1)} %convert_element_type.102), calls=%async_computation | async-start | bytes 8192 | tf_op jit(solution)/shard_map/all_to_all | solution.py:45
  19.8 13.2 %all-to-all-start.2 = ((bf16[8,16,2048]{2,1,0:T(8,128)(2,1)}), bf16[8,16,2048]{2,1,0:T(8,128)(2,1)S(1)}, u32[]{:S(2)}, u32[]{:S(2)}) async-start(bf16[8,16,2048]{2,1,0:T(8,128)(2,1)} %bitcast.5), calls=%async_computation.2 | async-start | bytes 1048576 | tf_op jit(solution)/shard_map/all_to_all | solution.py:43
  33.0 97.8 %all-to-all-start.1 = ((bf16[8,16,2048]{2,1,0:T(8,128)(2,1)}), bf16[8,16,2048]{2,1,0:T(8,128)(2,1)S(1)}, u32[]{:S(2)}, u32[]{:S(2)}) async-start(bf16[8,16,2048]{2,1,0:T(8,128)(2,1)} %bitcast.3), calls=%async_computation.1 | async-start | bytes 1048576 | tf_op jit(solution)/shard_map/all_to_all | solution.py:44
  36.5 155.8 %reduce-scatter.2.cloned.1.call-start = ((), (), s32[]{:S(2)}) async-start(), calls=%async_computation.8 | async-start | bytes 3932160 | tf_op jit(solution)/shard_map/reduce_scatter | solution.py:60
  133.6 58.7 %copy-start.1 = (bf16[1,512,768]{2,1,0:T(8,128)(2,1)S(1)}, bf16[1,512,768]{2,1,0:T(8,128)(2,1)}, u32[]{:S(2)}) copy-start(bf16[1,512,768]{2,1,0:T(8,128)(2,1)} %param.16) | copy-start | bytes 2359300
  133.6 58.7 %copy-start.2 = (bf16[1,512,768]{2,1,0:T(8,128)(2,1)S(1)}, bf16[1,512,768]{2,1,0:T(8,128)(2,1)}, u32[]{:S(2)}) copy-start(bf16[1,512,768]{2,1,0:T(8,128)(2,1)} %param.15) | copy-start | bytes 2359300
  133.6 58.7 %copy-start.3 = (bf16[1,512,768]{2,1,0:T(8,128)(2,1)S(1)}, bf16[1,512,768]{2,1,0:T(8,128)(2,1)}, u32[]{:S(2)}) copy-start(bf16[1,512,768]{2,1,0:T(8,128)(2,1)} %param.14) | copy-start | bytes 2359300
  226.7 5.3 %copy-start.7 = (s32[8]{0:T(128)S(1)}, s32[8]{0:T(128)}, u32[]{:S(2)}) copy-start(s32[8]{0:T(128)} %param.17) | copy-start | bytes 100
  228.2 16.3 %all-to-all-start.4 = ((bf16[8,2,24576]{2,1,0:T(2,128)(2,1)}), bf16[8,2,24576]{2,1,0:T(2,128)(2,1)S(1)}, u32[]{:S(2)}, u32[]{:S(2)}) async-start(bf16[8,2,24576]{2,1,0:T(2,128)(2,1)} %reshape.137), calls=%async_computation.5 | async-start | bytes 1572864 | tf_op jit(solution)/shard_map/all_to_all | solution.py:77
Sparse Core Ops, SparseCore 0:
  8.9 118.0 all-gather.1
  133.7 58.4 reduce-scatter.1
where the time goes:
time: 280 us; the launch traced here: 279 us
  waiting for transfers between devices  174 us (62%)
  blocking collectives  38.6 us (14%)
  starting transfers between devices  15.9 us (6%)
  other arithmetic  14.4 us (5%)
  between operations  13.6 us (5%)
  local copies, waits for them, and re-layouts  13.5 us (5%)
  matrix products  8.76 us (3%)
    all_gather x1, waiting for transfers between devices, shards(): lax.all_gather(gate_up, 'dp', axis=1, tiled=True)[0]  90.4 us
    reduce_scatter x1, waiting for transfers between devices, shards(): lax.psum_scatter(lax.dot_general(scaled, hidden, contract_rows, preferred...  58.6 us
    all_to_all x1, blocking collectives, shards(): lax.all_to_all(updated, 'dp', split_axis=1, concat_axis=0, tiled=True)  23.7 us
    all_to_all x1, blocking collectives, shards(): lax.all_to_all(picked, 'expert', split_axis=0, concat_axis=0, tiled=True)  15 us
    all_to_all x1, waiting for transfers between devices, shards(): lax.all_to_all(piece_flat, 'expert', split_axis=0, concat_axis=0, tiled=T...  12.5 us
    all_to_all x1, waiting for transfers between devices, shards(): lax.all_to_all(send_rows, 'expert', split_axis=0, concat_axis=0, tiled=True)  8.56 us
  transfers between devices with their start and end apart: 6, of which 5 were waited for; matrix products, arithmetic and copies ran while one was open for 3% of the time, Pallas kernels for 0%

commit v1 on v0

v1 whole, which is shorter than its diff:
```python
import functools

import jax
import jax.numpy as jnp
from jax import lax
from jax.experimental import pallas as pl
from jax.experimental.pallas import tpu as pltpu
from jax.sharding import PartitionSpec as P

OPT_STEP = 2


BETA_ONE = 0.9
BETA_TWO = 0.95
ADAM_EPS = 1e-08
LEARN_RATE = 0.25

BF16 = jnp.bfloat16
F32 = jnp.float32
LANES = 128
HALF = LANES // 2


def adam(down, moment1, moment2, grad):
    correct_one = 1.0 - BETA_ONE**OPT_STEP
    correct_two = 1.0 - BETA_TWO**OPT_STEP
    first = BETA_ONE * moment1.astype(F32) + (1.0 - BETA_ONE) * grad
    second = BETA_TWO * moment2.astype(F32) + (1.0 - BETA_TWO) * grad * grad
    direction = first / correct_one / (jnp.sqrt(second / correct_two) + ADAM_EPS)
    return (down.astype(F32) - LEARN_RATE * direction).astype(BF16)


def routed(tokens, cotangent, route_ids, route_gates, gate_up, down, moment1, moment2, placement):
    experts = lax.axis_size("expert")
    tok_rows = tokens.shape[0]
    width = tokens.shape[1]
    top_count = route_ids.shape[1]
    hidden_units = down.shape[2]
    capacity = min(tok_rows, 2 * tok_rows * top_count // experts)
    total_slots = experts * capacity
    route_hits = jnp.sum(
        (route_ids[:, :, None] == jnp.arange(experts, dtype=jnp.int32)).astype(jnp.int32), axis=1
    )
    earlier_hits = jnp.cumsum(route_hits, axis=0) - route_hits
    slot_index = jnp.take_along_axis(earlier_hits, route_ids, axis=1)
    target_slot = route_ids * capacity + slot_index
    matched = (target_slot[:, :, None] == jnp.arange(total_slots, dtype=jnp.int32)).astype(F32)
    picker = jnp.sum(matched, axis=1).astype(BF16)
    contract_rows = (((0,), (0,)), ((), ()))
    send_rows = lax.dot_general(picker, tokens, contract_rows, preferred_element_type=F32)
    send_rows = send_rows.astype(BF16).reshape(experts, capacity, width)
    send_grads = lax.dot_general(picker, cotangent, contract_rows, preferred_element_type=F32)
    send_grads = send_grads.astype(BF16).reshape(experts, capacity, width)
    send_gates = jnp.sum(matched * route_gates.astype(F32)[:, :, None], axis=(0, 1))
    send_gates = send_gates.astype(BF16).reshape(experts, capacity)
    rows_in, grads_in, gates_in = (
        lax.all_to_all(send_rows, "expert", split_axis=0, concat_axis=0, tiled=True),
        lax.all_to_all(send_grads, "expert", split_axis=0, concat_axis=0, tiled=True),
        lax.all_to_all(send_gates, "expert", split_axis=0, concat_axis=0, tiled=True),
    )
    pre_all = jnp.dot(
        rows_in.reshape(total_slots, width),
        lax.all_gather(gate_up, "dp", axis=1, tiled=True)[0],
        preferred_element_type=F32,
    )
    hidden = (jax.nn.silu(pre_all[:, :hidden_units]) * pre_all[:, hidden_units:]).astype(BF16)
    scaled = gates_in.reshape(total_slots, 1).astype(F32) * grads_in.reshape(
        total_slots, width
    ).astype(F32)
    partial = lax.dot_general(
        scaled.astype(BF16), hidden, contract_rows, preferred_element_type=F32
    ).astype(BF16)
    grad_share = lax.psum_scatter(partial, "dp", scatter_dimension=0, tiled=True).astype(F32)
    updated = adam(down[0], moment1[0], moment2[0], grad_share)
    column_block = lax.all_to_all(updated, "dp", split_axis=1, concat_axis=0, tiled=True)
    block_cols = column_block.shape[1]
    piece_flat = column_block.reshape(experts, width * block_cols // experts)
    spread = lax.all_to_all(piece_flat, "expert", split_axis=0, concat_axis=0, tiled=True)
    picked = jnp.take(spread, placement, axis=0)
    landed = lax.all_to_all(picked, "expert", split_axis=0, concat_axis=0, tiled=True)
    return landed.reshape(1, width, block_cols)


def partner(x, axis, flip):
    size = lax.axis_size(axis)
    return lax.ppermute(x, axis, [(i, i ^ flip) for i in range(size)])


def vmem(*shape_and_index):
    return pl.BlockSpec(*shape_and_index)


def smem():
    return pl.BlockSpec(memory_space=pltpu.SMEM)


def pack_rows_kernel(place, tok, cot, ids, gates, *outs):
    groups = len(outs)
    width = tok.shape[1]
    block = width // groups
    group = place[1]
    lane = lax.broadcasted_iota(jnp.int32, (tok.shape[0], LANES), 1)
    dense = jnp.zeros(lane.shape, F32)
    named = ids[...]
    weights = gates[...].astype(F32)
    for k in range(named.shape[1]):
        dense = dense + jnp.where(lane == named[:, k : k + 1], weights[:, k : k + 1], 0.0)
    dense = dense.astype(BF16)
    for flip, out in enumerate(outs):
        start = pl.multiple_of((group ^ flip) * block, LANES)
        out[:, :width] = tok[...]
        out[:, width : width + block] = cot[:, pl.ds(start, block)]
        out[:, width + block :] = dense


def pack_rows(place, tokens, cotangent, ids, gates, groups):
    rows, width = tokens.shape
    shape = jax.ShapeDtypeStruct((rows, width + width // groups + LANES), BF16)
    return pl.pallas_call(
        pack_rows_kernel,
        out_shape=[shape] * groups,
        in_specs=[smem()] + [pl.BlockSpec(memory_space=pltpu.VMEM)] * 4,
        name="pack_rows",
    )(place, tokens, cotangent, ids, gates)


def swap_halves(x):
    return jnp.concatenate([x[:, HALF:], x[:, :HALF]], axis=1)


def pack_weights_kernel(place, weights, *outs):
    groups = len(outs)
    hidden_units = weights.shape[1] // 2
    group = place[1]
    for flip, out in enumerate(outs):
        col = group ^ flip
        whole = pl.multiple_of(col * LANES, LANES)
        out[:, :LANES] = weights[:, pl.ds(whole, LANES)]
        out[:, LANES : 2 * LANES] = weights[
            :, pl.ds(pl.multiple_of(hidden_units + whole, LANES), LANES)
        ]
        shared = pl.multiple_of(groups * LANES + (col // 2) * LANES, LANES)
        gate = weights[:, pl.ds(shared, LANES)]
        up = weights[:, pl.ds(pl.multiple_of(hidden_units + shared, LANES), LANES)]

        @pl.when(col % 2 == 0)
        def _():
            out[:, 2 * LANES :] = jnp.concatenate([gate[:, :HALF], up[:, :HALF]], axis=1)

        @pl.when(col % 2 == 1)
        def _():
            out[:, 2 * LANES :] = jnp.concatenate([gate[:, HALF:], up[:, HALF:]], axis=1)


def pack_weights(place, weights, groups):
    rows, cols = weights.shape
    shape = jax.ShapeDtypeStruct((rows, cols // groups), BF16)
    return pl.pallas_call(
        pack_weights_kernel,
        out_shape=[shape] * groups,
        in_specs=[smem(), pl.BlockSpec(memory_space=pltpu.VMEM)],
        name="pack_weights",
    )(place, weights)


def order_groups_kernel(place, *refs):
    *blocks, out = refs
    for flip, block in enumerate(blocks):
        out[pl.ds(place[1] ^ flip, 1)] = block[...][None]


def order_groups(place, blocks):
    rows, width = blocks[0].shape
    out = pl.pallas_call(
        order_groups_kernel,
        out_shape=jax.ShapeDtypeStruct((len(blocks), rows, width), BF16),
        in_specs=[smem()] + [pl.BlockSpec(memory_space=pltpu.VMEM)] * len(blocks),
        name="order_groups",
    )(place, *blocks)
    return out.reshape(len(blocks) * rows, width)


def hidden_kernel(groups, pieces, place, *refs):
    row_refs, weight_refs, out, toks = refs[:pieces], refs[pieces:-2], refs[-2], refs[-1]
    rows, width = row_refs[0].shape
    block = width // groups
    total = pieces * rows
    for i, ref in enumerate(row_refs):
        toks[i * rows : (i + 1) * rows, :] = ref[...]
    pre = None
    for flip, ref in enumerate(weight_refs):
        start = pl.multiple_of((place[1] ^ flip) * block, LANES)
        term = jnp.dot(toks[:, pl.ds(start, block)], ref[...], preferred_element_type=F32)
        pre = term if pre is None else pre + term
    gate, up = pre[:, :LANES], pre[:, LANES : 2 * LANES]
    out[:total, :] = (gate / (1.0 + jnp.exp(-gate)) * up).astype(BF16)
    gate, up = pre[:, 2 * LANES : 2 * LANES + HALF], pre[:, 2 * LANES + HALF :]
    narrow = (gate / (1.0 + jnp.exp(-gate)) * up).astype(BF16)
    out[total:, :] = jnp.concatenate([narrow[: total // 2], narrow[total // 2 :]], axis=1)


def hidden_blocks(place, pieces, weights, width):
    groups = len(weights)
    rows = pieces[0].shape[0]
    total = rows * len(pieces)
    return pl.pallas_call(
        functools.partial(hidden_kernel, groups, len(pieces)),
        out_shape=jax.ShapeDtypeStruct((total + total // 2, LANES), BF16),
        grid=(1,),
        in_specs=[smem()]
        + [pl.BlockSpec((rows, width), lambda i: (0, 0))] * len(pieces)
        + [pl.BlockSpec(weights[0].shape, lambda i: (0, 0))] * groups,
        out_specs=pl.BlockSpec((total + total // 2, LANES), lambda i: (0, 0)),
        scratch_shapes=[pltpu.VMEM((total, width), BF16)],
        compiler_params=pltpu.CompilerParams(vmem_limit_bytes=48 * 1024 * 1024),
        name="hidden_blocks",
    )(place, *pieces, *weights)


def scaled_kernel(pieces, place, *refs):
    cot_refs, gate_refs, out = refs[:pieces], refs[pieces:-1], refs[-1]
    rows = cot_refs[0].shape[0]
    for i in range(pieces):
        gates = gate_refs[i][...].astype(F32)
        lane = lax.broadcasted_iota(jnp.int32, gates.shape, 1)
        gate = jnp.sum(jnp.where(lane == place[0], gates, 0.0), axis=1, keepdims=True)
        out[i * rows : (i + 1) * rows, :] = (gate * cot_refs[i][...].astype(F32)).astype(BF16)


def scaled_rows(place, pieces, width, block):
    rows = pieces[0].shape[0]
    return pl.pallas_call(
        functools.partial(scaled_kernel, len(pieces)),
        out_shape=jax.ShapeDtypeStruct((rows * len(pieces), block), BF16),
        grid=(1,),
        in_specs=[smem()]
        + [pl.BlockSpec((rows, block), lambda i: (0, width // block))] * len(pieces)
        + [pl.BlockSpec((rows, LANES), lambda i: (0, (width + block) // LANES))] * len(pieces),
        out_specs=pl.BlockSpec((rows * len(pieces), block), lambda i: (0, 0)),
        name="scaled_rows",
    )(place, *pieces, *pieces)


def update_kernel(groups, places, place, *refs):
    hid_refs, (scaled, down, first, second, out, hidden) = refs[:groups], refs[groups:]
    total = scaled.shape[0]
    features, units = down.shape
    cols = units // groups

    @pl.when(pl.program_id(0) == 0)
    def _():
        for own in range(groups):

            @pl.when(place[1] == own)
            def _():
                for col in range(groups):
                    ref = hid_refs[own ^ col]
                    hidden[:, col * LANES : (col + 1) * LANES] = ref[:total, :]
                    start = groups * LANES + col * HALF
                    hidden[: total // 2, start : start + HALF] = ref[total:, :HALF]
                    hidden[total // 2 :, start : start + HALF] = ref[total:, HALF:]

    grad = lax.dot_general(
        scaled[...], hidden[...], (((0,), (0,)), ((), ())), preferred_element_type=F32
    )
    updated = adam(down[...], first[...], second[...], grad)
    step = features // places
    for i in range(places):
        rows = updated[i * step : (i + 1) * step]
        for col in range(groups):
            piece = rows[:, col * cols : (col + 1) * cols]
            narrow = piece[:, LANES:]
            out[i * groups + col, :step, :] = piece[:, :LANES]
            out[i * groups + col, step:, :] = jnp.concatenate(
                [narrow[: step // 2], narrow[step // 2 :]], axis=1
            )


def update_pieces(place, hidden, scaled, down, first, second, experts):
    groups = len(hidden)
    total, features = scaled.shape
    units = down.shape[1]
    steps = 4
    chunk = features // steps
    places = experts // steps
    piece_rows = features // experts * (units // groups) // LANES
    return pl.pallas_call(
        functools.partial(update_kernel, groups, places),
        out_shape=jax.ShapeDtypeStruct((experts * groups, piece_rows, LANES), BF16),
        grid=(steps,),
        in_specs=[smem()]
        + [pl.BlockSpec(hidden[0].shape, lambda i: (0, 0))] * groups
        + [pl.BlockSpec((total, chunk), lambda i: (0, i))]
        + [pl.BlockSpec((chunk, units), lambda i: (i, 0))] * 3,
        out_specs=pl.BlockSpec((places * groups, piece_rows, LANES), lambda i: (i, 0, 0)),
        scratch_shapes=[pltpu.VMEM((total, units), BF16)],
        compiler_params=pltpu.CompilerParams(vmem_limit_bytes=48 * 1024 * 1024),
        name="update_pieces",
    )(place, *hidden, scaled, down, first, second)


def copy_kernel(order, x, out):
    out[...] = x[...]


def reorder(order, x):
    block = (1,) + x.shape[1:]
    return pl.pallas_call(
        copy_kernel,
        out_shape=jax.ShapeDtypeStruct(x.shape, x.dtype),
        grid_spec=pltpu.PrefetchScalarGridSpec(
            num_scalar_prefetch=1,
            grid=(x.shape[0],),
            in_specs=[pl.BlockSpec(block, lambda i, order: (order[i], 0, 0))],
            out_specs=pl.BlockSpec(block, lambda i, order: (i, 0, 0)),
        ),
        name="reorder",
    )(order, x)


def unpack_kernel(x, out):
    places = x.shape[0]
    step = out.shape[0] // places
    for i in range(places):
        base = i * step
        out[base : base + step, :LANES] = x[i, 0, :step, :]
        out[base : base + step // 2, LANES:] = x[i, 0, step:, :HALF]
        out[base + step // 2 : base + step, LANES:] = x[i, 0, step:, HALF:]


def unpack(x, width, cols):
    places, groups, piece_rows, _ = x.shape
    return pl.pallas_call(
        unpack_kernel,
        out_shape=jax.ShapeDtypeStruct((width, cols), BF16),
        grid=(groups,),
        in_specs=[pl.BlockSpec((places, 1, piece_rows, LANES), lambda g: (0, g, 0, 0))],
        out_specs=pl.BlockSpec((width // groups, cols), lambda g: (g, 0)),
        name="unpack",
    )(x)


def dense(tokens, cotangent, route_ids, route_gates, gate_up, down, moment1, moment2, placement):
    experts = lax.axis_size("expert")
    groups = lax.axis_size("dp")
    width = tokens.shape[1]
    units = down.shape[2]
    block = width // groups
    place = jnp.stack([lax.axis_index("expert"), lax.axis_index("dp")]).astype(jnp.int32)

    sent = pack_rows(place, tokens, cotangent, route_ids, route_gates, groups)
    own_weights, *sent_weights = pack_weights(place, gate_up[0], groups)
    blocks = [sent[0]] + [partner(sent[k], "dp", k) for k in range(1, groups)]
    weights = [own_weights] + [
        partner(sent_weights[k - 1], "dp", k) for k in range(1, groups)
    ]
    plane = order_groups(place, blocks)
    chips = [plane] + [partner(plane, "expert", k) for k in range(2, experts, 2)]
    pieces = chips + [partner(x, "expert", 1) for x in chips]

    own_hidden = hidden_blocks(place, pieces, weights, width)
    scaled = scaled_rows(place, pieces, width, block)
    hidden = [own_hidden] + [partner(own_hidden, "dp", k) for k in range(1, groups)]
    packed = update_pieces(place, hidden, scaled, down[0], moment1[0], moment2[0], experts)
    spread = lax.all_to_all(packed, ("expert", "dp"), 0, 0, tiled=True)
    piece_rows = spread.shape[1]
    picked = reorder(placement, spread.reshape(experts, groups * piece_rows, LANES))
    landed = lax.all_to_all(picked, "expert", 0, 0, tiled=True)
    out = unpack(landed.reshape(experts, groups, piece_rows, LANES), width, units // groups)
    return out[None]


def shards(tokens, cotangent, route_ids, *rest):
    every = route_ids.shape[1] == lax.axis_size("expert")
    return (dense if every else routed)(tokens, cotangent, route_ids, *rest)


def solution(mesh):
    placed = (
        P(("expert", "dp"), None),
        P(("expert", "dp"), None),
        P(("expert", "dp"), None),
        P(("expert", "dp"), None),
        P("expert", "dp", None),
        P("expert", "dp", None),
        P("expert", "dp", None),
        P("expert", "dp", None),
        P(),
    )
    return jax.shard_map(
        shards, mesh=mesh, in_specs=placed, out_specs=P("expert", None, "dp"), check_vma=False
    )
```

time: 280 us -> 137 us (0.49)
  waiting for transfers between devices: 174 us -> 38.3 us
  Pallas kernels: 0 us -> 24 us
  other arithmetic: 14.4 us -> 0.59 us
  between operations: 13.6 us -> 0.14 us
  matrix products: 8.76 us -> 0 us
  starting transfers between devices: 15.9 us -> 22.5 us
  local copies, waits for them, and re-layouts: 13.5 us -> 7.34 us
  blocking collectives: 38.6 us -> 43 us
    all_gather x1 -> x0, waiting for transfers between devices: 90.4 us -> none  [shards(): lax.all_gather(gate_up, 'dp', axis=1, tiled=True)[0]]
    reduce_scatter x1 -> x0, waiting for transfers between devices: 58.6 us -> none  [shards(): lax.psum_scatter(lax.dot_general(scaled, hidden, contract_rows, preferred...]
    ppermute x0 -> x16, waiting for transfers between devices: none -> 38.3 us  [partner(): return lax.ppermute(x, axis, [(i, i ^ flip) for i in range(size)])]
    all_to_all x4 -> x0, waiting for transfers between devices: 24.5 us -> none  [the longest x1 12.5 us: shards(): lax.all_to_all(piece_flat, 'expert', split_axis=0, concat_axis=0, tiled=T...]
    pallas_call x0 -> x8, Pallas kernels: none -> 24 us  [the longest x1 5.7 us: reorder(): pl.pallas_call(copy_kernel, out_shape=jax.ShapeDtypeStruct(x.shape, x.dty...]
    ppermute x0 -> x16, starting transfers between devices: none -> 22.5 us  [partner(): return lax.ppermute(x, axis, [(i, i ^ flip) for i in range(size)])]
    all_to_all x4 -> x0, starting transfers between devices: 15.9 us -> none  [the longest x1 5.17 us: shards(): lax.all_to_all(send_gates, 'expert', split_axis=0, concat_axis=0, tiled=T...]
    all_to_all x2 -> x0, other arithmetic: 10.2 us -> none  [the longest x1 5.47 us: shards(): lax.all_to_all(piece_flat, 'expert', split_axis=0, concat_axis=0, tiled=T...]
  transfers between devices with their start and end apart: 6 -> 16, of which waited for: 5 -> 9; matrix products, arithmetic and copies ran while one was open for 3% -> 1% of each run, Pallas kernels for 0% -> 4%
where the time goes in v1:
time: 137 us; the launch traced here: 136 us
  blocking collectives  43 us (31%)
  waiting for transfers between devices  38.3 us (28%)
  Pallas kernels  24 us (18%)
  starting transfers between devices  22.5 us (16%)
  local copies, waits for them, and re-layouts  7.34 us (5%)
    ppermute x16, waiting for transfers between devices, partner(): return lax.ppermute(x, axis, [(i, i ^ flip) for i in range(size)])  38.3 us
    all_to_all x1, blocking collectives, dense(): spread = lax.all_to_all(packed, ('expert', 'dp'), 0, 0, tiled=True)  26.2 us
    ppermute x16, starting transfers between devices, partner(): return lax.ppermute(x, axis, [(i, i ^ flip) for i in range(size)])  22.5 us
    all_to_all x1, blocking collectives, dense(): landed = lax.all_to_all(picked, 'expert', 0, 0, tiled=True)  16.7 us
    pallas_call x1, Pallas kernels, reorder(): pl.pallas_call(copy_kernel, out_shape=jax.ShapeDtypeStruct(x.shape, x.dty...  5.7 us
    unnamed x42, local copies, waits for them, and re-layouts  5.16 us
    pallas_call x1, Pallas kernels, update_pieces(): pl.pallas_call(functools.partial(update_kernel, groups, places), out_shap...  3.87 us
    pallas_call x1, Pallas kernels, unpack(): pl.pallas_call(unpack_kernel, out_shape=jax.ShapeDtypeStruct((width, cols...  3.47 us
  transfers between devices with their start and end apart: 16, of which 9 were waited for; matrix products, arithmetic and copies ran while one was open for 1% of the time, Pallas kernels for 4%

profile of v1, /device:TPU:0, one launch (start us, length us, event | category | flops | bytes accessed | tf_op | source)
XLA Modules:
  0.0 135.8 jit_solution(17798605514539597432)
XLA Ops:
  0.0 0.6 pad_add_fusion.place
  0.6 3.3 %pack_weights.1 = (bf16[512,384]{1,0:T(8,128)(2,1)}, bf16[512,384]{1,0:T(8,128)(2,1)}, bf16[512,384]{1,0:T(8,128)(2,1)}, bf16[512,384]{1,0:T(8,128)(2,1)}) custom-call(s32[2]{0:T(128)} %pad_add_fusion.place, bf16[512,1536]{1,0:T(8,128)(2,1)} %bitcast.23), custom_call_target="tpu_custom_call" | custom-call | tf_op jit(solution)/shard_map/pack_weights/pallas_call | solution.py:158
  3.9 3.0 %collective-permute-start.10 = (bf16[512,384]{1,0:T(8,128)(2,1)}, bf16[512,384]{1,0:T(8,128)(2,1)S(1)}, u32[]{:S(2)}, u32[]{:S(2)}) collective-permute-start(bf16[512,384]{1,0:T(8,128)(2,1)} %get-tuple-element.18), channel_id=1, source_target_pairs={{0,1},{1,0},{2,3},{3,2},{4,5},{5,4},{6,7},{7,6},{8,9},{9,8},{10,11... | collective-permute-start | bytes 1179656 | tf_op jit(solution)/shard_map/ppermute | solution.py:86
  6.9 0.7 copy.10.ids
  7.6 0.7 copy.11.gates
  8.3 1.7 %pack_rows.1 = (bf16[16,2688]{1,0:T(8,128)(2,1)}, bf16[16,2688]{1,0:T(8,128)(2,1)}, bf16[16,2688]{1,0:T(8,128)(2,1)}, bf16[16,2688]{1,0:T(8,128)(2,1)}) custom-call(s32[2]{0:T(128)} %pad_add_fusion.place, bf16[16,2048]{1,0:T(8,128)(2,1)} %tok.1, bf16[16,2048]{1,0:T(8,128)(2,1)} %cot.1, s32[16,8]{1,0:T(8,128)} %copy.10.ids, bf16[16,8]{1,0:T(8,128)(2,1)} %copy.11.gates), custom_call_target="tpu_custom_call" | custom-call | tf_op jit(solution)/shard_map/pack_rows/pallas_call | solution.py:119
  10.0 0.0 collective-permute-start
  10.0 3.0 %collective-permute-start.1 = (bf16[16,2688]{1,0:T(8,128)(2,1)}, bf16[16,2688]{1,0:T(8,128)(2,1)S(1)}, u32[]{:S(2)}, u32[]{:S(2)}) collective-permute-start(bf16[16,2688]{1,0:T(8,128)(2,1)} %get-tuple-element.15), channel_id=1, source_target_pairs={{0,2},{1,3},{2,0},{3,1},{4,6},{5,7},{6,4},{7,5},{8,10},{9,11},{10,... | collective-permute-start | bytes 258056 | tf_op jit(solution)/shard_map/ppermute | solution.py:86
  13.0 1.3 collective-permute-start.2
  14.4 1.7 %collective-permute-start.11 = (bf16[512,384]{1,0:T(8,128)(2,1)}, bf16[512,384]{1,0:T(8,128)(2,1)S(1)}, u32[]{:S(2)}, u32[]{:S(2)}) collective-permute-start(bf16[512,384]{1,0:T(8,128)(2,1)} %get-tuple-element.19), channel_id=1, source_target_pairs={{0,2},{1,3},{2,0},{3,1},{4,6},{5,7},{6,4},{7,5},{8,10},{9,11},{10,... | collective-permute-start | bytes 1179656 | tf_op jit(solution)/shard_map/ppermute | solution.py:86
  16.1 7.5 %collective-permute-done.refs_1_ = bf16[16,2688]{1,0:T(8,128)(2,1)S(1)} collective-permute-done((bf16[16,2688]{1,0:T(8,128)(2,1)}, bf16[16,2688]{1,0:T(8,128)(2,1)S(1)}, u32[]{:S(2)}, u32[]{:S(2)}) %collective-permute-start) | collective-permute-done | bytes 86048 | tf_op jit(solution)/shard_map/ppermute | solution.py:86
  23.6 1.6 %collective-permute-done.2.refs_3_ = bf16[16,2688]{1,0:T(8,128)(2,1)S(1)} collective-permute-done((bf16[16,2688]{1,0:T(8,128)(2,1)}, bf16[16,2688]{1,0:T(8,128)(2,1)S(1)}, u32[]{:S(2)}, u32[]{:S(2)}) %collective-permute-start.2) | collective-permute-done | bytes 86048 | tf_op jit(solution)/shard_map/ppermute | solution.py:86
  25.2 0.6 copy-done.17
  25.9 1.8 %order_groups.1 = bf16[4,16,2688]{2,1,0:T(8,128)(2,1)} custom-call(s32[2]{0:T(128)} %pad_add_fusion.place, bf16[16,2688]{1,0:T(8,128)(2,1)} %get-tuple-element.13.refs_0_, bf16[16,2688]{1,0:T(8,128)(2,1)} %copy-done.15, bf16[16,2688]{1,0:T(8,128)(2,1)} %copy-done.16, bf16[16,2688]{1,0:T(8,128)(2,1)} %copy-done.17), custom_call_target="tpu_custom_call" | custom-call | tf_op jit(solution)/shard_map/order_groups/pallas_call | solution.py:174
  27.6 1.5 %collective-permute-start.3 = (bf16[64,2688]{1,0:T(8,128)(2,1)}, bf16[64,2688]{1,0:T(8,128)(2,1)S(1)}, u32[]{:S(2)}, u32[]{:S(2)}) collective-permute-start(bf16[64,2688]{1,0:T(8,128)(2,1)} %bitcast.10), channel_id=1, source_target_pairs={{0,8},{4,12},{8,0},{12,4},{16,24},{20,28},{24,16},{28,20},{1,9},{5... | collective-permute-start | bytes 1032200 | tf_op jit(solution)/shard_map/ppermute | solution.py:86
  29.1 1.5 %collective-permute-start.4 = (bf16[64,2688]{1,0:T(8,128)(2,1)}, bf16[64,2688]{1,0:T(8,128)(2,1)S(1)}, u32[]{:S(2)}, u32[]{:S(2)}) collective-permute-start(bf16[64,2688]{1,0:T(8,128)(2,1)} %bitcast.11), channel_id=1, source_target_pairs={{0,16},{4,20},{8,24},{12,28},{16,0},{20,4},{24,8},{28,12},{1,17},{... | collective-permute-start | bytes 1032200 | tf_op jit(solution)/shard_map/ppermute | solution.py:86
  30.6 0.5 collective-permute-start.5
  31.1 0.0 collective-permute-done.10.refs_9_
  31.1 1.6 %collective-permute-start.12 = (bf16[512,384]{1,0:T(8,128)(2,1)}, bf16[512,384]{1,0:T(8,128)(2,1)S(1)}, u32[]{:S(2)}, u32[]{:S(2)}) collective-permute-start(bf16[512,384]{1,0:T(8,128)(2,1)} %get-tuple-element.20), channel_id=1, source_target_pairs={{0,3},{1,2},{2,1},{3,0},{4,7},{5,6},{6,5},{7,4},{8,11},{9,10},{10,... | collective-permute-start | bytes 1179656 | tf_op jit(solution)/shard_map/ppermute | solution.py:86
  32.8 15.9 %collective-permute-done.11.refs_10_ = bf16[512,384]{1,0:T(8,128)(2,1)S(1)} collective-permute-done((bf16[512,384]{1,0:T(8,128)(2,1)}, bf16[512,384]{1,0:T(8,128)(2,1)S(1)}, u32[]{:S(2)}, u32[]{:S(2)}) %collective-permute-start.11) | collective-permute-done | bytes 393248 | tf_op jit(solution)/shard_map/ppermute | solution.py:86
  48.6 0.0 collective-permute-start.6
  48.6 0.0 collective-permute-done.3.refs_1_.refs_9_
  48.6 0.5 collective-permute-start.7
  49.1 0.0 collective-permute-done.4.refs_2_.refs_10_
  49.1 0.1 collective-permute-start.8
  49.2 0.4 collective-permute-start.9
  49.7 0.8 collective-permute-done.6.refs_4_.refs_12_
  50.5 0.3 collective-permute-done.7.refs_5_.refs_13_
  50.8 0.5 collective-permute-done.8.refs_6_.refs_14_
  51.3 0.5 collective-permute-done.9.refs_7_.refs_15_
  51.8 1.1 copy-done
  52.9 1.0 copy-done.12
  53.9 2.1 %hidden_blocks.1.refs_0_ = bf16[768,128]{1,0:T(8,128)(2,1)S(1)} custom-call(s32[2]{0:T(128)S(1)} %copy-done.13, bf16[64,2688]{1,0:T(8,128)(2,1)S(1)} %bitcast.16, bf16[64,2688]{1,0:T(8,128)(2,1)S(1)} %collective-permute-done.3.refs_1_.refs_9_, bf16[64,2688]{1,0:T(8,128)(2,1)S(1)} %collective-permute-done.4.refs_2_.refs_10_, ...), custom_call_target="tpu_custom_call" | custom-call | tf_op jit(solution)/shard_map/hidden_blocks/pallas_call | solution.py:206
  56.0 0.0 copy-start.9
  56.0 4.2 %collective-permute-start.13 = (bf16[768,128]{1,0:T(8,128)(2,1)S(1)}, bf16[768,128]{1,0:T(8,128)(2,1)}, u32[]{:S(2)}, u32[]{:S(2)}) collective-permute-start(bf16[768,128]{1,0:T(8,128)(2,1)S(1)} %hidden_blocks.1.refs_0_), channel_id=1, source_target_pairs={{0,1},{1,0},{2,3},{3,2},{4,5},{5,4},{6,7},{7,6},{8,9},{9,8},{10,11... | collective-permute-start | bytes 589832 | tf_op jit(solution)/shard_map/ppermute | solution.py:86
  60.2 1.6 %collective-permute-start.14 = (bf16[768,128]{1,0:T(8,128)(2,1)S(1)}, bf16[768,128]{1,0:T(8,128)(2,1)S(1)}, u32[]{:S(2)}, u32[]{:S(2)}) collective-permute-start(bf16[768,128]{1,0:T(8,128)(2,1)S(1)} %hidden_blocks.1.refs_0_), channel_id=1, source_target_pairs={{0,2},{1,3},{2,0},{3,1},{4,6},{5,7},{6,4},{7,5},{8,10},{9,11},{10,... | collective-permute-start | bytes 589832 | tf_op jit(solution)/shard_map/ppermute | solution.py:86
  61.9 1.4 %collective-permute-start.15 = (bf16[768,128]{1,0:T(8,128)(2,1)S(1)}, bf16[768,128]{1,0:T(8,128)(2,1)S(1)}, u32[]{:S(2)}, u32[]{:S(2)}) collective-permute-start(bf16[768,128]{1,0:T(8,128)(2,1)S(1)} %hidden_blocks.1.refs_0_), channel_id=1, source_target_pairs={{0,3},{1,2},{2,1},{3,0},{4,7},{5,6},{6,5},{7,4},{8,11},{9,10},{10,... | collective-permute-start | bytes 589832 | tf_op jit(solution)/shard_map/ppermute | solution.py:86
  63.2 2.1 %scaled_rows.1.refs_4_ = bf16[512,512]{1,0:T(8,128)(2,1)} custom-call(s32[2]{0:T(128)} %pad_add_fusion.place, bf16[64,2688]{1,0:T(8,128)(2,1)} %bitcast.14, bf16[64,2688]{1,0:T(8,128)(2,1)} %copy-done.1, bf16[64,2688]{1,0:T(8,128)(2,1)} %copy-done.2, bf16[64,2688]{1,0:T(8,128)(2,1)} %copy-done.3, bf16[64,2688]{1,0:T(8,128)(2,1)} %copy-done.4, ...), custom_call_target="tpu_custom_call" | custom-call | tf_op jit(solution)/shard_map/scaled_rows/pallas_call | solution.py:232
  65.3 1.0 collective-permute-done.13.refs_1_
  66.3 10.2 %collective-permute-done.14.refs_2_ = bf16[768,128]{1,0:T(8,128)(2,1)S(1)} collective-permute-done((bf16[768,128]{1,0:T(8,128)(2,1)S(1)}, bf16[768,128]{1,0:T(8,128)(2,1)S(1)}, u32[]{:S(2)}, u32[]{:S(2)}) %collective-permute-start.14) | collective-permute-done | bytes 196640 | tf_op jit(solution)/shard_map/ppermute | solution.py:86
  76.6 0.0 copy-start.8
  76.6 1.0 copy-done.8
  77.6 3.9 %update_pieces.1 = bf16[32,96,128]{2,1,0:T(8,128)(2,1)S(1)} custom-call(s32[2]{0:T(128)S(1)} %copy-done.14, bf16[768,128]{1,0:T(8,128)(2,1)S(1)} %hidden_blocks.1.refs_0_, bf16[768,128]{1,0:T(8,128)(2,1)} %collective-permute-done.13.refs_1_, bf16[768,128]{1,0:T(8,128)(2,1)S(1)} %collective-permute-done.14.refs_2_, ...), custom_call_target="tpu_custom_call" | custom-call | tf_op jit(solution)/shard_map/update_pieces/pallas_call | solution.py:287
  81.5 26.2 %all_to_all.10 = bf16[32,96,128]{2,1,0:T(8,128)(2,1)} all-to-all(bf16[32,96,128]{2,1,0:T(8,128)(2,1)S(1)} %update_pieces.1), channel_id=1, replica_groups=mesh['expert'=8,'dp'=4] {'expert','dp'}, dimensions={0} | all-to-all | bytes 1572864 | tf_op jit(solution)/shard_map/all_to_all | solution.py:365
  107.7 5.7 %reorder.1 = bf16[8,384,128]{2,1,0:T(8,128)(2,1)} custom-call(s32[8]{0:T(128)} %order.1, bf16[8,384,128]{2,1,0:T(8,128)(2,1)} %bitcast.22), custom_call_target="tpu_custom_call" | custom-call | tf_op jit(solution)/shard_map/reorder/pallas_call | solution.py:308
  113.4 16.7 %all_to_all.11 = bf16[8,384,128]{2,1,0:T(8,128)(2,1)} all-to-all(bf16[8,384,128]{2,1,0:T(8,128)(2,1)} %reorder.1), channel_id=1, replica_groups=mesh['expert'=8,'dp'=4] {'expert'}, dimensions={0} | all-to-all | bytes 1572864 | tf_op jit(solution)/shard_map/all_to_all | solution.py:368
  130.2 3.5 %unpack.1 = bf16[2048,192]{1,0:T(8,128)(2,1)} custom-call(bf16[8,4,96,128]{3,2,1,0:T(8,128)(2,1)} %bitcast.21), custom_call_target="tpu_custom_call" | custom-call | tf_op jit(solution)/shard_map/unpack/pallas_call | solution.py:333
  133.6 2.2 %copy.12 = bf16[1,2048,192]{1,2,0:T(8,128)(2,1)} copy(bf16[1,2048,192]{2,1,0:T(8,128)(2,1)} %bitcast.20) | data formatting | bytes 1572864 | tf_op jit(solution)/shard_map/broadcast_in_dim | solution.py:370
  (38 shorter events, 0.1 us)
Async XLA Ops:
  0.0 6.9 %copy-start.18 = (s32[16,8]{0,1:T(8,128)S(1)}, s32[16,8]{0,1:T(8,128)}, u32[]{:S(2)}) copy-start(s32[16,8]{0,1:T(8,128)} %param.11) | copy-start | bytes 1540
  0.0 7.6 %copy-start.19 = (bf16[16,8]{0,1:T(8,128)(2,1)S(1)}, bf16[16,8]{0,1:T(8,128)(2,1)}, u32[]{:S(2)}) copy-start(bf16[16,8]{0,1:T(8,128)(2,1)} %param.12) | copy-start | bytes 772
  0.6 51.2 %copy-start.13 = (s32[2]{0:T(128)S(1)}, s32[2]{0:T(128)}, u32[]{:S(2)}) copy-start(s32[2]{0:T(128)} %pad_add_fusion.place) | copy-start | bytes 28
  3.9 27.2 %collective-permute-start.10 = (bf16[512,384]{1,0:T(8,128)(2,1)}, bf16[512,384]{1,0:T(8,128)(2,1)S(1)}, u32[]{:S(2)}, u32[]{:S(2)}) collective-permute-start(bf16[512,384]{1,0:T(8,128)(2,1)} %get-tuple-element.18), channel_id=1, source_target_pairs={{0,1},{1,0},{2,3},{3,2},{4,5},{5,4},{6,7},{7,6},{8,9},{9,8},{10,11... | collective-permute-start | bytes 1179656 | tf_op jit(solution)/shard_map/ppermute | solution.py:86
  10.0 13.6 %collective-permute-start = (bf16[16,2688]{1,0:T(8,128)(2,1)}, bf16[16,2688]{1,0:T(8,128)(2,1)S(1)}, u32[]{:S(2)}, u32[]{:S(2)}) collective-permute-start(bf16[16,2688]{1,0:T(8,128)(2,1)} %get-tuple-element.14), channel_id=1, source_target_pairs={{0,1},{1,0},{2,3},{3,2},{4,5},{5,4},{6,7},{7,6},{8,9},{9,8},{10,11... | collective-permute-start | bytes 258056 | tf_op jit(solution)/shard_map/ppermute | solution.py:86
  10.0 13.6 %collective-permute-start.1 = (bf16[16,2688]{1,0:T(8,128)(2,1)}, bf16[16,2688]{1,0:T(8,128)(2,1)S(1)}, u32[]{:S(2)}, u32[]{:S(2)}) collective-permute-start(bf16[16,2688]{1,0:T(8,128)(2,1)} %get-tuple-element.15), channel_id=1, source_target_pairs={{0,2},{1,3},{2,0},{3,1},{4,6},{5,7},{6,4},{7,5},{8,10},{9,11},{10,... | collective-permute-start | bytes 258056 | tf_op jit(solution)/shard_map/ppermute | solution.py:86
  13.0 12.2 %collective-permute-start.2 = (bf16[16,2688]{1,0:T(8,128)(2,1)}, bf16[16,2688]{1,0:T(8,128)(2,1)S(1)}, u32[]{:S(2)}, u32[]{:S(2)}) collective-permute-start(bf16[16,2688]{1,0:T(8,128)(2,1)} %get-tuple-element.16), channel_id=1, source_target_pairs={{0,3},{1,2},{2,1},{3,0},{4,7},{5,6},{6,5},{7,4},{8,11},{9,10},{10,... | collective-permute-start | bytes 258056 | tf_op jit(solution)/shard_map/ppermute | solution.py:86
  14.4 34.2 %collective-permute-start.11 = (bf16[512,384]{1,0:T(8,128)(2,1)}, bf16[512,384]{1,0:T(8,128)(2,1)S(1)}, u32[]{:S(2)}, u32[]{:S(2)}) collective-permute-start(bf16[512,384]{1,0:T(8,128)(2,1)} %get-tuple-element.19), channel_id=1, source_target_pairs={{0,2},{1,3},{2,0},{3,1},{4,6},{5,7},{6,4},{7,5},{8,10},{9,11},{10,... | collective-permute-start | bytes 1179656 | tf_op jit(solution)/shard_map/ppermute | solution.py:86
  23.6 1.6 %copy-start.15 = (bf16[16,2688]{1,0:T(8,128)(2,1)}, bf16[16,2688]{1,0:T(8,128)(2,1)S(1)}, u32[]{:S(2)}) copy-start(bf16[16,2688]{1,0:T(8,128)(2,1)S(1)} %collective-permute-done.refs_1_) | copy-start | bytes 258052
  23.6 1.6 %copy-start.16 = (bf16[16,2688]{1,0:T(8,128)(2,1)}, bf16[16,2688]{1,0:T(8,128)(2,1)S(1)}, u32[]{:S(2)}) copy-start(bf16[16,2688]{1,0:T(8,128)(2,1)S(1)} %collective-permute-done.1.refs_2_) | copy-start | bytes 258052
  25.2 0.6 copy-start.17
  27.6 21.0 %collective-permute-start.3 = (bf16[64,2688]{1,0:T(8,128)(2,1)}, bf16[64,2688]{1,0:T(8,128)(2,1)S(1)}, u32[]{:S(2)}, u32[]{:S(2)}) collective-permute-start(bf16[64,2688]{1,0:T(8,128)(2,1)} %bitcast.10), channel_id=1, source_target_pairs={{0,8},{4,12},{8,0},{12,4},{16,24},{20,28},{24,16},{28,20},{1,9},{5... | collective-permute-start | bytes 1032200 | tf_op jit(solution)/shard_map/ppermute | solution.py:86
  29.1 20.0 %collective-permute-start.4 = (bf16[64,2688]{1,0:T(8,128)(2,1)}, bf16[64,2688]{1,0:T(8,128)(2,1)S(1)}, u32[]{:S(2)}, u32[]{:S(2)}) collective-permute-start(bf16[64,2688]{1,0:T(8,128)(2,1)} %bitcast.11), channel_id=1, source_target_pairs={{0,16},{4,20},{8,24},{12,28},{16,0},{20,4},{24,8},{28,12},{1,17},{... | collective-permute-start | bytes 1032200 | tf_op jit(solution)/shard_map/ppermute | solution.py:86
  30.6 18.6 %collective-permute-start.5 = (bf16[64,2688]{1,0:T(8,128)(2,1)}, bf16[64,2688]{1,0:T(8,128)(2,1)S(1)}, u32[]{:S(2)}, u32[]{:S(2)}) collective-permute-start(bf16[64,2688]{1,0:T(8,128)(2,1)} %bitcast.12), channel_id=1, source_target_pairs={{0,24},{4,28},{8,16},{12,20},{16,8},{20,12},{24,0},{28,4},{1,25},{... | collective-permute-start | bytes 1032200 | tf_op jit(solution)/shard_map/ppermute | solution.py:86
  31.1 18.5 %collective-permute-start.12 = (bf16[512,384]{1,0:T(8,128)(2,1)}, bf16[512,384]{1,0:T(8,128)(2,1)S(1)}, u32[]{:S(2)}, u32[]{:S(2)}) collective-permute-start(bf16[512,384]{1,0:T(8,128)(2,1)} %get-tuple-element.20), channel_id=1, source_target_pairs={{0,3},{1,2},{2,1},{3,0},{4,7},{5,6},{6,5},{7,4},{8,11},{9,10},{10,... | collective-permute-start | bytes 1179656 | tf_op jit(solution)/shard_map/ppermute | solution.py:86
  48.6 1.9 %collective-permute-start.6 = (bf16[64,2688]{1,0:T(8,128)(2,1)}, bf16[64,2688]{1,0:T(8,128)(2,1)S(1)}, u32[]{:S(2)}, u32[]{:S(2)}) collective-permute-start(bf16[64,2688]{1,0:T(8,128)(2,1)} %bitcast.13), channel_id=1, source_target_pairs={{0,4},{4,0},{8,12},{12,8},{16,20},{20,16},{24,28},{28,24},{1,5},{5... | collective-permute-start | bytes 1032200 | tf_op jit(solution)/shard_map/ppermute | solution.py:86
  48.6 7.3 %copy-start.1 = (bf16[64,2688]{1,0:T(8,128)(2,1)}, bf16[64,2688]{1,0:T(8,128)(2,1)S(1)}, u32[]{:S(2)}) copy-start(bf16[64,2688]{1,0:T(8,128)(2,1)S(1)} %collective-permute-done.3.refs_1_.refs_9_) | copy-start | bytes 1032196
  48.6 2.1 %collective-permute-start.7 = (bf16[64,2688]{1,0:T(8,128)(2,1)S(1)}, bf16[64,2688]{1,0:T(8,128)(2,1)S(1)}, u32[]{:S(2)}, u32[]{:S(2)}) collective-permute-start(bf16[64,2688]{1,0:T(8,128)(2,1)S(1)} %collective-permute-done.3.refs_1_.refs_9_), channel_id=1, source_target_pairs={{0,4},{4,0},{8,12},{12,8},{16,20},{20,16},{24,28},{28,24},{1,5},{5... | collective-permute-start | bytes 1032200 | tf_op jit(solution)/shard_map/ppermute | solution.py:86
  49.1 6.8 %copy-start.2 = (bf16[64,2688]{1,0:T(8,128)(2,1)}, bf16[64,2688]{1,0:T(8,128)(2,1)S(1)}, u32[]{:S(2)}) copy-start(bf16[64,2688]{1,0:T(8,128)(2,1)S(1)} %collective-permute-done.4.refs_2_.refs_10_) | copy-start | bytes 1032196
  49.1 2.1 %collective-permute-start.8 = (bf16[64,2688]{1,0:T(8,128)(2,1)S(1)}, bf16[64,2688]{1,0:T(8,128)(2,1)S(1)}, u32[]{:S(2)}, u32[]{:S(2)}) collective-permute-start(bf16[64,2688]{1,0:T(8,128)(2,1)S(1)} %collective-permute-done.4.refs_2_.refs_10_), channel_id=1, source_target_pairs={{0,4},{4,0},{8,12},{12,8},{16,20},{20,16},{24,28},{28,24},{1,5},{5... | collective-permute-start | bytes 1032200 | tf_op jit(solution)/shard_map/ppermute | solution.py:86
  49.2 6.7 %copy-start.3 = (bf16[64,2688]{1,0:T(8,128)(2,1)}, bf16[64,2688]{1,0:T(8,128)(2,1)S(1)}, u32[]{:S(2)}) copy-start(bf16[64,2688]{1,0:T(8,128)(2,1)S(1)} %collective-permute-done.5.refs_3_.refs_11_) | copy-start | bytes 1032196
  49.2 2.5 %collective-permute-start.9 = (bf16[64,2688]{1,0:T(8,128)(2,1)S(1)}, bf16[64,2688]{1,0:T(8,128)(2,1)S(1)}, u32[]{:S(2)}, u32[]{:S(2)}) collective-permute-start(bf16[64,2688]{1,0:T(8,128)(2,1)S(1)} %collective-permute-done.5.refs_3_.refs_11_), channel_id=1, source_target_pairs={{0,4},{4,0},{8,12},{12,8},{16,20},{20,16},{24,28},{28,24},{1,5},{5... | collective-permute-start | bytes 1032200 | tf_op jit(solution)/shard_map/ppermute | solution.py:86
  50.5 5.5 %copy-start.4 = (bf16[64,2688]{1,0:T(8,128)(2,1)}, bf16[64,2688]{1,0:T(8,128)(2,1)S(1)}, u32[]{:S(2)}) copy-start(bf16[64,2688]{1,0:T(8,128)(2,1)S(1)} %collective-permute-done.6.refs_4_.refs_12_) | copy-start | bytes 1032196
  50.8 5.2 %copy-start.5 = (bf16[64,2688]{1,0:T(8,128)(2,1)}, bf16[64,2688]{1,0:T(8,128)(2,1)S(1)}, u32[]{:S(2)}) copy-start(bf16[64,2688]{1,0:T(8,128)(2,1)S(1)} %collective-permute-done.7.refs_5_.refs_13_) | copy-start | bytes 1032196
  51.3 4.7 %copy-start.6 = (bf16[64,2688]{1,0:T(8,128)(2,1)}, bf16[64,2688]{1,0:T(8,128)(2,1)S(1)}, u32[]{:S(2)}) copy-start(bf16[64,2688]{1,0:T(8,128)(2,1)S(1)} %collective-permute-done.8.refs_6_.refs_14_) | copy-start | bytes 1032196
  51.7 4.2 %copy-start.7 = (bf16[64,2688]{1,0:T(8,128)(2,1)}, bf16[64,2688]{1,0:T(8,128)(2,1)S(1)}, u32[]{:S(2)}) copy-start(bf16[64,2688]{1,0:T(8,128)(2,1)S(1)} %collective-permute-done.9.refs_7_.refs_15_) | copy-start | bytes 1032196
  51.8 1.1 copy-start
  52.9 1.0 copy-start.12
  56.0 20.6 %copy-start.9 = (bf16[1,512,768]{2,1,0:T(8,128)(2,1)S(1)}, bf16[1,512,768]{2,1,0:T(8,128)(2,1)}, u32[]{:S(2)}) copy-start(bf16[1,512,768]{2,1,0:T(8,128)(2,1)} %param.14) | copy-start | bytes 2359300
  56.0 20.6 %copy-start.14 = (s32[2]{0:T(128)S(1)}, s32[2]{0:T(128)}, u32[]{:S(2)}) copy-start(s32[2]{0:T(128)} %pad_add_fusion.place) | copy-start | bytes 28
  56.0 10.3 %collective-permute-start.13 = (bf16[768,128]{1,0:T(8,128)(2,1)S(1)}, bf16[768,128]{1,0:T(8,128)(2,1)}, u32[]{:S(2)}, u32[]{:S(2)}) collective-permute-start(bf16[768,128]{1,0:T(8,128)(2,1)S(1)} %hidden_blocks.1.refs_0_), channel_id=1, source_target_pairs={{0,1},{1,0},{2,3},{3,2},{4,5},{5,4},{6,7},{7,6},{8,9},{9,8},{10,11... | collective-permute-start | bytes 589832 | tf_op jit(solution)/shard_map/ppermute | solution.py:86
  60.2 16.3 %copy-start.10 = (bf16[1,512,768]{2,1,0:T(8,128)(2,1)S(1)}, bf16[1,512,768]{2,1,0:T(8,128)(2,1)}, u32[]{:S(2)}) copy-start(bf16[1,512,768]{2,1,0:T(8,128)(2,1)} %param.15) | copy-start | bytes 2359300
  60.2 16.3 %copy-start.11 = (bf16[1,512,768]{2,1,0:T(8,128)(2,1)S(1)}, bf16[1,512,768]{2,1,0:T(8,128)(2,1)}, u32[]{:S(2)}) copy-start(bf16[1,512,768]{2,1,0:T(8,128)(2,1)} %param.16) | copy-start | bytes 2359300
  60.2 16.3 %collective-permute-start.14 = (bf16[768,128]{1,0:T(8,128)(2,1)S(1)}, bf16[768,128]{1,0:T(8,128)(2,1)S(1)}, u32[]{:S(2)}, u32[]{:S(2)}) collective-permute-start(bf16[768,128]{1,0:T(8,128)(2,1)S(1)} %hidden_blocks.1.refs_0_), channel_id=1, source_target_pairs={{0,2},{1,3},{2,0},{3,1},{4,6},{5,7},{6,4},{7,5},{8,10},{9,11},{10,... | collective-permute-start | bytes 589832 | tf_op jit(solution)/shard_map/ppermute | solution.py:86
  61.9 14.7 %collective-permute-start.15 = (bf16[768,128]{1,0:T(8,128)(2,1)S(1)}, bf16[768,128]{1,0:T(8,128)(2,1)S(1)}, u32[]{:S(2)}, u32[]{:S(2)}) collective-permute-start(bf16[768,128]{1,0:T(8,128)(2,1)S(1)} %hidden_blocks.1.refs_0_), channel_id=1, source_target_pairs={{0,3},{1,2},{2,1},{3,0},{4,7},{5,6},{6,5},{7,4},{8,11},{9,10},{10,... | collective-permute-start | bytes 589832 | tf_op jit(solution)/shard_map/ppermute | solution.py:86
  76.6 1.0 copy-start.8

commit v2 on v1

v2 whole, which is shorter than its diff:
```python
import functools

import jax
import jax.numpy as jnp
from jax import lax
from jax.experimental import pallas as pl
from jax.experimental.pallas import tpu as pltpu
from jax.sharding import PartitionSpec as P

OPT_STEP = 2


BETA_ONE = 0.9
BETA_TWO = 0.95
ADAM_EPS = 1e-08
LEARN_RATE = 0.25

BF16 = jnp.bfloat16
F32 = jnp.float32
LANES = 128
HALF = LANES // 2
VMEM_BYTES = 48 * 1024 * 1024


def adam(down, moment1, moment2, grad):
    correct_one = 1.0 - BETA_ONE**OPT_STEP
    correct_two = 1.0 - BETA_TWO**OPT_STEP
    first = BETA_ONE * moment1.astype(F32) + (1.0 - BETA_ONE) * grad
    second = BETA_TWO * moment2.astype(F32) + (1.0 - BETA_TWO) * grad * grad
    direction = first / correct_one / (jnp.sqrt(second / correct_two) + ADAM_EPS)
    return (down.astype(F32) - LEARN_RATE * direction).astype(BF16)


def routed(tokens, cotangent, route_ids, route_gates, gate_up, down, moment1, moment2, placement):
    experts = lax.axis_size("expert")
    tok_rows = tokens.shape[0]
    width = tokens.shape[1]
    top_count = route_ids.shape[1]
    hidden_units = down.shape[2]
    capacity = min(tok_rows, 2 * tok_rows * top_count // experts)
    total_slots = experts * capacity
    route_hits = jnp.sum(
        (route_ids[:, :, None] == jnp.arange(experts, dtype=jnp.int32)).astype(jnp.int32), axis=1
    )
    earlier_hits = jnp.cumsum(route_hits, axis=0) - route_hits
    slot_index = jnp.take_along_axis(earlier_hits, route_ids, axis=1)
    target_slot = route_ids * capacity + slot_index
    matched = (target_slot[:, :, None] == jnp.arange(total_slots, dtype=jnp.int32)).astype(F32)
    picker = jnp.sum(matched, axis=1).astype(BF16)
    contract_rows = (((0,), (0,)), ((), ()))
    send_rows = lax.dot_general(picker, tokens, contract_rows, preferred_element_type=F32)
    send_rows = send_rows.astype(BF16).reshape(experts, capacity, width)
    send_grads = lax.dot_general(picker, cotangent, contract_rows, preferred_element_type=F32)
    send_grads = send_grads.astype(BF16).reshape(experts, capacity, width)
    send_gates = jnp.sum(matched * route_gates.astype(F32)[:, :, None], axis=(0, 1))
    send_gates = send_gates.astype(BF16).reshape(experts, capacity)
    rows_in, grads_in, gates_in = (
        lax.all_to_all(send_rows, "expert", split_axis=0, concat_axis=0, tiled=True),
        lax.all_to_all(send_grads, "expert", split_axis=0, concat_axis=0, tiled=True),
        lax.all_to_all(send_gates, "expert", split_axis=0, concat_axis=0, tiled=True),
    )
    pre_all = jnp.dot(
        rows_in.reshape(total_slots, width),
        lax.all_gather(gate_up, "dp", axis=1, tiled=True)[0],
        preferred_element_type=F32,
    )
    hidden = (jax.nn.silu(pre_all[:, :hidden_units]) * pre_all[:, hidden_units:]).astype(BF16)
    scaled = gates_in.reshape(total_slots, 1).astype(F32) * grads_in.reshape(
        total_slots, width
    ).astype(F32)
    partial = lax.dot_general(
        scaled.astype(BF16), hidden, contract_rows, preferred_element_type=F32
    ).astype(BF16)
    grad_share = lax.psum_scatter(partial, "dp", scatter_dimension=0, tiled=True).astype(F32)
    updated = adam(down[0], moment1[0], moment2[0], grad_share)
    column_block = lax.all_to_all(updated, "dp", split_axis=1, concat_axis=0, tiled=True)
    block_cols = column_block.shape[1]
    piece_flat = column_block.reshape(experts, width * block_cols // experts)
    spread = lax.all_to_all(piece_flat, "expert", split_axis=0, concat_axis=0, tiled=True)
    picked = jnp.take(spread, placement, axis=0)
    landed = lax.all_to_all(picked, "expert", split_axis=0, concat_axis=0, tiled=True)
    return landed.reshape(1, width, block_cols)


def partner(x, axis, flip):
    size = lax.axis_size(axis)
    return lax.ppermute(x, axis, [(i, i ^ flip) for i in range(size)])


def smem():
    return pl.BlockSpec(memory_space=pltpu.SMEM)


def whole():
    return pl.BlockSpec(memory_space=pltpu.VMEM)


def pack_rows_kernel(place, tok, cot, ids, gates, *outs):
    groups = len(outs)
    width = tok.shape[1]
    block = width // groups
    group = place[1]
    named = ids[...]
    weights = gates[...].astype(F32)
    expert = lax.broadcasted_iota(jnp.int32, (LANES, named.shape[1]), 0)
    table = jnp.zeros(expert.shape, F32)
    for k in range(named.shape[0]):
        table = table + jnp.where(expert == named[k : k + 1, :], weights[k : k + 1, :], 0.0)
    table = table.T.astype(BF16)
    for flip, out in enumerate(outs):
        start = pl.multiple_of((group ^ flip) * block, LANES)
        out[:, :width] = tok[...]
        out[:, width : width + block] = cot[:, pl.ds(start, block)]
        out[:, width + block :] = table


def pack_rows(place, tokens, cotangent, ids, gates, groups):
    rows, width = tokens.shape
    return pl.pallas_call(
        pack_rows_kernel,
        out_shape=[pltpu.VMEM((rows, width + width // groups + LANES), BF16)] * groups,
        in_specs=[smem()] + [whole()] * 4,
        name="pack_rows",
    )(place, tokens, cotangent, ids.T, gates.T)


def swap_halves(x):
    return jnp.concatenate([x[:, HALF:], x[:, :HALF]], axis=1)


def low_half(shape):
    return lax.broadcasted_iota(jnp.int32, shape, 1) < HALF


def pack_weights_kernel(parts, place, weights, *outs):
    groups = len(parts)
    hidden_units = weights.shape[1] // 2
    group = place[1]

    def write(flip, start, value):
        first = sum(parts[:flip])
        rows = value.shape[0] // parts[flip]
        for i in range(parts[flip]):
            outs[first + i][:, start : start + LANES] = value[i * rows : (i + 1) * rows]

    for pair in range(groups // 2):
        start = (groups + pair) * LANES
        gate = weights[:, start : start + LANES]
        up = swap_halves(weights[:, hidden_units + start : hidden_units + start + LANES])
        low = low_half(gate.shape)
        even, odd = jnp.where(low, gate, up), jnp.where(low, up, gate)
        for flip in range(groups):

            @pl.when((group ^ flip) == 2 * pair)
            def _():
                write(flip, 2 * LANES, even)

            @pl.when((group ^ flip) == 2 * pair + 1)
            def _():
                write(flip, 2 * LANES, odd)

    for flip in range(groups):
        start = pl.multiple_of((group ^ flip) * LANES, LANES)
        write(flip, 0, weights[:, pl.ds(start, LANES)])
        start = pl.multiple_of(hidden_units + start, LANES)
        write(flip, LANES, weights[:, pl.ds(start, LANES)])


def pack_weights(place, weights, parts):
    rows, cols = weights.shape
    outs = [pltpu.VMEM((rows // n, cols // len(parts)), BF16) for n in parts for _ in range(n)]
    return pl.pallas_call(
        functools.partial(pack_weights_kernel, parts),
        out_shape=outs,
        in_specs=[smem(), whole()],
        compiler_params=pltpu.CompilerParams(vmem_limit_bytes=VMEM_BYTES),
        name="pack_weights",
    )(place, weights)


def after(x, *others):
    return lax.optimization_barrier((x, *others))[0]


def in_vmem(x):
    return pltpu.with_memory_space_constraint(x, pltpu.VMEM)


def order_groups_kernel(place, *refs):
    *blocks, out = refs
    for flip, block in enumerate(blocks):
        out[pl.ds(place[1] ^ flip, 1)] = block[...][None]


def order_groups(place, blocks):
    rows, width = blocks[0].shape
    out = pl.pallas_call(
        order_groups_kernel,
        out_shape=pltpu.VMEM((len(blocks), rows, width), BF16),
        in_specs=[smem()] + [whole()] * len(blocks),
        name="order_groups",
    )(place, *[in_vmem(x) for x in blocks])
    return out.reshape(len(blocks) * rows, width)


def hidden_kernel(groups, pieces, spans, place, *refs):
    row_refs, weight_refs, out, toks = refs[:pieces], refs[pieces:-2], refs[-2], refs[-1]
    rows, width = row_refs[0].shape
    block = width // groups
    total = pieces * rows
    for i, ref in enumerate(row_refs):
        toks[i * rows : (i + 1) * rows, :] = ref[...]
    pre = None
    for (flip, first), ref in zip(spans, weight_refs, strict=True):
        start = pl.multiple_of((place[1] ^ flip) * block + first, LANES)
        depth = ref.shape[0]
        term = jnp.dot(toks[:, pl.ds(start, depth)], ref[...], preferred_element_type=F32)
        pre = term if pre is None else pre + term
    gate, up = pre[:, :LANES], pre[:, LANES : 2 * LANES]
    out[:total, :] = (gate / (1.0 + jnp.exp(-gate)) * up).astype(BF16)
    shared = pre[:, 2 * LANES :]
    narrow = shared / (1.0 + jnp.exp(-shared)) * swap_halves(shared)
    low = low_half((total // 2, LANES))
    top, bottom = narrow[: total // 2], swap_halves(narrow[total // 2 :])
    even = lax.rem(place[1], 2) == 0

    @pl.when(even)
    def _():
        out[total:, :] = jnp.where(low, top, bottom).astype(BF16)

    @pl.when(jnp.logical_not(even))
    def _():
        out[total:, :] = jnp.where(low, bottom, top).astype(BF16)


def hidden_blocks(place, pieces, weights, spans, width, groups):
    rows = pieces[0].shape[0]
    total = rows * len(pieces)
    return pl.pallas_call(
        functools.partial(hidden_kernel, groups, len(pieces), spans),
        out_shape=pltpu.VMEM((total + total // 2, LANES), BF16),
        grid=(1,),
        in_specs=[smem()]
        + [pl.BlockSpec((rows, width), lambda i: (0, 0))] * len(pieces)
        + [pl.BlockSpec(x.shape, lambda i: (0, 0)) for x in weights],
        out_specs=pl.BlockSpec((total + total // 2, LANES), lambda i: (0, 0)),
        scratch_shapes=[pltpu.VMEM((total, width), BF16)],
        compiler_params=pltpu.CompilerParams(vmem_limit_bytes=VMEM_BYTES),
        name="hidden_blocks",
    )(place, *[in_vmem(x) for x in [*pieces, *weights]])


def scaled_kernel(pieces, place, *refs):
    cot_refs, gate_refs, out = refs[:pieces], refs[pieces:-1], refs[-1]
    blocks = []
    for cot, table in zip(cot_refs, gate_refs, strict=True):
        gates = table[...].astype(F32)
        lane = lax.broadcasted_iota(jnp.int32, gates.shape, 1)
        gate = jnp.sum(jnp.where(lane == place[0], gates, 0.0), axis=1, keepdims=True)
        blocks.append((gate * cot[...].astype(F32)).astype(BF16))
    out[...] = jnp.concatenate(blocks, axis=0).T


def scaled_rows(place, pieces, width, block):
    rows = pieces[0].shape[0]
    total = rows * len(pieces)
    return pl.pallas_call(
        functools.partial(scaled_kernel, len(pieces)),
        out_shape=jax.ShapeDtypeStruct((block, total), BF16),
        grid=(1,),
        in_specs=[smem()]
        + [pl.BlockSpec((rows, block), lambda i: (0, width // block))] * len(pieces)
        + [pl.BlockSpec((rows, LANES), lambda i: (0, (width + block) // LANES))] * len(pieces),
        out_specs=pl.BlockSpec((block, total), lambda i: (0, 0)),
        compiler_params=pltpu.CompilerParams(vmem_limit_bytes=VMEM_BYTES),
        name="scaled_rows",
    )(place, *pieces, *pieces)


def update_kernel(groups, place, *refs):
    hid_refs, (scaled, down, first, second, out, hidden) = refs[:groups], refs[groups:]
    total = scaled.shape[1]
    units = down.shape[1]

    @pl.when(pl.program_id(0) == 0)
    def _():
        for own in range(groups):

            @pl.when(place[1] == own)
            def _():
                for col in range(groups):
                    hidden[:, col * LANES : (col + 1) * LANES] = hid_refs[own ^ col][:total, :]
                for col in range(0, groups, 2):
                    even, odd = hid_refs[own ^ col][total:, :], hid_refs[own ^ col ^ 1][total:, :]
                    low = low_half(even.shape)
                    start = (groups + col // 2) * LANES
                    hidden[: total // 2, start : start + LANES] = jnp.where(low, even, odd)
                    hidden[total // 2 :, start : start + LANES] = swap_halves(
                        jnp.where(low, odd, even)
                    )

    grad = jnp.dot(scaled[...], hidden[...], preferred_element_type=F32)
    updated = adam(down[...], first[...], second[...], grad).T
    cols = units // groups
    rows = out.shape[1]
    for i in range(out.shape[0] // groups):
        for col in range(groups):
            start = col * cols + i * rows
            out[i * groups + col] = updated[start : start + rows]


def update_pieces(place, hidden, scaled, down, first, second, experts):
    groups = len(hidden)
    features, total = scaled.shape
    units = down.shape[1]
    steps = features // LANES
    places = experts // steps
    piece_rows = units // groups // places
    return pl.pallas_call(
        functools.partial(update_kernel, groups),
        out_shape=jax.ShapeDtypeStruct((experts * groups, piece_rows, LANES), BF16),
        grid=(steps,),
        in_specs=[smem()]
        + [pl.BlockSpec(hidden[0].shape, lambda i: (0, 0))] * groups
        + [pl.BlockSpec((LANES, total), lambda i: (i, 0))]
        + [pl.BlockSpec((LANES, units), lambda i: (i, 0))] * 3,
        out_specs=pl.BlockSpec((places * groups, piece_rows, LANES), lambda i: (i, 0, 0)),
        scratch_shapes=[pltpu.VMEM((total, units), BF16)],
        compiler_params=pltpu.CompilerParams(vmem_limit_bytes=VMEM_BYTES),
        name="update_pieces",
    )(place, *hidden, scaled, down, first, second)


def pick_kernel(place, order, pieces, *outs):
    for flip, out in enumerate(outs):
        out[...] = pieces[order[place[0] ^ flip]]


def pick(place, order, pieces):
    experts = pieces.shape[0]
    return pl.pallas_call(
        pick_kernel,
        out_shape=[pltpu.VMEM(pieces.shape[1:], pieces.dtype)] * experts,
        in_specs=[smem(), smem(), whole()],
        out_specs=[whole()] * experts,
        name="pick",
    )(place, order, pieces)


def unpack_kernel(place, *refs):
    *pieces, out = refs
    groups, rows, _ = pieces[0].shape
    halves = out.shape[1] // rows
    block = out.shape[2] // groups
    for flip, piece in enumerate(pieces):
        spot = place[0] ^ flip
        top = pl.multiple_of((spot % halves) * rows, 16)
        for group in range(groups):
            left = pl.multiple_of(group * block + (spot // halves) * LANES, LANES)
            out[0, pl.ds(top, rows), pl.ds(left, LANES)] = piece[group]


def unpack(place, pieces, width, cols):
    return pl.pallas_call(
        unpack_kernel,
        out_shape=jax.ShapeDtypeStruct((1, cols, width), BF16),
        in_specs=[smem()] + [whole()] * len(pieces),
        out_specs=whole(),
        name="unpack",
    )(place, *[in_vmem(x) for x in pieces])


def dense(tokens, cotangent, route_ids, route_gates, gate_up, down, moment1, moment2, placement):
    experts = lax.axis_size("expert")
    groups = lax.axis_size("dp")
    width = tokens.shape[1]
    units = down.shape[2]
    block = width // groups
    place = jnp.stack([lax.axis_index("expert"), lax.axis_index("dp")]).astype(jnp.int32)

    parts = (1, 1, 1, 1)
    own, near, far, farthest = pack_weights(place, gate_up[0], parts)
    sent = pack_rows(place, tokens, cotangent, route_ids, route_gates, groups)
    blocks = [sent[0]] + [partner(sent[k], "dp", k) for k in range(1, groups)]
    far = partner(after(far, blocks[1]), "dp", 2)
    weights = [own, partner(after(near, far), "dp", 1), far, partner(after(farthest, far), "dp", 3)]
    spans = [(flip, i * (block // n)) for flip, n in enumerate(parts) for i in range(n)]
    plane = order_groups(place, blocks)
    chips = [plane] + [partner(plane, "expert", k) for k in range(2, experts, 2)]
    pieces = chips + [partner(x, "expert", 1) for x in chips]

    own_hidden = hidden_blocks(place, pieces, weights, spans, width, groups)
    scaled = scaled_rows(place, pieces, width, block)
    hidden = [own_hidden] + [partner(own_hidden, "dp", k) for k in range(1, groups)]
    moved = update_pieces(place, hidden, scaled, down[0], moment1[0], moment2[0], experts)
    spread = lax.all_to_all(moved, ("expert", "dp"), 0, 0, tiled=True)
    picked = pick(place, placement, spread.reshape(experts, groups, *spread.shape[1:]))
    landed = [picked[0]] + [partner(picked[k], "expert", k) for k in range(1, experts)]
    return unpack(place, landed, width, units // groups).transpose(0, 2, 1)


def shards(tokens, cotangent, route_ids, *rest):
    every = route_ids.shape[1] == lax.axis_size("expert")
    return (dense if every else routed)(tokens, cotangent, route_ids, *rest)


def solution(mesh):
    placed = (
        P(("expert", "dp"), None),
        P(("expert", "dp"), None),
        P(("expert", "dp"), None),
        P(("expert", "dp"), None),
        P("expert", "dp", None),
        P("expert", "dp", None),
        P("expert", "dp", None),
        P("expert", "dp", None),
        P(),
    )
    return jax.shard_map(
        shards, mesh=mesh, in_specs=placed, out_specs=P("expert", None, "dp"), check_vma=False
    )
```

time: 137 us -> 115 us (0.84)
  blocking collectives: 43 us -> 25.5 us
  Pallas kernels: 24 us -> 11.7 us
  waiting for transfers between devices: 38.3 us -> 49 us
  local copies, waits for them, and re-layouts: 7.34 us -> 2.07 us
  starting transfers between devices: 22.5 us -> 26.1 us
    all_to_all x2 -> x1, blocking collectives: 43 us -> 25.5 us  [dense(): spread = lax.all_to_all(moved, ('expert', 'dp'), 0, 0, tiled=True)]
    pallas_call x7, Pallas kernels: 21.9 us -> 10.8 us  [the longest x1 3.12 us: update_pieces(): pl.pallas_call(functools.partial(update_kernel, groups), out_shape=jax.Sh...]
    ppermute x16 -> x23, waiting for transfers between devices: 38.3 us -> 49 us  [partner(): return lax.ppermute(x, axis, [(i, i ^ flip) for i in range(size)])]
    ppermute x16 -> x23, starting transfers between devices: 22.5 us -> 26.1 us  [partner(): return lax.ppermute(x, axis, [(i, i ^ flip) for i in range(size)])]
    unnamed x42 -> x12, local copies, waits for them, and re-layouts: 5.16 us -> 2.07 us
    broadcast_in_dim x1 -> x0, local copies, waits for them, and re-layouts: 2.18 us -> none  [dense(): return out[None]]
  transfers between devices with their start and end apart: 16 -> 23, of which waited for: 9 -> 14; matrix products, arithmetic and copies ran while one was open for 1% -> 0% of each run, Pallas kernels for 4% -> 2%
where the time goes in v2:
time: 115 us
  waiting for transfers between devices  49 us (43%)
  starting transfers between devices  26.1 us (23%)
  blocking collectives  25.5 us (22%)
  Pallas kernels  11.7 us (10%)
  local copies, waits for them, and re-layouts  2.07 us (2%)
    ppermute x23, waiting for transfers between devices, partner(): return lax.ppermute(x, axis, [(i, i ^ flip) for i in range(size)])  49 us
    ppermute x23, starting transfers between devices, partner(): return lax.ppermute(x, axis, [(i, i ^ flip) for i in range(size)])  26.1 us
    all_to_all x1, blocking collectives, dense(): spread = lax.all_to_all(moved, ('expert', 'dp'), 0, 0, tiled=True)  25.5 us
    pallas_call x1, Pallas kernels, update_pieces(): pl.pallas_call(functools.partial(update_kernel, groups), out_shape=jax.Sh...  3.12 us
  transfers between devices with their start and end apart: 23, of which 14 were waited for; matrix products, arithmetic and copies ran while one was open for 0% of the time, Pallas kernels for 2%

profile of v2, /device:TPU:0, one launch (start us, length us, event | category | flops | bytes accessed | tf_op | source)
XLA Modules:
  0.0 115.1 jit_solution(3757201493178090843)
XLA Ops:
  0.0 0.6 pad_add_fusion.place
  0.6 1.0 pack_rows.1
  1.6 3.1 %collective-permute-start = (bf16[16,2688]{1,0:T(8,128)(2,1)S(1)}, bf16[16,2688]{1,0:T(8,128)(2,1)S(1)}, u32[]{:S(2)}, u32[]{:S(2)}) collective-permute-start(bf16[16,2688]{1,0:T(8,128)(2,1)S(1)} %get-tuple-element.25), channel_id=1, source_target_pairs={{0,1},{1,0},{2,3},{3,2},{4,5},{5,4},{6,7},{7,6},{8,9},{9,8},{10,11... | collective-permute-start | bytes 258056 | tf_op jit(solution)/shard_map/ppermute | solution.py:87
  4.7 2.6 %collective-permute-start.1 = (bf16[16,2688]{1,0:T(8,128)(2,1)S(1)}, bf16[16,2688]{1,0:T(8,128)(2,1)S(1)}, u32[]{:S(2)}, u32[]{:S(2)}) collective-permute-start(bf16[16,2688]{1,0:T(8,128)(2,1)S(1)} %get-tuple-element.26), channel_id=1, source_target_pairs={{0,2},{1,3},{2,0},{3,1},{4,6},{5,7},{6,4},{7,5},{8,10},{9,11},{10,... | collective-permute-start | bytes 258056 | tf_op jit(solution)/shard_map/ppermute | solution.py:87
  7.3 0.0 collective-permute-start.2
  7.3 1.4 %copy-done = bf16[1,512,1536]{2,1,0:T(8,128)(2,1)S(1)} copy-done((bf16[1,512,1536]{2,1,0:T(8,128)(2,1)S(1)}, bf16[1,512,1536]{2,1,0:T(8,128)(2,1)}, u32[]{:S(2)}) %copy-start) | copy-done | bytes 1572888
  8.7 0.6 copy-done.4
  9.3 1.0 pack_weights.1
  10.4 2.0 %collective-permute-start.10 = (bf16[512,384]{1,0:T(8,128)(2,1)S(1)}, bf16[512,384]{1,0:T(8,128)(2,1)S(1)}, u32[]{:S(2)}, u32[]{:S(2)}) collective-permute-start(bf16[512,384]{1,0:T(8,128)(2,1)S(1)} %get-tuple-element.31), channel_id=1, source_target_pairs={{0,2},{1,3},{2,0},{3,1},{4,6},{5,7},{6,4},{7,5},{8,10},{9,11},{10,... | collective-permute-start | bytes 1179656 | tf_op jit(solution)/shard_map/ppermute | solution.py:87
  12.3 10.4 %collective-permute-done.1.refs_2_ = bf16[16,2688]{1,0:T(8,128)(2,1)S(1)} collective-permute-done((bf16[16,2688]{1,0:T(8,128)(2,1)S(1)}, bf16[16,2688]{1,0:T(8,128)(2,1)S(1)}, u32[]{:S(2)}, u32[]{:S(2)}) %collective-permute-start.1) | collective-permute-done | bytes 86048 | tf_op jit(solution)/shard_map/ppermute | solution.py:87
  22.7 0.7 order_groups.1
  23.4 1.6 %collective-permute-start.3 = (bf16[64,2688]{1,0:T(8,128)(2,1)S(1)}, bf16[64,2688]{1,0:T(8,128)(2,1)S(1)}, u32[]{:S(2)}, u32[]{:S(2)}) collective-permute-start(bf16[64,2688]{1,0:T(8,128)(2,1)S(1)} %bitcast.11), channel_id=1, source_target_pairs={{0,8},{4,12},{8,0},{12,4},{16,24},{20,28},{24,16},{28,20},{1,9},{5... | collective-permute-start | bytes 1032200 | tf_op jit(solution)/shard_map/ppermute | solution.py:87
  24.9 1.5 %collective-permute-start.4 = (bf16[64,2688]{1,0:T(8,128)(2,1)S(1)}, bf16[64,2688]{1,0:T(8,128)(2,1)S(1)}, u32[]{:S(2)}, u32[]{:S(2)}) collective-permute-start(bf16[64,2688]{1,0:T(8,128)(2,1)S(1)} %bitcast.12), channel_id=1, source_target_pairs={{0,16},{4,20},{8,24},{12,28},{16,0},{20,4},{24,8},{28,12},{1,17},{... | collective-permute-start | bytes 1032200 | tf_op jit(solution)/shard_map/ppermute | solution.py:87
  26.5 0.5 collective-permute-start.5
  26.9 5.0 %collective-permute-done.10.refs_10_ = bf16[512,384]{1,0:T(8,128)(2,1)S(1)} collective-permute-done((bf16[512,384]{1,0:T(8,128)(2,1)S(1)}, bf16[512,384]{1,0:T(8,128)(2,1)S(1)}, u32[]{:S(2)}, u32[]{:S(2)}) %collective-permute-start.10) | collective-permute-done | bytes 393248 | tf_op jit(solution)/shard_map/ppermute | solution.py:87
  31.9 2.5 %collective-permute-start.12 = (bf16[512,384]{1,0:T(8,128)(2,1)S(1)}, bf16[512,384]{1,0:T(8,128)(2,1)S(1)}, u32[]{:S(2)}, u32[]{:S(2)}) collective-permute-start(bf16[512,384]{1,0:T(8,128)(2,1)S(1)} %get-tuple-element.34), channel_id=1, source_target_pairs={{0,3},{1,2},{2,1},{3,0},{4,7},{5,6},{6,5},{7,4},{8,11},{9,10},{10,... | collective-permute-start | bytes 1179656 | tf_op jit(solution)/shard_map/ppermute | solution.py:87
  34.4 1.5 %collective-permute-done.4.refs_2_.refs_10_ = bf16[64,2688]{1,0:T(8,128)(2,1)S(1)} collective-permute-done((bf16[64,2688]{1,0:T(8,128)(2,1)S(1)}, bf16[64,2688]{1,0:T(8,128)(2,1)S(1)}, u32[]{:S(2)}, u32[]{:S(2)}) %collective-permute-start.4) | collective-permute-done | bytes 344096 | tf_op jit(solution)/shard_map/ppermute | solution.py:87
  35.9 0.5 collective-permute-start.8
  36.4 0.1 collective-permute-start.9
  36.5 1.1 collective-permute-done.7.refs_5_.refs_13_
  37.5 0.5 collective-permute-done.8.refs_6_.refs_14_
  38.0 0.5 collective-permute-done.9.refs_7_.refs_15_
  38.5 4.7 %collective-permute-done.11.refs_9_ = bf16[512,384]{1,0:T(8,128)(2,1)S(1)} collective-permute-done((bf16[512,384]{1,0:T(8,128)(2,1)S(1)}, bf16[512,384]{1,0:T(8,128)(2,1)S(1)}, u32[]{:S(2)}, u32[]{:S(2)}) %collective-permute-start.11) | collective-permute-done | bytes 393248 | tf_op jit(solution)/shard_map/ppermute | solution.py:87
  43.3 7.9 %collective-permute-done.12.refs_11_ = bf16[512,384]{1,0:T(8,128)(2,1)S(1)} collective-permute-done((bf16[512,384]{1,0:T(8,128)(2,1)S(1)}, bf16[512,384]{1,0:T(8,128)(2,1)S(1)}, u32[]{:S(2)}, u32[]{:S(2)}) %collective-permute-start.12) | collective-permute-done | bytes 393248 | tf_op jit(solution)/shard_map/ppermute | solution.py:87
  51.2 2.1 %hidden_blocks.1.refs_0_ = bf16[768,128]{1,0:T(8,128)(2,1)S(1)} custom-call(s32[2]{0:T(128)S(1)} %copy-done.5, bf16[64,2688]{1,0:T(8,128)(2,1)S(1)} %bitcast.15, bf16[64,2688]{1,0:T(8,128)(2,1)S(1)} %collective-permute-done.3.refs_1_.refs_9_, bf16[64,2688]{1,0:T(8,128)(2,1)S(1)} %collective-permute-done.4.refs_2_.refs_10_, ...), custom_call_target="tpu_custom_call" | custom-call | tf_op jit(solution)/shard_map/hidden_blocks/pallas_call | solution.py:239
  53.2 0.0 copy-start.1
  53.2 0.0 copy-start.2
  53.3 0.0 copy-start.3
  53.3 1.7 %collective-permute-start.13 = (bf16[768,128]{1,0:T(8,128)(2,1)S(1)}, bf16[768,128]{1,0:T(8,128)(2,1)S(1)}, u32[]{:S(2)}, u32[]{:S(2)}) collective-permute-start(bf16[768,128]{1,0:T(8,128)(2,1)S(1)} %hidden_blocks.1.refs_0_), channel_id=1, source_target_pairs={{0,1},{1,0},{2,3},{3,2},{4,5},{5,4},{6,7},{7,6},{8,9},{9,8},{10,11... | collective-permute-start | bytes 589832 | tf_op jit(solution)/shard_map/ppermute | solution.py:87
  54.9 1.5 %collective-permute-start.14 = (bf16[768,128]{1,0:T(8,128)(2,1)S(1)}, bf16[768,128]{1,0:T(8,128)(2,1)S(1)}, u32[]{:S(2)}, u32[]{:S(2)}) collective-permute-start(bf16[768,128]{1,0:T(8,128)(2,1)S(1)} %hidden_blocks.1.refs_0_), channel_id=1, source_target_pairs={{0,2},{1,3},{2,0},{3,1},{4,6},{5,7},{6,4},{7,5},{8,10},{9,11},{10,... | collective-permute-start | bytes 589832 | tf_op jit(solution)/shard_map/ppermute | solution.py:87
  56.5 1.4 %collective-permute-start.15 = (bf16[768,128]{1,0:T(8,128)(2,1)S(1)}, bf16[768,128]{1,0:T(8,128)(2,1)S(1)}, u32[]{:S(2)}, u32[]{:S(2)}) collective-permute-start(bf16[768,128]{1,0:T(8,128)(2,1)S(1)} %hidden_blocks.1.refs_0_), channel_id=1, source_target_pairs={{0,3},{1,2},{2,1},{3,0},{4,7},{5,6},{6,5},{7,4},{8,11},{9,10},{10,... | collective-permute-start | bytes 589832 | tf_op jit(solution)/shard_map/ppermute | solution.py:87
  57.9 0.8 scaled_rows.1.refs_4_
  58.7 4.9 %collective-permute-done.13.refs_1_ = bf16[768,128]{1,0:T(8,128)(2,1)S(1)} collective-permute-done((bf16[768,128]{1,0:T(8,128)(2,1)S(1)}, bf16[768,128]{1,0:T(8,128)(2,1)S(1)}, u32[]{:S(2)}, u32[]{:S(2)}) %collective-permute-start.13) | collective-permute-done | bytes 196640 | tf_op jit(solution)/shard_map/ppermute | solution.py:87
  63.6 5.5 %collective-permute-done.14.refs_2_ = bf16[768,128]{1,0:T(8,128)(2,1)S(1)} collective-permute-done((bf16[768,128]{1,0:T(8,128)(2,1)S(1)}, bf16[768,128]{1,0:T(8,128)(2,1)S(1)}, u32[]{:S(2)}, u32[]{:S(2)}) %collective-permute-start.14) | collective-permute-done | bytes 196640 | tf_op jit(solution)/shard_map/ppermute | solution.py:87
  69.1 3.1 %update_pieces.1 = bf16[32,96,128]{2,1,0:T(8,128)(2,1)S(1)} custom-call(s32[2]{0:T(128)S(1)} %copy-done.5, bf16[768,128]{1,0:T(8,128)(2,1)S(1)} %hidden_blocks.1.refs_0_, bf16[768,128]{1,0:T(8,128)(2,1)S(1)} %collective-permute-done.13.refs_1_, bf16[768,128]{1,0:T(8,128)(2,1)S(1)} %collective-permute-done.14.refs_2_, ...), custom_call_target="tpu_custom_call" | custom-call | tf_op jit(solution)/shard_map/update_pieces/pallas_call | solution.py:319
  72.3 25.5 %all_to_all.5 = bf16[32,96,128]{2,1,0:T(8,128)(2,1)} all-to-all(bf16[32,96,128]{2,1,0:T(8,128)(2,1)S(1)} %update_pieces.1), channel_id=1, replica_groups=mesh['expert'=8,'dp'=4] {'expert','dp'}, dimensions={0} | all-to-all | bytes 1572864 | tf_op jit(solution)/shard_map/all_to_all | solution.py:396
  97.7 1.2 %pick.1 = (bf16[4,96,128]{2,1,0:T(8,128)(2,1)S(1)}, bf16[4,96,128]{2,1,0:T(8,128)(2,1)S(1)}, bf16[4,96,128]{2,1,0:T(8,128)(2,1)S(1)}, bf16[4,96,128]{2,1,0:T(8,1...) custom-call(s32[2]{0:T(128)} %pad_add_fusion.place, ...), custom_call_target="tpu_custom_call" | custom-call | tf_op jit(solution)/shard_map/pick/pallas_call | solution.py:341
  98.9 1.5 %collective-permute-start.16 = (bf16[4,96,128]{2,1,0:T(8,128)(2,1)S(1)}, bf16[4,96,128]{2,1,0:T(8,128)(2,1)S(1)}, u32[]{:S(2)}, u32[]{:S(2)}) collective-permute-start(bf16[4,96,128]{2,1,0:T(8,128)(2,1)S(1)} %get-tuple-element.36), channel_id=1, source_target_pairs={{0,4},{4,0},{8,12},{12,8},{16,20},{20,16},{24,28},{28,24},{1,5},{5... | collective-permute-start | bytes 294920 | tf_op jit(solution)/shard_map/ppermute | solution.py:87
  100.5 1.5 %collective-permute-start.17 = (bf16[4,96,128]{2,1,0:T(8,128)(2,1)S(1)}, bf16[4,96,128]{2,1,0:T(8,128)(2,1)S(1)}, u32[]{:S(2)}, u32[]{:S(2)}) collective-permute-start(bf16[4,96,128]{2,1,0:T(8,128)(2,1)S(1)} %get-tuple-element.37), channel_id=1, source_target_pairs={{0,8},{4,12},{8,0},{12,4},{16,24},{20,28},{24,16},{28,20},{1,9},{5... | collective-permute-start | bytes 294920 | tf_op jit(solution)/shard_map/ppermute | solution.py:87
  101.9 1.4 %collective-permute-start.19 = (bf16[4,96,128]{2,1,0:T(8,128)(2,1)S(1)}, bf16[4,96,128]{2,1,0:T(8,128)(2,1)S(1)}, u32[]{:S(2)}, u32[]{:S(2)}) collective-permute-start(bf16[4,96,128]{2,1,0:T(8,128)(2,1)S(1)} %get-tuple-element.39), channel_id=1, source_target_pairs={{0,16},{4,20},{8,24},{12,28},{16,0},{20,4},{24,8},{28,12},{1,17},{... | collective-permute-start | bytes 294920 | tf_op jit(solution)/shard_map/ppermute | solution.py:87
  103.4 0.6 collective-permute-start.20
  104.0 1.5 %collective-permute-start.21 = (bf16[4,96,128]{2,1,0:T(8,128)(2,1)S(1)}, bf16[4,96,128]{2,1,0:T(8,128)(2,1)S(1)}, u32[]{:S(2)}, u32[]{:S(2)}) collective-permute-start(bf16[4,96,128]{2,1,0:T(8,128)(2,1)S(1)} %get-tuple-element.41), channel_id=1, source_target_pairs={{0,24},{4,28},{8,16},{12,20},{16,8},{20,12},{24,0},{28,4},{1,25},{... | collective-permute-start | bytes 294920 | tf_op jit(solution)/shard_map/ppermute | solution.py:87
  105.4 0.1 collective-permute-done.17.refs_2_
  105.6 0.8 collective-permute-start.22
  106.4 0.7 collective-permute-done.18.refs_3_
  107.0 0.6 collective-permute-done.19.refs_4_
  107.6 5.7 %collective-permute-done.20.refs_5_ = bf16[4,96,128]{2,1,0:T(8,128)(2,1)S(1)} collective-permute-done((bf16[4,96,128]{2,1,0:T(8,128)(2,1)S(1)}, bf16[4,96,128]{2,1,0:T(8,128)(2,1)S(1)}, u32[]{:S(2)}, u32[]{:S(2)}) %collective-permute-start.20) | collective-permute-done | bytes 98336 | tf_op jit(solution)/shard_map/ppermute | solution.py:87
  113.3 1.7 %unpack.1 = bf16[1,192,2048]{2,1,0:T(8,128)(2,1)} custom-call(s32[2]{0:T(128)} %pad_add_fusion.place, bf16[4,96,128]{2,1,0:T(8,128)(2,1)S(1)} %get-tuple-element.35.refs_0_, bf16[4,96,128]{2,1,0:T(8,128)(2,1)S(1)} %collective-permute-done.16.refs_1_, bf16[4,96,128]{2,1,0:T(8,128)(2,1)S(1)} %collective-permute-done.17.refs_2_, ...), custom_call_target="tpu_custom_call" | custom-call | tf_op jit(solution)/shard_map/unpack/pallas_call | solution.py:364
  (20 shorter events, 0.0 us)
Async XLA Ops:
  0.6 50.6 %copy-start.5 = (s32[2]{0:T(128)S(1)}, s32[2]{0:T(128)}, u32[]{:S(2)}) copy-start(s32[2]{0:T(128)} %pad_add_fusion.place) | copy-start | bytes 28
  1.6 8.7 %collective-permute-start = (bf16[16,2688]{1,0:T(8,128)(2,1)S(1)}, bf16[16,2688]{1,0:T(8,128)(2,1)S(1)}, u32[]{:S(2)}, u32[]{:S(2)}) collective-permute-start(bf16[16,2688]{1,0:T(8,128)(2,1)S(1)} %get-tuple-element.25), channel_id=1, source_target_pairs={{0,1},{1,0},{2,3},{3,2},{4,5},{5,4},{6,7},{7,6},{8,9},{9,8},{10,11... | collective-permute-start | bytes 258056 | tf_op jit(solution)/shard_map/ppermute | solution.py:87
  4.7 18.0 %collective-permute-start.1 = (bf16[16,2688]{1,0:T(8,128)(2,1)S(1)}, bf16[16,2688]{1,0:T(8,128)(2,1)S(1)}, u32[]{:S(2)}, u32[]{:S(2)}) collective-permute-start(bf16[16,2688]{1,0:T(8,128)(2,1)S(1)} %get-tuple-element.26), channel_id=1, source_target_pairs={{0,2},{1,3},{2,0},{3,1},{4,6},{5,7},{6,4},{7,5},{8,10},{9,11},{10,... | collective-permute-start | bytes 258056 | tf_op jit(solution)/shard_map/ppermute | solution.py:87
  7.3 15.4 %collective-permute-start.2 = (bf16[16,2688]{1,0:T(8,128)(2,1)S(1)}, bf16[16,2688]{1,0:T(8,128)(2,1)S(1)}, u32[]{:S(2)}, u32[]{:S(2)}) collective-permute-start(bf16[16,2688]{1,0:T(8,128)(2,1)S(1)} %get-tuple-element.27), channel_id=1, source_target_pairs={{0,3},{1,2},{2,1},{3,0},{4,7},{5,6},{6,5},{7,4},{8,11},{9,10},{10,... | collective-permute-start | bytes 258056 | tf_op jit(solution)/shard_map/ppermute | solution.py:87
  7.3 1.4 %copy-start = (bf16[1,512,1536]{2,1,0:T(8,128)(2,1)S(1)}, bf16[1,512,1536]{2,1,0:T(8,128)(2,1)}, u32[]{:S(2)}) copy-start(bf16[1,512,1536]{2,1,0:T(8,128)(2,1)} %param.13) | copy-start | bytes 4718596
  8.7 0.6 copy-start.4
  10.4 21.6 %collective-permute-start.10 = (bf16[512,384]{1,0:T(8,128)(2,1)S(1)}, bf16[512,384]{1,0:T(8,128)(2,1)S(1)}, u32[]{:S(2)}, u32[]{:S(2)}) collective-permute-start(bf16[512,384]{1,0:T(8,128)(2,1)S(1)} %get-tuple-element.31), channel_id=1, source_target_pairs={{0,2},{1,3},{2,0},{3,1},{4,6},{5,7},{6,4},{7,5},{8,10},{9,11},{10,... | collective-permute-start | bytes 1179656 | tf_op jit(solution)/shard_map/ppermute | solution.py:87
  23.4 8.6 %collective-permute-start.3 = (bf16[64,2688]{1,0:T(8,128)(2,1)S(1)}, bf16[64,2688]{1,0:T(8,128)(2,1)S(1)}, u32[]{:S(2)}, u32[]{:S(2)}) collective-permute-start(bf16[64,2688]{1,0:T(8,128)(2,1)S(1)} %bitcast.11), channel_id=1, source_target_pairs={{0,8},{4,12},{8,0},{12,4},{16,24},{20,28},{24,16},{28,20},{1,9},{5... | collective-permute-start | bytes 1032200 | tf_op jit(solution)/shard_map/ppermute | solution.py:87
  24.9 10.9 %collective-permute-start.4 = (bf16[64,2688]{1,0:T(8,128)(2,1)S(1)}, bf16[64,2688]{1,0:T(8,128)(2,1)S(1)}, u32[]{:S(2)}, u32[]{:S(2)}) collective-permute-start(bf16[64,2688]{1,0:T(8,128)(2,1)S(1)} %bitcast.12), channel_id=1, source_target_pairs={{0,16},{4,20},{8,24},{12,28},{16,0},{20,4},{24,8},{28,12},{1,17},{... | collective-permute-start | bytes 1032200 | tf_op jit(solution)/shard_map/ppermute | solution.py:87
  26.5 9.4 %collective-permute-start.5 = (bf16[64,2688]{1,0:T(8,128)(2,1)S(1)}, bf16[64,2688]{1,0:T(8,128)(2,1)S(1)}, u32[]{:S(2)}, u32[]{:S(2)}) collective-permute-start(bf16[64,2688]{1,0:T(8,128)(2,1)S(1)} %bitcast.13), channel_id=1, source_target_pairs={{0,24},{4,28},{8,16},{12,20},{16,8},{20,12},{24,0},{28,4},{1,25},{... | collective-permute-start | bytes 1032200 | tf_op jit(solution)/shard_map/ppermute | solution.py:87
  26.9 9.5 %collective-permute-start.6 = (bf16[64,2688]{1,0:T(8,128)(2,1)S(1)}, bf16[64,2688]{1,0:T(8,128)(2,1)S(1)}, u32[]{:S(2)}, u32[]{:S(2)}) collective-permute-start(bf16[64,2688]{1,0:T(8,128)(2,1)S(1)} %bitcast.14), channel_id=1, source_target_pairs={{0,4},{4,0},{8,12},{12,8},{16,20},{20,16},{24,28},{28,24},{1,5},{5... | collective-permute-start | bytes 1032200 | tf_op jit(solution)/shard_map/ppermute | solution.py:87
  31.9 11.3 %collective-permute-start.11 = (bf16[512,384]{1,0:T(8,128)(2,1)S(1)}, bf16[512,384]{1,0:T(8,128)(2,1)S(1)}, u32[]{:S(2)}, u32[]{:S(2)}) collective-permute-start(bf16[512,384]{1,0:T(8,128)(2,1)S(1)} %get-tuple-element.32), channel_id=1, source_target_pairs={{0,1},{1,0},{2,3},{3,2},{4,5},{5,4},{6,7},{7,6},{8,9},{9,8},{10,11... | collective-permute-start | bytes 1179656 | tf_op jit(solution)/shard_map/ppermute | solution.py:87
  31.9 19.2 %collective-permute-start.12 = (bf16[512,384]{1,0:T(8,128)(2,1)S(1)}, bf16[512,384]{1,0:T(8,128)(2,1)S(1)}, u32[]{:S(2)}, u32[]{:S(2)}) collective-permute-start(bf16[512,384]{1,0:T(8,128)(2,1)S(1)} %get-tuple-element.34), channel_id=1, source_target_pairs={{0,3},{1,2},{2,1},{3,0},{4,7},{5,6},{6,5},{7,4},{8,11},{9,10},{10,... | collective-permute-start | bytes 1179656 | tf_op jit(solution)/shard_map/ppermute | solution.py:87
  35.9 1.7 %collective-permute-start.7 = (bf16[64,2688]{1,0:T(8,128)(2,1)S(1)}, bf16[64,2688]{1,0:T(8,128)(2,1)S(1)}, u32[]{:S(2)}, u32[]{:S(2)}) collective-permute-start(bf16[64,2688]{1,0:T(8,128)(2,1)S(1)} %collective-permute-done.3.refs_1_.refs_9_), channel_id=1, source_target_pairs={{0,4},{4,0},{8,12},{12,8},{16,20},{20,16},{24,28},{28,24},{1,5},{5... | collective-permute-start | bytes 1032200 | tf_op jit(solution)/shard_map/ppermute | solution.py:87
  35.9 2.1 %collective-permute-start.8 = (bf16[64,2688]{1,0:T(8,128)(2,1)S(1)}, bf16[64,2688]{1,0:T(8,128)(2,1)S(1)}, u32[]{:S(2)}, u32[]{:S(2)}) collective-permute-start(bf16[64,2688]{1,0:T(8,128)(2,1)S(1)} %collective-permute-done.4.refs_2_.refs_10_), channel_id=1, source_target_pairs={{0,4},{4,0},{8,12},{12,8},{16,20},{20,16},{24,28},{28,24},{1,5},{5... | collective-permute-start | bytes 1032200 | tf_op jit(solution)/shard_map/ppermute | solution.py:87
  36.4 2.1 %collective-permute-start.9 = (bf16[64,2688]{1,0:T(8,128)(2,1)S(1)}, bf16[64,2688]{1,0:T(8,128)(2,1)S(1)}, u32[]{:S(2)}, u32[]{:S(2)}) collective-permute-start(bf16[64,2688]{1,0:T(8,128)(2,1)S(1)} %collective-permute-done.5.refs_3_.refs_11_), channel_id=1, source_target_pairs={{0,4},{4,0},{8,12},{12,8},{16,20},{20,16},{24,28},{28,24},{1,5},{5... | collective-permute-start | bytes 1032200 | tf_op jit(solution)/shard_map/ppermute | solution.py:87
  53.2 15.9 %copy-start.1 = (bf16[1,512,768]{2,1,0:T(8,128)(2,1)S(1)}, bf16[1,512,768]{2,1,0:T(8,128)(2,1)}, u32[]{:S(2)}) copy-start(bf16[1,512,768]{2,1,0:T(8,128)(2,1)} %param.14) | copy-start | bytes 2359300
  53.2 15.9 %copy-start.2 = (bf16[1,512,768]{2,1,0:T(8,128)(2,1)S(1)}, bf16[1,512,768]{2,1,0:T(8,128)(2,1)}, u32[]{:S(2)}) copy-start(bf16[1,512,768]{2,1,0:T(8,128)(2,1)} %param.15) | copy-start | bytes 2359300
  53.3 15.9 %copy-start.3 = (bf16[1,512,768]{2,1,0:T(8,128)(2,1)S(1)}, bf16[1,512,768]{2,1,0:T(8,128)(2,1)}, u32[]{:S(2)}) copy-start(bf16[1,512,768]{2,1,0:T(8,128)(2,1)} %param.16) | copy-start | bytes 2359300
  53.3 10.4 %collective-permute-start.13 = (bf16[768,128]{1,0:T(8,128)(2,1)S(1)}, bf16[768,128]{1,0:T(8,128)(2,1)S(1)}, u32[]{:S(2)}, u32[]{:S(2)}) collective-permute-start(bf16[768,128]{1,0:T(8,128)(2,1)S(1)} %hidden_blocks.1.refs_0_), channel_id=1, source_target_pairs={{0,1},{1,0},{2,3},{3,2},{4,5},{5,4},{6,7},{7,6},{8,9},{9,8},{10,11... | collective-permute-start | bytes 589832 | tf_op jit(solution)/shard_map/ppermute | solution.py:87
  54.9 14.2 %collective-permute-start.14 = (bf16[768,128]{1,0:T(8,128)(2,1)S(1)}, bf16[768,128]{1,0:T(8,128)(2,1)S(1)}, u32[]{:S(2)}, u32[]{:S(2)}) collective-permute-start(bf16[768,128]{1,0:T(8,128)(2,1)S(1)} %hidden_blocks.1.refs_0_), channel_id=1, source_target_pairs={{0,2},{1,3},{2,0},{3,1},{4,6},{5,7},{6,4},{7,5},{8,10},{9,11},{10,... | collective-permute-start | bytes 589832 | tf_op jit(solution)/shard_map/ppermute | solution.py:87
  56.5 12.6 %collective-permute-start.15 = (bf16[768,128]{1,0:T(8,128)(2,1)S(1)}, bf16[768,128]{1,0:T(8,128)(2,1)S(1)}, u32[]{:S(2)}, u32[]{:S(2)}) collective-permute-start(bf16[768,128]{1,0:T(8,128)(2,1)S(1)} %hidden_blocks.1.refs_0_), channel_id=1, source_target_pairs={{0,3},{1,2},{2,1},{3,0},{4,7},{5,6},{6,5},{7,4},{8,11},{9,10},{10,... | collective-permute-start | bytes 589832 | tf_op jit(solution)/shard_map/ppermute | solution.py:87
  98.9 5.0 %collective-permute-start.16 = (bf16[4,96,128]{2,1,0:T(8,128)(2,1)S(1)}, bf16[4,96,128]{2,1,0:T(8,128)(2,1)S(1)}, u32[]{:S(2)}, u32[]{:S(2)}) collective-permute-start(bf16[4,96,128]{2,1,0:T(8,128)(2,1)S(1)} %get-tuple-element.36), channel_id=1, source_target_pairs={{0,4},{4,0},{8,12},{12,8},{16,20},{20,16},{24,28},{28,24},{1,5},{5... | collective-permute-start | bytes 294920 | tf_op jit(solution)/shard_map/ppermute | solution.py:87
  100.5 5.1 %collective-permute-start.17 = (bf16[4,96,128]{2,1,0:T(8,128)(2,1)S(1)}, bf16[4,96,128]{2,1,0:T(8,128)(2,1)S(1)}, u32[]{:S(2)}, u32[]{:S(2)}) collective-permute-start(bf16[4,96,128]{2,1,0:T(8,128)(2,1)S(1)} %get-tuple-element.37), channel_id=1, source_target_pairs={{0,8},{4,12},{8,0},{12,4},{16,24},{20,28},{24,16},{28,20},{1,9},{5... | collective-permute-start | bytes 294920 | tf_op jit(solution)/shard_map/ppermute | solution.py:87
  101.9 5.1 %collective-permute-start.18 = (bf16[4,96,128]{2,1,0:T(8,128)(2,1)S(1)}, bf16[4,96,128]{2,1,0:T(8,128)(2,1)S(1)}, u32[]{:S(2)}, u32[]{:S(2)}) collective-permute-start(bf16[4,96,128]{2,1,0:T(8,128)(2,1)S(1)} %get-tuple-element.38), channel_id=1, source_target_pairs={{0,12},{4,8},{8,4},{12,0},{16,28},{20,24},{24,20},{28,16},{1,13},{... | collective-permute-start | bytes 294920 | tf_op jit(solution)/shard_map/ppermute | solution.py:87
  101.9 5.7 %collective-permute-start.19 = (bf16[4,96,128]{2,1,0:T(8,128)(2,1)S(1)}, bf16[4,96,128]{2,1,0:T(8,128)(2,1)S(1)}, u32[]{:S(2)}, u32[]{:S(2)}) collective-permute-start(bf16[4,96,128]{2,1,0:T(8,128)(2,1)S(1)} %get-tuple-element.39), channel_id=1, source_target_pairs={{0,16},{4,20},{8,24},{12,28},{16,0},{20,4},{24,8},{28,12},{1,17},{... | collective-permute-start | bytes 294920 | tf_op jit(solution)/shard_map/ppermute | solution.py:87
  103.4 9.9 %collective-permute-start.20 = (bf16[4,96,128]{2,1,0:T(8,128)(2,1)S(1)}, bf16[4,96,128]{2,1,0:T(8,128)(2,1)S(1)}, u32[]{:S(2)}, u32[]{:S(2)}) collective-permute-start(bf16[4,96,128]{2,1,0:T(8,128)(2,1)S(1)} %get-tuple-element.40), channel_id=1, source_target_pairs={{0,20},{4,16},{8,28},{12,24},{16,4},{20,0},{24,12},{28,8},{1,21},{... | collective-permute-start | bytes 294920 | tf_op jit(solution)/shard_map/ppermute | solution.py:87
  104.0 9.4 %collective-permute-start.21 = (bf16[4,96,128]{2,1,0:T(8,128)(2,1)S(1)}, bf16[4,96,128]{2,1,0:T(8,128)(2,1)S(1)}, u32[]{:S(2)}, u32[]{:S(2)}) collective-permute-start(bf16[4,96,128]{2,1,0:T(8,128)(2,1)S(1)} %get-tuple-element.41), channel_id=1, source_target_pairs={{0,24},{4,28},{8,16},{12,20},{16,8},{20,12},{24,0},{28,4},{1,25},{... | collective-permute-start | bytes 294920 | tf_op jit(solution)/shard_map/ppermute | solution.py:87
  105.6 7.8 %collective-permute-start.22 = (bf16[4,96,128]{2,1,0:T(8,128)(2,1)S(1)}, bf16[4,96,128]{2,1,0:T(8,128)(2,1)S(1)}, u32[]{:S(2)}, u32[]{:S(2)}) collective-permute-start(bf16[4,96,128]{2,1,0:T(8,128)(2,1)S(1)} %get-tuple-element.42), channel_id=1, source_target_pairs={{0,28},{4,24},{8,20},{12,16},{16,12},{20,8},{24,4},{28,0},{1,29},{... | collective-permute-start | bytes 294920 | tf_op jit(solution)/shard_map/ppermute | solution.py:87

commit v3 on v2

--- a/solution.py
+++ b/solution.py
@@ -95,11 +95,11 @@
     return pl.BlockSpec(memory_space=pltpu.VMEM)
 
 
-def pack_rows_kernel(place, tok, cot, ids, gates, *outs):
+def pack_rows_kernel(tok, cot, ids, gates, *outs):
     groups = len(outs)
     width = tok.shape[1]
     block = width // groups
-    group = place[1]
+    group = lax.axis_index("dp")
     named = ids[...]
     weights = gates[...].astype(F32)
     expert = lax.broadcasted_iota(jnp.int32, (LANES, named.shape[1]), 0)
@@ -114,14 +114,14 @@
         out[:, width + block :] = table
 
 
-def pack_rows(place, tokens, cotangent, ids, gates, groups):
+def pack_rows(tokens, cotangent, ids, gates, groups):
     rows, width = tokens.shape
     return pl.pallas_call(
         pack_rows_kernel,
         out_shape=[pltpu.VMEM((rows, width + width // groups + LANES), BF16)] * groups,
-        in_specs=[smem()] + [whole()] * 4,
+        in_specs=[whole()] * 4,
         name="pack_rows",
-    )(place, tokens, cotangent, ids.T, gates.T)
+    )(tokens, cotangent, ids.T, gates.T)
 
 
 def swap_halves(x):
@@ -132,10 +132,10 @@
     return lax.broadcasted_iota(jnp.int32, shape, 1) < HALF
 
 
-def pack_weights_kernel(parts, place, weights, *outs):
+def pack_weights_kernel(parts, weights, *outs):
     groups = len(parts)
     hidden_units = weights.shape[1] // 2
-    group = place[1]
+    group = lax.axis_index("dp")
 
     def write(flip, start, value):
         first = sum(parts[:flip])
@@ -166,16 +166,16 @@
         write(flip, LANES, weights[:, pl.ds(start, LANES)])
 
 
-def pack_weights(place, weights, parts):
+def pack_weights(weights, parts):
     rows, cols = weights.shape
     outs = [pltpu.VMEM((rows // n, cols // len(parts)), BF16) for n in parts for _ in range(n)]
     return pl.pallas_call(
         functools.partial(pack_weights_kernel, parts),
         out_shape=outs,
-        in_specs=[smem(), whole()],
+        in_specs=[whole()],
         compiler_params=pltpu.CompilerParams(vmem_limit_bytes=VMEM_BYTES),
         name="pack_weights",
-    )(place, weights)
+    )(weights)
 
 
 def after(x, *others):
@@ -186,24 +186,24 @@
     return pltpu.with_memory_space_constraint(x, pltpu.VMEM)
 
 
-def order_groups_kernel(place, *refs):
+def order_groups_kernel(*refs):
     *blocks, out = refs
     for flip, block in enumerate(blocks):
-        out[pl.ds(place[1] ^ flip, 1)] = block[...][None]
-
-
-def order_groups(place, blocks):
+        out[pl.ds(lax.axis_index("dp") ^ flip, 1)] = block[...][None]
+
+
+def order_groups(blocks):
     rows, width = blocks[0].shape
     out = pl.pallas_call(
         order_groups_kernel,
         out_shape=pltpu.VMEM((len(blocks), rows, width), BF16),
-        in_specs=[smem()] + [whole()] * len(blocks),
+        in_specs=[whole()] * len(blocks),
         name="order_groups",
-    )(place, *[in_vmem(x) for x in blocks])
+    )(*[in_vmem(x) for x in blocks])
     return out.reshape(len(blocks) * rows, width)
 
 
-def hidden_kernel(groups, pieces, spans, place, *refs):
+def hidden_kernel(groups, pieces, spans, *refs):
     row_refs, weight_refs, out, toks = refs[:pieces], refs[pieces:-2], refs[-2], refs[-1]
     rows, width = row_refs[0].shape
     block = width // groups
@@ -212,7 +212,7 @@
         toks[i * rows : (i + 1) * rows, :] = ref[...]
     pre = None
     for (flip, first), ref in zip(spans, weight_refs, strict=True):
-        start = pl.multiple_of((place[1] ^ flip) * block + first, LANES)
+        start = pl.multiple_of((lax.axis_index("dp") ^ flip) * block + first, LANES)
         depth = ref.shape[0]
         term = jnp.dot(toks[:, pl.ds(start, depth)], ref[...], preferred_element_type=F32)
         pre = term if pre is None else pre + term
@@ -222,7 +222,7 @@
     narrow = shared / (1.0 + jnp.exp(-shared)) * swap_halves(shared)
     low = low_half((total // 2, LANES))
     top, bottom = narrow[: total // 2], swap_halves(narrow[total // 2 :])
-    even = lax.rem(place[1], 2) == 0
+    even = lax.rem(lax.axis_index("dp"), 2) == 0
 
     @pl.when(even)
     def _():
@@ -233,51 +233,49 @@
         out[total:, :] = jnp.where(low, bottom, top).astype(BF16)
 
 
-def hidden_blocks(place, pieces, weights, spans, width, groups):
+def hidden_blocks(pieces, weights, spans, width, groups):
     rows = pieces[0].shape[0]
     total = rows * len(pieces)
     return pl.pallas_call(
         functools.partial(hidden_kernel, groups, len(pieces), spans),
         out_shape=pltpu.VMEM((total + total // 2, LANES), BF16),
         grid=(1,),
-        in_specs=[smem()]
-        + [pl.BlockSpec((rows, width), lambda i: (0, 0))] * len(pieces)
+        in_specs=[pl.BlockSpec((rows, width), lambda i: (0, 0))] * len(pieces)
         + [pl.BlockSpec(x.shape, lambda i: (0, 0)) for x in weights],
         out_specs=pl.BlockSpec((total + total // 2, LANES), lambda i: (0, 0)),
         scratch_shapes=[pltpu.VMEM((total, width), BF16)],
         compiler_params=pltpu.CompilerParams(vmem_limit_bytes=VMEM_BYTES),
         name="hidden_blocks",
-    )(place, *[in_vmem(x) for x in [*pieces, *weights]])
-
-
-def scaled_kernel(pieces, place, *refs):
+    )(*[in_vmem(x) for x in [*pieces, *weights]])
+
+
+def scaled_kernel(pieces, *refs):
     cot_refs, gate_refs, out = refs[:pieces], refs[pieces:-1], refs[-1]
     blocks = []
     for cot, table in zip(cot_refs, gate_refs, strict=True):
         gates = table[...].astype(F32)
         lane = lax.broadcasted_iota(jnp.int32, gates.shape, 1)
-        gate = jnp.sum(jnp.where(lane == place[0], gates, 0.0), axis=1, keepdims=True)
+        gate = jnp.sum(jnp.where(lane == lax.axis_index("expert"), gates, 0.0), axis=1, keepdims=True)
         blocks.append((gate * cot[...].astype(F32)).astype(BF16))
     out[...] = jnp.concatenate(blocks, axis=0).T
 
 
-def scaled_rows(place, pieces, width, block):
+def scaled_rows(pieces, width, block):
     rows = pieces[0].shape[0]
     total = rows * len(pieces)
     return pl.pallas_call(
         functools.partial(scaled_kernel, len(pieces)),
         out_shape=jax.ShapeDtypeStruct((block, total), BF16),
         grid=(1,),
-        in_specs=[smem()]
-        + [pl.BlockSpec((rows, block), lambda i: (0, width // block))] * len(pieces)
+        in_specs=[pl.BlockSpec((rows, block), lambda i: (0, width // block))] * len(pieces)
         + [pl.BlockSpec((rows, LANES), lambda i: (0, (width + block) // LANES))] * len(pieces),
         out_specs=pl.BlockSpec((block, total), lambda i: (0, 0)),
         compiler_params=pltpu.CompilerParams(vmem_limit_bytes=VMEM_BYTES),
         name="scaled_rows",
-    )(place, *pieces, *pieces)
-
-
-def update_kernel(groups, place, *refs):
+    )(*pieces, *pieces)
+
+
+def update_kernel(groups, *refs):
     hid_refs, (scaled, down, first, second, out, hidden) = refs[:groups], refs[groups:]
     total = scaled.shape[1]
     units = down.shape[1]
@@ -286,7 +284,7 @@
     def _():
         for own in range(groups):
 
-            @pl.when(place[1] == own)
+            @pl.when(lax.axis_index("dp") == own)
             def _():
                 for col in range(groups):
                     hidden[:, col * LANES : (col + 1) * LANES] = hid_refs[own ^ col][:total, :]
@@ -309,7 +307,7 @@
             out[i * groups + col] = updated[start : start + rows]
 
 
-def update_pieces(place, hidden, scaled, down, first, second, experts):
+def update_pieces(hidden, scaled, down, first, second, experts):
     groups = len(hidden)
     features, total = scaled.shape
     units = down.shape[1]
@@ -320,54 +318,53 @@
         functools.partial(update_kernel, groups),
         out_shape=jax.ShapeDtypeStruct((experts * groups, piece_rows, LANES), BF16),
         grid=(steps,),
-        in_specs=[smem()]
-        + [pl.BlockSpec(hidden[0].shape, lambda i: (0, 0))] * groups
+        in_specs=[pl.BlockSpec(hidden[0].shape, lambda i: (0, 0))] * groups
         + [pl.BlockSpec((LANES, total), lambda i: (i, 0))]
         + [pl.BlockSpec((LANES, units), lambda i: (i, 0))] * 3,
         out_specs=pl.BlockSpec((places * groups, piece_rows, LANES), lambda i: (i, 0, 0)),
         scratch_shapes=[pltpu.VMEM((total, units), BF16)],
         compiler_params=pltpu.CompilerParams(vmem_limit_bytes=VMEM_BYTES),
         name="update_pieces",
-    )(place, *hidden, scaled, down, first, second)
-
-
-def pick_kernel(place, order, pieces, *outs):
+    )(*hidden, scaled, down, first, second)
+
+
+def pick_kernel(order, pieces, *outs):
     for flip, out in enumerate(outs):
-        out[...] = pieces[order[place[0] ^ flip]]
-
-
-def pick(place, order, pieces):
+        out[...] = pieces[order[lax.axis_index("expert") ^ flip]]
+
+
+def pick(order, pieces):
     experts = pieces.shape[0]
     return pl.pallas_call(
         pick_kernel,
         out_shape=[pltpu.VMEM(pieces.shape[1:], pieces.dtype)] * experts,
-        in_specs=[smem(), smem(), whole()],
+        in_specs=[smem(), whole()],
         out_specs=[whole()] * experts,
         name="pick",
-    )(place, order, pieces)
-
-
-def unpack_kernel(place, *refs):
+    )(order, pieces)
+
+
+def unpack_kernel(*refs):
     *pieces, out = refs
     groups, rows, _ = pieces[0].shape
     halves = out.shape[1] // rows
     block = out.shape[2] // groups
     for flip, piece in enumerate(pieces):
-        spot = place[0] ^ flip
+        spot = lax.axis_index("expert") ^ flip
         top = pl.multiple_of((spot % halves) * rows, 16)
         for group in range(groups):
             left = pl.multiple_of(group * block + (spot // halves) * LANES, LANES)
             out[0, pl.ds(top, rows), pl.ds(left, LANES)] = piece[group]
 
 
-def unpack(place, pieces, width, cols):
+def unpack(pieces, width, cols):
     return pl.pallas_call(
         unpack_kernel,
         out_shape=jax.ShapeDtypeStruct((1, cols, width), BF16),
-        in_specs=[smem()] + [whole()] * len(pieces),
+        in_specs=[whole()] * len(pieces),
         out_specs=whole(),
         name="unpack",
-    )(place, *[in_vmem(x) for x in pieces])
+    )(*[in_vmem(x) for x in pieces])
 
 
 def dense(tokens, cotangent, route_ids, route_gates, gate_up, down, moment1, moment2, placement):
@@ -376,27 +373,28 @@
     width = tokens.shape[1]
     units = down.shape[2]
     block = width // groups
-    place = jnp.stack([lax.axis_index("expert"), lax.axis_index("dp")]).astype(jnp.int32)
 
     parts = (1, 1, 1, 1)
-    own, near, far, farthest = pack_weights(place, gate_up[0], parts)
-    sent = pack_rows(place, tokens, cotangent, route_ids, route_gates, groups)
+    own, near, far, farthest = pack_weights(gate_up[0], parts)
+    sent = pack_rows(tokens, cotangent, route_ids, route_gates, groups)
     blocks = [sent[0]] + [partner(sent[k], "dp", k) for k in range(1, groups)]
-    far = partner(after(far, blocks[1]), "dp", 2)
-    weights = [own, partner(after(near, far), "dp", 1), far, partner(after(farthest, far), "dp", 3)]
     spans = [(flip, i * (block // n)) for flip, n in enumerate(parts) for i in range(n)]
-    plane = order_groups(place, blocks)
+    plane = order_groups(blocks)
     chips = [plane] + [partner(plane, "expert", k) for k in range(2, experts, 2)]
     pieces = chips + [partner(x, "expert", 1) for x in chips]
-
-    own_hidden = hidden_blocks(place, pieces, weights, spans, width, groups)
-    scaled = scaled_rows(place, pieces, width, block)
+    far = partner(after(far, blocks[1]), "dp", 2)
+    near = partner(after(near, chips[1]), "dp", 1)
+    farthest = partner(after(farthest, far), "dp", 3)
+    weights = [own, near, far, farthest]
+
+    own_hidden = hidden_blocks(pieces, weights, spans, width, groups)
+    scaled = scaled_rows(pieces, width, block)
     hidden = [own_hidden] + [partner(own_hidden, "dp", k) for k in range(1, groups)]
-    moved = update_pieces(place, hidden, scaled, down[0], moment1[0], moment2[0], experts)
+    moved = update_pieces(hidden, scaled, down[0], moment1[0], moment2[0], experts)
     spread = lax.all_to_all(moved, ("expert", "dp"), 0, 0, tiled=True)
-    picked = pick(place, placement, spread.reshape(experts, groups, *spread.shape[1:]))
+    picked = pick(placement, spread.reshape(experts, groups, *spread.shape[1:]))
     landed = [picked[0]] + [partner(picked[k], "expert", k) for k in range(1, experts)]
-    return unpack(place, landed, width, units // groups).transpose(0, 2, 1)
+    return unpack(landed, width, units // groups).transpose(0, 2, 1)
 
 
 def shards(tokens, cotangent, route_ids, *rest):

time: 115 us -> 108 us (0.939)
  waiting for transfers between devices: 49 us -> 40.9 us
  starting transfers between devices: 26.1 us -> 32.2 us
  Pallas kernels: 11.7 us -> 8.14 us
    ppermute x23, waiting for transfers between devices: 49 us -> 40.9 us  [partner(): return lax.ppermute(x, axis, [(i, i ^ flip) for i in range(size)])]
    ppermute x23, starting transfers between devices: 26.1 us -> 32.2 us  [partner(): return lax.ppermute(x, axis, [(i, i ^ flip) for i in range(size)])]
  transfers between devices with their start and end apart: 23 -> 23, of which waited for: 14 -> 13; matrix products, arithmetic and copies ran while one was open for 0% -> 0% of each run, Pallas kernels for 2% -> 1%
where the time goes in v3:
time: 108 us
  waiting for transfers between devices  40.9 us (38%)
  starting transfers between devices  32.2 us (30%)
  blocking collectives  25.1 us (23%)
  Pallas kernels  8.14 us (8%)
  local copies, waits for them, and re-layouts  1.43 us (1%)
    ppermute x23, waiting for transfers between devices, partner(): return lax.ppermute(x, axis, [(i, i ^ flip) for i in range(size)])  40.9 us
    ppermute x23, starting transfers between devices, partner(): return lax.ppermute(x, axis, [(i, i ^ flip) for i in range(size)])  32.2 us
    all_to_all x1, blocking collectives, dense(): spread = lax.all_to_all(moved, ('expert', 'dp'), 0, 0, tiled=True)  25.1 us
    pallas_call x1, Pallas kernels, update_pieces(): pl.pallas_call(functools.partial(update_kernel, groups), out_shape=jax.Sh...  2.54 us
  transfers between devices with their start and end apart: 23, of which 13 were waited for; matrix products, arithmetic and copies ran while one was open for 0% of the time, Pallas kernels for 1%

profile of v3, /device:TPU:0, one launch (start us, length us, event | category | flops | bytes accessed | tf_op | source)
XLA Modules:
  0.0 108.0 jit_solution(12116099691954877204)
XLA Ops:
  0.0 1.0 pack_rows.1
  1.0 3.1 %collective-permute-start = (bf16[16,2688]{1,0:T(8,128)(2,1)S(1)}, bf16[16,2688]{1,0:T(8,128)(2,1)S(1)}, u32[]{:S(2)}, u32[]{:S(2)}) collective-permute-start(bf16[16,2688]{1,0:T(8,128)(2,1)S(1)} %get-tuple-element.25), channel_id=1, source_target_pairs={{0,1},{1,0},{2,3},{3,2},{4,5},{5,4},{6,7},{7,6},{8,9},{9,8},{10,11... | collective-permute-start | bytes 258056 | tf_op jit(solution)/shard_map/ppermute | solution.py:87
  4.0 2.6 %collective-permute-start.1 = (bf16[16,2688]{1,0:T(8,128)(2,1)S(1)}, bf16[16,2688]{1,0:T(8,128)(2,1)S(1)}, u32[]{:S(2)}, u32[]{:S(2)}) collective-permute-start(bf16[16,2688]{1,0:T(8,128)(2,1)S(1)} %get-tuple-element.26), channel_id=1, source_target_pairs={{0,2},{1,3},{2,0},{3,1},{4,6},{5,7},{6,4},{7,5},{8,10},{9,11},{10,... | collective-permute-start | bytes 258056 | tf_op jit(solution)/shard_map/ppermute | solution.py:87
  6.6 0.0 collective-permute-start.2
  6.6 1.4 %copy-done = bf16[1,512,1536]{2,1,0:T(8,128)(2,1)S(1)} copy-done((bf16[1,512,1536]{2,1,0:T(8,128)(2,1)S(1)}, bf16[1,512,1536]{2,1,0:T(8,128)(2,1)}, u32[]{:S(2)}) %copy-start) | copy-done | bytes 1572888
  8.0 0.5 pack_weights.1
  8.5 0.0 collective-permute-done.refs_1_
  8.5 2.0 %collective-permute-start.11 = (bf16[512,384]{1,0:T(8,128)(2,1)S(1)}, bf16[512,384]{1,0:T(8,128)(2,1)S(1)}, u32[]{:S(2)}, u32[]{:S(2)}) collective-permute-start(bf16[512,384]{1,0:T(8,128)(2,1)S(1)} %get-tuple-element.32), channel_id=1, source_target_pairs={{0,2},{1,3},{2,0},{3,1},{4,6},{5,7},{6,4},{7,5},{8,10},{9,11},{10,... | collective-permute-start | bytes 1179656 | tf_op jit(solution)/shard_map/ppermute | solution.py:87
  10.5 11.5 %collective-permute-done.1.refs_2_ = bf16[16,2688]{1,0:T(8,128)(2,1)S(1)} collective-permute-done((bf16[16,2688]{1,0:T(8,128)(2,1)S(1)}, bf16[16,2688]{1,0:T(8,128)(2,1)S(1)}, u32[]{:S(2)}, u32[]{:S(2)}) %collective-permute-start.1) | collective-permute-done | bytes 86048 | tf_op jit(solution)/shard_map/ppermute | solution.py:87
  22.1 0.0 collective-permute-done.2.refs_3_
  22.1 1.6 %collective-permute-start.3 = (bf16[64,2688]{1,0:T(8,128)(2,1)S(1)}, bf16[64,2688]{1,0:T(8,128)(2,1)S(1)}, u32[]{:S(2)}, u32[]{:S(2)}) collective-permute-start(bf16[64,2688]{1,0:T(8,128)(2,1)S(1)} %bitcast.9), channel_id=1, source_target_pairs={{0,8},{4,12},{8,0},{12,4},{16,24},{20,28},{24,16},{28,20},{1,9},{5... | collective-permute-start | bytes 1032200 | tf_op jit(solution)/shard_map/ppermute | solution.py:87
  23.7 1.5 %collective-permute-start.4 = (bf16[64,2688]{1,0:T(8,128)(2,1)S(1)}, bf16[64,2688]{1,0:T(8,128)(2,1)S(1)}, u32[]{:S(2)}, u32[]{:S(2)}) collective-permute-start(bf16[64,2688]{1,0:T(8,128)(2,1)S(1)} %bitcast.10), channel_id=1, source_target_pairs={{0,16},{4,20},{8,24},{12,28},{16,0},{20,4},{24,8},{28,12},{1,17},{... | collective-permute-start | bytes 1032200 | tf_op jit(solution)/shard_map/ppermute | solution.py:87
  25.2 0.5 collective-permute-start.5
  25.7 0.0 collective-permute-start.6
  25.7 3.8 %collective-permute-done.3.refs_1_.refs_9_ = bf16[64,2688]{1,0:T(8,128)(2,1)S(1)} collective-permute-done((bf16[64,2688]{1,0:T(8,128)(2,1)S(1)}, bf16[64,2688]{1,0:T(8,128)(2,1)S(1)}, u32[]{:S(2)}, u32[]{:S(2)}) %collective-permute-start.3) | collective-permute-done | bytes 344096 | tf_op jit(solution)/shard_map/ppermute | solution.py:87
  29.4 6.2 %collective-permute-start.10 = (bf16[512,384]{1,0:T(8,128)(2,1)S(1)}, bf16[512,384]{1,0:T(8,128)(2,1)S(1)}, u32[]{:S(2)}, u32[]{:S(2)}) collective-permute-start(bf16[512,384]{1,0:T(8,128)(2,1)S(1)} %get-tuple-element.30), channel_id=1, source_target_pairs={{0,1},{1,0},{2,3},{3,2},{4,5},{5,4},{6,7},{7,6},{8,9},{9,8},{10,11... | collective-permute-start | bytes 1179656 | tf_op jit(solution)/shard_map/ppermute | solution.py:87
  35.6 2.6 %collective-permute-start.12 = (bf16[512,384]{1,0:T(8,128)(2,1)S(1)}, bf16[512,384]{1,0:T(8,128)(2,1)S(1)}, u32[]{:S(2)}, u32[]{:S(2)}) collective-permute-start(bf16[512,384]{1,0:T(8,128)(2,1)S(1)} %get-tuple-element.34), channel_id=1, source_target_pairs={{0,3},{1,2},{2,1},{3,0},{4,7},{5,6},{6,5},{7,4},{8,11},{9,10},{10,... | collective-permute-start | bytes 1179656 | tf_op jit(solution)/shard_map/ppermute | solution.py:87
  38.2 0.5 collective-permute-start.8
  38.7 0.1 collective-permute-start.9
  38.8 1.1 collective-permute-done.7.refs_5_.refs_13_
  39.8 0.5 collective-permute-done.8.refs_6_.refs_14_
  40.3 0.5 collective-permute-done.9.refs_7_.refs_15_
  40.8 3.7 %collective-permute-done.10.refs_9_ = bf16[512,384]{1,0:T(8,128)(2,1)S(1)} collective-permute-done((bf16[512,384]{1,0:T(8,128)(2,1)S(1)}, bf16[512,384]{1,0:T(8,128)(2,1)S(1)}, u32[]{:S(2)}, u32[]{:S(2)}) %collective-permute-start.10) | collective-permute-done | bytes 393248 | tf_op jit(solution)/shard_map/ppermute | solution.py:87
  44.5 4.8 %collective-permute-done.12.refs_11_ = bf16[512,384]{1,0:T(8,128)(2,1)S(1)} collective-permute-done((bf16[512,384]{1,0:T(8,128)(2,1)S(1)}, bf16[512,384]{1,0:T(8,128)(2,1)S(1)}, u32[]{:S(2)}, u32[]{:S(2)}) %collective-permute-start.12) | collective-permute-done | bytes 393248 | tf_op jit(solution)/shard_map/ppermute | solution.py:87
  49.3 1.5 %hidden_blocks.1.refs_0_ = bf16[768,128]{1,0:T(8,128)(2,1)S(1)} custom-call(bf16[64,2688]{1,0:T(8,128)(2,1)S(1)} %bitcast.13, bf16[64,2688]{1,0:T(8,128)(2,1)S(1)} %collective-permute-done.3.refs_1_.refs_9_, bf16[64,2688]{1,0:T(8,128)(2,1)S(1)} %collective-permute-done.4.refs_2_.refs_10_, bf16[64,2688]{1,0:T(8,128)(2,1)S(1)} %collective-permute-done.5.refs_3_.refs_11_, ...), custom_call_target="tpu_custom_call" | custom-call | tf_op jit(solution)/shard_map/hidden_blocks/pallas_call | solution.py:239
  50.8 0.0 copy-start.1
  50.8 0.0 copy-start.2
  50.8 0.0 copy-start.3
  50.8 0.1 collective-permute-start.13
  50.9 2.6 %collective-permute-start.14 = (bf16[768,128]{1,0:T(8,128)(2,1)S(1)}, bf16[768,128]{1,0:T(8,128)(2,1)S(1)}, u32[]{:S(2)}, u32[]{:S(2)}) collective-permute-start(bf16[768,128]{1,0:T(8,128)(2,1)S(1)} %hidden_blocks.1.refs_0_), channel_id=1, source_target_pairs={{0,2},{1,3},{2,0},{3,1},{4,6},{5,7},{6,4},{7,5},{8,10},{9,11},{10,... | collective-permute-start | bytes 589832 | tf_op jit(solution)/shard_map/ppermute | solution.py:87
  53.5 1.8 %collective-permute-start.15 = (bf16[768,128]{1,0:T(8,128)(2,1)S(1)}, bf16[768,128]{1,0:T(8,128)(2,1)S(1)}, u32[]{:S(2)}, u32[]{:S(2)}) collective-permute-start(bf16[768,128]{1,0:T(8,128)(2,1)S(1)} %hidden_blocks.1.refs_0_), channel_id=1, source_target_pairs={{0,3},{1,2},{2,1},{3,0},{4,7},{5,6},{6,5},{7,4},{8,11},{9,10},{10,... | collective-permute-start | bytes 589832 | tf_op jit(solution)/shard_map/ppermute | solution.py:87
  55.3 0.3 scaled_rows.1.refs_4_
  55.6 2.5 %collective-permute-done.13.refs_1_ = bf16[768,128]{1,0:T(8,128)(2,1)S(1)} collective-permute-done((bf16[768,128]{1,0:T(8,128)(2,1)S(1)}, bf16[768,128]{1,0:T(8,128)(2,1)S(1)}, u32[]{:S(2)}, u32[]{:S(2)}) %collective-permute-start.13) | collective-permute-done | bytes 196640 | tf_op jit(solution)/shard_map/ppermute | solution.py:87
  58.1 5.5 %collective-permute-done.14.refs_2_ = bf16[768,128]{1,0:T(8,128)(2,1)S(1)} collective-permute-done((bf16[768,128]{1,0:T(8,128)(2,1)S(1)}, bf16[768,128]{1,0:T(8,128)(2,1)S(1)}, u32[]{:S(2)}, u32[]{:S(2)}) %collective-permute-start.14) | collective-permute-done | bytes 196640 | tf_op jit(solution)/shard_map/ppermute | solution.py:87
  63.6 2.5 %update_pieces.1 = bf16[32,96,128]{2,1,0:T(8,128)(2,1)S(1)} custom-call(bf16[768,128]{1,0:T(8,128)(2,1)S(1)} %hidden_blocks.1.refs_0_, bf16[768,128]{1,0:T(8,128)(2,1)S(1)} %collective-permute-done.13.refs_1_, bf16[768,128]{1,0:T(8,128)(2,1)S(1)} %collective-permute-done.14.refs_2_, bf16[768,128]{1,0:T(8,128)(2,1)S(1)} %collective-permute-done.15.refs_3_, ...), custom_call_target="tpu_custom_call" | custom-call | tf_op jit(solution)/shard_map/update_pieces/pallas_call | solution.py:317
  66.2 25.1 %all_to_all.5 = bf16[32,96,128]{2,1,0:T(8,128)(2,1)} all-to-all(bf16[32,96,128]{2,1,0:T(8,128)(2,1)S(1)} %update_pieces.1), channel_id=1, replica_groups=mesh['expert'=8,'dp'=4] {'expert','dp'}, dimensions={0} | all-to-all | bytes 1572864 | tf_op jit(solution)/shard_map/all_to_all | solution.py:394
  91.3 1.2 %pick.1 = (bf16[4,96,128]{2,1,0:T(8,128)(2,1)S(1)}, bf16[4,96,128]{2,1,0:T(8,128)(2,1)S(1)}, bf16[4,96,128]{2,1,0:T(8,128)(2,1)S(1)}, bf16[4,96,128]{2,1,0:T(8,1...) custom-call(s32[8]{0:T(128)} %order.1, ...), custom_call_target="tpu_custom_call" | custom-call | tf_op jit(solution)/shard_map/pick/pallas_call | solution.py:338
  92.5 1.5 %collective-permute-start.16 = (bf16[4,96,128]{2,1,0:T(8,128)(2,1)S(1)}, bf16[4,96,128]{2,1,0:T(8,128)(2,1)S(1)}, u32[]{:S(2)}, u32[]{:S(2)}) collective-permute-start(bf16[4,96,128]{2,1,0:T(8,128)(2,1)S(1)} %get-tuple-element.36), channel_id=1, source_target_pairs={{0,4},{4,0},{8,12},{12,8},{16,20},{20,16},{24,28},{28,24},{1,5},{5... | collective-permute-start | bytes 294920 | tf_op jit(solution)/shard_map/ppermute | solution.py:87
  94.1 1.5 %collective-permute-start.17 = (bf16[4,96,128]{2,1,0:T(8,128)(2,1)S(1)}, bf16[4,96,128]{2,1,0:T(8,128)(2,1)S(1)}, u32[]{:S(2)}, u32[]{:S(2)}) collective-permute-start(bf16[4,96,128]{2,1,0:T(8,128)(2,1)S(1)} %get-tuple-element.37), channel_id=1, source_target_pairs={{0,8},{4,12},{8,0},{12,4},{16,24},{20,28},{24,16},{28,20},{1,9},{5... | collective-permute-start | bytes 294920 | tf_op jit(solution)/shard_map/ppermute | solution.py:87
  95.5 1.4 %collective-permute-start.19 = (bf16[4,96,128]{2,1,0:T(8,128)(2,1)S(1)}, bf16[4,96,128]{2,1,0:T(8,128)(2,1)S(1)}, u32[]{:S(2)}, u32[]{:S(2)}) collective-permute-start(bf16[4,96,128]{2,1,0:T(8,128)(2,1)S(1)} %get-tuple-element.39), channel_id=1, source_target_pairs={{0,16},{4,20},{8,24},{12,28},{16,0},{20,4},{24,8},{28,12},{1,17},{... | collective-permute-start | bytes 294920 | tf_op jit(solution)/shard_map/ppermute | solution.py:87
  97.0 0.6 collective-permute-start.20
  97.6 1.5 %collective-permute-start.21 = (bf16[4,96,128]{2,1,0:T(8,128)(2,1)S(1)}, bf16[4,96,128]{2,1,0:T(8,128)(2,1)S(1)}, u32[]{:S(2)}, u32[]{:S(2)}) collective-permute-start(bf16[4,96,128]{2,1,0:T(8,128)(2,1)S(1)} %get-tuple-element.41), channel_id=1, source_target_pairs={{0,24},{4,28},{8,16},{12,20},{16,8},{20,12},{24,0},{28,4},{1,25},{... | collective-permute-start | bytes 294920 | tf_op jit(solution)/shard_map/ppermute | solution.py:87
  99.0 0.1 collective-permute-done.17.refs_2_
  99.2 0.8 collective-permute-start.22
  100.0 0.7 collective-permute-done.18.refs_3_
  100.6 0.6 collective-permute-done.19.refs_4_
  101.2 5.7 %collective-permute-done.20.refs_5_ = bf16[4,96,128]{2,1,0:T(8,128)(2,1)S(1)} collective-permute-done((bf16[4,96,128]{2,1,0:T(8,128)(2,1)S(1)}, bf16[4,96,128]{2,1,0:T(8,128)(2,1)S(1)}, u32[]{:S(2)}, u32[]{:S(2)}) %collective-permute-start.20) | collective-permute-done | bytes 98336 | tf_op jit(solution)/shard_map/ppermute | solution.py:87
  106.9 1.1 unpack.1
  (15 shorter events, 0.1 us)
Async XLA Ops:
  1.0 7.6 %collective-permute-start = (bf16[16,2688]{1,0:T(8,128)(2,1)S(1)}, bf16[16,2688]{1,0:T(8,128)(2,1)S(1)}, u32[]{:S(2)}, u32[]{:S(2)}) collective-permute-start(bf16[16,2688]{1,0:T(8,128)(2,1)S(1)} %get-tuple-element.25), channel_id=1, source_target_pairs={{0,1},{1,0},{2,3},{3,2},{4,5},{5,4},{6,7},{7,6},{8,9},{9,8},{10,11... | collective-permute-start | bytes 258056 | tf_op jit(solution)/shard_map/ppermute | solution.py:87
  4.0 18.0 %collective-permute-start.1 = (bf16[16,2688]{1,0:T(8,128)(2,1)S(1)}, bf16[16,2688]{1,0:T(8,128)(2,1)S(1)}, u32[]{:S(2)}, u32[]{:S(2)}) collective-permute-start(bf16[16,2688]{1,0:T(8,128)(2,1)S(1)} %get-tuple-element.26), channel_id=1, source_target_pairs={{0,2},{1,3},{2,0},{3,1},{4,6},{5,7},{6,4},{7,5},{8,10},{9,11},{10,... | collective-permute-start | bytes 258056 | tf_op jit(solution)/shard_map/ppermute | solution.py:87
  6.6 15.4 %collective-permute-start.2 = (bf16[16,2688]{1,0:T(8,128)(2,1)S(1)}, bf16[16,2688]{1,0:T(8,128)(2,1)S(1)}, u32[]{:S(2)}, u32[]{:S(2)}) collective-permute-start(bf16[16,2688]{1,0:T(8,128)(2,1)S(1)} %get-tuple-element.27), channel_id=1, source_target_pairs={{0,3},{1,2},{2,1},{3,0},{4,7},{5,6},{6,5},{7,4},{8,11},{9,10},{10,... | collective-permute-start | bytes 258056 | tf_op jit(solution)/shard_map/ppermute | solution.py:87
  6.6 1.4 %copy-start = (bf16[1,512,1536]{2,1,0:T(8,128)(2,1)S(1)}, bf16[1,512,1536]{2,1,0:T(8,128)(2,1)}, u32[]{:S(2)}) copy-start(bf16[1,512,1536]{2,1,0:T(8,128)(2,1)} %param.13) | copy-start | bytes 4718596
  8.5 27.0 %collective-permute-start.11 = (bf16[512,384]{1,0:T(8,128)(2,1)S(1)}, bf16[512,384]{1,0:T(8,128)(2,1)S(1)}, u32[]{:S(2)}, u32[]{:S(2)}) collective-permute-start(bf16[512,384]{1,0:T(8,128)(2,1)S(1)} %get-tuple-element.32), channel_id=1, source_target_pairs={{0,2},{1,3},{2,0},{3,1},{4,6},{5,7},{6,4},{7,5},{8,10},{9,11},{10,... | collective-permute-start | bytes 1179656 | tf_op jit(solution)/shard_map/ppermute | solution.py:87
  22.1 7.3 %collective-permute-start.3 = (bf16[64,2688]{1,0:T(8,128)(2,1)S(1)}, bf16[64,2688]{1,0:T(8,128)(2,1)S(1)}, u32[]{:S(2)}, u32[]{:S(2)}) collective-permute-start(bf16[64,2688]{1,0:T(8,128)(2,1)S(1)} %bitcast.9), channel_id=1, source_target_pairs={{0,8},{4,12},{8,0},{12,4},{16,24},{20,28},{24,16},{28,20},{1,9},{5... | collective-permute-start | bytes 1032200 | tf_op jit(solution)/shard_map/ppermute | solution.py:87
  23.7 14.5 %collective-permute-start.4 = (bf16[64,2688]{1,0:T(8,128)(2,1)S(1)}, bf16[64,2688]{1,0:T(8,128)(2,1)S(1)}, u32[]{:S(2)}, u32[]{:S(2)}) collective-permute-start(bf16[64,2688]{1,0:T(8,128)(2,1)S(1)} %bitcast.10), channel_id=1, source_target_pairs={{0,16},{4,20},{8,24},{12,28},{16,0},{20,4},{24,8},{28,12},{1,17},{... | collective-permute-start | bytes 1032200 | tf_op jit(solution)/shard_map/ppermute | solution.py:87
  25.2 13.0 %collective-permute-start.5 = (bf16[64,2688]{1,0:T(8,128)(2,1)S(1)}, bf16[64,2688]{1,0:T(8,128)(2,1)S(1)}, u32[]{:S(2)}, u32[]{:S(2)}) collective-permute-start(bf16[64,2688]{1,0:T(8,128)(2,1)S(1)} %bitcast.11), channel_id=1, source_target_pairs={{0,24},{4,28},{8,16},{12,20},{16,8},{20,12},{24,0},{28,4},{1,25},{... | collective-permute-start | bytes 1032200 | tf_op jit(solution)/shard_map/ppermute | solution.py:87
  25.7 13.1 %collective-permute-start.6 = (bf16[64,2688]{1,0:T(8,128)(2,1)S(1)}, bf16[64,2688]{1,0:T(8,128)(2,1)S(1)}, u32[]{:S(2)}, u32[]{:S(2)}) collective-permute-start(bf16[64,2688]{1,0:T(8,128)(2,1)S(1)} %bitcast.12), channel_id=1, source_target_pairs={{0,4},{4,0},{8,12},{12,8},{16,20},{20,16},{24,28},{28,24},{1,5},{5... | collective-permute-start | bytes 1032200 | tf_op jit(solution)/shard_map/ppermute | solution.py:87
  29.4 15.1 %collective-permute-start.10 = (bf16[512,384]{1,0:T(8,128)(2,1)S(1)}, bf16[512,384]{1,0:T(8,128)(2,1)S(1)}, u32[]{:S(2)}, u32[]{:S(2)}) collective-permute-start(bf16[512,384]{1,0:T(8,128)(2,1)S(1)} %get-tuple-element.30), channel_id=1, source_target_pairs={{0,1},{1,0},{2,3},{3,2},{4,5},{5,4},{6,7},{7,6},{8,9},{9,8},{10,11... | collective-permute-start | bytes 1179656 | tf_op jit(solution)/shard_map/ppermute | solution.py:87
  35.6 13.7 %collective-permute-start.12 = (bf16[512,384]{1,0:T(8,128)(2,1)S(1)}, bf16[512,384]{1,0:T(8,128)(2,1)S(1)}, u32[]{:S(2)}, u32[]{:S(2)}) collective-permute-start(bf16[512,384]{1,0:T(8,128)(2,1)S(1)} %get-tuple-element.34), channel_id=1, source_target_pairs={{0,3},{1,2},{2,1},{3,0},{4,7},{5,6},{6,5},{7,4},{8,11},{9,10},{10,... | collective-permute-start | bytes 1179656 | tf_op jit(solution)/shard_map/ppermute | solution.py:87
  38.2 1.7 %collective-permute-start.7 = (bf16[64,2688]{1,0:T(8,128)(2,1)S(1)}, bf16[64,2688]{1,0:T(8,128)(2,1)S(1)}, u32[]{:S(2)}, u32[]{:S(2)}) collective-permute-start(bf16[64,2688]{1,0:T(8,128)(2,1)S(1)} %collective-permute-done.3.refs_1_.refs_9_), channel_id=1, source_target_pairs={{0,4},{4,0},{8,12},{12,8},{16,20},{20,16},{24,28},{28,24},{1,5},{5... | collective-permute-start | bytes 1032200 | tf_op jit(solution)/shard_map/ppermute | solution.py:87
  38.2 2.1 %collective-permute-start.8 = (bf16[64,2688]{1,0:T(8,128)(2,1)S(1)}, bf16[64,2688]{1,0:T(8,128)(2,1)S(1)}, u32[]{:S(2)}, u32[]{:S(2)}) collective-permute-start(bf16[64,2688]{1,0:T(8,128)(2,1)S(1)} %collective-permute-done.4.refs_2_.refs_10_), channel_id=1, source_target_pairs={{0,4},{4,0},{8,12},{12,8},{16,20},{20,16},{24,28},{28,24},{1,5},{5... | collective-permute-start | bytes 1032200 | tf_op jit(solution)/shard_map/ppermute | solution.py:87
  38.7 2.1 %collective-permute-start.9 = (bf16[64,2688]{1,0:T(8,128)(2,1)S(1)}, bf16[64,2688]{1,0:T(8,128)(2,1)S(1)}, u32[]{:S(2)}, u32[]{:S(2)}) collective-permute-start(bf16[64,2688]{1,0:T(8,128)(2,1)S(1)} %collective-permute-done.5.refs_3_.refs_11_), channel_id=1, source_target_pairs={{0,4},{4,0},{8,12},{12,8},{16,20},{20,16},{24,28},{28,24},{1,5},{5... | collective-permute-start | bytes 1032200 | tf_op jit(solution)/shard_map/ppermute | solution.py:87
  50.8 12.8 %copy-start.1 = (bf16[1,512,768]{2,1,0:T(8,128)(2,1)S(1)}, bf16[1,512,768]{2,1,0:T(8,128)(2,1)}, u32[]{:S(2)}) copy-start(bf16[1,512,768]{2,1,0:T(8,128)(2,1)} %param.14) | copy-start | bytes 2359300
  50.8 12.8 %copy-start.2 = (bf16[1,512,768]{2,1,0:T(8,128)(2,1)S(1)}, bf16[1,512,768]{2,1,0:T(8,128)(2,1)}, u32[]{:S(2)}) copy-start(bf16[1,512,768]{2,1,0:T(8,128)(2,1)} %param.15) | copy-start | bytes 2359300
  50.8 12.8 %copy-start.3 = (bf16[1,512,768]{2,1,0:T(8,128)(2,1)S(1)}, bf16[1,512,768]{2,1,0:T(8,128)(2,1)}, u32[]{:S(2)}) copy-start(bf16[1,512,768]{2,1,0:T(8,128)(2,1)} %param.16) | copy-start | bytes 2359300
  50.8 7.3 %collective-permute-start.13 = (bf16[768,128]{1,0:T(8,128)(2,1)S(1)}, bf16[768,128]{1,0:T(8,128)(2,1)S(1)}, u32[]{:S(2)}, u32[]{:S(2)}) collective-permute-start(bf16[768,128]{1,0:T(8,128)(2,1)S(1)} %hidden_blocks.1.refs_0_), channel_id=1, source_target_pairs={{0,1},{1,0},{2,3},{3,2},{4,5},{5,4},{6,7},{7,6},{8,9},{9,8},{10,11... | collective-permute-start | bytes 589832 | tf_op jit(solution)/shard_map/ppermute | solution.py:87
  50.9 12.7 %collective-permute-start.14 = (bf16[768,128]{1,0:T(8,128)(2,1)S(1)}, bf16[768,128]{1,0:T(8,128)(2,1)S(1)}, u32[]{:S(2)}, u32[]{:S(2)}) collective-permute-start(bf16[768,128]{1,0:T(8,128)(2,1)S(1)} %hidden_blocks.1.refs_0_), channel_id=1, source_target_pairs={{0,2},{1,3},{2,0},{3,1},{4,6},{5,7},{6,4},{7,5},{8,10},{9,11},{10,... | collective-permute-start | bytes 589832 | tf_op jit(solution)/shard_map/ppermute | solution.py:87
  53.5 10.2 %collective-permute-start.15 = (bf16[768,128]{1,0:T(8,128)(2,1)S(1)}, bf16[768,128]{1,0:T(8,128)(2,1)S(1)}, u32[]{:S(2)}, u32[]{:S(2)}) collective-permute-start(bf16[768,128]{1,0:T(8,128)(2,1)S(1)} %hidden_blocks.1.refs_0_), channel_id=1, source_target_pairs={{0,3},{1,2},{2,1},{3,0},{4,7},{5,6},{6,5},{7,4},{8,11},{9,10},{10,... | collective-permute-start | bytes 589832 | tf_op jit(solution)/shard_map/ppermute | solution.py:87
  92.5 5.0 %collective-permute-start.16 = (bf16[4,96,128]{2,1,0:T(8,128)(2,1)S(1)}, bf16[4,96,128]{2,1,0:T(8,128)(2,1)S(1)}, u32[]{:S(2)}, u32[]{:S(2)}) collective-permute-start(bf16[4,96,128]{2,1,0:T(8,128)(2,1)S(1)} %get-tuple-element.36), channel_id=1, source_target_pairs={{0,4},{4,0},{8,12},{12,8},{16,20},{20,16},{24,28},{28,24},{1,5},{5... | collective-permute-start | bytes 294920 | tf_op jit(solution)/shard_map/ppermute | solution.py:87
  94.1 5.1 %collective-permute-start.17 = (bf16[4,96,128]{2,1,0:T(8,128)(2,1)S(1)}, bf16[4,96,128]{2,1,0:T(8,128)(2,1)S(1)}, u32[]{:S(2)}, u32[]{:S(2)}) collective-permute-start(bf16[4,96,128]{2,1,0:T(8,128)(2,1)S(1)} %get-tuple-element.37), channel_id=1, source_target_pairs={{0,8},{4,12},{8,0},{12,4},{16,24},{20,28},{24,16},{28,20},{1,9},{5... | collective-permute-start | bytes 294920 | tf_op jit(solution)/shard_map/ppermute | solution.py:87
  95.5 5.1 %collective-permute-start.18 = (bf16[4,96,128]{2,1,0:T(8,128)(2,1)S(1)}, bf16[4,96,128]{2,1,0:T(8,128)(2,1)S(1)}, u32[]{:S(2)}, u32[]{:S(2)}) collective-permute-start(bf16[4,96,128]{2,1,0:T(8,128)(2,1)S(1)} %get-tuple-element.38), channel_id=1, source_target_pairs={{0,12},{4,8},{8,4},{12,0},{16,28},{20,24},{24,20},{28,16},{1,13},{... | collective-permute-start | bytes 294920 | tf_op jit(solution)/shard_map/ppermute | solution.py:87
  95.5 5.7 %collective-permute-start.19 = (bf16[4,96,128]{2,1,0:T(8,128)(2,1)S(1)}, bf16[4,96,128]{2,1,0:T(8,128)(2,1)S(1)}, u32[]{:S(2)}, u32[]{:S(2)}) collective-permute-start(bf16[4,96,128]{2,1,0:T(8,128)(2,1)S(1)} %get-tuple-element.39), channel_id=1, source_target_pairs={{0,16},{4,20},{8,24},{12,28},{16,0},{20,4},{24,8},{28,12},{1,17},{... | collective-permute-start | bytes 294920 | tf_op jit(solution)/shard_map/ppermute | solution.py:87
  97.0 9.9 %collective-permute-start.20 = (bf16[4,96,128]{2,1,0:T(8,128)(2,1)S(1)}, bf16[4,96,128]{2,1,0:T(8,128)(2,1)S(1)}, u32[]{:S(2)}, u32[]{:S(2)}) collective-permute-start(bf16[4,96,128]{2,1,0:T(8,128)(2,1)S(1)} %get-tuple-element.40), channel_id=1, source_target_pairs={{0,20},{4,16},{8,28},{12,24},{16,4},{20,0},{24,12},{28,8},{1,21},{... | collective-permute-start | bytes 294920 | tf_op jit(solution)/shard_map/ppermute | solution.py:87
  97.6 9.4 %collective-permute-start.21 = (bf16[4,96,128]{2,1,0:T(8,128)(2,1)S(1)}, bf16[4,96,128]{2,1,0:T(8,128)(2,1)S(1)}, u32[]{:S(2)}, u32[]{:S(2)}) collective-permute-start(bf16[4,96,128]{2,1,0:T(8,128)(2,1)S(1)} %get-tuple-element.41), channel_id=1, source_target_pairs={{0,24},{4,28},{8,16},{12,20},{16,8},{20,12},{24,0},{28,4},{1,25},{... | collective-permute-start | bytes 294920 | tf_op jit(solution)/shard_map/ppermute | solution.py:87
  99.2 7.8 %collective-permute-start.22 = (bf16[4,96,128]{2,1,0:T(8,128)(2,1)S(1)}, bf16[4,96,128]{2,1,0:T(8,128)(2,1)S(1)}, u32[]{:S(2)}, u32[]{:S(2)}) collective-permute-start(bf16[4,96,128]{2,1,0:T(8,128)(2,1)S(1)} %get-tuple-element.42), channel_id=1, source_target_pairs={{0,28},{4,24},{8,20},{12,16},{16,12},{20,8},{24,4},{28,0},{1,29},{... | collective-permute-start | bytes 294920 | tf_op jit(solution)/shard_map/ppermute | solution.py:87

commit v4 on v3

v4 whole, which is shorter than its diff:
```python
import functools

import jax
import jax.numpy as jnp
from jax import lax
from jax.experimental import pallas as pl
from jax.experimental.pallas import tpu as pltpu
from jax.sharding import PartitionSpec as P

OPT_STEP = 2


BETA_ONE = 0.9
BETA_TWO = 0.95
ADAM_EPS = 1e-08
LEARN_RATE = 0.25

BF16 = jnp.bfloat16
F32 = jnp.float32
LANES = 128
HALF = LANES // 2
CORES = 2
VMEM_BYTES = 24 * 1024 * 1024


def adam(down, moment1, moment2, grad):
    correct_one = 1.0 - BETA_ONE**OPT_STEP
    correct_two = 1.0 - BETA_TWO**OPT_STEP
    first = BETA_ONE * moment1.astype(F32) + (1.0 - BETA_ONE) * grad
    second = BETA_TWO * moment2.astype(F32) + (1.0 - BETA_TWO) * grad * grad
    direction = first / correct_one / (jnp.sqrt(second / correct_two) + ADAM_EPS)
    return (down.astype(F32) - LEARN_RATE * direction).astype(BF16)


def routed(tokens, cotangent, route_ids, route_gates, gate_up, down, moment1, moment2, placement):
    experts = lax.axis_size("expert")
    tok_rows = tokens.shape[0]
    width = tokens.shape[1]
    top_count = route_ids.shape[1]
    hidden_units = down.shape[2]
    capacity = min(tok_rows, 2 * tok_rows * top_count // experts)
    total_slots = experts * capacity
    route_hits = jnp.sum(
        (route_ids[:, :, None] == jnp.arange(experts, dtype=jnp.int32)).astype(jnp.int32), axis=1
    )
    earlier_hits = jnp.cumsum(route_hits, axis=0) - route_hits
    slot_index = jnp.take_along_axis(earlier_hits, route_ids, axis=1)
    target_slot = route_ids * capacity + slot_index
    matched = (target_slot[:, :, None] == jnp.arange(total_slots, dtype=jnp.int32)).astype(F32)
    picker = jnp.sum(matched, axis=1).astype(BF16)
    contract_rows = (((0,), (0,)), ((), ()))
    send_rows = lax.dot_general(picker, tokens, contract_rows, preferred_element_type=F32)
    send_rows = send_rows.astype(BF16).reshape(experts, capacity, width)
    send_grads = lax.dot_general(picker, cotangent, contract_rows, preferred_element_type=F32)
    send_grads = send_grads.astype(BF16).reshape(experts, capacity, width)
    send_gates = jnp.sum(matched * route_gates.astype(F32)[:, :, None], axis=(0, 1))
    send_gates = send_gates.astype(BF16).reshape(experts, capacity)
    rows_in, grads_in, gates_in = (
        lax.all_to_all(send_rows, "expert", split_axis=0, concat_axis=0, tiled=True),
        lax.all_to_all(send_grads, "expert", split_axis=0, concat_axis=0, tiled=True),
        lax.all_to_all(send_gates, "expert", split_axis=0, concat_axis=0, tiled=True),
    )
    pre_all = jnp.dot(
        rows_in.reshape(total_slots, width),
        lax.all_gather(gate_up, "dp", axis=1, tiled=True)[0],
        preferred_element_type=F32,
    )
    hidden = (jax.nn.silu(pre_all[:, :hidden_units]) * pre_all[:, hidden_units:]).astype(BF16)
    scaled = gates_in.reshape(total_slots, 1).astype(F32) * grads_in.reshape(
        total_slots, width
    ).astype(F32)
    partial = lax.dot_general(
        scaled.astype(BF16), hidden, contract_rows, preferred_element_type=F32
    ).astype(BF16)
    grad_share = lax.psum_scatter(partial, "dp", scatter_dimension=0, tiled=True).astype(F32)
    updated = adam(down[0], moment1[0], moment2[0], grad_share)
    column_block = lax.all_to_all(updated, "dp", split_axis=1, concat_axis=0, tiled=True)
    block_cols = column_block.shape[1]
    piece_flat = column_block.reshape(experts, width * block_cols // experts)
    spread = lax.all_to_all(piece_flat, "expert", split_axis=0, concat_axis=0, tiled=True)
    picked = jnp.take(spread, placement, axis=0)
    landed = lax.all_to_all(picked, "expert", split_axis=0, concat_axis=0, tiled=True)
    return landed.reshape(1, width, block_cols)


def partner(x, axis, flip):
    size = lax.axis_size(axis)
    return lax.ppermute(x, axis, [(i, i ^ flip) for i in range(size)])


def smem():
    return pl.BlockSpec(memory_space=pltpu.SMEM)


def whole():
    return pl.BlockSpec(memory_space=pltpu.VMEM)


def pack_rows_kernel(tok, cot, ids, gates, *outs):
    groups = len(outs)
    width = tok.shape[1]
    block = width // groups
    group = lax.axis_index("dp")
    named = ids[...]
    weights = gates[...].astype(F32)
    expert = lax.broadcasted_iota(jnp.int32, (LANES, named.shape[1]), 0)
    table = jnp.zeros(expert.shape, F32)
    for k in range(named.shape[0]):
        table = table + jnp.where(expert == named[k : k + 1, :], weights[k : k + 1, :], 0.0)
    table = table.T.astype(BF16)
    for flip, out in enumerate(outs):
        start = pl.multiple_of((group ^ flip) * block, LANES)
        out[:, :width] = tok[...]
        out[:, width : width + block] = cot[:, pl.ds(start, block)]
        out[:, width + block :] = table


def pack_rows(tokens, cotangent, ids, gates, groups):
    rows, width = tokens.shape
    return pl.pallas_call(
        pack_rows_kernel,
        out_shape=[pltpu.VMEM((rows, width + width // groups + LANES), BF16)] * groups,
        in_specs=[whole()] * 4,
        name="pack_rows",
    )(tokens, cotangent, ids.T, gates.T)


def swap_halves(x):
    return jnp.concatenate([x[:, HALF:], x[:, :HALF]], axis=1)


def low_half(shape):
    return lax.broadcasted_iota(jnp.int32, shape, 1) < HALF


def pack_weights_kernel(weights, *outs):
    groups = len(outs)
    hidden_units = weights.shape[1] // 2
    group = lax.axis_index("dp")
    low = low_half((weights.shape[0], LANES))
    for pair in range(groups // 2):
        gate, up = (
            [
                weights[:, start + i * LANES : start + (i + 1) * LANES]
                for i in range(pair * 3, pair * 3 + 3)
            ]
            for start in (0, hidden_units)
        )
        even = gate[0], up[0], jnp.where(low, gate[1], swap_halves(up[1]))
        odd = (
            swap_halves(jnp.where(low, gate[2], gate[1])),
            swap_halves(jnp.where(low, up[2], up[1])),
            jnp.where(low, swap_halves(up[2]), gate[2]),
        )
        for parity, tiles in enumerate((even, odd)):
            for flip, out in enumerate(outs):

                @pl.when((group ^ flip) == 2 * pair + parity)
                def _():
                    for i, tile in enumerate(tiles):
                        out[:, i * LANES : (i + 1) * LANES] = tile


def pack_weights(weights, groups):
    rows, cols = weights.shape
    return pl.pallas_call(
        pack_weights_kernel,
        out_shape=[pltpu.VMEM((rows, cols // groups), BF16)] * groups,
        in_specs=[whole()],
        compiler_params=pltpu.CompilerParams(vmem_limit_bytes=VMEM_BYTES),
        name="pack_weights",
    )(weights)


def after(x, *others):
    return lax.optimization_barrier((x, *others))[0]


def in_vmem(x):
    return pltpu.with_memory_space_constraint(x, pltpu.VMEM)


def order_groups_kernel(*refs):
    *blocks, out = refs
    for flip, block in enumerate(blocks):
        out[pl.ds(lax.axis_index("dp") ^ flip, 1)] = block[...][None]


def order_groups(blocks):
    rows, width = blocks[0].shape
    out = pl.pallas_call(
        order_groups_kernel,
        out_shape=pltpu.VMEM((len(blocks), rows, width), BF16),
        in_specs=[whole()] * len(blocks),
        name="order_groups",
    )(*[in_vmem(x) for x in blocks])
    return out.reshape(len(blocks) * rows, width)


def silu(x):
    return x / (1.0 + jnp.exp(-x))


def hidden_kernel(pieces, bounds, *refs):
    row_refs, refs = refs[:pieces], refs[pieces:]
    groups = lax.axis_size("dp")
    weight_refs, outs, (toks, hidden) = refs[:groups], refs[groups:-2], refs[-2:]
    rows, width = row_refs[0].shape[0], toks.shape[1]
    block = width // groups
    group = lax.axis_index("dp")
    for i, ref in enumerate(row_refs):
        toks[i * rows : (i + 1) * rows, :] = ref[:, :width]
    pre = None
    for flip, ref in enumerate(weight_refs):
        start = pl.multiple_of((group ^ flip) * block, LANES)
        term = jnp.dot(toks[:, pl.ds(start, block)], ref[...], preferred_element_type=F32)
        pre = term if pre is None else pre + term
    gate, up, shared = (pre[:, i * LANES : (i + 1) * LANES] for i in range(3))
    hidden[:LANES, :] = (silu(gate) * up).T.astype(BF16)
    halves = (silu(shared) * swap_halves(shared)).T.astype(BF16)
    for parity in range(2):

        @pl.when(lax.rem(group, 2) == parity)
        def _():
            hidden[LANES:, :] = halves[parity * HALF : (parity + 1) * HALF]

    for (start, end), out in zip(bounds, outs, strict=True):
        out[...] = hidden[start:end, :]


def hidden_units(pieces, weights, width, bounds):
    rows = pieces[0].shape[0]
    total = rows * len(pieces)
    return pl.pallas_call(
        functools.partial(hidden_kernel, len(pieces), bounds),
        out_shape=[pltpu.VMEM((end - start, total), BF16) for start, end in bounds],
        in_specs=[whole()] * (len(pieces) + len(weights)),
        scratch_shapes=[
            pltpu.VMEM((total, width), BF16),
            pltpu.VMEM((weights[0].shape[1] // 2, total), BF16),
        ],
        compiler_params=pltpu.CompilerParams(vmem_limit_bytes=VMEM_BYTES),
        name="hidden_units",
    )(*[in_vmem(x) for x in [*pieces, *weights]])


def scaled_kernel(start, *refs):
    *pieces, out = refs
    rows, block = pieces[0].shape[0], out.shape[1]
    blocks = []
    for piece in pieces:
        gates = piece[:, start + block :].astype(F32)
        lane = lax.broadcasted_iota(jnp.int32, gates.shape, 1)
        here = lane == lax.axis_index("expert")
        gate = jnp.sum(jnp.where(here, gates, 0.0), axis=1, keepdims=True)
        cot = piece[:, start : start + block].astype(F32)
        blocks.append((gate * cot).astype(BF16))
    out[...] = jnp.concatenate(blocks, axis=0)


def scaled_rows(pieces, width, block):
    total = pieces[0].shape[0] * len(pieces)
    return pl.pallas_call(
        functools.partial(scaled_kernel, width),
        out_shape=pltpu.VMEM((total, block), BF16),
        in_specs=[whole()] * len(pieces),
        compiler_params=pltpu.CompilerParams(vmem_limit_bytes=VMEM_BYTES),
        name="scaled_rows",
    )(*[in_vmem(x) for x in pieces])


def flip_kernel(*refs):
    half = len(refs) // 2
    for x, out in zip(refs[:half], refs[half:], strict=True):
        out[...] = x[...].T


def transposed(*arrays):
    return pl.pallas_call(
        flip_kernel,
        out_shape=[pltpu.VMEM(x.shape[::-1], x.dtype) for x in arrays],
        in_specs=[whole()] * len(arrays),
        compiler_params=pltpu.CompilerParams(vmem_limit_bytes=VMEM_BYTES),
        name="transposed",
    )(*arrays)


def update_kernel(start, *refs):
    groups = lax.axis_size("dp")
    hid_refs, (scaled, down, first, second), refs = refs[:groups], refs[groups : groups + 4], refs[groups + 4 :]
    outs, hidden = refs[:-1], refs[-1]
    rows = hid_refs[0].shape[0]
    cols = down.shape[0] // groups
    for flip, ref in enumerate(hid_refs):
        hidden[flip * rows : (flip + 1) * rows, :] = ref[...]
    for flip, out in enumerate(outs):
        tile = (lax.axis_index("expert") // CORES) ^ flip
        lanes = pl.ds(pl.multiple_of(tile * LANES, LANES), LANES)
        grad = jnp.dot(hidden[...], scaled[:, lanes], preferred_element_type=F32)
        for other in range(groups):
            at = pl.multiple_of((lax.axis_index("dp") ^ other) * cols + start, 16)
            here = pl.ds(at, rows), lanes
            part = grad[other * rows : (other + 1) * rows]
            out[other] = adam(down[here], first[here], second[here], part)


def update_tiles(hidden, scaled, state, start, chips):
    groups = len(hidden)
    rows, total = hidden[0].shape
    return pl.pallas_call(
        functools.partial(update_kernel, start),
        out_shape=[pltpu.VMEM((groups, rows, scaled.shape[1] // chips), BF16)] * chips,
        in_specs=[whole()] * (groups + 4),
        scratch_shapes=[pltpu.VMEM((groups * rows, total), BF16)],
        compiler_params=pltpu.CompilerParams(vmem_limit_bytes=VMEM_BYTES),
        name="update_tiles",
    )(*[in_vmem(x) for x in [*hidden, scaled, *state]])


def regroup_kernel(*refs):
    chips = lax.axis_size("expert") // CORES
    tiles, outs = refs[:chips], refs[chips:]
    own = lax.axis_index("expert") // CORES
    for flip, tile in enumerate(tiles):
        for other, out in enumerate(outs):
            out[pl.ds(own ^ flip, 1)] = tile[other][None]


def regroup(tiles):
    groups, *tile = tiles[0].shape
    return pl.pallas_call(
        regroup_kernel,
        out_shape=[pltpu.VMEM((len(tiles), *tile), BF16)] * groups,
        in_specs=[whole()] * len(tiles),
        name="regroup",
    )(*[in_vmem(x) for x in tiles])


def pick_kernel(order, *refs):
    groups, chips = lax.axis_size("dp"), lax.axis_size("expert") // CORES
    kept, swapped, outs = refs[:groups], refs[groups : 2 * groups], refs[2 * groups :]
    spot = lax.axis_index("expert")
    core = lax.rem(spot, CORES)
    for flip, out in enumerate(outs):
        source = order[spot ^ (flip * CORES)]
        chip, here = source // CORES, lax.rem(source, CORES) == core

        @pl.when(here)
        def _():
            for i in range(groups):
                out[i] = kept[i][chip]

        @pl.when(jnp.logical_not(here))
        def _():
            for i in range(groups):
                out[i] = swapped[i][chip]


def pick(order, kept, swapped):
    chips, *tile = kept[0].shape
    return pl.pallas_call(
        pick_kernel,
        out_shape=[pltpu.VMEM((len(kept), *tile), BF16)] * chips,
        in_specs=[smem()] + [whole()] * (2 * len(kept)),
        name="pick",
    )(order, *[in_vmem(x) for x in [*kept, *swapped]])


def unpack_kernel(bounds, *refs):
    *pieces, out = refs
    groups = pieces[0].shape[0]
    block = out.shape[2] // groups
    chips = len(pieces) // len(bounds)
    for i, piece in enumerate(pieces):
        start, end = bounds[i // chips]
        tile = (lax.axis_index("expert") // CORES) ^ (i % chips)
        for other in range(groups):
            left = (lax.axis_index("dp") ^ other) * block + tile * LANES
            out[0, start:end, pl.ds(pl.multiple_of(left, LANES), LANES)] = piece[other]


def unpack(pieces, bounds, width, cols):
    return pl.pallas_call(
        functools.partial(unpack_kernel, bounds),
        out_shape=jax.ShapeDtypeStruct((1, cols, width), BF16),
        in_specs=[whole()] * len(pieces),
        out_specs=whole(),
        name="unpack",
    )(*[in_vmem(x) for x in pieces])


def dense(tokens, cotangent, route_ids, route_gates, gate_up, down, moment1, moment2, placement):
    experts = lax.axis_size("expert")
    groups = lax.axis_size("dp")
    width = tokens.shape[1]
    units = down.shape[2]
    block = width // groups

    own, near, far, farthest = pack_weights(gate_up[0], groups)
    sent = pack_rows(tokens, cotangent, route_ids, route_gates, groups)
    blocks = [sent[0]] + [partner(sent[k], "dp", k) for k in range(1, groups)]
    state = transposed(down[0], moment1[0], moment2[0])
    plane = order_groups([after(blocks[0], state[0]), *blocks[1:]])
    chips = [plane] + [partner(plane, "expert", k) for k in range(2, experts, 2)]
    pieces = chips + [partner(x, "expert", 1) for x in chips]
    far = partner(after(far, blocks[1]), "dp", 2)
    near = partner(after(near, chips[1]), "dp", 1)
    farthest = partner(after(farthest, far), "dp", 3)

    cols = units // groups
    bounds = ((0, cols),)
    parts = hidden_units(pieces, [own, near, far, farthest], width, bounds)
    scaled = scaled_rows(pieces, width, block)
    landed = []
    for (start, _), part in zip(bounds, parts, strict=True):
        hidden = [part] + [partner(part, "dp", k) for k in range(1, groups)]
        tiles = update_tiles(hidden, scaled, state, start, experts // CORES)
        tiles = [tiles[0]] + [
            partner(tiles[k], "expert", k * CORES) for k in range(1, len(tiles))
        ]
        split = regroup(tiles)
        kept = [split[0]] + [partner(split[k], "dp", k) for k in range(1, groups)]
        swapped = [partner(x, "expert", 1) for x in kept]
        picked = pick(placement, kept, swapped)
        landed += [picked[0]] + [
            partner(picked[k], "expert", k * CORES) for k in range(1, len(picked))
        ]
    return unpack(landed, bounds, width, cols).transpose(0, 2, 1)


def shards(tokens, cotangent, route_ids, *rest):
    every = route_ids.shape[1] == lax.axis_size("expert")
    return (dense if every else routed)(tokens, cotangent, route_ids, *rest)


def solution(mesh):
    placed = (
        P(("expert", "dp"), None),
        P(("expert", "dp"), None),
        P(("expert", "dp"), None),
        P(("expert", "dp"), None),
        P("expert", "dp", None),
        P("expert", "dp", None),
        P("expert", "dp", None),
        P("expert", "dp", None),
        P(),
    )
    return jax.shard_map(
        shards, mesh=mesh, in_specs=placed, out_specs=P("expert", None, "dp"), check_vma=False
    )
```

time: 108 us -> 105 us (0.972)
  blocking collectives: 25.1 us -> 0 us
  waiting for transfers between devices: 40.9 us -> 54.1 us
  starting transfers between devices: 32.2 us -> 38.1 us
  Pallas kernels: 8.14 us -> 9.55 us
  local copies, waits for them, and re-layouts: 1.43 us -> 2.56 us
    all_to_all x1 -> x0, blocking collectives: 25.1 us -> none  [dense(): spread = lax.all_to_all(moved, ('expert', 'dp'), 0, 0, tiled=True)]
    ppermute x23 -> x29, waiting for transfers between devices: 40.9 us -> 54.1 us  [partner(): return lax.ppermute(x, axis, [(i, i ^ flip) for i in range(size)])]
    ppermute x23 -> x29, starting transfers between devices: 32.2 us -> 38.1 us  [partner(): return lax.ppermute(x, axis, [(i, i ^ flip) for i in range(size)])]
    pallas_call x6 -> x8, Pallas kernels: 7.13 us -> 8.53 us  [the longest x1 2.57 us: hidden_units(): pl.pallas_call(functools.partial(hidden_kernel, len(pieces), bounds), out...]
    unnamed x8 -> x12, local copies, waits for them, and re-layouts: 1.43 us -> 2.56 us
  transfers between devices with their start and end apart: 23 -> 29, of which waited for: 13 -> 19; matrix products, arithmetic and copies ran while one was open for 0% -> 0% of each run, Pallas kernels for 1% -> 2%
where the time goes in v4:
time: 105 us; the launch traced here: 104 us
  waiting for transfers between devices  54.1 us (52%)
  starting transfers between devices  38.1 us (36%)
  Pallas kernels  9.55 us (9%)
  local copies, waits for them, and re-layouts  2.56 us (2%)
    ppermute x29, waiting for transfers between devices, partner(): return lax.ppermute(x, axis, [(i, i ^ flip) for i in range(size)])  54.1 us
    ppermute x29, starting transfers between devices, partner(): return lax.ppermute(x, axis, [(i, i ^ flip) for i in range(size)])  38.1 us
    pallas_call x1, Pallas kernels, hidden_units(): pl.pallas_call(functools.partial(hidden_kernel, len(pieces), bounds), out...  2.57 us
    unnamed x12, local copies, waits for them, and re-layouts  2.56 us
  transfers between devices with their start and end apart: 29, of which 19 were waited for; matrix products, arithmetic and copies ran while one was open for 0% of the time, Pallas kernels for 2%

profile of v4, /device:TPU:0, one launch (start us, length us, event | category | flops | bytes accessed | tf_op | source)
XLA Modules:
  0.0 104.4 jit_solution(13300113766367997638)
XLA Ops:
  0.0 1.0 pack_rows.1
  1.0 3.1 %collective-permute-start = (bf16[16,2688]{1,0:T(8,128)(2,1)S(1)}, bf16[16,2688]{1,0:T(8,128)(2,1)S(1)}, u32[]{:S(2)}, u32[]{:S(2)}) collective-permute-start(bf16[16,2688]{1,0:T(8,128)(2,1)S(1)} %get-tuple-element.35), channel_id=1, source_target_pairs={{0,1},{1,0},{2,3},{3,2},{4,5},{5,4},{6,7},{7,6},{8,9},{9,8},{10,11... | collective-permute-start | bytes 258056 | tf_op jit(solution)/shard_map/ppermute | solution.py:88
  4.0 2.6 %collective-permute-start.1 = (bf16[16,2688]{1,0:T(8,128)(2,1)S(1)}, bf16[16,2688]{1,0:T(8,128)(2,1)S(1)}, u32[]{:S(2)}, u32[]{:S(2)}) collective-permute-start(bf16[16,2688]{1,0:T(8,128)(2,1)S(1)} %get-tuple-element.36), channel_id=1, source_target_pairs={{0,2},{1,3},{2,0},{3,1},{4,6},{5,7},{6,4},{7,5},{8,10},{9,11},{10,... | collective-permute-start | bytes 258056 | tf_op jit(solution)/shard_map/ppermute | solution.py:88
  6.6 1.4 %copy-done = bf16[1,512,1536]{2,1,0:T(8,128)(2,1)S(1)} copy-done((bf16[1,512,1536]{2,1,0:T(8,128)(2,1)S(1)}, bf16[1,512,1536]{2,1,0:T(8,128)(2,1)}, u32[]{:S(2)}) %copy-start) | copy-done | bytes 1572888
  8.0 1.4 %pack_weights.1 = (bf16[512,384]{1,0:T(8,128)(2,1)S(1)}, bf16[512,384]{1,0:T(8,128)(2,1)S(1)}, bf16[512,384]{1,0:T(8,128)(2,1)}, bf16[512,384]{1,0:T(8,128)(2,1)S(1)}) custom-call(bf16[512,1536]{1,0:T(8,128)(2,1)S(1)} %bitcast.14), custom_call_target="tpu_custom_call" | custom-call | tf_op jit(solution)/shard_map/pack_weights/pallas_call | solution.py:166
  9.5 1.9 %collective-permute-start.11 = (bf16[512,384]{1,0:T(8,128)(2,1)}, bf16[512,384]{1,0:T(8,128)(2,1)}, u32[]{:S(2)}, u32[]{:S(2)}) collective-permute-start(bf16[512,384]{1,0:T(8,128)(2,1)} %get-tuple-element.42), channel_id=1, source_target_pairs={{0,2},{1,3},{2,0},{3,1},{4,6},{5,7},{6,4},{7,5},{8,10},{9,11},{10,... | collective-permute-start | bytes 1179656 | tf_op jit(solution)/shard_map/ppermute | solution.py:88
  11.4 1.1 %copy-done.3 = bf16[1,512,768]{2,1,0:T(8,128)(2,1)S(1)} copy-done((bf16[1,512,768]{2,1,0:T(8,128)(2,1)S(1)}, bf16[1,512,768]{2,1,0:T(8,128)(2,1)}, u32[]{:S(2)}) %copy-start.3) | copy-done | bytes 786456
  12.5 0.7 transposed.1
  13.2 8.9 %collective-permute-done.1.refs_2_ = bf16[16,2688]{1,0:T(8,128)(2,1)S(1)} collective-permute-done((bf16[16,2688]{1,0:T(8,128)(2,1)S(1)}, bf16[16,2688]{1,0:T(8,128)(2,1)S(1)}, u32[]{:S(2)}, u32[]{:S(2)}) %collective-permute-start.1) | collective-permute-done | bytes 86048 | tf_op jit(solution)/shard_map/ppermute | solution.py:88
  22.1 1.6 %collective-permute-start.3 = (bf16[64,2688]{1,0:T(8,128)(2,1)S(1)}, bf16[64,2688]{1,0:T(8,128)(2,1)S(1)}, u32[]{:S(2)}, u32[]{:S(2)}) collective-permute-start(bf16[64,2688]{1,0:T(8,128)(2,1)S(1)} %bitcast.8), channel_id=1, source_target_pairs={{0,8},{4,12},{8,0},{12,4},{16,24},{20,28},{24,16},{28,20},{1,9},{5... | collective-permute-start | bytes 1032200 | tf_op jit(solution)/shard_map/ppermute | solution.py:88
  23.7 1.5 %collective-permute-start.5 = (bf16[64,2688]{1,0:T(8,128)(2,1)S(1)}, bf16[64,2688]{1,0:T(8,128)(2,1)S(1)}, u32[]{:S(2)}, u32[]{:S(2)}) collective-permute-start(bf16[64,2688]{1,0:T(8,128)(2,1)S(1)} %bitcast.9), channel_id=1, source_target_pairs={{0,24},{4,28},{8,16},{12,20},{16,8},{20,12},{24,0},{28,4},{1,25},{... | collective-permute-start | bytes 1032200 | tf_op jit(solution)/shard_map/ppermute | solution.py:88
  25.2 0.5 collective-permute-start.4
  25.7 3.8 %collective-permute-done.3.refs_1_ = bf16[64,2688]{1,0:T(8,128)(2,1)S(1)} collective-permute-done((bf16[64,2688]{1,0:T(8,128)(2,1)S(1)}, bf16[64,2688]{1,0:T(8,128)(2,1)S(1)}, u32[]{:S(2)}, u32[]{:S(2)}) %collective-permute-start.3) | collective-permute-done | bytes 344096 | tf_op jit(solution)/shard_map/ppermute | solution.py:88
  29.4 6.1 %collective-permute-start.10 = (bf16[512,384]{1,0:T(8,128)(2,1)}, bf16[512,384]{1,0:T(8,128)(2,1)S(1)}, u32[]{:S(2)}, u32[]{:S(2)}) collective-permute-start(bf16[512,384]{1,0:T(8,128)(2,1)} %copy-done.5), channel_id=1, source_target_pairs={{0,1},{1,0},{2,3},{3,2},{4,5},{5,4},{6,7},{7,6},{8,9},{9,8},{10,11... | collective-permute-start | bytes 1179656 | tf_op jit(solution)/shard_map/ppermute | solution.py:88
  35.6 2.6 %collective-permute-start.12 = (bf16[512,384]{1,0:T(8,128)(2,1)}, bf16[512,384]{1,0:T(8,128)(2,1)S(1)}, u32[]{:S(2)}, u32[]{:S(2)}) collective-permute-start(bf16[512,384]{1,0:T(8,128)(2,1)} %copy-done.4), channel_id=1, source_target_pairs={{0,3},{1,2},{2,1},{3,0},{4,7},{5,6},{6,5},{7,4},{8,11},{9,10},{10,... | collective-permute-start | bytes 1179656 | tf_op jit(solution)/shard_map/ppermute | solution.py:88
  38.2 0.5 collective-permute-start.8
  38.8 1.1 %collective-permute-done.9.refs_7_ = bf16[64,2688]{1,0:T(8,128)(2,1)S(1)} collective-permute-done((bf16[64,2688]{1,0:T(8,128)(2,1)S(1)}, bf16[64,2688]{1,0:T(8,128)(2,1)S(1)}, u32[]{:S(2)}, u32[]{:S(2)}) %collective-permute-start.9) | collective-permute-done | bytes 344096 | tf_op jit(solution)/shard_map/ppermute | solution.py:88
  39.8 0.5 collective-permute-done.8.refs_6_
  40.3 0.5 collective-permute-done.7.refs_5_
  40.8 3.9 %collective-permute-done.10.refs_9_ = bf16[512,384]{1,0:T(8,128)(2,1)S(1)} collective-permute-done((bf16[512,384]{1,0:T(8,128)(2,1)}, bf16[512,384]{1,0:T(8,128)(2,1)S(1)}, u32[]{:S(2)}, u32[]{:S(2)}) %collective-permute-start.10) | collective-permute-done | bytes 393248 | tf_op jit(solution)/shard_map/ppermute | solution.py:88
  44.7 5.2 %collective-permute-done.12.refs_11_ = bf16[512,384]{1,0:T(8,128)(2,1)S(1)} collective-permute-done((bf16[512,384]{1,0:T(8,128)(2,1)}, bf16[512,384]{1,0:T(8,128)(2,1)S(1)}, u32[]{:S(2)}, u32[]{:S(2)}) %collective-permute-start.12) | collective-permute-done | bytes 393248 | tf_op jit(solution)/shard_map/ppermute | solution.py:88
  49.9 2.6 %hidden_units.1.refs_0_ = bf16[192,512]{1,0:T(8,128)(2,1)S(1)} custom-call(bf16[64,2688]{1,0:T(8,128)(2,1)S(1)} %bitcast.12, bf16[64,2688]{1,0:T(8,128)(2,1)S(1)} %collective-permute-done.3.refs_1_, bf16[64,2688]{1,0:T(8,128)(2,1)S(1)} %collective-permute-done.4.refs_2_, bf16[64,2688]{1,0:T(8,128)(2,1)S(1)} %collective-permute-done.5.refs_3_, ...), custom_call_target="tpu_custom_call" | custom-call | tf_op jit(solution)/shard_map/hidden_units/pallas_call | solution.py:234
  52.5 1.5 %collective-permute-start.15 = (bf16[192,512]{1,0:T(8,128)(2,1)S(1)}, bf16[192,512]{1,0:T(8,128)(2,1)S(1)}, u32[]{:S(2)}, u32[]{:S(2)}) collective-permute-start(bf16[192,512]{1,0:T(8,128)(2,1)S(1)} %hidden_units.1.refs_0_), channel_id=1, source_target_pairs={{0,3},{1,2},{2,1},{3,0},{4,7},{5,6},{6,5},{7,4},{8,11},{9,10},{10,... | collective-permute-start | bytes 589832 | tf_op jit(solution)/shard_map/ppermute | solution.py:88
  54.0 4.0 %collective-permute-start.14 = (bf16[192,512]{1,0:T(8,128)(2,1)S(1)}, bf16[192,512]{1,0:T(8,128)(2,1)S(1)}, u32[]{:S(2)}, u32[]{:S(2)}) collective-permute-start(bf16[192,512]{1,0:T(8,128)(2,1)S(1)} %hidden_units.1.refs_0_), channel_id=1, source_target_pairs={{0,2},{1,3},{2,0},{3,1},{4,6},{5,7},{6,4},{7,5},{8,10},{9,11},{10,... | collective-permute-start | bytes 589832 | tf_op jit(solution)/shard_map/ppermute | solution.py:88
  58.0 0.2 scaled_rows.1.refs_4_
  58.2 1.8 %collective-permute-done.15.refs_3_ = bf16[192,512]{1,0:T(8,128)(2,1)S(1)} collective-permute-done((bf16[192,512]{1,0:T(8,128)(2,1)S(1)}, bf16[192,512]{1,0:T(8,128)(2,1)S(1)}, u32[]{:S(2)}, u32[]{:S(2)}) %collective-permute-start.15) | collective-permute-done | bytes 196640 | tf_op jit(solution)/shard_map/ppermute | solution.py:88
  60.0 6.3 %collective-permute-done.14.refs_2_ = bf16[192,512]{1,0:T(8,128)(2,1)S(1)} collective-permute-done((bf16[192,512]{1,0:T(8,128)(2,1)S(1)}, bf16[192,512]{1,0:T(8,128)(2,1)S(1)}, u32[]{:S(2)}, u32[]{:S(2)}) %collective-permute-start.14) | collective-permute-done | bytes 196640 | tf_op jit(solution)/shard_map/ppermute | solution.py:88
  66.3 1.8 %update_tiles.1 = (bf16[4,192,128]{2,1,0:T(8,128)(2,1)S(1)}, bf16[4,192,128]{2,1,0:T(8,128)(2,1)S(1)}, bf16[4,192,128]{2,1,0:T(8,128)(2,1)S(1)}, bf16[4,192,128]{2,1,0:T(8,128)(2,1)S(1)}) custom-call(bf16[192,512]{1,0:T(8,128)(2,1)S(1)} %hidden_units.1.refs_0_, bf16[192,512]{1,0:T(8,128)(2,1)S(1)} %collective-permute-done.13.refs_1_, ...), custom_call_target="tpu_custom_call" | custom-call | tf_op jit(solution)/shard_map/update_tiles/pallas_call | solution.py:310
  68.1 1.6 %collective-permute-start.16 = (bf16[4,192,128]{2,1,0:T(8,128)(2,1)S(1)}, bf16[4,192,128]{2,1,0:T(8,128)(2,1)S(1)}, u32[]{:S(2)}, u32[]{:S(2)}) collective-permute-start(bf16[4,192,128]{2,1,0:T(8,128)(2,1)S(1)} %get-tuple-element.48), channel_id=1, source_target_pairs={{0,8},{4,12},{8,0},{12,4},{16,24},{20,28},{24,16},{28,20},{1,9},{5... | collective-permute-start | bytes 589832 | tf_op jit(solution)/shard_map/ppermute | solution.py:88
  69.7 1.5 %collective-permute-start.17 = (bf16[4,192,128]{2,1,0:T(8,128)(2,1)S(1)}, bf16[4,192,128]{2,1,0:T(8,128)(2,1)S(1)}, u32[]{:S(2)}, u32[]{:S(2)}) collective-permute-start(bf16[4,192,128]{2,1,0:T(8,128)(2,1)S(1)} %get-tuple-element.49), channel_id=1, source_target_pairs={{0,16},{4,20},{8,24},{12,28},{16,0},{20,4},{24,8},{28,12},{1,17},{... | collective-permute-start | bytes 589832 | tf_op jit(solution)/shard_map/ppermute | solution.py:88
  71.2 0.5 collective-permute-start.18
  71.7 2.2 %collective-permute-done.16.refs_1_ = bf16[4,192,128]{2,1,0:T(8,128)(2,1)S(1)} collective-permute-done((bf16[4,192,128]{2,1,0:T(8,128)(2,1)S(1)}, bf16[4,192,128]{2,1,0:T(8,128)(2,1)S(1)}, u32[]{:S(2)}, u32[]{:S(2)}) %collective-permute-start.16) | collective-permute-done | bytes 196640 | tf_op jit(solution)/shard_map/ppermute | solution.py:88
  73.8 2.6 %collective-permute-done.17.refs_2_ = bf16[4,192,128]{2,1,0:T(8,128)(2,1)S(1)} collective-permute-done((bf16[4,192,128]{2,1,0:T(8,128)(2,1)S(1)}, bf16[4,192,128]{2,1,0:T(8,128)(2,1)S(1)}, u32[]{:S(2)}, u32[]{:S(2)}) %collective-permute-start.17) | collective-permute-done | bytes 196640 | tf_op jit(solution)/shard_map/ppermute | solution.py:88
  76.5 1.2 %collective-permute-done.18.refs_3_ = bf16[4,192,128]{2,1,0:T(8,128)(2,1)S(1)} collective-permute-done((bf16[4,192,128]{2,1,0:T(8,128)(2,1)S(1)}, bf16[4,192,128]{2,1,0:T(8,128)(2,1)S(1)}, u32[]{:S(2)}, u32[]{:S(2)}) %collective-permute-start.18) | collective-permute-done | bytes 196640 | tf_op jit(solution)/shard_map/ppermute | solution.py:88
  77.9 2.4 %collective-permute-start.20 = (bf16[4,192,128]{2,1,0:T(8,128)(2,1)S(1)}, bf16[4,192,128]{2,1,0:T(8,128)(2,1)S(1)}, u32[]{:S(2)}, u32[]{:S(2)}) collective-permute-start(bf16[4,192,128]{2,1,0:T(8,128)(2,1)S(1)} %get-tuple-element.53), channel_id=1, source_target_pairs={{0,2},{1,3},{2,0},{3,1},{4,6},{5,7},{6,4},{7,5},{8,10},{9,11},{10,... | collective-permute-start | bytes 589832 | tf_op jit(solution)/shard_map/ppermute | solution.py:88
  80.3 1.9 %collective-permute-start.21 = (bf16[4,192,128]{2,1,0:T(8,128)(2,1)S(1)}, bf16[4,192,128]{2,1,0:T(8,128)(2,1)S(1)}, u32[]{:S(2)}, u32[]{:S(2)}) collective-permute-start(bf16[4,192,128]{2,1,0:T(8,128)(2,1)S(1)} %get-tuple-element.54), channel_id=1, source_target_pairs={{0,3},{1,2},{2,1},{3,0},{4,7},{5,6},{6,5},{7,4},{8,11},{9,10},{10,... | collective-permute-start | bytes 589832 | tf_op jit(solution)/shard_map/ppermute | solution.py:88
  82.3 2.7 %collective-permute-done.19.refs_1_ = bf16[4,192,128]{2,1,0:T(8,128)(2,1)S(1)} collective-permute-done((bf16[4,192,128]{2,1,0:T(8,128)(2,1)S(1)}, bf16[4,192,128]{2,1,0:T(8,128)(2,1)S(1)}, u32[]{:S(2)}, u32[]{:S(2)}) %collective-permute-start.19) | collective-permute-done | bytes 196640 | tf_op jit(solution)/shard_map/ppermute | solution.py:88
  85.0 3.8 %collective-permute-done.20.refs_2_ = bf16[4,192,128]{2,1,0:T(8,128)(2,1)S(1)} collective-permute-done((bf16[4,192,128]{2,1,0:T(8,128)(2,1)S(1)}, bf16[4,192,128]{2,1,0:T(8,128)(2,1)S(1)}, u32[]{:S(2)}, u32[]{:S(2)}) %collective-permute-start.20) | collective-permute-done | bytes 196640 | tf_op jit(solution)/shard_map/ppermute | solution.py:88
  88.8 0.5 collective-permute-start.25
  89.3 0.9 collective-permute-done.24.refs_6_
  90.2 0.3 collective-permute-done.25.refs_7_
  90.5 0.8 pick.1
  91.3 0.7 collective-permute-start.26
  92.0 1.1 %collective-permute-start.27 = (bf16[4,192,128]{2,1,0:T(8,128)(2,1)S(1)}, bf16[4,192,128]{2,1,0:T(8,128)(2,1)S(1)}, u32[]{:S(2)}, u32[]{:S(2)}) collective-permute-start(bf16[4,192,128]{2,1,0:T(8,128)(2,1)S(1)} %get-tuple-element.57), channel_id=1, source_target_pairs={{0,16},{4,20},{8,24},{12,28},{16,0},{20,4},{24,8},{28,12},{1,17},{... | collective-permute-start | bytes 589832 | tf_op jit(solution)/shard_map/ppermute | solution.py:88
  93.1 1.7 %collective-permute-start.28 = (bf16[4,192,128]{2,1,0:T(8,128)(2,1)S(1)}, bf16[4,192,128]{2,1,0:T(8,128)(2,1)S(1)}, u32[]{:S(2)}, u32[]{:S(2)}) collective-permute-start(bf16[4,192,128]{2,1,0:T(8,128)(2,1)S(1)} %get-tuple-element.58), channel_id=1, source_target_pairs={{0,24},{4,28},{8,16},{12,20},{16,8},{20,12},{24,0},{28,4},{1,25},{... | collective-permute-start | bytes 589832 | tf_op jit(solution)/shard_map/ppermute | solution.py:88
  94.9 4.2 %collective-permute-done.26.refs_1_ = bf16[4,192,128]{2,1,0:T(8,128)(2,1)S(1)} collective-permute-done((bf16[4,192,128]{2,1,0:T(8,128)(2,1)S(1)}, bf16[4,192,128]{2,1,0:T(8,128)(2,1)S(1)}, u32[]{:S(2)}, u32[]{:S(2)}) %collective-permute-start.26) | collective-permute-done | bytes 196640 | tf_op jit(solution)/shard_map/ppermute | solution.py:88
  99.2 4.1 %collective-permute-done.28.refs_3_ = bf16[4,192,128]{2,1,0:T(8,128)(2,1)S(1)} collective-permute-done((bf16[4,192,128]{2,1,0:T(8,128)(2,1)S(1)}, bf16[4,192,128]{2,1,0:T(8,128)(2,1)S(1)}, u32[]{:S(2)}, u32[]{:S(2)}) %collective-permute-start.28) | collective-permute-done | bytes 196640 | tf_op jit(solution)/shard_map/ppermute | solution.py:88
  103.3 1.1 %unpack.1 = bf16[1,192,2048]{2,1,0:T(8,128)(2,1)} custom-call(bf16[4,192,128]{2,1,0:T(8,128)(2,1)S(1)} %get-tuple-element.55.refs_0_, bf16[4,192,128]{2,1,0:T(8,128)(2,1)S(1)} %collective-permute-done.26.refs_1_, bf16[4,192,128]{2,1,0:T(8,128)(2,1)S(1)} %collective-permute-done.27.refs_2_, bf16[4,192,128]{2,1,0:T(8,128)(2,1)S(1)} %collective-permute-done.28.refs_3_), custom_call_target="tpu_custom_call" | custom-call | tf_op jit(solution)/shard_map/unpack/pallas_call | solution.py:383
  (32 shorter events, 0.4 us)
Async XLA Ops:
  1.0 8.5 %collective-permute-start = (bf16[16,2688]{1,0:T(8,128)(2,1)S(1)}, bf16[16,2688]{1,0:T(8,128)(2,1)S(1)}, u32[]{:S(2)}, u32[]{:S(2)}) collective-permute-start(bf16[16,2688]{1,0:T(8,128)(2,1)S(1)} %get-tuple-element.35), channel_id=1, source_target_pairs={{0,1},{1,0},{2,3},{3,2},{4,5},{5,4},{6,7},{7,6},{8,9},{9,8},{10,11... | collective-permute-start | bytes 258056 | tf_op jit(solution)/shard_map/ppermute | solution.py:88
  4.0 18.0 %collective-permute-start.1 = (bf16[16,2688]{1,0:T(8,128)(2,1)S(1)}, bf16[16,2688]{1,0:T(8,128)(2,1)S(1)}, u32[]{:S(2)}, u32[]{:S(2)}) collective-permute-start(bf16[16,2688]{1,0:T(8,128)(2,1)S(1)} %get-tuple-element.36), channel_id=1, source_target_pairs={{0,2},{1,3},{2,0},{3,1},{4,6},{5,7},{6,4},{7,5},{8,10},{9,11},{10,... | collective-permute-start | bytes 258056 | tf_op jit(solution)/shard_map/ppermute | solution.py:88
  6.6 15.4 %collective-permute-start.2 = (bf16[16,2688]{1,0:T(8,128)(2,1)S(1)}, bf16[16,2688]{1,0:T(8,128)(2,1)S(1)}, u32[]{:S(2)}, u32[]{:S(2)}) collective-permute-start(bf16[16,2688]{1,0:T(8,128)(2,1)S(1)} %get-tuple-element.37), channel_id=1, source_target_pairs={{0,3},{1,2},{2,1},{3,0},{4,7},{5,6},{6,5},{7,4},{8,11},{9,10},{10,... | collective-permute-start | bytes 258056 | tf_op jit(solution)/shard_map/ppermute | solution.py:88
  6.6 1.4 %copy-start = (bf16[1,512,1536]{2,1,0:T(8,128)(2,1)S(1)}, bf16[1,512,1536]{2,1,0:T(8,128)(2,1)}, u32[]{:S(2)}) copy-start(bf16[1,512,1536]{2,1,0:T(8,128)(2,1)} %param.13) | copy-start | bytes 4718596
  8.0 3.3 %copy-start.1 = (bf16[1,512,768]{2,1,0:T(8,128)(2,1)S(1)}, bf16[1,512,768]{2,1,0:T(8,128)(2,1)}, u32[]{:S(2)}) copy-start(bf16[1,512,768]{2,1,0:T(8,128)(2,1)} %param.14) | copy-start | bytes 2359300
  8.0 3.3 %copy-start.2 = (bf16[1,512,768]{2,1,0:T(8,128)(2,1)S(1)}, bf16[1,512,768]{2,1,0:T(8,128)(2,1)}, u32[]{:S(2)}) copy-start(bf16[1,512,768]{2,1,0:T(8,128)(2,1)} %param.15) | copy-start | bytes 2359300
  9.4 12.6 %copy-start.4 = (bf16[512,384]{1,0:T(8,128)(2,1)}, bf16[512,384]{1,0:T(8,128)(2,1)S(1)}, u32[]{:S(2)}) copy-start(bf16[512,384]{1,0:T(8,128)(2,1)S(1)} %get-tuple-element.44) | copy-start | bytes 1179652
  9.4 12.6 %copy-start.5 = (bf16[512,384]{1,0:T(8,128)(2,1)}, bf16[512,384]{1,0:T(8,128)(2,1)S(1)}, u32[]{:S(2)}) copy-start(bf16[512,384]{1,0:T(8,128)(2,1)S(1)} %get-tuple-element.40) | copy-start | bytes 1179652
  9.5 26.1 %collective-permute-start.11 = (bf16[512,384]{1,0:T(8,128)(2,1)}, bf16[512,384]{1,0:T(8,128)(2,1)}, u32[]{:S(2)}, u32[]{:S(2)}) collective-permute-start(bf16[512,384]{1,0:T(8,128)(2,1)} %get-tuple-element.42), channel_id=1, source_target_pairs={{0,2},{1,3},{2,0},{3,1},{4,6},{5,7},{6,4},{7,5},{8,10},{9,11},{10,... | collective-permute-start | bytes 1179656 | tf_op jit(solution)/shard_map/ppermute | solution.py:88
  11.4 1.1 %copy-start.3 = (bf16[1,512,768]{2,1,0:T(8,128)(2,1)S(1)}, bf16[1,512,768]{2,1,0:T(8,128)(2,1)}, u32[]{:S(2)}) copy-start(bf16[1,512,768]{2,1,0:T(8,128)(2,1)} %param.16) | copy-start | bytes 2359300
  22.1 7.3 %collective-permute-start.3 = (bf16[64,2688]{1,0:T(8,128)(2,1)S(1)}, bf16[64,2688]{1,0:T(8,128)(2,1)S(1)}, u32[]{:S(2)}, u32[]{:S(2)}) collective-permute-start(bf16[64,2688]{1,0:T(8,128)(2,1)S(1)} %bitcast.8), channel_id=1, source_target_pairs={{0,8},{4,12},{8,0},{12,4},{16,24},{20,28},{24,16},{28,20},{1,9},{5... | collective-permute-start | bytes 1032200 | tf_op jit(solution)/shard_map/ppermute | solution.py:88
  23.7 14.5 %collective-permute-start.5 = (bf16[64,2688]{1,0:T(8,128)(2,1)S(1)}, bf16[64,2688]{1,0:T(8,128)(2,1)S(1)}, u32[]{:S(2)}, u32[]{:S(2)}) collective-permute-start(bf16[64,2688]{1,0:T(8,128)(2,1)S(1)} %bitcast.9), channel_id=1, source_target_pairs={{0,24},{4,28},{8,16},{12,20},{16,8},{20,12},{24,0},{28,4},{1,25},{... | collective-permute-start | bytes 1032200 | tf_op jit(solution)/shard_map/ppermute | solution.py:88
  25.2 13.0 %collective-permute-start.4 = (bf16[64,2688]{1,0:T(8,128)(2,1)S(1)}, bf16[64,2688]{1,0:T(8,128)(2,1)S(1)}, u32[]{:S(2)}, u32[]{:S(2)}) collective-permute-start(bf16[64,2688]{1,0:T(8,128)(2,1)S(1)} %bitcast.10), channel_id=1, source_target_pairs={{0,16},{4,20},{8,24},{12,28},{16,0},{20,4},{24,8},{28,12},{1,17},{... | collective-permute-start | bytes 1032200 | tf_op jit(solution)/shard_map/ppermute | solution.py:88
  25.7 13.0 %collective-permute-start.6 = (bf16[64,2688]{1,0:T(8,128)(2,1)S(1)}, bf16[64,2688]{1,0:T(8,128)(2,1)S(1)}, u32[]{:S(2)}, u32[]{:S(2)}) collective-permute-start(bf16[64,2688]{1,0:T(8,128)(2,1)S(1)} %bitcast.11), channel_id=1, source_target_pairs={{0,4},{4,0},{8,12},{12,8},{16,20},{20,16},{24,28},{28,24},{1,5},{5... | collective-permute-start | bytes 1032200 | tf_op jit(solution)/shard_map/ppermute | solution.py:88
  29.4 15.3 %collective-permute-start.10 = (bf16[512,384]{1,0:T(8,128)(2,1)}, bf16[512,384]{1,0:T(8,128)(2,1)S(1)}, u32[]{:S(2)}, u32[]{:S(2)}) collective-permute-start(bf16[512,384]{1,0:T(8,128)(2,1)} %copy-done.5), channel_id=1, source_target_pairs={{0,1},{1,0},{2,3},{3,2},{4,5},{5,4},{6,7},{7,6},{8,9},{9,8},{10,11... | collective-permute-start | bytes 1179656 | tf_op jit(solution)/shard_map/ppermute | solution.py:88
  35.6 14.3 %collective-permute-start.12 = (bf16[512,384]{1,0:T(8,128)(2,1)}, bf16[512,384]{1,0:T(8,128)(2,1)S(1)}, u32[]{:S(2)}, u32[]{:S(2)}) collective-permute-start(bf16[512,384]{1,0:T(8,128)(2,1)} %copy-done.4), channel_id=1, source_target_pairs={{0,3},{1,2},{2,1},{3,0},{4,7},{5,6},{6,5},{7,4},{8,11},{9,10},{10,... | collective-permute-start | bytes 1179656 | tf_op jit(solution)/shard_map/ppermute | solution.py:88
  38.2 1.7 %collective-permute-start.9 = (bf16[64,2688]{1,0:T(8,128)(2,1)S(1)}, bf16[64,2688]{1,0:T(8,128)(2,1)S(1)}, u32[]{:S(2)}, u32[]{:S(2)}) collective-permute-start(bf16[64,2688]{1,0:T(8,128)(2,1)S(1)} %collective-permute-done.5.refs_3_), channel_id=1, source_target_pairs={{0,4},{4,0},{8,12},{12,8},{16,20},{20,16},{24,28},{28,24},{1,5},{5... | collective-permute-start | bytes 1032200 | tf_op jit(solution)/shard_map/ppermute | solution.py:88
  38.2 2.1 %collective-permute-start.8 = (bf16[64,2688]{1,0:T(8,128)(2,1)S(1)}, bf16[64,2688]{1,0:T(8,128)(2,1)S(1)}, u32[]{:S(2)}, u32[]{:S(2)}) collective-permute-start(bf16[64,2688]{1,0:T(8,128)(2,1)S(1)} %collective-permute-done.4.refs_2_), channel_id=1, source_target_pairs={{0,4},{4,0},{8,12},{12,8},{16,20},{20,16},{24,28},{28,24},{1,5},{5... | collective-permute-start | bytes 1032200 | tf_op jit(solution)/shard_map/ppermute | solution.py:88
  38.7 2.1 %collective-permute-start.7 = (bf16[64,2688]{1,0:T(8,128)(2,1)S(1)}, bf16[64,2688]{1,0:T(8,128)(2,1)S(1)}, u32[]{:S(2)}, u32[]{:S(2)}) collective-permute-start(bf16[64,2688]{1,0:T(8,128)(2,1)S(1)} %collective-permute-done.3.refs_1_), channel_id=1, source_target_pairs={{0,4},{4,0},{8,12},{12,8},{16,20},{20,16},{24,28},{28,24},{1,5},{5... | collective-permute-start | bytes 1032200 | tf_op jit(solution)/shard_map/ppermute | solution.py:88
  52.5 7.6 %collective-permute-start.15 = (bf16[192,512]{1,0:T(8,128)(2,1)S(1)}, bf16[192,512]{1,0:T(8,128)(2,1)S(1)}, u32[]{:S(2)}, u32[]{:S(2)}) collective-permute-start(bf16[192,512]{1,0:T(8,128)(2,1)S(1)} %hidden_units.1.refs_0_), channel_id=1, source_target_pairs={{0,3},{1,2},{2,1},{3,0},{4,7},{5,6},{6,5},{7,4},{8,11},{9,10},{10,... | collective-permute-start | bytes 589832 | tf_op jit(solution)/shard_map/ppermute | solution.py:88
  54.0 12.3 %collective-permute-start.14 = (bf16[192,512]{1,0:T(8,128)(2,1)S(1)}, bf16[192,512]{1,0:T(8,128)(2,1)S(1)}, u32[]{:S(2)}, u32[]{:S(2)}) collective-permute-start(bf16[192,512]{1,0:T(8,128)(2,1)S(1)} %hidden_units.1.refs_0_), channel_id=1, source_target_pairs={{0,2},{1,3},{2,0},{3,1},{4,6},{5,7},{6,4},{7,5},{8,10},{9,11},{10,... | collective-permute-start | bytes 589832 | tf_op jit(solution)/shard_map/ppermute | solution.py:88
  58.0 8.3 %collective-permute-start.13 = (bf16[192,512]{1,0:T(8,128)(2,1)S(1)}, bf16[192,512]{1,0:T(8,128)(2,1)S(1)}, u32[]{:S(2)}, u32[]{:S(2)}) collective-permute-start(bf16[192,512]{1,0:T(8,128)(2,1)S(1)} %hidden_units.1.refs_0_), channel_id=1, source_target_pairs={{0,1},{1,0},{2,3},{3,2},{4,5},{5,4},{6,7},{7,6},{8,9},{9,8},{10,11... | collective-permute-start | bytes 589832 | tf_op jit(solution)/shard_map/ppermute | solution.py:88
  68.1 5.7 %collective-permute-start.16 = (bf16[4,192,128]{2,1,0:T(8,128)(2,1)S(1)}, bf16[4,192,128]{2,1,0:T(8,128)(2,1)S(1)}, u32[]{:S(2)}, u32[]{:S(2)}) collective-permute-start(bf16[4,192,128]{2,1,0:T(8,128)(2,1)S(1)} %get-tuple-element.48), channel_id=1, source_target_pairs={{0,8},{4,12},{8,0},{12,4},{16,24},{20,28},{24,16},{28,20},{1,9},{5... | collective-permute-start | bytes 589832 | tf_op jit(solution)/shard_map/ppermute | solution.py:88
  69.7 6.8 %collective-permute-start.17 = (bf16[4,192,128]{2,1,0:T(8,128)(2,1)S(1)}, bf16[4,192,128]{2,1,0:T(8,128)(2,1)S(1)}, u32[]{:S(2)}, u32[]{:S(2)}) collective-permute-start(bf16[4,192,128]{2,1,0:T(8,128)(2,1)S(1)} %get-tuple-element.49), channel_id=1, source_target_pairs={{0,16},{4,20},{8,24},{12,28},{16,0},{20,4},{24,8},{28,12},{1,17},{... | collective-permute-start | bytes 589832 | tf_op jit(solution)/shard_map/ppermute | solution.py:88
  71.2 6.6 %collective-permute-start.18 = (bf16[4,192,128]{2,1,0:T(8,128)(2,1)S(1)}, bf16[4,192,128]{2,1,0:T(8,128)(2,1)S(1)}, u32[]{:S(2)}, u32[]{:S(2)}) collective-permute-start(bf16[4,192,128]{2,1,0:T(8,128)(2,1)S(1)} %get-tuple-element.50), channel_id=1, source_target_pairs={{0,24},{4,28},{8,16},{12,20},{16,8},{20,12},{24,0},{28,4},{1,25},{... | collective-permute-start | bytes 589832 | tf_op jit(solution)/shard_map/ppermute | solution.py:88
  77.8 7.2 %collective-permute-start.19 = (bf16[4,192,128]{2,1,0:T(8,128)(2,1)S(1)}, bf16[4,192,128]{2,1,0:T(8,128)(2,1)S(1)}, u32[]{:S(2)}, u32[]{:S(2)}) collective-permute-start(bf16[4,192,128]{2,1,0:T(8,128)(2,1)S(1)} %get-tuple-element.52), channel_id=1, source_target_pairs={{0,1},{1,0},{2,3},{3,2},{4,5},{5,4},{6,7},{7,6},{8,9},{9,8},{10,11... | collective-permute-start | bytes 589832 | tf_op jit(solution)/shard_map/ppermute | solution.py:88
  77.9 10.9 %collective-permute-start.20 = (bf16[4,192,128]{2,1,0:T(8,128)(2,1)S(1)}, bf16[4,192,128]{2,1,0:T(8,128)(2,1)S(1)}, u32[]{:S(2)}, u32[]{:S(2)}) collective-permute-start(bf16[4,192,128]{2,1,0:T(8,128)(2,1)S(1)} %get-tuple-element.53), channel_id=1, source_target_pairs={{0,2},{1,3},{2,0},{3,1},{4,6},{5,7},{6,4},{7,5},{8,10},{9,11},{10,... | collective-permute-start | bytes 589832 | tf_op jit(solution)/shard_map/ppermute | solution.py:88
  80.3 8.5 %collective-permute-start.21 = (bf16[4,192,128]{2,1,0:T(8,128)(2,1)S(1)}, bf16[4,192,128]{2,1,0:T(8,128)(2,1)S(1)}, u32[]{:S(2)}, u32[]{:S(2)}) collective-permute-start(bf16[4,192,128]{2,1,0:T(8,128)(2,1)S(1)} %get-tuple-element.54), channel_id=1, source_target_pairs={{0,3},{1,2},{2,1},{3,0},{4,7},{5,6},{6,5},{7,4},{8,11},{9,10},{10,... | collective-permute-start | bytes 589832 | tf_op jit(solution)/shard_map/ppermute | solution.py:88
  82.3 7.0 %collective-permute-start.22 = (bf16[4,192,128]{2,1,0:T(8,128)(2,1)S(1)}, bf16[4,192,128]{2,1,0:T(8,128)(2,1)S(1)}, u32[]{:S(2)}, u32[]{:S(2)}) collective-permute-start(bf16[4,192,128]{2,1,0:T(8,128)(2,1)S(1)} %get-tuple-element.51.refs_0_), channel_id=1, source_target_pairs={{0,4},{4,0},{8,12},{12,8},{16,20},{20,16},{24,28},{28,24},{1,5},{5... | collective-permute-start | bytes 589832 | tf_op jit(solution)/shard_map/ppermute | solution.py:88
  85.0 4.3 %collective-permute-start.23 = (bf16[4,192,128]{2,1,0:T(8,128)(2,1)S(1)}, bf16[4,192,128]{2,1,0:T(8,128)(2,1)S(1)}, u32[]{:S(2)}, u32[]{:S(2)}) collective-permute-start(bf16[4,192,128]{2,1,0:T(8,128)(2,1)S(1)} %collective-permute-done.19.refs_1_), channel_id=1, source_target_pairs={{0,4},{4,0},{8,12},{12,8},{16,20},{20,16},{24,28},{28,24},{1,5},{5... | collective-permute-start | bytes 589832 | tf_op jit(solution)/shard_map/ppermute | solution.py:88
  88.8 1.4 %collective-permute-start.24 = (bf16[4,192,128]{2,1,0:T(8,128)(2,1)S(1)}, bf16[4,192,128]{2,1,0:T(8,128)(2,1)S(1)}, u32[]{:S(2)}, u32[]{:S(2)}) collective-permute-start(bf16[4,192,128]{2,1,0:T(8,128)(2,1)S(1)} %collective-permute-done.20.refs_2_), channel_id=1, source_target_pairs={{0,4},{4,0},{8,12},{12,8},{16,20},{20,16},{24,28},{28,24},{1,5},{5... | collective-permute-start | bytes 589832 | tf_op jit(solution)/shard_map/ppermute | solution.py:88
  88.8 1.7 %collective-permute-start.25 = (bf16[4,192,128]{2,1,0:T(8,128)(2,1)S(1)}, bf16[4,192,128]{2,1,0:T(8,128)(2,1)S(1)}, u32[]{:S(2)}, u32[]{:S(2)}) collective-permute-start(bf16[4,192,128]{2,1,0:T(8,128)(2,1)S(1)} %collective-permute-done.21.refs_3_), channel_id=1, source_target_pairs={{0,4},{4,0},{8,12},{12,8},{16,20},{20,16},{24,28},{28,24},{1,5},{5... | collective-permute-start | bytes 589832 | tf_op jit(solution)/shard_map/ppermute | solution.py:88
  91.3 7.8 %collective-permute-start.26 = (bf16[4,192,128]{2,1,0:T(8,128)(2,1)S(1)}, bf16[4,192,128]{2,1,0:T(8,128)(2,1)S(1)}, u32[]{:S(2)}, u32[]{:S(2)}) collective-permute-start(bf16[4,192,128]{2,1,0:T(8,128)(2,1)S(1)} %get-tuple-element.56), channel_id=1, source_target_pairs={{0,8},{4,12},{8,0},{12,4},{16,24},{20,28},{24,16},{28,20},{1,9},{5... | collective-permute-start | bytes 589832 | tf_op jit(solution)/shard_map/ppermute | solution.py:88
  92.0 7.2 %collective-permute-start.27 = (bf16[4,192,128]{2,1,0:T(8,128)(2,1)S(1)}, bf16[4,192,128]{2,1,0:T(8,128)(2,1)S(1)}, u32[]{:S(2)}, u32[]{:S(2)}) collective-permute-start(bf16[4,192,128]{2,1,0:T(8,128)(2,1)S(1)} %get-tuple-element.57), channel_id=1, source_target_pairs={{0,16},{4,20},{8,24},{12,28},{16,0},{20,4},{24,8},{28,12},{1,17},{... | collective-permute-start | bytes 589832 | tf_op jit(solution)/shard_map/ppermute | solution.py:88
  93.1 10.1 %collective-permute-start.28 = (bf16[4,192,128]{2,1,0:T(8,128)(2,1)S(1)}, bf16[4,192,128]{2,1,0:T(8,128)(2,1)S(1)}, u32[]{:S(2)}, u32[]{:S(2)}) collective-permute-start(bf16[4,192,128]{2,1,0:T(8,128)(2,1)S(1)} %get-tuple-element.58), channel_id=1, source_target_pairs={{0,24},{4,28},{8,16},{12,20},{16,8},{20,12},{24,0},{28,4},{1,25},{... | collective-permute-start | bytes 589832 | tf_op jit(solution)/shard_map/ppermute | solution.py:88

commit v5 on v4

--- a/solution.py
+++ b/solution.py
@@ -201,47 +201,73 @@
     return x / (1.0 + jnp.exp(-x))
 
 
-def hidden_kernel(pieces, bounds, *refs):
+def start_kernel(pieces, flips, *refs):
     row_refs, refs = refs[:pieces], refs[pieces:]
-    groups = lax.axis_size("dp")
-    weight_refs, outs, (toks, hidden) = refs[:groups], refs[groups:-2], refs[-2:]
-    rows, width = row_refs[0].shape[0], toks.shape[1]
-    block = width // groups
+    weight_refs, (pre, kept, toks) = refs[: len(flips)], refs[len(flips) :]
+    rows, width = row_refs[0].shape
+    block = weight_refs[0].shape[0]
     group = lax.axis_index("dp")
     for i, ref in enumerate(row_refs):
-        toks[i * rows : (i + 1) * rows, :] = ref[:, :width]
-    pre = None
-    for flip, ref in enumerate(weight_refs):
+        toks[i * rows : (i + 1) * rows, :] = ref[...]
+    total = None
+    for flip, ref in zip(flips, weight_refs, strict=True):
         start = pl.multiple_of((group ^ flip) * block, LANES)
         term = jnp.dot(toks[:, pl.ds(start, block)], ref[...], preferred_element_type=F32)
-        pre = term if pre is None else pre + term
+        total = term if total is None else total + term
+    pre[...] = total
+    rest = sorted(set(range(lax.axis_size("dp"))) - set(flips))
+    for i, flip in enumerate(rest):
+        start = pl.multiple_of((group ^ flip) * block, LANES)
+        kept[:, i * block : (i + 1) * block] = toks[:, pl.ds(start, block)]
+
+
+def start_hidden(pieces, weights, flips, width):
+    rows = pieces[0].shape[0]
+    total = rows * len(pieces)
+    block, cols = weights[0].shape
+    left = width - block * len(flips)
+    return pl.pallas_call(
+        functools.partial(start_kernel, len(pieces), flips),
+        out_shape=[pltpu.VMEM((total, cols), F32), pltpu.VMEM((total, left), BF16)],
+        grid=(1,),
+        in_specs=[pl.BlockSpec((rows, width), lambda i: (0, 0))] * len(pieces)
+        + [pl.BlockSpec((block, cols), lambda i: (0, 0))] * len(weights),
+        out_specs=[
+            pl.BlockSpec((total, cols), lambda i: (0, 0)),
+            pl.BlockSpec((total, left), lambda i: (0, 0)),
+        ],
+        scratch_shapes=[pltpu.VMEM((total, width), BF16)],
+        compiler_params=pltpu.CompilerParams(vmem_limit_bytes=VMEM_BYTES),
+        name="start_hidden",
+    )(*[in_vmem(x) for x in [*pieces, *weights]])
+
+
+def hidden_kernel(partial, rows, *refs):
+    *weights, hidden = refs
+    pre = partial[...]
+    for i, ref in enumerate(weights):
+        block = ref.shape[0]
+        part = rows[:, i * block : (i + 1) * block]
+        pre = pre + jnp.dot(part, ref[...], preferred_element_type=F32)
     gate, up, shared = (pre[:, i * LANES : (i + 1) * LANES] for i in range(3))
     hidden[:LANES, :] = (silu(gate) * up).T.astype(BF16)
     halves = (silu(shared) * swap_halves(shared)).T.astype(BF16)
     for parity in range(2):
 
-        @pl.when(lax.rem(group, 2) == parity)
+        @pl.when(lax.rem(lax.axis_index("dp"), 2) == parity)
         def _():
             hidden[LANES:, :] = halves[parity * HALF : (parity + 1) * HALF]
 
-    for (start, end), out in zip(bounds, outs, strict=True):
-        out[...] = hidden[start:end, :]
-
-
-def hidden_units(pieces, weights, width, bounds):
-    rows = pieces[0].shape[0]
-    total = rows * len(pieces)
-    return pl.pallas_call(
-        functools.partial(hidden_kernel, len(pieces), bounds),
-        out_shape=[pltpu.VMEM((end - start, total), BF16) for start, end in bounds],
-        in_specs=[whole()] * (len(pieces) + len(weights)),
-        scratch_shapes=[
-            pltpu.VMEM((total, width), BF16),
-            pltpu.VMEM((weights[0].shape[1] // 2, total), BF16),
-        ],
-        compiler_params=pltpu.CompilerParams(vmem_limit_bytes=VMEM_BYTES),
-        name="hidden_units",
-    )(*[in_vmem(x) for x in [*pieces, *weights]])
+
+def end_hidden(partial, rows, weights):
+    args = [partial, rows, *weights]
+    return pl.pallas_call(
+        hidden_kernel,
+        out_shape=pltpu.VMEM((partial.shape[1] // 2, rows.shape[0]), BF16),
+        in_specs=[whole()] * len(args),
+        compiler_params=pltpu.CompilerParams(vmem_limit_bytes=VMEM_BYTES),
+        name="end_hidden",
+    )(*[in_vmem(x) for x in args])
 
 
 def scaled_kernel(start, *refs):
@@ -285,33 +311,33 @@
     )(*arrays)
 
 
-def update_kernel(start, *refs):
+def update_kernel(flips, *refs):
     groups = lax.axis_size("dp")
-    hid_refs, (scaled, down, first, second), refs = refs[:groups], refs[groups : groups + 4], refs[groups + 4 :]
+    count = len(flips)
+    hid_refs, (scaled, down, first, second), refs = refs[:count], refs[count : count + 4], refs[count + 4 :]
     outs, hidden = refs[:-1], refs[-1]
-    rows = hid_refs[0].shape[0]
     cols = down.shape[0] // groups
-    for flip, ref in enumerate(hid_refs):
-        hidden[flip * rows : (flip + 1) * rows, :] = ref[...]
-    for flip, out in enumerate(outs):
-        tile = (lax.axis_index("expert") // CORES) ^ flip
+    for i, ref in enumerate(hid_refs):
+        hidden[i * cols : (i + 1) * cols, :] = ref[...]
+    for chip_flip, out in enumerate(outs):
+        tile = (lax.axis_index("expert") // CORES) ^ chip_flip
         lanes = pl.ds(pl.multiple_of(tile * LANES, LANES), LANES)
         grad = jnp.dot(hidden[...], scaled[:, lanes], preferred_element_type=F32)
-        for other in range(groups):
-            at = pl.multiple_of((lax.axis_index("dp") ^ other) * cols + start, 16)
-            here = pl.ds(at, rows), lanes
-            part = grad[other * rows : (other + 1) * rows]
-            out[other] = adam(down[here], first[here], second[here], part)
-
-
-def update_tiles(hidden, scaled, state, start, chips):
-    groups = len(hidden)
-    rows, total = hidden[0].shape
-    return pl.pallas_call(
-        functools.partial(update_kernel, start),
-        out_shape=[pltpu.VMEM((groups, rows, scaled.shape[1] // chips), BF16)] * chips,
-        in_specs=[whole()] * (groups + 4),
-        scratch_shapes=[pltpu.VMEM((groups * rows, total), BF16)],
+        for i, flip in enumerate(flips):
+            at = pl.multiple_of((lax.axis_index("dp") ^ flip) * cols, 16)
+            here = pl.ds(at, cols), lanes
+            part = grad[i * cols : (i + 1) * cols]
+            out[i] = adam(down[here], first[here], second[here], part)
+
+
+def update_tiles(hidden, flips, scaled, state, chips):
+    cols, total = hidden[0].shape
+    count = len(flips)
+    return pl.pallas_call(
+        functools.partial(update_kernel, flips),
+        out_shape=[pltpu.VMEM((count, cols, scaled.shape[1] // chips), BF16)] * chips,
+        in_specs=[whole()] * (count + 4),
+        scratch_shapes=[pltpu.VMEM((count * cols, total), BF16)],
         compiler_params=pltpu.CompilerParams(vmem_limit_bytes=VMEM_BYTES),
         name="update_tiles",
     )(*[in_vmem(x) for x in [*hidden, scaled, *state]])
@@ -336,9 +362,8 @@
     )(*[in_vmem(x) for x in tiles])
 
 
-def pick_kernel(order, *refs):
-    groups, chips = lax.axis_size("dp"), lax.axis_size("expert") // CORES
-    kept, swapped, outs = refs[:groups], refs[groups : 2 * groups], refs[2 * groups :]
+def pick_kernel(count, order, *refs):
+    kept, swapped, outs = refs[:count], refs[count : 2 * count], refs[2 * count :]
     spot = lax.axis_index("expert")
     core = lax.rem(spot, CORES)
     for flip, out in enumerate(outs):
@@ -347,41 +372,40 @@
 
         @pl.when(here)
         def _():
-            for i in range(groups):
+            for i in range(count):
                 out[i] = kept[i][chip]
 
         @pl.when(jnp.logical_not(here))
         def _():
-            for i in range(groups):
+            for i in range(count):
                 out[i] = swapped[i][chip]
 
 
 def pick(order, kept, swapped):
     chips, *tile = kept[0].shape
-    return pl.pallas_call(
-        pick_kernel,
-        out_shape=[pltpu.VMEM((len(kept), *tile), BF16)] * chips,
-        in_specs=[smem()] + [whole()] * (2 * len(kept)),
+    count = len(kept)
+    return pl.pallas_call(
+        functools.partial(pick_kernel, count),
+        out_shape=[pltpu.VMEM((count, *tile), BF16)] * chips,
+        in_specs=[smem()] + [whole()] * (2 * count),
         name="pick",
     )(order, *[in_vmem(x) for x in [*kept, *swapped]])
 
 
-def unpack_kernel(bounds, *refs):
+def unpack_kernel(sets, *refs):
     *pieces, out = refs
-    groups = pieces[0].shape[0]
-    block = out.shape[2] // groups
-    chips = len(pieces) // len(bounds)
+    chips = len(pieces) // len(sets)
+    block = out.shape[2] // sum(map(len, sets))
     for i, piece in enumerate(pieces):
-        start, end = bounds[i // chips]
         tile = (lax.axis_index("expert") // CORES) ^ (i % chips)
-        for other in range(groups):
-            left = (lax.axis_index("dp") ^ other) * block + tile * LANES
-            out[0, start:end, pl.ds(pl.multiple_of(left, LANES), LANES)] = piece[other]
-
-
-def unpack(pieces, bounds, width, cols):
-    return pl.pallas_call(
-        functools.partial(unpack_kernel, bounds),
+        for j, flip in enumerate(sets[i // chips]):
+            left = (lax.axis_index("dp") ^ flip) * block + tile * LANES
+            out[0, :, pl.ds(pl.multiple_of(left, LANES), LANES)] = piece[j]
+
+
+def unpack(pieces, sets, width, cols):
+    return pl.pallas_call(
+        functools.partial(unpack_kernel, sets),
         out_shape=jax.ShapeDtypeStruct((1, cols, width), BF16),
         in_specs=[whole()] * len(pieces),
         out_specs=whole(),
@@ -408,24 +432,29 @@
     farthest = partner(after(farthest, far), "dp", 3)
 
     cols = units // groups
-    bounds = ((0, cols),)
-    parts = hidden_units(pieces, [own, near, far, farthest], width, bounds)
+    partial, rows = start_hidden(pieces, [own, far, near], (0, 2, 1), width)
+    part = end_hidden(partial, rows, [farthest])
     scaled = scaled_rows(pieces, width, block)
+    across = partner(part, "dp", 2)
+    hidden = [part, partner(part, "dp", 1), across, partner(across, "dp", 1)]
+    planes = experts // CORES
+    sets = (0, 2), (1, 3)
     landed = []
-    for (start, _), part in zip(bounds, parts, strict=True):
-        hidden = [part] + [partner(part, "dp", k) for k in range(1, groups)]
-        tiles = update_tiles(hidden, scaled, state, start, experts // CORES)
+    for flips in sets:
+        tiles = update_tiles([hidden[k] for k in flips], flips, scaled, state, planes)
         tiles = [tiles[0]] + [
-            partner(tiles[k], "expert", k * CORES) for k in range(1, len(tiles))
+            partner(tiles[k], "expert", k * CORES) for k in range(1, planes)
         ]
         split = regroup(tiles)
-        kept = [split[0]] + [partner(split[k], "dp", k) for k in range(1, groups)]
+        kept = [
+            partner(x, "dp", k) if k else x for k, x in zip(flips, split, strict=True)
+        ]
         swapped = [partner(x, "expert", 1) for x in kept]
         picked = pick(placement, kept, swapped)
         landed += [picked[0]] + [
-            partner(picked[k], "expert", k * CORES) for k in range(1, len(picked))
+            partner(picked[k], "expert", k * CORES) for k in range(1, planes)
         ]
-    return unpack(landed, bounds, width, cols).transpose(0, 2, 1)
+    return unpack(landed, sets, width, cols).transpose(0, 2, 1)
 
 
 def shards(tokens, cotangent, route_ids, *rest):

time: 105 us -> 99.3 us (0.946)
  waiting for transfers between devices: 54.1 us -> 43.3 us
  starting transfers between devices: 38.1 us -> 42.3 us
  Pallas kernels: 9.55 us -> 10.7 us
    ppermute x29 -> x35, waiting for transfers between devices: 54.1 us -> 43.3 us  [partner(): return lax.ppermute(x, axis, [(i, i ^ flip) for i in range(size)])]
    ppermute x29 -> x35, starting transfers between devices: 38.1 us -> 42.3 us  [partner(): return lax.ppermute(x, axis, [(i, i ^ flip) for i in range(size)])]
    pallas_call x4 -> x7, Pallas kernels: 6.24 us -> 7.42 us  [the longest x1 2.23 us: start_hidden(): pl.pallas_call(functools.partial(start_kernel, len(pieces), flips), out_s...]
  transfers between devices with their start and end apart: 29 -> 35, of which waited for: 19 -> 18; matrix products, arithmetic and copies ran while one was open for 0% -> 0% of each run, Pallas kernels for 2% -> 8%
where the time goes in v5:
time: 99.3 us; the launch traced here: 99 us
  waiting for transfers between devices  43.3 us (44%)
  starting transfers between devices  42.3 us (43%)
  Pallas kernels  10.7 us (11%)
  local copies, waits for them, and re-layouts  2.56 us (3%)
    ppermute x35, waiting for transfers between devices, partner(): return lax.ppermute(x, axis, [(i, i ^ flip) for i in range(size)])  43.3 us
    ppermute x35, starting transfers between devices, partner(): return lax.ppermute(x, axis, [(i, i ^ flip) for i in range(size)])  42.3 us
    unnamed x12, local copies, waits for them, and re-layouts  2.56 us
    pallas_call x1, Pallas kernels, start_hidden(): pl.pallas_call(functools.partial(start_kernel, len(pieces), flips), out_s...  2.23 us
  transfers between devices with their start and end apart: 35, of which 18 were waited for; matrix products, arithmetic and copies ran while one was open for 0% of the time, Pallas kernels for 8%

profile of v5, /device:TPU:0, one launch (start us, length us, event | category | flops | bytes accessed | tf_op | source)
XLA Modules:
  0.0 99.0 jit_solution(14198956300322469155)
XLA Ops:
  0.0 1.0 pack_rows.1
  1.0 3.1 %collective-permute-start = (bf16[16,2688]{1,0:T(8,128)(2,1)S(1)}, bf16[16,2688]{1,0:T(8,128)(2,1)S(1)}, u32[]{:S(2)}, u32[]{:S(2)}) collective-permute-start(bf16[16,2688]{1,0:T(8,128)(2,1)S(1)} %get-tuple-element.45), channel_id=1, source_target_pairs={{0,1},{1,0},{2,3},{3,2},{4,5},{5,4},{6,7},{7,6},{8,9},{9,8},{10,11... | collective-permute-start | bytes 258056 | tf_op jit(solution)/shard_map/ppermute | solution.py:88
  4.0 2.6 %collective-permute-start.1 = (bf16[16,2688]{1,0:T(8,128)(2,1)S(1)}, bf16[16,2688]{1,0:T(8,128)(2,1)S(1)}, u32[]{:S(2)}, u32[]{:S(2)}) collective-permute-start(bf16[16,2688]{1,0:T(8,128)(2,1)S(1)} %get-tuple-element.46), channel_id=1, source_target_pairs={{0,2},{1,3},{2,0},{3,1},{4,6},{5,7},{6,4},{7,5},{8,10},{9,11},{10,... | collective-permute-start | bytes 258056 | tf_op jit(solution)/shard_map/ppermute | solution.py:88
  6.6 1.4 %copy-done = bf16[1,512,1536]{2,1,0:T(8,128)(2,1)S(1)} copy-done((bf16[1,512,1536]{2,1,0:T(8,128)(2,1)S(1)}, bf16[1,512,1536]{2,1,0:T(8,128)(2,1)}, u32[]{:S(2)}) %copy-start) | copy-done | bytes 1572888
  8.0 1.4 %pack_weights.1 = (bf16[512,384]{1,0:T(8,128)(2,1)S(1)}, bf16[512,384]{1,0:T(8,128)(2,1)S(1)}, bf16[512,384]{1,0:T(8,128)(2,1)}, bf16[512,384]{1,0:T(8,128)(2,1)S(1)}) custom-call(bf16[512,1536]{1,0:T(8,128)(2,1)S(1)} %bitcast.14), custom_call_target="tpu_custom_call" | custom-call | tf_op jit(solution)/shard_map/pack_weights/pallas_call | solution.py:166
  9.5 1.9 %collective-permute-start.10 = (bf16[512,384]{1,0:T(8,128)(2,1)}, bf16[512,384]{1,0:T(8,128)(2,1)}, u32[]{:S(2)}, u32[]{:S(2)}) collective-permute-start(bf16[512,384]{1,0:T(8,128)(2,1)} %get-tuple-element.50), channel_id=1, source_target_pairs={{0,2},{1,3},{2,0},{3,1},{4,6},{5,7},{6,4},{7,5},{8,10},{9,11},{10,... | collective-permute-start | bytes 1179656 | tf_op jit(solution)/shard_map/ppermute | solution.py:88
  11.4 1.1 %copy-done.3 = bf16[1,512,768]{2,1,0:T(8,128)(2,1)S(1)} copy-done((bf16[1,512,768]{2,1,0:T(8,128)(2,1)S(1)}, bf16[1,512,768]{2,1,0:T(8,128)(2,1)}, u32[]{:S(2)}) %copy-start.3) | copy-done | bytes 786456
  12.5 0.7 transposed.1
  13.2 8.9 %collective-permute-done.1.refs_2_ = bf16[16,2688]{1,0:T(8,128)(2,1)S(1)} collective-permute-done((bf16[16,2688]{1,0:T(8,128)(2,1)S(1)}, bf16[16,2688]{1,0:T(8,128)(2,1)S(1)}, u32[]{:S(2)}, u32[]{:S(2)}) %collective-permute-start.1) | collective-permute-done | bytes 86048 | tf_op jit(solution)/shard_map/ppermute | solution.py:88
  22.1 1.6 %collective-permute-start.3 = (bf16[64,2688]{1,0:T(8,128)(2,1)S(1)}, bf16[64,2688]{1,0:T(8,128)(2,1)S(1)}, u32[]{:S(2)}, u32[]{:S(2)}) collective-permute-start(bf16[64,2688]{1,0:T(8,128)(2,1)S(1)} %bitcast.8), channel_id=1, source_target_pairs={{0,8},{4,12},{8,0},{12,4},{16,24},{20,28},{24,16},{28,20},{1,9},{5... | collective-permute-start | bytes 1032200 | tf_op jit(solution)/shard_map/ppermute | solution.py:88
  23.7 1.5 %collective-permute-start.5 = (bf16[64,2688]{1,0:T(8,128)(2,1)S(1)}, bf16[64,2688]{1,0:T(8,128)(2,1)S(1)}, u32[]{:S(2)}, u32[]{:S(2)}) collective-permute-start(bf16[64,2688]{1,0:T(8,128)(2,1)S(1)} %bitcast.9), channel_id=1, source_target_pairs={{0,24},{4,28},{8,16},{12,20},{16,8},{20,12},{24,0},{28,4},{1,25},{... | collective-permute-start | bytes 1032200 | tf_op jit(solution)/shard_map/ppermute | solution.py:88
  25.7 3.8 %collective-permute-done.3.refs_1_ = bf16[64,2688]{1,0:T(8,128)(2,1)S(1)} collective-permute-done((bf16[64,2688]{1,0:T(8,128)(2,1)S(1)}, bf16[64,2688]{1,0:T(8,128)(2,1)S(1)}, u32[]{:S(2)}, u32[]{:S(2)}) %collective-permute-start.3) | collective-permute-done | bytes 344096 | tf_op jit(solution)/shard_map/ppermute | solution.py:88
  29.4 6.1 %collective-permute-start.11 = (bf16[512,384]{1,0:T(8,128)(2,1)}, bf16[512,384]{1,0:T(8,128)(2,1)S(1)}, u32[]{:S(2)}, u32[]{:S(2)}) collective-permute-start(bf16[512,384]{1,0:T(8,128)(2,1)} %copy-done.5), channel_id=1, source_target_pairs={{0,1},{1,0},{2,3},{3,2},{4,5},{5,4},{6,7},{7,6},{8,9},{9,8},{10,11... | collective-permute-start | bytes 1179656 | tf_op jit(solution)/shard_map/ppermute | solution.py:88
  35.6 2.6 %collective-permute-start.12 = (bf16[512,384]{1,0:T(8,128)(2,1)}, bf16[512,384]{1,0:T(8,128)(2,1)S(1)}, u32[]{:S(2)}, u32[]{:S(2)}) collective-permute-start(bf16[512,384]{1,0:T(8,128)(2,1)} %copy-done.4), channel_id=1, source_target_pairs={{0,3},{1,2},{2,1},{3,0},{4,7},{5,6},{6,5},{7,4},{8,11},{9,10},{10,... | collective-permute-start | bytes 1179656 | tf_op jit(solution)/shard_map/ppermute | solution.py:88
  38.8 1.1 %collective-permute-done.9.refs_7_ = bf16[64,2688]{1,0:T(8,128)(2,1)S(1)} collective-permute-done((bf16[64,2688]{1,0:T(8,128)(2,1)S(1)}, bf16[64,2688]{1,0:T(8,128)(2,1)S(1)}, u32[]{:S(2)}, u32[]{:S(2)}) %collective-permute-start.9) | collective-permute-done | bytes 344096 | tf_op jit(solution)/shard_map/ppermute | solution.py:88
  40.8 3.9 %collective-permute-done.11.refs_10_ = bf16[512,384]{1,0:T(8,128)(2,1)S(1)} collective-permute-done((bf16[512,384]{1,0:T(8,128)(2,1)}, bf16[512,384]{1,0:T(8,128)(2,1)S(1)}, u32[]{:S(2)}, u32[]{:S(2)}) %collective-permute-start.11) | collective-permute-done | bytes 393248 | tf_op jit(solution)/shard_map/ppermute | solution.py:88
  44.7 2.2 %start_hidden.1 = (f32[512,384]{1,0:T(8,128)S(1)}, bf16[512,512]{1,0:T(8,128)(2,1)S(1)}) custom-call(bf16[64,2688]{1,0:T(8,128)(2,1)S(1)} %bitcast.12, bf16[64,2688]{1,0:T(8,128)(2,1)S(1)} %collective-permute-done.3.refs_1_, bf16[64,2688]{1,0:T(8,128)(2,1)S(1)} %collective-permute-done.4.refs_2_, bf16[64,2688]{1,0:T(8,128)(2,1)S(1)} %collective-permute-done.5.refs_3_, ...), custom_call_target="tpu_custom_call" | custom-call | tf_op jit(solution)/shard_map/start_hidden/pallas_call | solution.py:229
  47.0 2.0 %collective-permute-done.12.refs_0_ = bf16[512,384]{1,0:T(8,128)(2,1)S(1)} collective-permute-done((bf16[512,384]{1,0:T(8,128)(2,1)}, bf16[512,384]{1,0:T(8,128)(2,1)S(1)}, u32[]{:S(2)}, u32[]{:S(2)}) %collective-permute-start.12) | collective-permute-done | bytes 393248 | tf_op jit(solution)/shard_map/ppermute | solution.py:88
  49.0 0.6 end_hidden.1.refs_0_
  49.8 2.9 %collective-permute-start.23 = (bf16[192,512]{1,0:T(8,128)(2,1)S(1)}, bf16[192,512]{1,0:T(8,128)(2,1)S(1)}, u32[]{:S(2)}, u32[]{:S(2)}) collective-permute-start(bf16[192,512]{1,0:T(8,128)(2,1)S(1)} %end_hidden.1.refs_0_), channel_id=1, source_target_pairs={{0,1},{1,0},{2,3},{3,2},{4,5},{5,4},{6,7},{7,6},{8,9},{9,8},{10,11... | collective-permute-start | bytes 589832 | tf_op jit(solution)/shard_map/ppermute | solution.py:88
  52.6 5.9 %collective-permute-done.13.refs_1_ = bf16[192,512]{1,0:T(8,128)(2,1)S(1)} collective-permute-done((bf16[192,512]{1,0:T(8,128)(2,1)S(1)}, bf16[192,512]{1,0:T(8,128)(2,1)S(1)}, u32[]{:S(2)}, u32[]{:S(2)}) %collective-permute-start.13) | collective-permute-done | bytes 196640 | tf_op jit(solution)/shard_map/ppermute | solution.py:88
  58.7 1.0 update_tiles.2
  59.7 1.6 %collective-permute-start.14 = (bf16[2,192,128]{2,1,0:T(8,128)(2,1)S(1)}, bf16[2,192,128]{2,1,0:T(8,128)(2,1)S(1)}, u32[]{:S(2)}, u32[]{:S(2)}) collective-permute-start(bf16[2,192,128]{2,1,0:T(8,128)(2,1)S(1)} %get-tuple-element.60), channel_id=1, source_target_pairs={{0,8},{4,12},{8,0},{12,4},{16,24},{20,28},{24,16},{28,20},{1,9},{5... | collective-permute-start | bytes 294920 | tf_op jit(solution)/shard_map/ppermute | solution.py:88
  61.2 1.5 %collective-permute-start.15 = (bf16[2,192,128]{2,1,0:T(8,128)(2,1)S(1)}, bf16[2,192,128]{2,1,0:T(8,128)(2,1)S(1)}, u32[]{:S(2)}, u32[]{:S(2)}) collective-permute-start(bf16[2,192,128]{2,1,0:T(8,128)(2,1)S(1)} %get-tuple-element.61), channel_id=1, source_target_pairs={{0,16},{4,20},{8,24},{12,28},{16,0},{20,4},{24,8},{28,12},{1,17},{... | collective-permute-start | bytes 294920 | tf_op jit(solution)/shard_map/ppermute | solution.py:88
  63.2 1.0 collective-permute-done.24.refs_1_
  64.2 0.9 update_tiles.3
  65.1 1.6 %collective-permute-start.25 = (bf16[2,192,128]{2,1,0:T(8,128)(2,1)S(1)}, bf16[2,192,128]{2,1,0:T(8,128)(2,1)S(1)}, u32[]{:S(2)}, u32[]{:S(2)}) collective-permute-start(bf16[2,192,128]{2,1,0:T(8,128)(2,1)S(1)} %get-tuple-element.70), channel_id=1, source_target_pairs={{0,8},{4,12},{8,0},{12,4},{16,24},{20,28},{24,16},{28,20},{1,9},{5... | collective-permute-start | bytes 294920 | tf_op jit(solution)/shard_map/ppermute | solution.py:88
  66.7 1.5 %collective-permute-start.26 = (bf16[2,192,128]{2,1,0:T(8,128)(2,1)S(1)}, bf16[2,192,128]{2,1,0:T(8,128)(2,1)S(1)}, u32[]{:S(2)}, u32[]{:S(2)}) collective-permute-start(bf16[2,192,128]{2,1,0:T(8,128)(2,1)S(1)} %get-tuple-element.71), channel_id=1, source_target_pairs={{0,16},{4,20},{8,24},{12,28},{16,0},{20,4},{24,8},{28,12},{1,17},{... | collective-permute-start | bytes 294920 | tf_op jit(solution)/shard_map/ppermute | solution.py:88
  68.7 0.5 collective-permute-done.16.refs_3_
  69.3 1.4 %collective-permute-start.17 = (bf16[4,192,128]{2,1,0:T(8,128)(2,1)S(1)}, bf16[4,192,128]{2,1,0:T(8,128)(2,1)S(1)}, u32[]{:S(2)}, u32[]{:S(2)}) collective-permute-start(bf16[4,192,128]{2,1,0:T(8,128)(2,1)S(1)} %get-tuple-element.64), channel_id=1, source_target_pairs={{0,2},{1,3},{2,0},{3,1},{4,6},{5,7},{6,4},{7,5},{8,10},{9,11},{10,... | collective-permute-start | bytes 589832 | tf_op jit(solution)/shard_map/ppermute | solution.py:88
  70.7 0.6 collective-permute-done.26.refs_2_
  71.3 2.4 %collective-permute-done.27.refs_3_ = bf16[2,192,128]{2,1,0:T(8,128)(2,1)S(1)} collective-permute-done((bf16[2,192,128]{2,1,0:T(8,128)(2,1)S(1)}, bf16[2,192,128]{2,1,0:T(8,128)(2,1)S(1)}, u32[]{:S(2)}, u32[]{:S(2)}) %collective-permute-start.27) | collective-permute-done | bytes 98336 | tf_op jit(solution)/shard_map/ppermute | solution.py:88
  73.8 1.1 %collective-permute-start.28 = (bf16[4,192,128]{2,1,0:T(8,128)(2,1)S(1)}, bf16[4,192,128]{2,1,0:T(8,128)(2,1)S(1)}, u32[]{:S(2)}, u32[]{:S(2)}) collective-permute-start(bf16[4,192,128]{2,1,0:T(8,128)(2,1)S(1)} %get-tuple-element.73), channel_id=1, source_target_pairs={{0,1},{1,0},{2,3},{3,2},{4,5},{5,4},{6,7},{7,6},{8,9},{9,8},{10,11... | collective-permute-start | bytes 589832 | tf_op jit(solution)/shard_map/ppermute | solution.py:88
  74.9 1.6 %collective-permute-start.29 = (bf16[4,192,128]{2,1,0:T(8,128)(2,1)S(1)}, bf16[4,192,128]{2,1,0:T(8,128)(2,1)S(1)}, u32[]{:S(2)}, u32[]{:S(2)}) collective-permute-start(bf16[4,192,128]{2,1,0:T(8,128)(2,1)S(1)} %get-tuple-element.74), channel_id=1, source_target_pairs={{0,3},{1,2},{2,1},{3,0},{4,7},{5,6},{6,5},{7,4},{8,11},{9,10},{10,... | collective-permute-start | bytes 589832 | tf_op jit(solution)/shard_map/ppermute | solution.py:88
  76.5 7.3 %collective-permute-done.17.refs_1_ = bf16[4,192,128]{2,1,0:T(8,128)(2,1)S(1)} collective-permute-done((bf16[4,192,128]{2,1,0:T(8,128)(2,1)S(1)}, bf16[4,192,128]{2,1,0:T(8,128)(2,1)S(1)}, u32[]{:S(2)}, u32[]{:S(2)}) %collective-permute-start.17) | collective-permute-done | bytes 196640 | tf_op jit(solution)/shard_map/ppermute | solution.py:88
  84.4 0.9 collective-permute-done.19.refs_3_
  85.3 0.8 pick.2
  86.0 0.7 collective-permute-start.20
  86.8 1.0 collective-permute-start.21
  87.7 1.9 %collective-permute-start.22 = (bf16[2,192,128]{2,1,0:T(8,128)(2,1)S(1)}, bf16[2,192,128]{2,1,0:T(8,128)(2,1)S(1)}, u32[]{:S(2)}, u32[]{:S(2)}) collective-permute-start(bf16[2,192,128]{2,1,0:T(8,128)(2,1)S(1)} %get-tuple-element.68), channel_id=1, source_target_pairs={{0,24},{4,28},{8,16},{12,20},{16,8},{20,12},{24,0},{28,4},{1,25},{... | collective-permute-start | bytes 294920 | tf_op jit(solution)/shard_map/ppermute | solution.py:88
  89.6 0.8 pick.3
  90.4 0.7 collective-permute-start.32
  91.1 1.0 collective-permute-start.33
  92.1 1.9 %collective-permute-start.34 = (bf16[2,192,128]{2,1,0:T(8,128)(2,1)S(1)}, bf16[2,192,128]{2,1,0:T(8,128)(2,1)S(1)}, u32[]{:S(2)}, u32[]{:S(2)}) collective-permute-start(bf16[2,192,128]{2,1,0:T(8,128)(2,1)S(1)} %get-tuple-element.78), channel_id=1, source_target_pairs={{0,24},{4,28},{8,16},{12,20},{16,8},{20,12},{24,0},{28,4},{1,25},{... | collective-permute-start | bytes 294920 | tf_op jit(solution)/shard_map/ppermute | solution.py:88
  94.4 1.8 %collective-permute-done.32.refs_5_ = bf16[2,192,128]{2,1,0:T(8,128)(2,1)S(1)} collective-permute-done((bf16[2,192,128]{2,1,0:T(8,128)(2,1)S(1)}, bf16[2,192,128]{2,1,0:T(8,128)(2,1)S(1)}, u32[]{:S(2)}, u32[]{:S(2)}) %collective-permute-start.32) | collective-permute-done | bytes 98336 | tf_op jit(solution)/shard_map/ppermute | solution.py:88
  96.2 0.7 collective-permute-done.33.refs_6_
  96.8 1.1 %collective-permute-done.34.refs_7_ = bf16[2,192,128]{2,1,0:T(8,128)(2,1)S(1)} collective-permute-done((bf16[2,192,128]{2,1,0:T(8,128)(2,1)S(1)}, bf16[2,192,128]{2,1,0:T(8,128)(2,1)S(1)}, u32[]{:S(2)}, u32[]{:S(2)}) %collective-permute-start.34) | collective-permute-done | bytes 98336 | tf_op jit(solution)/shard_map/ppermute | solution.py:88
  97.9 1.1 %unpack.1 = bf16[1,192,2048]{2,1,0:T(8,128)(2,1)} custom-call(bf16[2,192,128]{2,1,0:T(8,128)(2,1)S(1)} %get-tuple-element.65.refs_0_, bf16[2,192,128]{2,1,0:T(8,128)(2,1)S(1)} %collective-permute-done.20.refs_1_, bf16[2,192,128]{2,1,0:T(8,128)(2,1)S(1)} %collective-permute-done.21.refs_2_, bf16[2,192,128]{2,1,0:T(8,128)(2,1)S(1)} %collective-permute-done.22.refs_3_, ...), custom_call_target="tpu_custom_call" | custom-call | tf_op jit(solution)/shard_map/unpack/pallas_call | solution.py:407
  (48 shorter events, 4.5 us)
Async XLA Ops:
  1.0 8.5 %collective-permute-start = (bf16[16,2688]{1,0:T(8,128)(2,1)S(1)}, bf16[16,2688]{1,0:T(8,128)(2,1)S(1)}, u32[]{:S(2)}, u32[]{:S(2)}) collective-permute-start(bf16[16,2688]{1,0:T(8,128)(2,1)S(1)} %get-tuple-element.45), channel_id=1, source_target_pairs={{0,1},{1,0},{2,3},{3,2},{4,5},{5,4},{6,7},{7,6},{8,9},{9,8},{10,11... | collective-permute-start | bytes 258056 | tf_op jit(solution)/shard_map/ppermute | solution.py:88
  4.0 18.0 %collective-permute-start.1 = (bf16[16,2688]{1,0:T(8,128)(2,1)S(1)}, bf16[16,2688]{1,0:T(8,128)(2,1)S(1)}, u32[]{:S(2)}, u32[]{:S(2)}) collective-permute-start(bf16[16,2688]{1,0:T(8,128)(2,1)S(1)} %get-tuple-element.46), channel_id=1, source_target_pairs={{0,2},{1,3},{2,0},{3,1},{4,6},{5,7},{6,4},{7,5},{8,10},{9,11},{10,... | collective-permute-start | bytes 258056 | tf_op jit(solution)/shard_map/ppermute | solution.py:88
  6.6 15.4 %collective-permute-start.2 = (bf16[16,2688]{1,0:T(8,128)(2,1)S(1)}, bf16[16,2688]{1,0:T(8,128)(2,1)S(1)}, u32[]{:S(2)}, u32[]{:S(2)}) collective-permute-start(bf16[16,2688]{1,0:T(8,128)(2,1)S(1)} %get-tuple-element.47), channel_id=1, source_target_pairs={{0,3},{1,2},{2,1},{3,0},{4,7},{5,6},{6,5},{7,4},{8,11},{9,10},{10,... | collective-permute-start | bytes 258056 | tf_op jit(solution)/shard_map/ppermute | solution.py:88
  6.6 1.4 %copy-start = (bf16[1,512,1536]{2,1,0:T(8,128)(2,1)S(1)}, bf16[1,512,1536]{2,1,0:T(8,128)(2,1)}, u32[]{:S(2)}) copy-start(bf16[1,512,1536]{2,1,0:T(8,128)(2,1)} %param.13) | copy-start | bytes 4718596
  8.0 3.3 %copy-start.1 = (bf16[1,512,768]{2,1,0:T(8,128)(2,1)S(1)}, bf16[1,512,768]{2,1,0:T(8,128)(2,1)}, u32[]{:S(2)}) copy-start(bf16[1,512,768]{2,1,0:T(8,128)(2,1)} %param.14) | copy-start | bytes 2359300
  8.0 3.3 %copy-start.2 = (bf16[1,512,768]{2,1,0:T(8,128)(2,1)S(1)}, bf16[1,512,768]{2,1,0:T(8,128)(2,1)}, u32[]{:S(2)}) copy-start(bf16[1,512,768]{2,1,0:T(8,128)(2,1)} %param.15) | copy-start | bytes 2359300
  9.4 12.6 %copy-start.4 = (bf16[512,384]{1,0:T(8,128)(2,1)}, bf16[512,384]{1,0:T(8,128)(2,1)S(1)}, u32[]{:S(2)}) copy-start(bf16[512,384]{1,0:T(8,128)(2,1)S(1)} %get-tuple-element.56) | copy-start | bytes 1179652
  9.4 12.6 %copy-start.5 = (bf16[512,384]{1,0:T(8,128)(2,1)}, bf16[512,384]{1,0:T(8,128)(2,1)S(1)}, u32[]{:S(2)}) copy-start(bf16[512,384]{1,0:T(8,128)(2,1)S(1)} %get-tuple-element.52) | copy-start | bytes 1179652
  9.5 26.1 %collective-permute-start.10 = (bf16[512,384]{1,0:T(8,128)(2,1)}, bf16[512,384]{1,0:T(8,128)(2,1)}, u32[]{:S(2)}, u32[]{:S(2)}) collective-permute-start(bf16[512,384]{1,0:T(8,128)(2,1)} %get-tuple-element.50), channel_id=1, source_target_pairs={{0,2},{1,3},{2,0},{3,1},{4,6},{5,7},{6,4},{7,5},{8,10},{9,11},{10,... | collective-permute-start | bytes 1179656 | tf_op jit(solution)/shard_map/ppermute | solution.py:88
  11.4 1.1 %copy-start.3 = (bf16[1,512,768]{2,1,0:T(8,128)(2,1)S(1)}, bf16[1,512,768]{2,1,0:T(8,128)(2,1)}, u32[]{:S(2)}) copy-start(bf16[1,512,768]{2,1,0:T(8,128)(2,1)} %param.16) | copy-start | bytes 2359300
  22.1 7.3 %collective-permute-start.3 = (bf16[64,2688]{1,0:T(8,128)(2,1)S(1)}, bf16[64,2688]{1,0:T(8,128)(2,1)S(1)}, u32[]{:S(2)}, u32[]{:S(2)}) collective-permute-start(bf16[64,2688]{1,0:T(8,128)(2,1)S(1)} %bitcast.8), channel_id=1, source_target_pairs={{0,8},{4,12},{8,0},{12,4},{16,24},{20,28},{24,16},{28,20},{1,9},{5... | collective-permute-start | bytes 1032200 | tf_op jit(solution)/shard_map/ppermute | solution.py:88
  23.7 14.5 %collective-permute-start.5 = (bf16[64,2688]{1,0:T(8,128)(2,1)S(1)}, bf16[64,2688]{1,0:T(8,128)(2,1)S(1)}, u32[]{:S(2)}, u32[]{:S(2)}) collective-permute-start(bf16[64,2688]{1,0:T(8,128)(2,1)S(1)} %bitcast.9), channel_id=1, source_target_pairs={{0,24},{4,28},{8,16},{12,20},{16,8},{20,12},{24,0},{28,4},{1,25},{... | collective-permute-start | bytes 1032200 | tf_op jit(solution)/shard_map/ppermute | solution.py:88
  25.2 13.0 %collective-permute-start.4 = (bf16[64,2688]{1,0:T(8,128)(2,1)S(1)}, bf16[64,2688]{1,0:T(8,128)(2,1)S(1)}, u32[]{:S(2)}, u32[]{:S(2)}) collective-permute-start(bf16[64,2688]{1,0:T(8,128)(2,1)S(1)} %bitcast.10), channel_id=1, source_target_pairs={{0,16},{4,20},{8,24},{12,28},{16,0},{20,4},{24,8},{28,12},{1,17},{... | collective-permute-start | bytes 1032200 | tf_op jit(solution)/shard_map/ppermute | solution.py:88
  25.7 13.0 %collective-permute-start.6 = (bf16[64,2688]{1,0:T(8,128)(2,1)S(1)}, bf16[64,2688]{1,0:T(8,128)(2,1)S(1)}, u32[]{:S(2)}, u32[]{:S(2)}) collective-permute-start(bf16[64,2688]{1,0:T(8,128)(2,1)S(1)} %bitcast.11), channel_id=1, source_target_pairs={{0,4},{4,0},{8,12},{12,8},{16,20},{20,16},{24,28},{28,24},{1,5},{5... | collective-permute-start | bytes 1032200 | tf_op jit(solution)/shard_map/ppermute | solution.py:88
  29.4 15.3 %collective-permute-start.11 = (bf16[512,384]{1,0:T(8,128)(2,1)}, bf16[512,384]{1,0:T(8,128)(2,1)S(1)}, u32[]{:S(2)}, u32[]{:S(2)}) collective-permute-start(bf16[512,384]{1,0:T(8,128)(2,1)} %copy-done.5), channel_id=1, source_target_pairs={{0,1},{1,0},{2,3},{3,2},{4,5},{5,4},{6,7},{7,6},{8,9},{9,8},{10,11... | collective-permute-start | bytes 1179656 | tf_op jit(solution)/shard_map/ppermute | solution.py:88
  35.6 13.4 %collective-permute-start.12 = (bf16[512,384]{1,0:T(8,128)(2,1)}, bf16[512,384]{1,0:T(8,128)(2,1)S(1)}, u32[]{:S(2)}, u32[]{:S(2)}) collective-permute-start(bf16[512,384]{1,0:T(8,128)(2,1)} %copy-done.4), channel_id=1, source_target_pairs={{0,3},{1,2},{2,1},{3,0},{4,7},{5,6},{6,5},{7,4},{8,11},{9,10},{10,... | collective-permute-start | bytes 1179656 | tf_op jit(solution)/shard_map/ppermute | solution.py:88
  38.2 1.7 %collective-permute-start.9 = (bf16[64,2688]{1,0:T(8,128)(2,1)S(1)}, bf16[64,2688]{1,0:T(8,128)(2,1)S(1)}, u32[]{:S(2)}, u32[]{:S(2)}) collective-permute-start(bf16[64,2688]{1,0:T(8,128)(2,1)S(1)} %collective-permute-done.5.refs_3_), channel_id=1, source_target_pairs={{0,4},{4,0},{8,12},{12,8},{16,20},{20,16},{24,28},{28,24},{1,5},{5... | collective-permute-start | bytes 1032200 | tf_op jit(solution)/shard_map/ppermute | solution.py:88
  38.2 2.1 %collective-permute-start.8 = (bf16[64,2688]{1,0:T(8,128)(2,1)S(1)}, bf16[64,2688]{1,0:T(8,128)(2,1)S(1)}, u32[]{:S(2)}, u32[]{:S(2)}) collective-permute-start(bf16[64,2688]{1,0:T(8,128)(2,1)S(1)} %collective-permute-done.4.refs_2_), channel_id=1, source_target_pairs={{0,4},{4,0},{8,12},{12,8},{16,20},{20,16},{24,28},{28,24},{1,5},{5... | collective-permute-start | bytes 1032200 | tf_op jit(solution)/shard_map/ppermute | solution.py:88
  38.7 2.1 %collective-permute-start.7 = (bf16[64,2688]{1,0:T(8,128)(2,1)S(1)}, bf16[64,2688]{1,0:T(8,128)(2,1)S(1)}, u32[]{:S(2)}, u32[]{:S(2)}) collective-permute-start(bf16[64,2688]{1,0:T(8,128)(2,1)S(1)} %collective-permute-done.3.refs_1_), channel_id=1, source_target_pairs={{0,4},{4,0},{8,12},{12,8},{16,20},{20,16},{24,28},{28,24},{1,5},{5... | collective-permute-start | bytes 1032200 | tf_op jit(solution)/shard_map/ppermute | solution.py:88
  49.7 8.8 %collective-permute-start.13 = (bf16[192,512]{1,0:T(8,128)(2,1)S(1)}, bf16[192,512]{1,0:T(8,128)(2,1)S(1)}, u32[]{:S(2)}, u32[]{:S(2)}) collective-permute-start(bf16[192,512]{1,0:T(8,128)(2,1)S(1)} %end_hidden.1.refs_0_), channel_id=1, source_target_pairs={{0,2},{1,3},{2,0},{3,1},{4,6},{5,7},{6,4},{7,5},{8,10},{9,11},{10,... | collective-permute-start | bytes 589832 | tf_op jit(solution)/shard_map/ppermute | solution.py:88
  49.8 13.5 %collective-permute-start.23 = (bf16[192,512]{1,0:T(8,128)(2,1)S(1)}, bf16[192,512]{1,0:T(8,128)(2,1)S(1)}, u32[]{:S(2)}, u32[]{:S(2)}) collective-permute-start(bf16[192,512]{1,0:T(8,128)(2,1)S(1)} %end_hidden.1.refs_0_), channel_id=1, source_target_pairs={{0,1},{1,0},{2,3},{3,2},{4,5},{5,4},{6,7},{7,6},{8,9},{9,8},{10,11... | collective-permute-start | bytes 589832 | tf_op jit(solution)/shard_map/ppermute | solution.py:88
  58.5 5.7 %collective-permute-start.24 = (bf16[192,512]{1,0:T(8,128)(2,1)S(1)}, bf16[192,512]{1,0:T(8,128)(2,1)S(1)}, u32[]{:S(2)}, u32[]{:S(2)}) collective-permute-start(bf16[192,512]{1,0:T(8,128)(2,1)S(1)} %collective-permute-done.13.refs_1_), channel_id=1, source_target_pairs={{0,1},{1,0},{2,3},{3,2},{4,5},{5,4},{6,7},{7,6},{8,9},{9,8},{10,11... | collective-permute-start | bytes 589832 | tf_op jit(solution)/shard_map/ppermute | solution.py:88
  59.7 8.5 %collective-permute-start.14 = (bf16[2,192,128]{2,1,0:T(8,128)(2,1)S(1)}, bf16[2,192,128]{2,1,0:T(8,128)(2,1)S(1)}, u32[]{:S(2)}, u32[]{:S(2)}) collective-permute-start(bf16[2,192,128]{2,1,0:T(8,128)(2,1)S(1)} %get-tuple-element.60), channel_id=1, source_target_pairs={{0,8},{4,12},{8,0},{12,4},{16,24},{20,28},{24,16},{28,20},{1,9},{5... | collective-permute-start | bytes 294920 | tf_op jit(solution)/shard_map/ppermute | solution.py:88
  61.2 7.5 %collective-permute-start.15 = (bf16[2,192,128]{2,1,0:T(8,128)(2,1)S(1)}, bf16[2,192,128]{2,1,0:T(8,128)(2,1)S(1)}, u32[]{:S(2)}, u32[]{:S(2)}) collective-permute-start(bf16[2,192,128]{2,1,0:T(8,128)(2,1)S(1)} %get-tuple-element.61), channel_id=1, source_target_pairs={{0,16},{4,20},{8,24},{12,28},{16,0},{20,4},{24,8},{28,12},{1,17},{... | collective-permute-start | bytes 294920 | tf_op jit(solution)/shard_map/ppermute | solution.py:88
  62.7 6.5 %collective-permute-start.16 = (bf16[2,192,128]{2,1,0:T(8,128)(2,1)S(1)}, bf16[2,192,128]{2,1,0:T(8,128)(2,1)S(1)}, u32[]{:S(2)}, u32[]{:S(2)}) collective-permute-start(bf16[2,192,128]{2,1,0:T(8,128)(2,1)S(1)} %get-tuple-element.62), channel_id=1, source_target_pairs={{0,24},{4,28},{8,16},{12,20},{16,8},{20,12},{24,0},{28,4},{1,25},{... | collective-permute-start | bytes 294920 | tf_op jit(solution)/shard_map/ppermute | solution.py:88
  65.1 5.6 %collective-permute-start.25 = (bf16[2,192,128]{2,1,0:T(8,128)(2,1)S(1)}, bf16[2,192,128]{2,1,0:T(8,128)(2,1)S(1)}, u32[]{:S(2)}, u32[]{:S(2)}) collective-permute-start(bf16[2,192,128]{2,1,0:T(8,128)(2,1)S(1)} %get-tuple-element.70), channel_id=1, source_target_pairs={{0,8},{4,12},{8,0},{12,4},{16,24},{20,28},{24,16},{28,20},{1,9},{5... | collective-permute-start | bytes 294920 | tf_op jit(solution)/shard_map/ppermute | solution.py:88
  66.7 4.6 %collective-permute-start.26 = (bf16[2,192,128]{2,1,0:T(8,128)(2,1)S(1)}, bf16[2,192,128]{2,1,0:T(8,128)(2,1)S(1)}, u32[]{:S(2)}, u32[]{:S(2)}) collective-permute-start(bf16[2,192,128]{2,1,0:T(8,128)(2,1)S(1)} %get-tuple-element.71), channel_id=1, source_target_pairs={{0,16},{4,20},{8,24},{12,28},{16,0},{20,4},{24,8},{28,12},{1,17},{... | collective-permute-start | bytes 294920 | tf_op jit(solution)/shard_map/ppermute | solution.py:88
  68.2 5.5 %collective-permute-start.27 = (bf16[2,192,128]{2,1,0:T(8,128)(2,1)S(1)}, bf16[2,192,128]{2,1,0:T(8,128)(2,1)S(1)}, u32[]{:S(2)}, u32[]{:S(2)}) collective-permute-start(bf16[2,192,128]{2,1,0:T(8,128)(2,1)S(1)} %get-tuple-element.72), channel_id=1, source_target_pairs={{0,24},{4,28},{8,16},{12,20},{16,8},{20,12},{24,0},{28,4},{1,25},{... | collective-permute-start | bytes 294920 | tf_op jit(solution)/shard_map/ppermute | solution.py:88
  69.3 14.6 %collective-permute-start.17 = (bf16[4,192,128]{2,1,0:T(8,128)(2,1)S(1)}, bf16[4,192,128]{2,1,0:T(8,128)(2,1)S(1)}, u32[]{:S(2)}, u32[]{:S(2)}) collective-permute-start(bf16[4,192,128]{2,1,0:T(8,128)(2,1)S(1)} %get-tuple-element.64), channel_id=1, source_target_pairs={{0,2},{1,3},{2,0},{3,1},{4,6},{5,7},{6,4},{7,5},{8,10},{9,11},{10,... | collective-permute-start | bytes 589832 | tf_op jit(solution)/shard_map/ppermute | solution.py:88
  73.8 10.1 %collective-permute-start.28 = (bf16[4,192,128]{2,1,0:T(8,128)(2,1)S(1)}, bf16[4,192,128]{2,1,0:T(8,128)(2,1)S(1)}, u32[]{:S(2)}, u32[]{:S(2)}) collective-permute-start(bf16[4,192,128]{2,1,0:T(8,128)(2,1)S(1)} %get-tuple-element.73), channel_id=1, source_target_pairs={{0,1},{1,0},{2,3},{3,2},{4,5},{5,4},{6,7},{7,6},{8,9},{9,8},{10,11... | collective-permute-start | bytes 589832 | tf_op jit(solution)/shard_map/ppermute | solution.py:88
  74.9 9.4 %collective-permute-start.29 = (bf16[4,192,128]{2,1,0:T(8,128)(2,1)S(1)}, bf16[4,192,128]{2,1,0:T(8,128)(2,1)S(1)}, u32[]{:S(2)}, u32[]{:S(2)}) collective-permute-start(bf16[4,192,128]{2,1,0:T(8,128)(2,1)S(1)} %get-tuple-element.74), channel_id=1, source_target_pairs={{0,3},{1,2},{2,1},{3,0},{4,7},{5,6},{6,5},{7,4},{8,11},{9,10},{10,... | collective-permute-start | bytes 589832 | tf_op jit(solution)/shard_map/ppermute | solution.py:88
  76.5 7.9 %collective-permute-start.18 = (bf16[4,192,128]{2,1,0:T(8,128)(2,1)S(1)}, bf16[4,192,128]{2,1,0:T(8,128)(2,1)S(1)}, u32[]{:S(2)}, u32[]{:S(2)}) collective-permute-start(bf16[4,192,128]{2,1,0:T(8,128)(2,1)S(1)} %get-tuple-element.63.refs_0_), channel_id=1, source_target_pairs={{0,4},{4,0},{8,12},{12,8},{16,20},{20,16},{24,28},{28,24},{1,5},{5... | collective-permute-start | bytes 589832 | tf_op jit(solution)/shard_map/ppermute | solution.py:88
  83.8 1.4 %collective-permute-start.19 = (bf16[4,192,128]{2,1,0:T(8,128)(2,1)S(1)}, bf16[4,192,128]{2,1,0:T(8,128)(2,1)S(1)}, u32[]{:S(2)}, u32[]{:S(2)}) collective-permute-start(bf16[4,192,128]{2,1,0:T(8,128)(2,1)S(1)} %collective-permute-done.17.refs_1_), channel_id=1, source_target_pairs={{0,4},{4,0},{8,12},{12,8},{16,20},{20,16},{24,28},{28,24},{1,5},{5... | collective-permute-start | bytes 589832 | tf_op jit(solution)/shard_map/ppermute | solution.py:88
  83.9 5.7 %collective-permute-start.30 = (bf16[4,192,128]{2,1,0:T(8,128)(2,1)S(1)}, bf16[4,192,128]{2,1,0:T(8,128)(2,1)S(1)}, u32[]{:S(2)}, u32[]{:S(2)}) collective-permute-start(bf16[4,192,128]{2,1,0:T(8,128)(2,1)S(1)} %collective-permute-done.28.refs_0_), channel_id=1, source_target_pairs={{0,4},{4,0},{8,12},{12,8},{16,20},{20,16},{24,28},{28,24},{1,5},{5... | collective-permute-start | bytes 589832 | tf_op jit(solution)/shard_map/ppermute | solution.py:88
  84.3 5.3 %collective-permute-start.31 = (bf16[4,192,128]{2,1,0:T(8,128)(2,1)S(1)}, bf16[4,192,128]{2,1,0:T(8,128)(2,1)S(1)}, u32[]{:S(2)}, u32[]{:S(2)}) collective-permute-start(bf16[4,192,128]{2,1,0:T(8,128)(2,1)S(1)} %collective-permute-done.29.refs_1_), channel_id=1, source_target_pairs={{0,4},{4,0},{8,12},{12,8},{16,20},{20,16},{24,28},{28,24},{1,5},{5... | collective-permute-start | bytes 589832 | tf_op jit(solution)/shard_map/ppermute | solution.py:88
  86.0 6.0 %collective-permute-start.20 = (bf16[2,192,128]{2,1,0:T(8,128)(2,1)S(1)}, bf16[2,192,128]{2,1,0:T(8,128)(2,1)S(1)}, u32[]{:S(2)}, u32[]{:S(2)}) collective-permute-start(bf16[2,192,128]{2,1,0:T(8,128)(2,1)S(1)} %get-tuple-element.66), channel_id=1, source_target_pairs={{0,8},{4,12},{8,0},{12,4},{16,24},{20,28},{24,16},{28,20},{1,9},{5... | collective-permute-start | bytes 294920 | tf_op jit(solution)/shard_map/ppermute | solution.py:88
  86.8 7.2 %collective-permute-start.21 = (bf16[2,192,128]{2,1,0:T(8,128)(2,1)S(1)}, bf16[2,192,128]{2,1,0:T(8,128)(2,1)S(1)}, u32[]{:S(2)}, u32[]{:S(2)}) collective-permute-start(bf16[2,192,128]{2,1,0:T(8,128)(2,1)S(1)} %get-tuple-element.67), channel_id=1, source_target_pairs={{0,16},{4,20},{8,24},{12,28},{16,0},{20,4},{24,8},{28,12},{1,17},{... | collective-permute-start | bytes 294920 | tf_op jit(solution)/shard_map/ppermute | solution.py:88
  87.7 6.6 %collective-permute-start.22 = (bf16[2,192,128]{2,1,0:T(8,128)(2,1)S(1)}, bf16[2,192,128]{2,1,0:T(8,128)(2,1)S(1)}, u32[]{:S(2)}, u32[]{:S(2)}) collective-permute-start(bf16[2,192,128]{2,1,0:T(8,128)(2,1)S(1)} %get-tuple-element.68), channel_id=1, source_target_pairs={{0,24},{4,28},{8,16},{12,20},{16,8},{20,12},{24,0},{28,4},{1,25},{... | collective-permute-start | bytes 294920 | tf_op jit(solution)/shard_map/ppermute | solution.py:88
  90.4 5.8 %collective-permute-start.32 = (bf16[2,192,128]{2,1,0:T(8,128)(2,1)S(1)}, bf16[2,192,128]{2,1,0:T(8,128)(2,1)S(1)}, u32[]{:S(2)}, u32[]{:S(2)}) collective-permute-start(bf16[2,192,128]{2,1,0:T(8,128)(2,1)S(1)} %get-tuple-element.76), channel_id=1, source_target_pairs={{0,8},{4,12},{8,0},{12,4},{16,24},{20,28},{24,16},{28,20},{1,9},{5... | collective-permute-start | bytes 294920 | tf_op jit(solution)/shard_map/ppermute | solution.py:88
  91.1 5.7 %collective-permute-start.33 = (bf16[2,192,128]{2,1,0:T(8,128)(2,1)S(1)}, bf16[2,192,128]{2,1,0:T(8,128)(2,1)S(1)}, u32[]{:S(2)}, u32[]{:S(2)}) collective-permute-start(bf16[2,192,128]{2,1,0:T(8,128)(2,1)S(1)} %get-tuple-element.77), channel_id=1, source_target_pairs={{0,16},{4,20},{8,24},{12,28},{16,0},{20,4},{24,8},{28,12},{1,17},{... | collective-permute-start | bytes 294920 | tf_op jit(solution)/shard_map/ppermute | solution.py:88
  92.1 5.9 %collective-permute-start.34 = (bf16[2,192,128]{2,1,0:T(8,128)(2,1)S(1)}, bf16[2,192,128]{2,1,0:T(8,128)(2,1)S(1)}, u32[]{:S(2)}, u32[]{:S(2)}) collective-permute-start(bf16[2,192,128]{2,1,0:T(8,128)(2,1)S(1)} %get-tuple-element.78), channel_id=1, source_target_pairs={{0,24},{4,28},{8,16},{12,20},{16,8},{20,12},{24,0},{28,4},{1,25},{... | collective-permute-start | bytes 294920 | tf_op jit(solution)/shard_map/ppermute | solution.py:88

commit v6 on v5

--- a/solution.py
+++ b/solution.py
@@ -438,19 +438,19 @@
     across = partner(part, "dp", 2)
     hidden = [part, partner(part, "dp", 1), across, partner(across, "dp", 1)]
     planes = experts // CORES
-    sets = (0, 2), (1, 3)
-    landed = []
-    for flips in sets:
+    kept = {}
+    for flips in ((0, 3), (1, 2)):
         tiles = update_tiles([hidden[k] for k in flips], flips, scaled, state, planes)
         tiles = [tiles[0]] + [
             partner(tiles[k], "expert", k * CORES) for k in range(1, planes)
         ]
-        split = regroup(tiles)
-        kept = [
-            partner(x, "dp", k) if k else x for k, x in zip(flips, split, strict=True)
-        ]
-        swapped = [partner(x, "expert", 1) for x in kept]
-        picked = pick(placement, kept, swapped)
+        for k, x in zip(flips, regroup(tiles), strict=True):
+            kept[k] = partner(x, "dp", k) if k else x
+    swapped = {k: partner(x, "expert", 1) for k, x in kept.items()}
+    sets = ((1, 0), (3, 2))
+    landed = []
+    for flips in sets:
+        picked = pick(placement, [kept[k] for k in flips], [swapped[k] for k in flips])
         landed += [picked[0]] + [
             partner(picked[k], "expert", k * CORES) for k in range(1, planes)
         ]

time: 99.3 us -> 98.1 us (0.988)
  waiting for transfers between devices: 43.3 us -> 41.8 us
    ppermute x35, waiting for transfers between devices: 43.3 us -> 41.8 us  [partner(): return lax.ppermute(x, axis, [(i, i ^ flip) for i in range(size)])]
where the time goes in v6:
time: 98.1 us; the launch traced here: 97.8 us
  starting transfers between devices  42.6 us (43%)
  waiting for transfers between devices  41.8 us (43%)
  Pallas kernels  10.7 us (11%)
  local copies, waits for them, and re-layouts  2.56 us (3%)
    ppermute x35, starting transfers between devices, partner(): return lax.ppermute(x, axis, [(i, i ^ flip) for i in range(size)])  42.6 us
    ppermute x35, waiting for transfers between devices, partner(): return lax.ppermute(x, axis, [(i, i ^ flip) for i in range(size)])  41.8 us
    unnamed x12, local copies, waits for them, and re-layouts  2.56 us
    pallas_call x1, Pallas kernels, start_hidden(): pl.pallas_call(functools.partial(start_kernel, len(pieces), flips), out_s...  2.23 us
  transfers between devices with their start and end apart: 35, of which 18 were waited for; matrix products, arithmetic and copies ran while one was open for 0% of the time, Pallas kernels for 8%

profile of v6, /device:TPU:0, one launch (start us, length us, event | category | flops | bytes accessed | tf_op | source)
XLA Modules:
  0.0 97.8 jit_solution(16879304213235996189)
XLA Ops:
  0.0 1.0 pack_rows.1
  1.0 3.1 %collective-permute-start = (bf16[16,2688]{1,0:T(8,128)(2,1)S(1)}, bf16[16,2688]{1,0:T(8,128)(2,1)S(1)}, u32[]{:S(2)}, u32[]{:S(2)}) collective-permute-start(bf16[16,2688]{1,0:T(8,128)(2,1)S(1)} %get-tuple-element.45), channel_id=1, source_target_pairs={{0,1},{1,0},{2,3},{3,2},{4,5},{5,4},{6,7},{7,6},{8,9},{9,8},{10,11... | collective-permute-start | bytes 258056 | tf_op jit(solution)/shard_map/ppermute | solution.py:88
  4.0 2.6 %collective-permute-start.1 = (bf16[16,2688]{1,0:T(8,128)(2,1)S(1)}, bf16[16,2688]{1,0:T(8,128)(2,1)S(1)}, u32[]{:S(2)}, u32[]{:S(2)}) collective-permute-start(bf16[16,2688]{1,0:T(8,128)(2,1)S(1)} %get-tuple-element.46), channel_id=1, source_target_pairs={{0,2},{1,3},{2,0},{3,1},{4,6},{5,7},{6,4},{7,5},{8,10},{9,11},{10,... | collective-permute-start | bytes 258056 | tf_op jit(solution)/shard_map/ppermute | solution.py:88
  6.6 1.4 %copy-done = bf16[1,512,1536]{2,1,0:T(8,128)(2,1)S(1)} copy-done((bf16[1,512,1536]{2,1,0:T(8,128)(2,1)S(1)}, bf16[1,512,1536]{2,1,0:T(8,128)(2,1)}, u32[]{:S(2)}) %copy-start) | copy-done | bytes 1572888
  8.0 1.4 %pack_weights.1 = (bf16[512,384]{1,0:T(8,128)(2,1)S(1)}, bf16[512,384]{1,0:T(8,128)(2,1)S(1)}, bf16[512,384]{1,0:T(8,128)(2,1)}, bf16[512,384]{1,0:T(8,128)(2,1)S(1)}) custom-call(bf16[512,1536]{1,0:T(8,128)(2,1)S(1)} %bitcast.14), custom_call_target="tpu_custom_call" | custom-call | tf_op jit(solution)/shard_map/pack_weights/pallas_call | solution.py:166
  9.5 1.9 %collective-permute-start.10 = (bf16[512,384]{1,0:T(8,128)(2,1)}, bf16[512,384]{1,0:T(8,128)(2,1)}, u32[]{:S(2)}, u32[]{:S(2)}) collective-permute-start(bf16[512,384]{1,0:T(8,128)(2,1)} %get-tuple-element.50), channel_id=1, source_target_pairs={{0,2},{1,3},{2,0},{3,1},{4,6},{5,7},{6,4},{7,5},{8,10},{9,11},{10,... | collective-permute-start | bytes 1179656 | tf_op jit(solution)/shard_map/ppermute | solution.py:88
  11.4 1.1 %copy-done.3 = bf16[1,512,768]{2,1,0:T(8,128)(2,1)S(1)} copy-done((bf16[1,512,768]{2,1,0:T(8,128)(2,1)S(1)}, bf16[1,512,768]{2,1,0:T(8,128)(2,1)}, u32[]{:S(2)}) %copy-start.3) | copy-done | bytes 786456
  12.5 0.7 transposed.1
  13.2 8.9 %collective-permute-done.1.refs_2_ = bf16[16,2688]{1,0:T(8,128)(2,1)S(1)} collective-permute-done((bf16[16,2688]{1,0:T(8,128)(2,1)S(1)}, bf16[16,2688]{1,0:T(8,128)(2,1)S(1)}, u32[]{:S(2)}, u32[]{:S(2)}) %collective-permute-start.1) | collective-permute-done | bytes 86048 | tf_op jit(solution)/shard_map/ppermute | solution.py:88
  22.1 1.6 %collective-permute-start.3 = (bf16[64,2688]{1,0:T(8,128)(2,1)S(1)}, bf16[64,2688]{1,0:T(8,128)(2,1)S(1)}, u32[]{:S(2)}, u32[]{:S(2)}) collective-permute-start(bf16[64,2688]{1,0:T(8,128)(2,1)S(1)} %bitcast.8), channel_id=1, source_target_pairs={{0,8},{4,12},{8,0},{12,4},{16,24},{20,28},{24,16},{28,20},{1,9},{5... | collective-permute-start | bytes 1032200 | tf_op jit(solution)/shard_map/ppermute | solution.py:88
  23.7 1.5 %collective-permute-start.5 = (bf16[64,2688]{1,0:T(8,128)(2,1)S(1)}, bf16[64,2688]{1,0:T(8,128)(2,1)S(1)}, u32[]{:S(2)}, u32[]{:S(2)}) collective-permute-start(bf16[64,2688]{1,0:T(8,128)(2,1)S(1)} %bitcast.9), channel_id=1, source_target_pairs={{0,24},{4,28},{8,16},{12,20},{16,8},{20,12},{24,0},{28,4},{1,25},{... | collective-permute-start | bytes 1032200 | tf_op jit(solution)/shard_map/ppermute | solution.py:88
  25.7 3.8 %collective-permute-done.3.refs_1_ = bf16[64,2688]{1,0:T(8,128)(2,1)S(1)} collective-permute-done((bf16[64,2688]{1,0:T(8,128)(2,1)S(1)}, bf16[64,2688]{1,0:T(8,128)(2,1)S(1)}, u32[]{:S(2)}, u32[]{:S(2)}) %collective-permute-start.3) | collective-permute-done | bytes 344096 | tf_op jit(solution)/shard_map/ppermute | solution.py:88
  29.4 6.1 %collective-permute-start.11 = (bf16[512,384]{1,0:T(8,128)(2,1)}, bf16[512,384]{1,0:T(8,128)(2,1)S(1)}, u32[]{:S(2)}, u32[]{:S(2)}) collective-permute-start(bf16[512,384]{1,0:T(8,128)(2,1)} %copy-done.5), channel_id=1, source_target_pairs={{0,1},{1,0},{2,3},{3,2},{4,5},{5,4},{6,7},{7,6},{8,9},{9,8},{10,11... | collective-permute-start | bytes 1179656 | tf_op jit(solution)/shard_map/ppermute | solution.py:88
  35.6 2.6 %collective-permute-start.12 = (bf16[512,384]{1,0:T(8,128)(2,1)}, bf16[512,384]{1,0:T(8,128)(2,1)S(1)}, u32[]{:S(2)}, u32[]{:S(2)}) collective-permute-start(bf16[512,384]{1,0:T(8,128)(2,1)} %copy-done.4), channel_id=1, source_target_pairs={{0,3},{1,2},{2,1},{3,0},{4,7},{5,6},{6,5},{7,4},{8,11},{9,10},{10,... | collective-permute-start | bytes 1179656 | tf_op jit(solution)/shard_map/ppermute | solution.py:88
  38.8 1.1 %collective-permute-done.9.refs_7_ = bf16[64,2688]{1,0:T(8,128)(2,1)S(1)} collective-permute-done((bf16[64,2688]{1,0:T(8,128)(2,1)S(1)}, bf16[64,2688]{1,0:T(8,128)(2,1)S(1)}, u32[]{:S(2)}, u32[]{:S(2)}) %collective-permute-start.9) | collective-permute-done | bytes 344096 | tf_op jit(solution)/shard_map/ppermute | solution.py:88
  40.8 3.9 %collective-permute-done.11.refs_10_ = bf16[512,384]{1,0:T(8,128)(2,1)S(1)} collective-permute-done((bf16[512,384]{1,0:T(8,128)(2,1)}, bf16[512,384]{1,0:T(8,128)(2,1)S(1)}, u32[]{:S(2)}, u32[]{:S(2)}) %collective-permute-start.11) | collective-permute-done | bytes 393248 | tf_op jit(solution)/shard_map/ppermute | solution.py:88
  44.7 2.2 %start_hidden.1 = (f32[512,384]{1,0:T(8,128)S(1)}, bf16[512,512]{1,0:T(8,128)(2,1)S(1)}) custom-call(bf16[64,2688]{1,0:T(8,128)(2,1)S(1)} %bitcast.12, bf16[64,2688]{1,0:T(8,128)(2,1)S(1)} %collective-permute-done.3.refs_1_, bf16[64,2688]{1,0:T(8,128)(2,1)S(1)} %collective-permute-done.4.refs_2_, bf16[64,2688]{1,0:T(8,128)(2,1)S(1)} %collective-permute-done.5.refs_3_, ...), custom_call_target="tpu_custom_call" | custom-call | tf_op jit(solution)/shard_map/start_hidden/pallas_call | solution.py:229
  47.0 2.0 %collective-permute-done.12.refs_0_ = bf16[512,384]{1,0:T(8,128)(2,1)S(1)} collective-permute-done((bf16[512,384]{1,0:T(8,128)(2,1)}, bf16[512,384]{1,0:T(8,128)(2,1)S(1)}, u32[]{:S(2)}, u32[]{:S(2)}) %collective-permute-start.12) | collective-permute-done | bytes 393248 | tf_op jit(solution)/shard_map/ppermute | solution.py:88
  49.8 2.9 %collective-permute-start.13 = (bf16[192,512]{1,0:T(8,128)(2,1)S(1)}, bf16[192,512]{1,0:T(8,128)(2,1)S(1)}, u32[]{:S(2)}, u32[]{:S(2)}) collective-permute-start(bf16[192,512]{1,0:T(8,128)(2,1)S(1)} %end_hidden.1.refs_0_), channel_id=1, source_target_pairs={{0,1},{1,0},{2,3},{3,2},{4,5},{5,4},{6,7},{7,6},{8,9},{9,8},{10,11... | collective-permute-start | bytes 589832 | tf_op jit(solution)/shard_map/ppermute | solution.py:88
  52.6 5.9 %collective-permute-done.14.refs_1_ = bf16[192,512]{1,0:T(8,128)(2,1)S(1)} collective-permute-done((bf16[192,512]{1,0:T(8,128)(2,1)S(1)}, bf16[192,512]{1,0:T(8,128)(2,1)S(1)}, u32[]{:S(2)}, u32[]{:S(2)}) %collective-permute-start.14) | collective-permute-done | bytes 196640 | tf_op jit(solution)/shard_map/ppermute | solution.py:88
  58.7 0.9 collective-permute-done.13.refs_0_
  59.6 0.9 update_tiles.2
  60.6 1.6 %collective-permute-start.15 = (bf16[2,192,128]{2,1,0:T(8,128)(2,1)S(1)}, bf16[2,192,128]{2,1,0:T(8,128)(2,1)S(1)}, u32[]{:S(2)}, u32[]{:S(2)}) collective-permute-start(bf16[2,192,128]{2,1,0:T(8,128)(2,1)S(1)} %get-tuple-element.60), channel_id=1, source_target_pairs={{0,8},{4,12},{8,0},{12,4},{16,24},{20,28},{24,16},{28,20},{1,9},{5... | collective-permute-start | bytes 294920 | tf_op jit(solution)/shard_map/ppermute | solution.py:88
  62.1 1.0 %collective-permute-start.16 = (bf16[2,192,128]{2,1,0:T(8,128)(2,1)S(1)}, bf16[2,192,128]{2,1,0:T(8,128)(2,1)S(1)}, u32[]{:S(2)}, u32[]{:S(2)}) collective-permute-start(bf16[2,192,128]{2,1,0:T(8,128)(2,1)S(1)} %get-tuple-element.61), channel_id=1, source_target_pairs={{0,16},{4,20},{8,24},{12,28},{16,0},{20,4},{24,8},{28,12},{1,17},{... | collective-permute-start | bytes 294920 | tf_op jit(solution)/shard_map/ppermute | solution.py:88
  63.1 1.0 %collective-permute-start.17 = (bf16[2,192,128]{2,1,0:T(8,128)(2,1)S(1)}, bf16[2,192,128]{2,1,0:T(8,128)(2,1)S(1)}, u32[]{:S(2)}, u32[]{:S(2)}) collective-permute-start(bf16[2,192,128]{2,1,0:T(8,128)(2,1)S(1)} %get-tuple-element.62), channel_id=1, source_target_pairs={{0,24},{4,28},{8,16},{12,20},{16,8},{20,12},{24,0},{28,4},{1,25},{... | collective-permute-start | bytes 294920 | tf_op jit(solution)/shard_map/ppermute | solution.py:88
  64.2 0.9 update_tiles.3
  65.1 1.6 %collective-permute-start.20 = (bf16[2,192,128]{2,1,0:T(8,128)(2,1)S(1)}, bf16[2,192,128]{2,1,0:T(8,128)(2,1)S(1)}, u32[]{:S(2)}, u32[]{:S(2)}) collective-permute-start(bf16[2,192,128]{2,1,0:T(8,128)(2,1)S(1)} %get-tuple-element.65), channel_id=1, source_target_pairs={{0,8},{4,12},{8,0},{12,4},{16,24},{20,28},{24,16},{28,20},{1,9},{5... | collective-permute-start | bytes 294920 | tf_op jit(solution)/shard_map/ppermute | solution.py:88
  66.7 1.5 %collective-permute-start.21 = (bf16[2,192,128]{2,1,0:T(8,128)(2,1)S(1)}, bf16[2,192,128]{2,1,0:T(8,128)(2,1)S(1)}, u32[]{:S(2)}, u32[]{:S(2)}) collective-permute-start(bf16[2,192,128]{2,1,0:T(8,128)(2,1)S(1)} %get-tuple-element.66), channel_id=1, source_target_pairs={{0,16},{4,20},{8,24},{12,28},{16,0},{20,4},{24,8},{28,12},{1,17},{... | collective-permute-start | bytes 294920 | tf_op jit(solution)/shard_map/ppermute | solution.py:88
  68.7 0.7 collective-permute-done.17.refs_3_
  69.4 1.2 %collective-permute-start.18 = (bf16[4,192,128]{2,1,0:T(8,128)(2,1)S(1)}, bf16[4,192,128]{2,1,0:T(8,128)(2,1)S(1)}, u32[]{:S(2)}, u32[]{:S(2)}) collective-permute-start(bf16[4,192,128]{2,1,0:T(8,128)(2,1)S(1)} %get-tuple-element.63), channel_id=1, source_target_pairs={{0,1},{1,0},{2,3},{3,2},{4,5},{5,4},{6,7},{7,6},{8,9},{9,8},{10,11... | collective-permute-start | bytes 589832 | tf_op jit(solution)/shard_map/ppermute | solution.py:88
  70.6 1.6 %collective-permute-start.29 = (bf16[4,192,128]{2,1,0:T(8,128)(2,1)S(1)}, bf16[4,192,128]{2,1,0:T(8,128)(2,1)S(1)}, u32[]{:S(2)}, u32[]{:S(2)}) collective-permute-start(bf16[4,192,128]{2,1,0:T(8,128)(2,1)S(1)} %get-tuple-element.74), channel_id=1, source_target_pairs={{0,2},{1,3},{2,0},{3,1},{4,6},{5,7},{6,4},{7,5},{8,10},{9,11},{10,... | collective-permute-start | bytes 589832 | tf_op jit(solution)/shard_map/ppermute | solution.py:88
  72.2 1.5 %collective-permute-done.22.refs_3_ = bf16[2,192,128]{2,1,0:T(8,128)(2,1)S(1)} collective-permute-done((bf16[2,192,128]{2,1,0:T(8,128)(2,1)S(1)}, bf16[2,192,128]{2,1,0:T(8,128)(2,1)S(1)}, u32[]{:S(2)}, u32[]{:S(2)}) %collective-permute-start.22) | collective-permute-done | bytes 98336 | tf_op jit(solution)/shard_map/ppermute | solution.py:88
  73.8 1.7 %collective-permute-start.28 = (bf16[4,192,128]{2,1,0:T(8,128)(2,1)S(1)}, bf16[4,192,128]{2,1,0:T(8,128)(2,1)S(1)}, u32[]{:S(2)}, u32[]{:S(2)}) collective-permute-start(bf16[4,192,128]{2,1,0:T(8,128)(2,1)S(1)} %get-tuple-element.73), channel_id=1, source_target_pairs={{0,3},{1,2},{2,1},{3,0},{4,7},{5,6},{6,5},{7,4},{8,11},{9,10},{10,... | collective-permute-start | bytes 589832 | tf_op jit(solution)/shard_map/ppermute | solution.py:88
  75.5 3.1 %collective-permute-done.18.refs_0_ = bf16[4,192,128]{2,1,0:T(8,128)(2,1)S(1)} collective-permute-done((bf16[4,192,128]{2,1,0:T(8,128)(2,1)S(1)}, bf16[4,192,128]{2,1,0:T(8,128)(2,1)S(1)}, u32[]{:S(2)}, u32[]{:S(2)}) %collective-permute-start.18) | collective-permute-done | bytes 196640 | tf_op jit(solution)/shard_map/ppermute | solution.py:88
  78.6 4.3 %collective-permute-done.29.refs_1_ = bf16[4,192,128]{2,1,0:T(8,128)(2,1)S(1)} collective-permute-done((bf16[4,192,128]{2,1,0:T(8,128)(2,1)S(1)}, bf16[4,192,128]{2,1,0:T(8,128)(2,1)S(1)}, u32[]{:S(2)}, u32[]{:S(2)}) %collective-permute-start.29) | collective-permute-done | bytes 196640 | tf_op jit(solution)/shard_map/ppermute | solution.py:88
  83.4 0.8 pick.2
  84.2 1.5 %collective-permute-start.25 = (bf16[2,192,128]{2,1,0:T(8,128)(2,1)S(1)}, bf16[2,192,128]{2,1,0:T(8,128)(2,1)S(1)}, u32[]{:S(2)}, u32[]{:S(2)}) collective-permute-start(bf16[2,192,128]{2,1,0:T(8,128)(2,1)S(1)} %get-tuple-element.70), channel_id=1, source_target_pairs={{0,8},{4,12},{8,0},{12,4},{16,24},{20,28},{24,16},{28,20},{1,9},{5... | collective-permute-start | bytes 294920 | tf_op jit(solution)/shard_map/ppermute | solution.py:88
  85.7 1.1 %collective-permute-start.26 = (bf16[2,192,128]{2,1,0:T(8,128)(2,1)S(1)}, bf16[2,192,128]{2,1,0:T(8,128)(2,1)S(1)}, u32[]{:S(2)}, u32[]{:S(2)}) collective-permute-start(bf16[2,192,128]{2,1,0:T(8,128)(2,1)S(1)} %get-tuple-element.71), channel_id=1, source_target_pairs={{0,16},{4,20},{8,24},{12,28},{16,0},{20,4},{24,8},{28,12},{1,17},{... | collective-permute-start | bytes 294920 | tf_op jit(solution)/shard_map/ppermute | solution.py:88
  86.8 0.9 collective-permute-start.27
  87.8 0.8 pick.3
  88.5 1.5 %collective-permute-start.32 = (bf16[2,192,128]{2,1,0:T(8,128)(2,1)S(1)}, bf16[2,192,128]{2,1,0:T(8,128)(2,1)S(1)}, u32[]{:S(2)}, u32[]{:S(2)}) collective-permute-start(bf16[2,192,128]{2,1,0:T(8,128)(2,1)S(1)} %get-tuple-element.76), channel_id=1, source_target_pairs={{0,8},{4,12},{8,0},{12,4},{16,24},{20,28},{24,16},{28,20},{1,9},{5... | collective-permute-start | bytes 294920 | tf_op jit(solution)/shard_map/ppermute | solution.py:88
  90.1 1.1 %collective-permute-start.33 = (bf16[2,192,128]{2,1,0:T(8,128)(2,1)S(1)}, bf16[2,192,128]{2,1,0:T(8,128)(2,1)S(1)}, u32[]{:S(2)}, u32[]{:S(2)}) collective-permute-start(bf16[2,192,128]{2,1,0:T(8,128)(2,1)S(1)} %get-tuple-element.77), channel_id=1, source_target_pairs={{0,16},{4,20},{8,24},{12,28},{16,0},{20,4},{24,8},{28,12},{1,17},{... | collective-permute-start | bytes 294920 | tf_op jit(solution)/shard_map/ppermute | solution.py:88
  91.2 0.9 collective-permute-start.34
  92.1 1.1 %collective-permute-done.27.refs_3_ = bf16[2,192,128]{2,1,0:T(8,128)(2,1)S(1)} collective-permute-done((bf16[2,192,128]{2,1,0:T(8,128)(2,1)S(1)}, bf16[2,192,128]{2,1,0:T(8,128)(2,1)S(1)}, u32[]{:S(2)}, u32[]{:S(2)}) %collective-permute-start.27) | collective-permute-done | bytes 98336 | tf_op jit(solution)/shard_map/ppermute | solution.py:88
  93.2 1.0 %collective-permute-done.32.refs_5_ = bf16[2,192,128]{2,1,0:T(8,128)(2,1)S(1)} collective-permute-done((bf16[2,192,128]{2,1,0:T(8,128)(2,1)S(1)}, bf16[2,192,128]{2,1,0:T(8,128)(2,1)S(1)}, u32[]{:S(2)}, u32[]{:S(2)}) %collective-permute-start.32) | collective-permute-done | bytes 98336 | tf_op jit(solution)/shard_map/ppermute | solution.py:88
  94.2 1.4 %collective-permute-done.33.refs_6_ = bf16[2,192,128]{2,1,0:T(8,128)(2,1)S(1)} collective-permute-done((bf16[2,192,128]{2,1,0:T(8,128)(2,1)S(1)}, bf16[2,192,128]{2,1,0:T(8,128)(2,1)S(1)}, u32[]{:S(2)}, u32[]{:S(2)}) %collective-permute-start.33) | collective-permute-done | bytes 98336 | tf_op jit(solution)/shard_map/ppermute | solution.py:88
  95.6 1.1 %collective-permute-done.34.refs_7_ = bf16[2,192,128]{2,1,0:T(8,128)(2,1)S(1)} collective-permute-done((bf16[2,192,128]{2,1,0:T(8,128)(2,1)S(1)}, bf16[2,192,128]{2,1,0:T(8,128)(2,1)S(1)}, u32[]{:S(2)}, u32[]{:S(2)}) %collective-permute-start.34) | collective-permute-done | bytes 98336 | tf_op jit(solution)/shard_map/ppermute | solution.py:88
  96.7 1.1 %unpack.1 = bf16[1,192,2048]{2,1,0:T(8,128)(2,1)} custom-call(bf16[2,192,128]{2,1,0:T(8,128)(2,1)S(1)} %get-tuple-element.69.refs_0_, bf16[2,192,128]{2,1,0:T(8,128)(2,1)S(1)} %collective-permute-done.25.refs_1_, bf16[2,192,128]{2,1,0:T(8,128)(2,1)S(1)} %collective-permute-done.26.refs_2_, bf16[2,192,128]{2,1,0:T(8,128)(2,1)S(1)} %collective-permute-done.27.refs_3_, ...), custom_call_target="tpu_custom_call" | custom-call | tf_op jit(solution)/shard_map/unpack/pallas_call | solution.py:407
  (48 shorter events, 4.2 us)
Async XLA Ops:
  1.0 8.5 %collective-permute-start = (bf16[16,2688]{1,0:T(8,128)(2,1)S(1)}, bf16[16,2688]{1,0:T(8,128)(2,1)S(1)}, u32[]{:S(2)}, u32[]{:S(2)}) collective-permute-start(bf16[16,2688]{1,0:T(8,128)(2,1)S(1)} %get-tuple-element.45), channel_id=1, source_target_pairs={{0,1},{1,0},{2,3},{3,2},{4,5},{5,4},{6,7},{7,6},{8,9},{9,8},{10,11... | collective-permute-start | bytes 258056 | tf_op jit(solution)/shard_map/ppermute | solution.py:88
  4.0 18.0 %collective-permute-start.1 = (bf16[16,2688]{1,0:T(8,128)(2,1)S(1)}, bf16[16,2688]{1,0:T(8,128)(2,1)S(1)}, u32[]{:S(2)}, u32[]{:S(2)}) collective-permute-start(bf16[16,2688]{1,0:T(8,128)(2,1)S(1)} %get-tuple-element.46), channel_id=1, source_target_pairs={{0,2},{1,3},{2,0},{3,1},{4,6},{5,7},{6,4},{7,5},{8,10},{9,11},{10,... | collective-permute-start | bytes 258056 | tf_op jit(solution)/shard_map/ppermute | solution.py:88
  6.6 15.4 %collective-permute-start.2 = (bf16[16,2688]{1,0:T(8,128)(2,1)S(1)}, bf16[16,2688]{1,0:T(8,128)(2,1)S(1)}, u32[]{:S(2)}, u32[]{:S(2)}) collective-permute-start(bf16[16,2688]{1,0:T(8,128)(2,1)S(1)} %get-tuple-element.47), channel_id=1, source_target_pairs={{0,3},{1,2},{2,1},{3,0},{4,7},{5,6},{6,5},{7,4},{8,11},{9,10},{10,... | collective-permute-start | bytes 258056 | tf_op jit(solution)/shard_map/ppermute | solution.py:88
  6.6 1.4 %copy-start = (bf16[1,512,1536]{2,1,0:T(8,128)(2,1)S(1)}, bf16[1,512,1536]{2,1,0:T(8,128)(2,1)}, u32[]{:S(2)}) copy-start(bf16[1,512,1536]{2,1,0:T(8,128)(2,1)} %param.13) | copy-start | bytes 4718596
  8.0 3.3 %copy-start.1 = (bf16[1,512,768]{2,1,0:T(8,128)(2,1)S(1)}, bf16[1,512,768]{2,1,0:T(8,128)(2,1)}, u32[]{:S(2)}) copy-start(bf16[1,512,768]{2,1,0:T(8,128)(2,1)} %param.14) | copy-start | bytes 2359300
  8.0 3.3 %copy-start.2 = (bf16[1,512,768]{2,1,0:T(8,128)(2,1)S(1)}, bf16[1,512,768]{2,1,0:T(8,128)(2,1)}, u32[]{:S(2)}) copy-start(bf16[1,512,768]{2,1,0:T(8,128)(2,1)} %param.15) | copy-start | bytes 2359300
  9.4 12.6 %copy-start.4 = (bf16[512,384]{1,0:T(8,128)(2,1)}, bf16[512,384]{1,0:T(8,128)(2,1)S(1)}, u32[]{:S(2)}) copy-start(bf16[512,384]{1,0:T(8,128)(2,1)S(1)} %get-tuple-element.56) | copy-start | bytes 1179652
  9.4 12.6 %copy-start.5 = (bf16[512,384]{1,0:T(8,128)(2,1)}, bf16[512,384]{1,0:T(8,128)(2,1)S(1)}, u32[]{:S(2)}) copy-start(bf16[512,384]{1,0:T(8,128)(2,1)S(1)} %get-tuple-element.52) | copy-start | bytes 1179652
  9.5 26.1 %collective-permute-start.10 = (bf16[512,384]{1,0:T(8,128)(2,1)}, bf16[512,384]{1,0:T(8,128)(2,1)}, u32[]{:S(2)}, u32[]{:S(2)}) collective-permute-start(bf16[512,384]{1,0:T(8,128)(2,1)} %get-tuple-element.50), channel_id=1, source_target_pairs={{0,2},{1,3},{2,0},{3,1},{4,6},{5,7},{6,4},{7,5},{8,10},{9,11},{10,... | collective-permute-start | bytes 1179656 | tf_op jit(solution)/shard_map/ppermute | solution.py:88
  11.4 1.1 %copy-start.3 = (bf16[1,512,768]{2,1,0:T(8,128)(2,1)S(1)}, bf16[1,512,768]{2,1,0:T(8,128)(2,1)}, u32[]{:S(2)}) copy-start(bf16[1,512,768]{2,1,0:T(8,128)(2,1)} %param.16) | copy-start | bytes 2359300
  22.1 7.3 %collective-permute-start.3 = (bf16[64,2688]{1,0:T(8,128)(2,1)S(1)}, bf16[64,2688]{1,0:T(8,128)(2,1)S(1)}, u32[]{:S(2)}, u32[]{:S(2)}) collective-permute-start(bf16[64,2688]{1,0:T(8,128)(2,1)S(1)} %bitcast.8), channel_id=1, source_target_pairs={{0,8},{4,12},{8,0},{12,4},{16,24},{20,28},{24,16},{28,20},{1,9},{5... | collective-permute-start | bytes 1032200 | tf_op jit(solution)/shard_map/ppermute | solution.py:88
  23.7 14.5 %collective-permute-start.5 = (bf16[64,2688]{1,0:T(8,128)(2,1)S(1)}, bf16[64,2688]{1,0:T(8,128)(2,1)S(1)}, u32[]{:S(2)}, u32[]{:S(2)}) collective-permute-start(bf16[64,2688]{1,0:T(8,128)(2,1)S(1)} %bitcast.9), channel_id=1, source_target_pairs={{0,24},{4,28},{8,16},{12,20},{16,8},{20,12},{24,0},{28,4},{1,25},{... | collective-permute-start | bytes 1032200 | tf_op jit(solution)/shard_map/ppermute | solution.py:88
  25.2 13.0 %collective-permute-start.4 = (bf16[64,2688]{1,0:T(8,128)(2,1)S(1)}, bf16[64,2688]{1,0:T(8,128)(2,1)S(1)}, u32[]{:S(2)}, u32[]{:S(2)}) collective-permute-start(bf16[64,2688]{1,0:T(8,128)(2,1)S(1)} %bitcast.10), channel_id=1, source_target_pairs={{0,16},{4,20},{8,24},{12,28},{16,0},{20,4},{24,8},{28,12},{1,17},{... | collective-permute-start | bytes 1032200 | tf_op jit(solution)/shard_map/ppermute | solution.py:88
  25.7 13.0 %collective-permute-start.6 = (bf16[64,2688]{1,0:T(8,128)(2,1)S(1)}, bf16[64,2688]{1,0:T(8,128)(2,1)S(1)}, u32[]{:S(2)}, u32[]{:S(2)}) collective-permute-start(bf16[64,2688]{1,0:T(8,128)(2,1)S(1)} %bitcast.11), channel_id=1, source_target_pairs={{0,4},{4,0},{8,12},{12,8},{16,20},{20,16},{24,28},{28,24},{1,5},{5... | collective-permute-start | bytes 1032200 | tf_op jit(solution)/shard_map/ppermute | solution.py:88
  29.4 15.3 %collective-permute-start.11 = (bf16[512,384]{1,0:T(8,128)(2,1)}, bf16[512,384]{1,0:T(8,128)(2,1)S(1)}, u32[]{:S(2)}, u32[]{:S(2)}) collective-permute-start(bf16[512,384]{1,0:T(8,128)(2,1)} %copy-done.5), channel_id=1, source_target_pairs={{0,1},{1,0},{2,3},{3,2},{4,5},{5,4},{6,7},{7,6},{8,9},{9,8},{10,11... | collective-permute-start | bytes 1179656 | tf_op jit(solution)/shard_map/ppermute | solution.py:88
  35.6 13.4 %collective-permute-start.12 = (bf16[512,384]{1,0:T(8,128)(2,1)}, bf16[512,384]{1,0:T(8,128)(2,1)S(1)}, u32[]{:S(2)}, u32[]{:S(2)}) collective-permute-start(bf16[512,384]{1,0:T(8,128)(2,1)} %copy-done.4), channel_id=1, source_target_pairs={{0,3},{1,2},{2,1},{3,0},{4,7},{5,6},{6,5},{7,4},{8,11},{9,10},{10,... | collective-permute-start | bytes 1179656 | tf_op jit(solution)/shard_map/ppermute | solution.py:88
  38.2 1.7 %collective-permute-start.9 = (bf16[64,2688]{1,0:T(8,128)(2,1)S(1)}, bf16[64,2688]{1,0:T(8,128)(2,1)S(1)}, u32[]{:S(2)}, u32[]{:S(2)}) collective-permute-start(bf16[64,2688]{1,0:T(8,128)(2,1)S(1)} %collective-permute-done.5.refs_3_), channel_id=1, source_target_pairs={{0,4},{4,0},{8,12},{12,8},{16,20},{20,16},{24,28},{28,24},{1,5},{5... | collective-permute-start | bytes 1032200 | tf_op jit(solution)/shard_map/ppermute | solution.py:88
  38.2 2.1 %collective-permute-start.8 = (bf16[64,2688]{1,0:T(8,128)(2,1)S(1)}, bf16[64,2688]{1,0:T(8,128)(2,1)S(1)}, u32[]{:S(2)}, u32[]{:S(2)}) collective-permute-start(bf16[64,2688]{1,0:T(8,128)(2,1)S(1)} %collective-permute-done.4.refs_2_), channel_id=1, source_target_pairs={{0,4},{4,0},{8,12},{12,8},{16,20},{20,16},{24,28},{28,24},{1,5},{5... | collective-permute-start | bytes 1032200 | tf_op jit(solution)/shard_map/ppermute | solution.py:88
  38.7 2.1 %collective-permute-start.7 = (bf16[64,2688]{1,0:T(8,128)(2,1)S(1)}, bf16[64,2688]{1,0:T(8,128)(2,1)S(1)}, u32[]{:S(2)}, u32[]{:S(2)}) collective-permute-start(bf16[64,2688]{1,0:T(8,128)(2,1)S(1)} %collective-permute-done.3.refs_1_), channel_id=1, source_target_pairs={{0,4},{4,0},{8,12},{12,8},{16,20},{20,16},{24,28},{28,24},{1,5},{5... | collective-permute-start | bytes 1032200 | tf_op jit(solution)/shard_map/ppermute | solution.py:88
  49.7 8.8 %collective-permute-start.14 = (bf16[192,512]{1,0:T(8,128)(2,1)S(1)}, bf16[192,512]{1,0:T(8,128)(2,1)S(1)}, u32[]{:S(2)}, u32[]{:S(2)}) collective-permute-start(bf16[192,512]{1,0:T(8,128)(2,1)S(1)} %end_hidden.1.refs_0_), channel_id=1, source_target_pairs={{0,2},{1,3},{2,0},{3,1},{4,6},{5,7},{6,4},{7,5},{8,10},{9,11},{10,... | collective-permute-start | bytes 589832 | tf_op jit(solution)/shard_map/ppermute | solution.py:88
  49.8 9.9 %collective-permute-start.13 = (bf16[192,512]{1,0:T(8,128)(2,1)S(1)}, bf16[192,512]{1,0:T(8,128)(2,1)S(1)}, u32[]{:S(2)}, u32[]{:S(2)}) collective-permute-start(bf16[192,512]{1,0:T(8,128)(2,1)S(1)} %end_hidden.1.refs_0_), channel_id=1, source_target_pairs={{0,1},{1,0},{2,3},{3,2},{4,5},{5,4},{6,7},{7,6},{8,9},{9,8},{10,11... | collective-permute-start | bytes 589832 | tf_op jit(solution)/shard_map/ppermute | solution.py:88
  58.5 5.7 %collective-permute-start.19 = (bf16[192,512]{1,0:T(8,128)(2,1)S(1)}, bf16[192,512]{1,0:T(8,128)(2,1)S(1)}, u32[]{:S(2)}, u32[]{:S(2)}) collective-permute-start(bf16[192,512]{1,0:T(8,128)(2,1)S(1)} %collective-permute-done.14.refs_1_), channel_id=1, source_target_pairs={{0,1},{1,0},{2,3},{3,2},{4,5},{5,4},{6,7},{7,6},{8,9},{9,8},{10,11... | collective-permute-start | bytes 589832 | tf_op jit(solution)/shard_map/ppermute | solution.py:88
  60.6 7.6 %collective-permute-start.15 = (bf16[2,192,128]{2,1,0:T(8,128)(2,1)S(1)}, bf16[2,192,128]{2,1,0:T(8,128)(2,1)S(1)}, u32[]{:S(2)}, u32[]{:S(2)}) collective-permute-start(bf16[2,192,128]{2,1,0:T(8,128)(2,1)S(1)} %get-tuple-element.60), channel_id=1, source_target_pairs={{0,8},{4,12},{8,0},{12,4},{16,24},{20,28},{24,16},{28,20},{1,9},{5... | collective-permute-start | bytes 294920 | tf_op jit(solution)/shard_map/ppermute | solution.py:88
  62.1 6.6 %collective-permute-start.16 = (bf16[2,192,128]{2,1,0:T(8,128)(2,1)S(1)}, bf16[2,192,128]{2,1,0:T(8,128)(2,1)S(1)}, u32[]{:S(2)}, u32[]{:S(2)}) collective-permute-start(bf16[2,192,128]{2,1,0:T(8,128)(2,1)S(1)} %get-tuple-element.61), channel_id=1, source_target_pairs={{0,16},{4,20},{8,24},{12,28},{16,0},{20,4},{24,8},{28,12},{1,17},{... | collective-permute-start | bytes 294920 | tf_op jit(solution)/shard_map/ppermute | solution.py:88
  63.1 6.3 %collective-permute-start.17 = (bf16[2,192,128]{2,1,0:T(8,128)(2,1)S(1)}, bf16[2,192,128]{2,1,0:T(8,128)(2,1)S(1)}, u32[]{:S(2)}, u32[]{:S(2)}) collective-permute-start(bf16[2,192,128]{2,1,0:T(8,128)(2,1)S(1)} %get-tuple-element.62), channel_id=1, source_target_pairs={{0,24},{4,28},{8,16},{12,20},{16,8},{20,12},{24,0},{28,4},{1,25},{... | collective-permute-start | bytes 294920 | tf_op jit(solution)/shard_map/ppermute | solution.py:88
  65.1 7.0 %collective-permute-start.20 = (bf16[2,192,128]{2,1,0:T(8,128)(2,1)S(1)}, bf16[2,192,128]{2,1,0:T(8,128)(2,1)S(1)}, u32[]{:S(2)}, u32[]{:S(2)}) collective-permute-start(bf16[2,192,128]{2,1,0:T(8,128)(2,1)S(1)} %get-tuple-element.65), channel_id=1, source_target_pairs={{0,8},{4,12},{8,0},{12,4},{16,24},{20,28},{24,16},{28,20},{1,9},{5... | collective-permute-start | bytes 294920 | tf_op jit(solution)/shard_map/ppermute | solution.py:88
  66.7 5.5 %collective-permute-start.21 = (bf16[2,192,128]{2,1,0:T(8,128)(2,1)S(1)}, bf16[2,192,128]{2,1,0:T(8,128)(2,1)S(1)}, u32[]{:S(2)}, u32[]{:S(2)}) collective-permute-start(bf16[2,192,128]{2,1,0:T(8,128)(2,1)S(1)} %get-tuple-element.66), channel_id=1, source_target_pairs={{0,16},{4,20},{8,24},{12,28},{16,0},{20,4},{24,8},{28,12},{1,17},{... | collective-permute-start | bytes 294920 | tf_op jit(solution)/shard_map/ppermute | solution.py:88
  68.2 5.5 %collective-permute-start.22 = (bf16[2,192,128]{2,1,0:T(8,128)(2,1)S(1)}, bf16[2,192,128]{2,1,0:T(8,128)(2,1)S(1)}, u32[]{:S(2)}, u32[]{:S(2)}) collective-permute-start(bf16[2,192,128]{2,1,0:T(8,128)(2,1)S(1)} %get-tuple-element.67), channel_id=1, source_target_pairs={{0,24},{4,28},{8,16},{12,20},{16,8},{20,12},{24,0},{28,4},{1,25},{... | collective-permute-start | bytes 294920 | tf_op jit(solution)/shard_map/ppermute | solution.py:88
  69.4 9.2 %collective-permute-start.18 = (bf16[4,192,128]{2,1,0:T(8,128)(2,1)S(1)}, bf16[4,192,128]{2,1,0:T(8,128)(2,1)S(1)}, u32[]{:S(2)}, u32[]{:S(2)}) collective-permute-start(bf16[4,192,128]{2,1,0:T(8,128)(2,1)S(1)} %get-tuple-element.63), channel_id=1, source_target_pairs={{0,1},{1,0},{2,3},{3,2},{4,5},{5,4},{6,7},{7,6},{8,9},{9,8},{10,11... | collective-permute-start | bytes 589832 | tf_op jit(solution)/shard_map/ppermute | solution.py:88
  70.6 12.3 %collective-permute-start.29 = (bf16[4,192,128]{2,1,0:T(8,128)(2,1)S(1)}, bf16[4,192,128]{2,1,0:T(8,128)(2,1)S(1)}, u32[]{:S(2)}, u32[]{:S(2)}) collective-permute-start(bf16[4,192,128]{2,1,0:T(8,128)(2,1)S(1)} %get-tuple-element.74), channel_id=1, source_target_pairs={{0,2},{1,3},{2,0},{3,1},{4,6},{5,7},{6,4},{7,5},{8,10},{9,11},{10,... | collective-permute-start | bytes 589832 | tf_op jit(solution)/shard_map/ppermute | solution.py:88
  73.8 9.1 %collective-permute-start.28 = (bf16[4,192,128]{2,1,0:T(8,128)(2,1)S(1)}, bf16[4,192,128]{2,1,0:T(8,128)(2,1)S(1)}, u32[]{:S(2)}, u32[]{:S(2)}) collective-permute-start(bf16[4,192,128]{2,1,0:T(8,128)(2,1)S(1)} %get-tuple-element.73), channel_id=1, source_target_pairs={{0,3},{1,2},{2,1},{3,0},{4,7},{5,6},{6,5},{7,4},{8,11},{9,10},{10,... | collective-permute-start | bytes 589832 | tf_op jit(solution)/shard_map/ppermute | solution.py:88
  75.5 8.0 %collective-permute-start.24 = (bf16[4,192,128]{2,1,0:T(8,128)(2,1)S(1)}, bf16[4,192,128]{2,1,0:T(8,128)(2,1)S(1)}, u32[]{:S(2)}, u32[]{:S(2)}) collective-permute-start(bf16[4,192,128]{2,1,0:T(8,128)(2,1)S(1)} %get-tuple-element.68.refs_1_), channel_id=1, source_target_pairs={{0,4},{4,0},{8,12},{12,8},{16,20},{20,16},{24,28},{28,24},{1,5},{5... | collective-permute-start | bytes 589832 | tf_op jit(solution)/shard_map/ppermute | solution.py:88
  78.6 4.8 %collective-permute-start.23 = (bf16[4,192,128]{2,1,0:T(8,128)(2,1)S(1)}, bf16[4,192,128]{2,1,0:T(8,128)(2,1)S(1)}, u32[]{:S(2)}, u32[]{:S(2)}) collective-permute-start(bf16[4,192,128]{2,1,0:T(8,128)(2,1)S(1)} %collective-permute-done.18.refs_0_), channel_id=1, source_target_pairs={{0,4},{4,0},{8,12},{12,8},{16,20},{20,16},{24,28},{28,24},{1,5},{5... | collective-permute-start | bytes 589832 | tf_op jit(solution)/shard_map/ppermute | solution.py:88
  82.9 4.9 %collective-permute-start.31 = (bf16[4,192,128]{2,1,0:T(8,128)(2,1)S(1)}, bf16[4,192,128]{2,1,0:T(8,128)(2,1)S(1)}, u32[]{:S(2)}, u32[]{:S(2)}) collective-permute-start(bf16[4,192,128]{2,1,0:T(8,128)(2,1)S(1)} %collective-permute-done.29.refs_1_), channel_id=1, source_target_pairs={{0,4},{4,0},{8,12},{12,8},{16,20},{20,16},{24,28},{28,24},{1,5},{5... | collective-permute-start | bytes 589832 | tf_op jit(solution)/shard_map/ppermute | solution.py:88
  82.9 4.8 %collective-permute-start.30 = (bf16[4,192,128]{2,1,0:T(8,128)(2,1)S(1)}, bf16[4,192,128]{2,1,0:T(8,128)(2,1)S(1)}, u32[]{:S(2)}, u32[]{:S(2)}) collective-permute-start(bf16[4,192,128]{2,1,0:T(8,128)(2,1)S(1)} %collective-permute-done.28.refs_0_), channel_id=1, source_target_pairs={{0,4},{4,0},{8,12},{12,8},{16,20},{20,16},{24,28},{28,24},{1,5},{5... | collective-permute-start | bytes 589832 | tf_op jit(solution)/shard_map/ppermute | solution.py:88
  84.2 7.0 %collective-permute-start.25 = (bf16[2,192,128]{2,1,0:T(8,128)(2,1)S(1)}, bf16[2,192,128]{2,1,0:T(8,128)(2,1)S(1)}, u32[]{:S(2)}, u32[]{:S(2)}) collective-permute-start(bf16[2,192,128]{2,1,0:T(8,128)(2,1)S(1)} %get-tuple-element.70), channel_id=1, source_target_pairs={{0,8},{4,12},{8,0},{12,4},{16,24},{20,28},{24,16},{28,20},{1,9},{5... | collective-permute-start | bytes 294920 | tf_op jit(solution)/shard_map/ppermute | solution.py:88
  85.7 6.4 %collective-permute-start.26 = (bf16[2,192,128]{2,1,0:T(8,128)(2,1)S(1)}, bf16[2,192,128]{2,1,0:T(8,128)(2,1)S(1)}, u32[]{:S(2)}, u32[]{:S(2)}) collective-permute-start(bf16[2,192,128]{2,1,0:T(8,128)(2,1)S(1)} %get-tuple-element.71), channel_id=1, source_target_pairs={{0,16},{4,20},{8,24},{12,28},{16,0},{20,4},{24,8},{28,12},{1,17},{... | collective-permute-start | bytes 294920 | tf_op jit(solution)/shard_map/ppermute | solution.py:88
  86.8 6.3 %collective-permute-start.27 = (bf16[2,192,128]{2,1,0:T(8,128)(2,1)S(1)}, bf16[2,192,128]{2,1,0:T(8,128)(2,1)S(1)}, u32[]{:S(2)}, u32[]{:S(2)}) collective-permute-start(bf16[2,192,128]{2,1,0:T(8,128)(2,1)S(1)} %get-tuple-element.72), channel_id=1, source_target_pairs={{0,24},{4,28},{8,16},{12,20},{16,8},{20,12},{24,0},{28,4},{1,25},{... | collective-permute-start | bytes 294920 | tf_op jit(solution)/shard_map/ppermute | solution.py:88
  88.5 5.7 %collective-permute-start.32 = (bf16[2,192,128]{2,1,0:T(8,128)(2,1)S(1)}, bf16[2,192,128]{2,1,0:T(8,128)(2,1)S(1)}, u32[]{:S(2)}, u32[]{:S(2)}) collective-permute-start(bf16[2,192,128]{2,1,0:T(8,128)(2,1)S(1)} %get-tuple-element.76), channel_id=1, source_target_pairs={{0,8},{4,12},{8,0},{12,4},{16,24},{20,28},{24,16},{28,20},{1,9},{5... | collective-permute-start | bytes 294920 | tf_op jit(solution)/shard_map/ppermute | solution.py:88
  90.1 5.6 %collective-permute-start.33 = (bf16[2,192,128]{2,1,0:T(8,128)(2,1)S(1)}, bf16[2,192,128]{2,1,0:T(8,128)(2,1)S(1)}, u32[]{:S(2)}, u32[]{:S(2)}) collective-permute-start(bf16[2,192,128]{2,1,0:T(8,128)(2,1)S(1)} %get-tuple-element.77), channel_id=1, source_target_pairs={{0,16},{4,20},{8,24},{12,28},{16,0},{20,4},{24,8},{28,12},{1,17},{... | collective-permute-start | bytes 294920 | tf_op jit(solution)/shard_map/ppermute | solution.py:88
  91.2 5.5 %collective-permute-start.34 = (bf16[2,192,128]{2,1,0:T(8,128)(2,1)S(1)}, bf16[2,192,128]{2,1,0:T(8,128)(2,1)S(1)}, u32[]{:S(2)}, u32[]{:S(2)}) collective-permute-start(bf16[2,192,128]{2,1,0:T(8,128)(2,1)S(1)} %get-tuple-element.78), channel_id=1, source_target_pairs={{0,24},{4,28},{8,16},{12,20},{16,8},{20,12},{24,0},{28,4},{1,25},{... | collective-permute-start | bytes 294920 | tf_op jit(solution)/shard_map/ppermute | solution.py:88

commit v7 on v6

--- a/solution.py
+++ b/solution.py
@@ -392,25 +392,37 @@
     )(order, *[in_vmem(x) for x in [*kept, *swapped]])
 
 
-def unpack_kernel(sets, *refs):
-    *pieces, out = refs
-    chips = len(pieces) // len(sets)
-    block = out.shape[2] // sum(map(len, sets))
+def unpack_kernel(flips, *refs):
+    chips = lax.axis_size("expert") // CORES
+    pieces, (out, sems) = refs[:chips], refs[-2:]
+    block = out.shape[2] // lax.axis_size("dp")
+    copies = []
     for i, piece in enumerate(pieces):
-        tile = (lax.axis_index("expert") // CORES) ^ (i % chips)
-        for j, flip in enumerate(sets[i // chips]):
+        tile = (lax.axis_index("expert") // CORES) ^ i
+        for j, flip in enumerate(flips):
             left = (lax.axis_index("dp") ^ flip) * block + tile * LANES
-            out[0, :, pl.ds(pl.multiple_of(left, LANES), LANES)] = piece[j]
-
-
-def unpack(pieces, sets, width, cols):
-    return pl.pallas_call(
-        functools.partial(unpack_kernel, sets),
+            lanes = pl.ds(pl.multiple_of(left, LANES), LANES)
+            copies.append(
+                pltpu.make_async_copy(piece.at[j], out.at[0, :, lanes], sems.at[len(copies)])
+            )
+    for copy in copies:
+        copy.start()
+    for copy in copies:
+        copy.wait()
+
+
+def unpack(pieces, flips, width, cols, out):
+    given = [] if out is None else [out]
+    anywhere = pl.BlockSpec(memory_space=pl.ANY)
+    return pl.pallas_call(
+        functools.partial(unpack_kernel, flips),
         out_shape=jax.ShapeDtypeStruct((1, cols, width), BF16),
-        in_specs=[whole()] * len(pieces),
-        out_specs=whole(),
+        in_specs=[whole()] * len(pieces) + [anywhere] * len(given),
+        out_specs=anywhere,
+        scratch_shapes=[pltpu.SemaphoreType.DMA((len(pieces) * len(flips),))],
+        input_output_aliases={len(pieces): 0} if given else {},
         name="unpack",
-    )(*[in_vmem(x) for x in pieces])
+    )(*[in_vmem(x) for x in pieces], *given)
 
 
 def dense(tokens, cotangent, route_ids, route_gates, gate_up, down, moment1, moment2, placement):
@@ -448,13 +460,14 @@
             kept[k] = partner(x, "dp", k) if k else x
     swapped = {k: partner(x, "expert", 1) for k, x in kept.items()}
     sets = ((1, 0), (3, 2))
-    landed = []
+    out = None
     for flips in sets:
         picked = pick(placement, [kept[k] for k in flips], [swapped[k] for k in flips])
-        landed += [picked[0]] + [
+        landed = [picked[0]] + [
             partner(picked[k], "expert", k * CORES) for k in range(1, planes)
         ]
-    return unpack(landed, sets, width, cols).transpose(0, 2, 1)
+        out = unpack(landed, flips, width, cols, out)
+    return out.transpose(0, 2, 1)
 
 
 def shards(tokens, cotangent, route_ids, *rest):

time: 98.1 us -> 97.8 us (level)
  waiting for transfers between devices: 41.8 us -> 40.5 us
    ppermute x35, waiting for transfers between devices: 41.8 us -> 40.5 us  [partner(): return lax.ppermute(x, axis, [(i, i ^ flip) for i in range(size)])]
  transfers between devices with their start and end apart: 35 -> 35, of which waited for: 18 -> 18; matrix products, arithmetic and copies ran while one was open for 0% -> 0% of each run, Pallas kernels for 8% -> 9%
where the time goes in v7:
time: 97.8 us; the launch traced here: 97.5 us
  starting transfers between devices  43.1 us (44%)
  waiting for transfers between devices  40.5 us (41%)
  Pallas kernels  11.2 us (11%)
  local copies, waits for them, and re-layouts  2.56 us (3%)
    ppermute x35, starting transfers between devices, partner(): return lax.ppermute(x, axis, [(i, i ^ flip) for i in range(size)])  43.1 us
    ppermute x35, waiting for transfers between devices, partner(): return lax.ppermute(x, axis, [(i, i ^ flip) for i in range(size)])  40.5 us
    unnamed x12, local copies, waits for them, and re-layouts  2.56 us
    pallas_call x1, Pallas kernels, start_hidden(): pl.pallas_call(functools.partial(start_kernel, len(pieces), flips), out_s...  2.23 us
  transfers between devices with their start and end apart: 35, of which 18 were waited for; matrix products, arithmetic and copies ran while one was open for 0% of the time, Pallas kernels for 9%

profile of v7, /device:TPU:0, one launch (start us, length us, event | category | flops | bytes accessed | tf_op | source)
XLA Modules:
  0.0 97.5 jit_solution(5938509208769361937)
XLA Ops:
  0.0 1.0 %pack_rows.1 = (bf16[16,2688]{1,0:T(8,128)(2,1)S(1)}, bf16[16,2688]{1,0:T(8,128)(2,1)S(1)}, bf16[16,2688]{1,0:T(8,128)(2,1)S(1)}, bf16[16,2688]{1,0:T(8,128)(2,1)S(1)}) custom-call(bf16[16,2048]{1,0:T(8,128)(2,1)} %tok.1, bf16[16,2048]{1,0:T(8,128)(2,1)} %cot.1, s32[8,16]{1,0:T(8,128)} %bitcast.18, bf16[8,16]{1,0:T(8,128)(2,1)} %bitcast.19), custom_call_target="tpu_custom_call" | custom-call | tf_op jit(solution)/shard_map/pack_rows/pallas_call | solution.py:120
  1.0 3.1 %collective-permute-start = (bf16[16,2688]{1,0:T(8,128)(2,1)S(1)}, bf16[16,2688]{1,0:T(8,128)(2,1)S(1)}, u32[]{:S(2)}, u32[]{:S(2)}) collective-permute-start(bf16[16,2688]{1,0:T(8,128)(2,1)S(1)} %get-tuple-element.45), channel_id=1, source_target_pairs={{0,1},{1,0},{2,3},{3,2},{4,5},{5,4},{6,7},{7,6},{8,9},{9,8},{10,11... | collective-permute-start | bytes 258056 | tf_op jit(solution)/shard_map/ppermute | solution.py:88
  4.0 2.6 %collective-permute-start.1 = (bf16[16,2688]{1,0:T(8,128)(2,1)S(1)}, bf16[16,2688]{1,0:T(8,128)(2,1)S(1)}, u32[]{:S(2)}, u32[]{:S(2)}) collective-permute-start(bf16[16,2688]{1,0:T(8,128)(2,1)S(1)} %get-tuple-element.46), channel_id=1, source_target_pairs={{0,2},{1,3},{2,0},{3,1},{4,6},{5,7},{6,4},{7,5},{8,10},{9,11},{10,... | collective-permute-start | bytes 258056 | tf_op jit(solution)/shard_map/ppermute | solution.py:88
  6.6 1.4 %copy-done = bf16[1,512,1536]{2,1,0:T(8,128)(2,1)S(1)} copy-done((bf16[1,512,1536]{2,1,0:T(8,128)(2,1)S(1)}, bf16[1,512,1536]{2,1,0:T(8,128)(2,1)}, u32[]{:S(2)}) %copy-start) | copy-done | bytes 1572888
  8.0 1.4 %pack_weights.1 = (bf16[512,384]{1,0:T(8,128)(2,1)S(1)}, bf16[512,384]{1,0:T(8,128)(2,1)S(1)}, bf16[512,384]{1,0:T(8,128)(2,1)}, bf16[512,384]{1,0:T(8,128)(2,1)S(1)}) custom-call(bf16[512,1536]{1,0:T(8,128)(2,1)S(1)} %bitcast.14), custom_call_target="tpu_custom_call" | custom-call | tf_op jit(solution)/shard_map/pack_weights/pallas_call | solution.py:166
  9.5 1.9 %collective-permute-start.10 = (bf16[512,384]{1,0:T(8,128)(2,1)}, bf16[512,384]{1,0:T(8,128)(2,1)}, u32[]{:S(2)}, u32[]{:S(2)}) collective-permute-start(bf16[512,384]{1,0:T(8,128)(2,1)} %get-tuple-element.50), channel_id=1, source_target_pairs={{0,2},{1,3},{2,0},{3,1},{4,6},{5,7},{6,4},{7,5},{8,10},{9,11},{10,... | collective-permute-start | bytes 1179656 | tf_op jit(solution)/shard_map/ppermute | solution.py:88
  11.4 1.1 %copy-done.3 = bf16[1,512,768]{2,1,0:T(8,128)(2,1)S(1)} copy-done((bf16[1,512,768]{2,1,0:T(8,128)(2,1)S(1)}, bf16[1,512,768]{2,1,0:T(8,128)(2,1)}, u32[]{:S(2)}) %copy-start.3) | copy-done | bytes 786456
  12.5 0.7 transposed.1
  13.2 8.9 %collective-permute-done.1.refs_2_ = bf16[16,2688]{1,0:T(8,128)(2,1)S(1)} collective-permute-done((bf16[16,2688]{1,0:T(8,128)(2,1)S(1)}, bf16[16,2688]{1,0:T(8,128)(2,1)S(1)}, u32[]{:S(2)}, u32[]{:S(2)}) %collective-permute-start.1) | collective-permute-done | bytes 86048 | tf_op jit(solution)/shard_map/ppermute | solution.py:88
  22.1 1.6 %collective-permute-start.3 = (bf16[64,2688]{1,0:T(8,128)(2,1)S(1)}, bf16[64,2688]{1,0:T(8,128)(2,1)S(1)}, u32[]{:S(2)}, u32[]{:S(2)}) collective-permute-start(bf16[64,2688]{1,0:T(8,128)(2,1)S(1)} %bitcast.8), channel_id=1, source_target_pairs={{0,8},{4,12},{8,0},{12,4},{16,24},{20,28},{24,16},{28,20},{1,9},{5... | collective-permute-start | bytes 1032200 | tf_op jit(solution)/shard_map/ppermute | solution.py:88
  23.7 1.5 %collective-permute-start.5 = (bf16[64,2688]{1,0:T(8,128)(2,1)S(1)}, bf16[64,2688]{1,0:T(8,128)(2,1)S(1)}, u32[]{:S(2)}, u32[]{:S(2)}) collective-permute-start(bf16[64,2688]{1,0:T(8,128)(2,1)S(1)} %bitcast.9), channel_id=1, source_target_pairs={{0,24},{4,28},{8,16},{12,20},{16,8},{20,12},{24,0},{28,4},{1,25},{... | collective-permute-start | bytes 1032200 | tf_op jit(solution)/shard_map/ppermute | solution.py:88
  25.7 3.8 %collective-permute-done.3.refs_1_ = bf16[64,2688]{1,0:T(8,128)(2,1)S(1)} collective-permute-done((bf16[64,2688]{1,0:T(8,128)(2,1)S(1)}, bf16[64,2688]{1,0:T(8,128)(2,1)S(1)}, u32[]{:S(2)}, u32[]{:S(2)}) %collective-permute-start.3) | collective-permute-done | bytes 344096 | tf_op jit(solution)/shard_map/ppermute | solution.py:88
  29.4 6.1 %collective-permute-start.11 = (bf16[512,384]{1,0:T(8,128)(2,1)}, bf16[512,384]{1,0:T(8,128)(2,1)S(1)}, u32[]{:S(2)}, u32[]{:S(2)}) collective-permute-start(bf16[512,384]{1,0:T(8,128)(2,1)} %copy-done.5), channel_id=1, source_target_pairs={{0,1},{1,0},{2,3},{3,2},{4,5},{5,4},{6,7},{7,6},{8,9},{9,8},{10,11... | collective-permute-start | bytes 1179656 | tf_op jit(solution)/shard_map/ppermute | solution.py:88
  35.6 2.6 %collective-permute-start.12 = (bf16[512,384]{1,0:T(8,128)(2,1)}, bf16[512,384]{1,0:T(8,128)(2,1)S(1)}, u32[]{:S(2)}, u32[]{:S(2)}) collective-permute-start(bf16[512,384]{1,0:T(8,128)(2,1)} %copy-done.4), channel_id=1, source_target_pairs={{0,3},{1,2},{2,1},{3,0},{4,7},{5,6},{6,5},{7,4},{8,11},{9,10},{10,... | collective-permute-start | bytes 1179656 | tf_op jit(solution)/shard_map/ppermute | solution.py:88
  38.8 1.1 %collective-permute-done.9.refs_7_ = bf16[64,2688]{1,0:T(8,128)(2,1)S(1)} collective-permute-done((bf16[64,2688]{1,0:T(8,128)(2,1)S(1)}, bf16[64,2688]{1,0:T(8,128)(2,1)S(1)}, u32[]{:S(2)}, u32[]{:S(2)}) %collective-permute-start.9) | collective-permute-done | bytes 344096 | tf_op jit(solution)/shard_map/ppermute | solution.py:88
  40.8 3.9 %collective-permute-done.11.refs_10_ = bf16[512,384]{1,0:T(8,128)(2,1)S(1)} collective-permute-done((bf16[512,384]{1,0:T(8,128)(2,1)}, bf16[512,384]{1,0:T(8,128)(2,1)S(1)}, u32[]{:S(2)}, u32[]{:S(2)}) %collective-permute-start.11) | collective-permute-done | bytes 393248 | tf_op jit(solution)/shard_map/ppermute | solution.py:88
  44.7 2.2 %start_hidden.1 = (f32[512,384]{1,0:T(8,128)S(1)}, bf16[512,512]{1,0:T(8,128)(2,1)S(1)}) custom-call(bf16[64,2688]{1,0:T(8,128)(2,1)S(1)} %bitcast.12, bf16[64,2688]{1,0:T(8,128)(2,1)S(1)} %collective-permute-done.3.refs_1_, bf16[64,2688]{1,0:T(8,128)(2,1)S(1)} %collective-permute-done.4.refs_2_, bf16[64,2688]{1,0:T(8,128)(2,1)S(1)} %collective-permute-done.5.refs_3_, ...), custom_call_target="tpu_custom_call" | custom-call | tf_op jit(solution)/shard_map/start_hidden/pallas_call | solution.py:229
  47.0 2.0 %collective-permute-done.12.refs_0_ = bf16[512,384]{1,0:T(8,128)(2,1)S(1)} collective-permute-done((bf16[512,384]{1,0:T(8,128)(2,1)}, bf16[512,384]{1,0:T(8,128)(2,1)S(1)}, u32[]{:S(2)}, u32[]{:S(2)}) %collective-permute-start.12) | collective-permute-done | bytes 393248 | tf_op jit(solution)/shard_map/ppermute | solution.py:88
  49.8 2.9 %collective-permute-start.19 = (bf16[192,512]{1,0:T(8,128)(2,1)S(1)}, bf16[192,512]{1,0:T(8,128)(2,1)S(1)}, u32[]{:S(2)}, u32[]{:S(2)}) collective-permute-start(bf16[192,512]{1,0:T(8,128)(2,1)S(1)} %end_hidden.1.refs_0_), channel_id=1, source_target_pairs={{0,1},{1,0},{2,3},{3,2},{4,5},{5,4},{6,7},{7,6},{8,9},{9,8},{10,11... | collective-permute-start | bytes 589832 | tf_op jit(solution)/shard_map/ppermute | solution.py:88
  52.6 5.9 %collective-permute-done.13.refs_1_ = bf16[192,512]{1,0:T(8,128)(2,1)S(1)} collective-permute-done((bf16[192,512]{1,0:T(8,128)(2,1)S(1)}, bf16[192,512]{1,0:T(8,128)(2,1)S(1)}, u32[]{:S(2)}, u32[]{:S(2)}) %collective-permute-start.13) | collective-permute-done | bytes 196640 | tf_op jit(solution)/shard_map/ppermute | solution.py:88
  58.7 0.9 collective-permute-done.19.refs_0_
  59.6 0.9 update_tiles.3
  60.6 1.6 %collective-permute-start.20 = (bf16[2,192,128]{2,1,0:T(8,128)(2,1)S(1)}, bf16[2,192,128]{2,1,0:T(8,128)(2,1)S(1)}, u32[]{:S(2)}, u32[]{:S(2)}) collective-permute-start(bf16[2,192,128]{2,1,0:T(8,128)(2,1)S(1)} %get-tuple-element.65), channel_id=1, source_target_pairs={{0,8},{4,12},{8,0},{12,4},{16,24},{20,28},{24,16},{28,20},{1,9},{5... | collective-permute-start | bytes 294920 | tf_op jit(solution)/shard_map/ppermute | solution.py:88
  62.1 1.0 %collective-permute-start.21 = (bf16[2,192,128]{2,1,0:T(8,128)(2,1)S(1)}, bf16[2,192,128]{2,1,0:T(8,128)(2,1)S(1)}, u32[]{:S(2)}, u32[]{:S(2)}) collective-permute-start(bf16[2,192,128]{2,1,0:T(8,128)(2,1)S(1)} %get-tuple-element.66), channel_id=1, source_target_pairs={{0,16},{4,20},{8,24},{12,28},{16,0},{20,4},{24,8},{28,12},{1,17},{... | collective-permute-start | bytes 294920 | tf_op jit(solution)/shard_map/ppermute | solution.py:88
  63.1 1.0 %collective-permute-start.22 = (bf16[2,192,128]{2,1,0:T(8,128)(2,1)S(1)}, bf16[2,192,128]{2,1,0:T(8,128)(2,1)S(1)}, u32[]{:S(2)}, u32[]{:S(2)}) collective-permute-start(bf16[2,192,128]{2,1,0:T(8,128)(2,1)S(1)} %get-tuple-element.67), channel_id=1, source_target_pairs={{0,24},{4,28},{8,16},{12,20},{16,8},{20,12},{24,0},{28,4},{1,25},{... | collective-permute-start | bytes 294920 | tf_op jit(solution)/shard_map/ppermute | solution.py:88
  64.2 0.9 update_tiles.2
  65.1 1.6 %collective-permute-start.15 = (bf16[2,192,128]{2,1,0:T(8,128)(2,1)S(1)}, bf16[2,192,128]{2,1,0:T(8,128)(2,1)S(1)}, u32[]{:S(2)}, u32[]{:S(2)}) collective-permute-start(bf16[2,192,128]{2,1,0:T(8,128)(2,1)S(1)} %get-tuple-element.60), channel_id=1, source_target_pairs={{0,8},{4,12},{8,0},{12,4},{16,24},{20,28},{24,16},{28,20},{1,9},{5... | collective-permute-start | bytes 294920 | tf_op jit(solution)/shard_map/ppermute | solution.py:88
  66.7 1.5 %collective-permute-start.16 = (bf16[2,192,128]{2,1,0:T(8,128)(2,1)S(1)}, bf16[2,192,128]{2,1,0:T(8,128)(2,1)S(1)}, u32[]{:S(2)}, u32[]{:S(2)}) collective-permute-start(bf16[2,192,128]{2,1,0:T(8,128)(2,1)S(1)} %get-tuple-element.61), channel_id=1, source_target_pairs={{0,16},{4,20},{8,24},{12,28},{16,0},{20,4},{24,8},{28,12},{1,17},{... | collective-permute-start | bytes 294920 | tf_op jit(solution)/shard_map/ppermute | solution.py:88
  68.7 0.7 collective-permute-done.22.refs_3_
  69.4 1.2 %collective-permute-start.29 = (bf16[4,192,128]{2,1,0:T(8,128)(2,1)S(1)}, bf16[4,192,128]{2,1,0:T(8,128)(2,1)S(1)}, u32[]{:S(2)}, u32[]{:S(2)}) collective-permute-start(bf16[4,192,128]{2,1,0:T(8,128)(2,1)S(1)} %get-tuple-element.73), channel_id=1, source_target_pairs={{0,1},{1,0},{2,3},{3,2},{4,5},{5,4},{6,7},{7,6},{8,9},{9,8},{10,11... | collective-permute-start | bytes 589832 | tf_op jit(solution)/shard_map/ppermute | solution.py:88
  70.6 1.6 %collective-permute-start.23 = (bf16[4,192,128]{2,1,0:T(8,128)(2,1)S(1)}, bf16[4,192,128]{2,1,0:T(8,128)(2,1)S(1)}, u32[]{:S(2)}, u32[]{:S(2)}) collective-permute-start(bf16[4,192,128]{2,1,0:T(8,128)(2,1)S(1)} %get-tuple-element.68), channel_id=1, source_target_pairs={{0,2},{1,3},{2,0},{3,1},{4,6},{5,7},{6,4},{7,5},{8,10},{9,11},{10,... | collective-permute-start | bytes 589832 | tf_op jit(solution)/shard_map/ppermute | solution.py:88
  72.2 1.5 %collective-permute-done.17.refs_3_ = bf16[2,192,128]{2,1,0:T(8,128)(2,1)S(1)} collective-permute-done((bf16[2,192,128]{2,1,0:T(8,128)(2,1)S(1)}, bf16[2,192,128]{2,1,0:T(8,128)(2,1)S(1)}, u32[]{:S(2)}, u32[]{:S(2)}) %collective-permute-start.17) | collective-permute-done | bytes 98336 | tf_op jit(solution)/shard_map/ppermute | solution.py:88
  73.8 1.7 %collective-permute-start.18 = (bf16[4,192,128]{2,1,0:T(8,128)(2,1)S(1)}, bf16[4,192,128]{2,1,0:T(8,128)(2,1)S(1)}, u32[]{:S(2)}, u32[]{:S(2)}) collective-permute-start(bf16[4,192,128]{2,1,0:T(8,128)(2,1)S(1)} %get-tuple-element.63), channel_id=1, source_target_pairs={{0,3},{1,2},{2,1},{3,0},{4,7},{5,6},{6,5},{7,4},{8,11},{9,10},{10,... | collective-permute-start | bytes 589832 | tf_op jit(solution)/shard_map/ppermute | solution.py:88
  75.5 3.1 %collective-permute-done.29.refs_0_ = bf16[4,192,128]{2,1,0:T(8,128)(2,1)S(1)} collective-permute-done((bf16[4,192,128]{2,1,0:T(8,128)(2,1)S(1)}, bf16[4,192,128]{2,1,0:T(8,128)(2,1)S(1)}, u32[]{:S(2)}, u32[]{:S(2)}) %collective-permute-start.29) | collective-permute-done | bytes 196640 | tf_op jit(solution)/shard_map/ppermute | solution.py:88
  79.1 3.8 %collective-permute-done.23.refs_1_ = bf16[4,192,128]{2,1,0:T(8,128)(2,1)S(1)} collective-permute-done((bf16[4,192,128]{2,1,0:T(8,128)(2,1)S(1)}, bf16[4,192,128]{2,1,0:T(8,128)(2,1)S(1)}, u32[]{:S(2)}, u32[]{:S(2)}) %collective-permute-start.23) | collective-permute-done | bytes 196640 | tf_op jit(solution)/shard_map/ppermute | solution.py:88
  83.4 0.8 pick.3
  84.2 1.5 %collective-permute-start.32 = (bf16[2,192,128]{2,1,0:T(8,128)(2,1)S(1)}, bf16[2,192,128]{2,1,0:T(8,128)(2,1)S(1)}, u32[]{:S(2)}, u32[]{:S(2)}) collective-permute-start(bf16[2,192,128]{2,1,0:T(8,128)(2,1)S(1)} %get-tuple-element.76), channel_id=1, source_target_pairs={{0,8},{4,12},{8,0},{12,4},{16,24},{20,28},{24,16},{28,20},{1,9},{5... | collective-permute-start | bytes 294920 | tf_op jit(solution)/shard_map/ppermute | solution.py:88
  85.7 1.1 %collective-permute-start.33 = (bf16[2,192,128]{2,1,0:T(8,128)(2,1)S(1)}, bf16[2,192,128]{2,1,0:T(8,128)(2,1)S(1)}, u32[]{:S(2)}, u32[]{:S(2)}) collective-permute-start(bf16[2,192,128]{2,1,0:T(8,128)(2,1)S(1)} %get-tuple-element.77), channel_id=1, source_target_pairs={{0,16},{4,20},{8,24},{12,28},{16,0},{20,4},{24,8},{28,12},{1,17},{... | collective-permute-start | bytes 294920 | tf_op jit(solution)/shard_map/ppermute | solution.py:88
  86.8 0.9 collective-permute-start.34
  87.8 0.8 pick.2
  88.5 1.5 %collective-permute-start.26 = (bf16[2,192,128]{2,1,0:T(8,128)(2,1)S(1)}, bf16[2,192,128]{2,1,0:T(8,128)(2,1)S(1)}, u32[]{:S(2)}, u32[]{:S(2)}) collective-permute-start(bf16[2,192,128]{2,1,0:T(8,128)(2,1)S(1)} %get-tuple-element.70), channel_id=1, source_target_pairs={{0,8},{4,12},{8,0},{12,4},{16,24},{20,28},{24,16},{28,20},{1,9},{5... | collective-permute-start | bytes 294920 | tf_op jit(solution)/shard_map/ppermute | solution.py:88
  90.1 1.1 %collective-permute-start.27 = (bf16[2,192,128]{2,1,0:T(8,128)(2,1)S(1)}, bf16[2,192,128]{2,1,0:T(8,128)(2,1)S(1)}, u32[]{:S(2)}, u32[]{:S(2)}) collective-permute-start(bf16[2,192,128]{2,1,0:T(8,128)(2,1)S(1)} %get-tuple-element.71), channel_id=1, source_target_pairs={{0,16},{4,20},{8,24},{12,28},{16,0},{20,4},{24,8},{28,12},{1,17},{... | collective-permute-start | bytes 294920 | tf_op jit(solution)/shard_map/ppermute | solution.py:88
  91.2 0.9 collective-permute-start.28
  92.1 1.1 %collective-permute-done.34.refs_3_ = bf16[2,192,128]{2,1,0:T(8,128)(2,1)S(1)} collective-permute-done((bf16[2,192,128]{2,1,0:T(8,128)(2,1)S(1)}, bf16[2,192,128]{2,1,0:T(8,128)(2,1)S(1)}, u32[]{:S(2)}, u32[]{:S(2)}) %collective-permute-start.34) | collective-permute-done | bytes 98336 | tf_op jit(solution)/shard_map/ppermute | solution.py:88
  93.2 0.8 unpack.2.refs_4_
  94.2 1.5 %collective-permute-done.27.refs_2_ = bf16[2,192,128]{2,1,0:T(8,128)(2,1)S(1)} collective-permute-done((bf16[2,192,128]{2,1,0:T(8,128)(2,1)S(1)}, bf16[2,192,128]{2,1,0:T(8,128)(2,1)S(1)}, u32[]{:S(2)}, u32[]{:S(2)}) %collective-permute-start.27) | collective-permute-done | bytes 98336 | tf_op jit(solution)/shard_map/ppermute | solution.py:88
  95.7 1.0 %collective-permute-done.28.refs_3_ = bf16[2,192,128]{2,1,0:T(8,128)(2,1)S(1)} collective-permute-done((bf16[2,192,128]{2,1,0:T(8,128)(2,1)S(1)}, bf16[2,192,128]{2,1,0:T(8,128)(2,1)S(1)}, u32[]{:S(2)}, u32[]{:S(2)}) %collective-permute-start.28) | collective-permute-done | bytes 98336 | tf_op jit(solution)/shard_map/ppermute | solution.py:88
  96.7 0.8 unpack.3
  (49 shorter events, 4.9 us)
Async XLA Ops:
  1.0 8.5 %collective-permute-start = (bf16[16,2688]{1,0:T(8,128)(2,1)S(1)}, bf16[16,2688]{1,0:T(8,128)(2,1)S(1)}, u32[]{:S(2)}, u32[]{:S(2)}) collective-permute-start(bf16[16,2688]{1,0:T(8,128)(2,1)S(1)} %get-tuple-element.45), channel_id=1, source_target_pairs={{0,1},{1,0},{2,3},{3,2},{4,5},{5,4},{6,7},{7,6},{8,9},{9,8},{10,11... | collective-permute-start | bytes 258056 | tf_op jit(solution)/shard_map/ppermute | solution.py:88
  4.0 18.0 %collective-permute-start.1 = (bf16[16,2688]{1,0:T(8,128)(2,1)S(1)}, bf16[16,2688]{1,0:T(8,128)(2,1)S(1)}, u32[]{:S(2)}, u32[]{:S(2)}) collective-permute-start(bf16[16,2688]{1,0:T(8,128)(2,1)S(1)} %get-tuple-element.46), channel_id=1, source_target_pairs={{0,2},{1,3},{2,0},{3,1},{4,6},{5,7},{6,4},{7,5},{8,10},{9,11},{10,... | collective-permute-start | bytes 258056 | tf_op jit(solution)/shard_map/ppermute | solution.py:88
  6.6 15.4 %collective-permute-start.2 = (bf16[16,2688]{1,0:T(8,128)(2,1)S(1)}, bf16[16,2688]{1,0:T(8,128)(2,1)S(1)}, u32[]{:S(2)}, u32[]{:S(2)}) collective-permute-start(bf16[16,2688]{1,0:T(8,128)(2,1)S(1)} %get-tuple-element.47), channel_id=1, source_target_pairs={{0,3},{1,2},{2,1},{3,0},{4,7},{5,6},{6,5},{7,4},{8,11},{9,10},{10,... | collective-permute-start | bytes 258056 | tf_op jit(solution)/shard_map/ppermute | solution.py:88
  6.6 1.4 %copy-start = (bf16[1,512,1536]{2,1,0:T(8,128)(2,1)S(1)}, bf16[1,512,1536]{2,1,0:T(8,128)(2,1)}, u32[]{:S(2)}) copy-start(bf16[1,512,1536]{2,1,0:T(8,128)(2,1)} %param.13) | copy-start | bytes 4718596
  8.0 3.3 %copy-start.1 = (bf16[1,512,768]{2,1,0:T(8,128)(2,1)S(1)}, bf16[1,512,768]{2,1,0:T(8,128)(2,1)}, u32[]{:S(2)}) copy-start(bf16[1,512,768]{2,1,0:T(8,128)(2,1)} %param.14) | copy-start | bytes 2359300
  8.0 3.3 %copy-start.2 = (bf16[1,512,768]{2,1,0:T(8,128)(2,1)S(1)}, bf16[1,512,768]{2,1,0:T(8,128)(2,1)}, u32[]{:S(2)}) copy-start(bf16[1,512,768]{2,1,0:T(8,128)(2,1)} %param.15) | copy-start | bytes 2359300
  9.4 12.6 %copy-start.4 = (bf16[512,384]{1,0:T(8,128)(2,1)}, bf16[512,384]{1,0:T(8,128)(2,1)S(1)}, u32[]{:S(2)}) copy-start(bf16[512,384]{1,0:T(8,128)(2,1)S(1)} %get-tuple-element.56) | copy-start | bytes 1179652
  9.4 12.6 %copy-start.5 = (bf16[512,384]{1,0:T(8,128)(2,1)}, bf16[512,384]{1,0:T(8,128)(2,1)S(1)}, u32[]{:S(2)}) copy-start(bf16[512,384]{1,0:T(8,128)(2,1)S(1)} %get-tuple-element.52) | copy-start | bytes 1179652
  9.5 26.1 %collective-permute-start.10 = (bf16[512,384]{1,0:T(8,128)(2,1)}, bf16[512,384]{1,0:T(8,128)(2,1)}, u32[]{:S(2)}, u32[]{:S(2)}) collective-permute-start(bf16[512,384]{1,0:T(8,128)(2,1)} %get-tuple-element.50), channel_id=1, source_target_pairs={{0,2},{1,3},{2,0},{3,1},{4,6},{5,7},{6,4},{7,5},{8,10},{9,11},{10,... | collective-permute-start | bytes 1179656 | tf_op jit(solution)/shard_map/ppermute | solution.py:88
  11.4 1.1 %copy-start.3 = (bf16[1,512,768]{2,1,0:T(8,128)(2,1)S(1)}, bf16[1,512,768]{2,1,0:T(8,128)(2,1)}, u32[]{:S(2)}) copy-start(bf16[1,512,768]{2,1,0:T(8,128)(2,1)} %param.16) | copy-start | bytes 2359300
  22.1 7.3 %collective-permute-start.3 = (bf16[64,2688]{1,0:T(8,128)(2,1)S(1)}, bf16[64,2688]{1,0:T(8,128)(2,1)S(1)}, u32[]{:S(2)}, u32[]{:S(2)}) collective-permute-start(bf16[64,2688]{1,0:T(8,128)(2,1)S(1)} %bitcast.8), channel_id=1, source_target_pairs={{0,8},{4,12},{8,0},{12,4},{16,24},{20,28},{24,16},{28,20},{1,9},{5... | collective-permute-start | bytes 1032200 | tf_op jit(solution)/shard_map/ppermute | solution.py:88
  23.7 14.5 %collective-permute-start.5 = (bf16[64,2688]{1,0:T(8,128)(2,1)S(1)}, bf16[64,2688]{1,0:T(8,128)(2,1)S(1)}, u32[]{:S(2)}, u32[]{:S(2)}) collective-permute-start(bf16[64,2688]{1,0:T(8,128)(2,1)S(1)} %bitcast.9), channel_id=1, source_target_pairs={{0,24},{4,28},{8,16},{12,20},{16,8},{20,12},{24,0},{28,4},{1,25},{... | collective-permute-start | bytes 1032200 | tf_op jit(solution)/shard_map/ppermute | solution.py:88
  25.2 13.0 %collective-permute-start.4 = (bf16[64,2688]{1,0:T(8,128)(2,1)S(1)}, bf16[64,2688]{1,0:T(8,128)(2,1)S(1)}, u32[]{:S(2)}, u32[]{:S(2)}) collective-permute-start(bf16[64,2688]{1,0:T(8,128)(2,1)S(1)} %bitcast.10), channel_id=1, source_target_pairs={{0,16},{4,20},{8,24},{12,28},{16,0},{20,4},{24,8},{28,12},{1,17},{... | collective-permute-start | bytes 1032200 | tf_op jit(solution)/shard_map/ppermute | solution.py:88
  25.7 13.0 %collective-permute-start.6 = (bf16[64,2688]{1,0:T(8,128)(2,1)S(1)}, bf16[64,2688]{1,0:T(8,128)(2,1)S(1)}, u32[]{:S(2)}, u32[]{:S(2)}) collective-permute-start(bf16[64,2688]{1,0:T(8,128)(2,1)S(1)} %bitcast.11), channel_id=1, source_target_pairs={{0,4},{4,0},{8,12},{12,8},{16,20},{20,16},{24,28},{28,24},{1,5},{5... | collective-permute-start | bytes 1032200 | tf_op jit(solution)/shard_map/ppermute | solution.py:88
  29.4 15.3 %collective-permute-start.11 = (bf16[512,384]{1,0:T(8,128)(2,1)}, bf16[512,384]{1,0:T(8,128)(2,1)S(1)}, u32[]{:S(2)}, u32[]{:S(2)}) collective-permute-start(bf16[512,384]{1,0:T(8,128)(2,1)} %copy-done.5), channel_id=1, source_target_pairs={{0,1},{1,0},{2,3},{3,2},{4,5},{5,4},{6,7},{7,6},{8,9},{9,8},{10,11... | collective-permute-start | bytes 1179656 | tf_op jit(solution)/shard_map/ppermute | solution.py:88
  35.6 13.4 %collective-permute-start.12 = (bf16[512,384]{1,0:T(8,128)(2,1)}, bf16[512,384]{1,0:T(8,128)(2,1)S(1)}, u32[]{:S(2)}, u32[]{:S(2)}) collective-permute-start(bf16[512,384]{1,0:T(8,128)(2,1)} %copy-done.4), channel_id=1, source_target_pairs={{0,3},{1,2},{2,1},{3,0},{4,7},{5,6},{6,5},{7,4},{8,11},{9,10},{10,... | collective-permute-start | bytes 1179656 | tf_op jit(solution)/shard_map/ppermute | solution.py:88
  38.2 1.7 %collective-permute-start.9 = (bf16[64,2688]{1,0:T(8,128)(2,1)S(1)}, bf16[64,2688]{1,0:T(8,128)(2,1)S(1)}, u32[]{:S(2)}, u32[]{:S(2)}) collective-permute-start(bf16[64,2688]{1,0:T(8,128)(2,1)S(1)} %collective-permute-done.5.refs_3_), channel_id=1, source_target_pairs={{0,4},{4,0},{8,12},{12,8},{16,20},{20,16},{24,28},{28,24},{1,5},{5... | collective-permute-start | bytes 1032200 | tf_op jit(solution)/shard_map/ppermute | solution.py:88
  38.2 2.1 %collective-permute-start.8 = (bf16[64,2688]{1,0:T(8,128)(2,1)S(1)}, bf16[64,2688]{1,0:T(8,128)(2,1)S(1)}, u32[]{:S(2)}, u32[]{:S(2)}) collective-permute-start(bf16[64,2688]{1,0:T(8,128)(2,1)S(1)} %collective-permute-done.4.refs_2_), channel_id=1, source_target_pairs={{0,4},{4,0},{8,12},{12,8},{16,20},{20,16},{24,28},{28,24},{1,5},{5... | collective-permute-start | bytes 1032200 | tf_op jit(solution)/shard_map/ppermute | solution.py:88
  38.7 2.1 %collective-permute-start.7 = (bf16[64,2688]{1,0:T(8,128)(2,1)S(1)}, bf16[64,2688]{1,0:T(8,128)(2,1)S(1)}, u32[]{:S(2)}, u32[]{:S(2)}) collective-permute-start(bf16[64,2688]{1,0:T(8,128)(2,1)S(1)} %collective-permute-done.3.refs_1_), channel_id=1, source_target_pairs={{0,4},{4,0},{8,12},{12,8},{16,20},{20,16},{24,28},{28,24},{1,5},{5... | collective-permute-start | bytes 1032200 | tf_op jit(solution)/shard_map/ppermute | solution.py:88
  49.7 8.8 %collective-permute-start.13 = (bf16[192,512]{1,0:T(8,128)(2,1)S(1)}, bf16[192,512]{1,0:T(8,128)(2,1)S(1)}, u32[]{:S(2)}, u32[]{:S(2)}) collective-permute-start(bf16[192,512]{1,0:T(8,128)(2,1)S(1)} %end_hidden.1.refs_0_), channel_id=1, source_target_pairs={{0,2},{1,3},{2,0},{3,1},{4,6},{5,7},{6,4},{7,5},{8,10},{9,11},{10,... | collective-permute-start | bytes 589832 | tf_op jit(solution)/shard_map/ppermute | solution.py:88
  49.8 9.9 %collective-permute-start.19 = (bf16[192,512]{1,0:T(8,128)(2,1)S(1)}, bf16[192,512]{1,0:T(8,128)(2,1)S(1)}, u32[]{:S(2)}, u32[]{:S(2)}) collective-permute-start(bf16[192,512]{1,0:T(8,128)(2,1)S(1)} %end_hidden.1.refs_0_), channel_id=1, source_target_pairs={{0,1},{1,0},{2,3},{3,2},{4,5},{5,4},{6,7},{7,6},{8,9},{9,8},{10,11... | collective-permute-start | bytes 589832 | tf_op jit(solution)/shard_map/ppermute | solution.py:88
  58.5 5.7 %collective-permute-start.14 = (bf16[192,512]{1,0:T(8,128)(2,1)S(1)}, bf16[192,512]{1,0:T(8,128)(2,1)S(1)}, u32[]{:S(2)}, u32[]{:S(2)}) collective-permute-start(bf16[192,512]{1,0:T(8,128)(2,1)S(1)} %collective-permute-done.13.refs_1_), channel_id=1, source_target_pairs={{0,1},{1,0},{2,3},{3,2},{4,5},{5,4},{6,7},{7,6},{8,9},{9,8},{10,11... | collective-permute-start | bytes 589832 | tf_op jit(solution)/shard_map/ppermute | solution.py:88
  60.6 7.6 %collective-permute-start.20 = (bf16[2,192,128]{2,1,0:T(8,128)(2,1)S(1)}, bf16[2,192,128]{2,1,0:T(8,128)(2,1)S(1)}, u32[]{:S(2)}, u32[]{:S(2)}) collective-permute-start(bf16[2,192,128]{2,1,0:T(8,128)(2,1)S(1)} %get-tuple-element.65), channel_id=1, source_target_pairs={{0,8},{4,12},{8,0},{12,4},{16,24},{20,28},{24,16},{28,20},{1,9},{5... | collective-permute-start | bytes 294920 | tf_op jit(solution)/shard_map/ppermute | solution.py:88
  62.1 6.6 %collective-permute-start.21 = (bf16[2,192,128]{2,1,0:T(8,128)(2,1)S(1)}, bf16[2,192,128]{2,1,0:T(8,128)(2,1)S(1)}, u32[]{:S(2)}, u32[]{:S(2)}) collective-permute-start(bf16[2,192,128]{2,1,0:T(8,128)(2,1)S(1)} %get-tuple-element.66), channel_id=1, source_target_pairs={{0,16},{4,20},{8,24},{12,28},{16,0},{20,4},{24,8},{28,12},{1,17},{... | collective-permute-start | bytes 294920 | tf_op jit(solution)/shard_map/ppermute | solution.py:88
  63.1 6.3 %collective-permute-start.22 = (bf16[2,192,128]{2,1,0:T(8,128)(2,1)S(1)}, bf16[2,192,128]{2,1,0:T(8,128)(2,1)S(1)}, u32[]{:S(2)}, u32[]{:S(2)}) collective-permute-start(bf16[2,192,128]{2,1,0:T(8,128)(2,1)S(1)} %get-tuple-element.67), channel_id=1, source_target_pairs={{0,24},{4,28},{8,16},{12,20},{16,8},{20,12},{24,0},{28,4},{1,25},{... | collective-permute-start | bytes 294920 | tf_op jit(solution)/shard_map/ppermute | solution.py:88
  65.1 7.0 %collective-permute-start.15 = (bf16[2,192,128]{2,1,0:T(8,128)(2,1)S(1)}, bf16[2,192,128]{2,1,0:T(8,128)(2,1)S(1)}, u32[]{:S(2)}, u32[]{:S(2)}) collective-permute-start(bf16[2,192,128]{2,1,0:T(8,128)(2,1)S(1)} %get-tuple-element.60), channel_id=1, source_target_pairs={{0,8},{4,12},{8,0},{12,4},{16,24},{20,28},{24,16},{28,20},{1,9},{5... | collective-permute-start | bytes 294920 | tf_op jit(solution)/shard_map/ppermute | solution.py:88
  66.7 5.5 %collective-permute-start.16 = (bf16[2,192,128]{2,1,0:T(8,128)(2,1)S(1)}, bf16[2,192,128]{2,1,0:T(8,128)(2,1)S(1)}, u32[]{:S(2)}, u32[]{:S(2)}) collective-permute-start(bf16[2,192,128]{2,1,0:T(8,128)(2,1)S(1)} %get-tuple-element.61), channel_id=1, source_target_pairs={{0,16},{4,20},{8,24},{12,28},{16,0},{20,4},{24,8},{28,12},{1,17},{... | collective-permute-start | bytes 294920 | tf_op jit(solution)/shard_map/ppermute | solution.py:88
  68.2 5.5 %collective-permute-start.17 = (bf16[2,192,128]{2,1,0:T(8,128)(2,1)S(1)}, bf16[2,192,128]{2,1,0:T(8,128)(2,1)S(1)}, u32[]{:S(2)}, u32[]{:S(2)}) collective-permute-start(bf16[2,192,128]{2,1,0:T(8,128)(2,1)S(1)} %get-tuple-element.62), channel_id=1, source_target_pairs={{0,24},{4,28},{8,16},{12,20},{16,8},{20,12},{24,0},{28,4},{1,25},{... | collective-permute-start | bytes 294920 | tf_op jit(solution)/shard_map/ppermute | solution.py:88
  69.4 9.2 %collective-permute-start.29 = (bf16[4,192,128]{2,1,0:T(8,128)(2,1)S(1)}, bf16[4,192,128]{2,1,0:T(8,128)(2,1)S(1)}, u32[]{:S(2)}, u32[]{:S(2)}) collective-permute-start(bf16[4,192,128]{2,1,0:T(8,128)(2,1)S(1)} %get-tuple-element.73), channel_id=1, source_target_pairs={{0,1},{1,0},{2,3},{3,2},{4,5},{5,4},{6,7},{7,6},{8,9},{9,8},{10,11... | collective-permute-start | bytes 589832 | tf_op jit(solution)/shard_map/ppermute | solution.py:88
  70.6 12.3 %collective-permute-start.23 = (bf16[4,192,128]{2,1,0:T(8,128)(2,1)S(1)}, bf16[4,192,128]{2,1,0:T(8,128)(2,1)S(1)}, u32[]{:S(2)}, u32[]{:S(2)}) collective-permute-start(bf16[4,192,128]{2,1,0:T(8,128)(2,1)S(1)} %get-tuple-element.68), channel_id=1, source_target_pairs={{0,2},{1,3},{2,0},{3,1},{4,6},{5,7},{6,4},{7,5},{8,10},{9,11},{10,... | collective-permute-start | bytes 589832 | tf_op jit(solution)/shard_map/ppermute | solution.py:88
  73.8 9.1 %collective-permute-start.18 = (bf16[4,192,128]{2,1,0:T(8,128)(2,1)S(1)}, bf16[4,192,128]{2,1,0:T(8,128)(2,1)S(1)}, u32[]{:S(2)}, u32[]{:S(2)}) collective-permute-start(bf16[4,192,128]{2,1,0:T(8,128)(2,1)S(1)} %get-tuple-element.63), channel_id=1, source_target_pairs={{0,3},{1,2},{2,1},{3,0},{4,7},{5,6},{6,5},{7,4},{8,11},{9,10},{10,... | collective-permute-start | bytes 589832 | tf_op jit(solution)/shard_map/ppermute | solution.py:88
  78.6 4.8 %collective-permute-start.30 = (bf16[4,192,128]{2,1,0:T(8,128)(2,1)S(1)}, bf16[4,192,128]{2,1,0:T(8,128)(2,1)S(1)}, u32[]{:S(2)}, u32[]{:S(2)}) collective-permute-start(bf16[4,192,128]{2,1,0:T(8,128)(2,1)S(1)} %collective-permute-done.29.refs_0_), channel_id=1, source_target_pairs={{0,4},{4,0},{8,12},{12,8},{16,20},{20,16},{24,28},{28,24},{1,5},{5... | collective-permute-start | bytes 589832 | tf_op jit(solution)/shard_map/ppermute | solution.py:88
  78.6 4.8 %collective-permute-start.31 = (bf16[4,192,128]{2,1,0:T(8,128)(2,1)S(1)}, bf16[4,192,128]{2,1,0:T(8,128)(2,1)S(1)}, u32[]{:S(2)}, u32[]{:S(2)}) collective-permute-start(bf16[4,192,128]{2,1,0:T(8,128)(2,1)S(1)} %get-tuple-element.74.refs_1_), channel_id=1, source_target_pairs={{0,4},{4,0},{8,12},{12,8},{16,20},{20,16},{24,28},{28,24},{1,5},{5... | collective-permute-start | bytes 589832 | tf_op jit(solution)/shard_map/ppermute | solution.py:88
  82.9 4.8 %collective-permute-start.25 = (bf16[4,192,128]{2,1,0:T(8,128)(2,1)S(1)}, bf16[4,192,128]{2,1,0:T(8,128)(2,1)S(1)}, u32[]{:S(2)}, u32[]{:S(2)}) collective-permute-start(bf16[4,192,128]{2,1,0:T(8,128)(2,1)S(1)} %collective-permute-done.23.refs_1_), channel_id=1, source_target_pairs={{0,4},{4,0},{8,12},{12,8},{16,20},{20,16},{24,28},{28,24},{1,5},{5... | collective-permute-start | bytes 589832 | tf_op jit(solution)/shard_map/ppermute | solution.py:88
  82.9 4.8 %collective-permute-start.24 = (bf16[4,192,128]{2,1,0:T(8,128)(2,1)S(1)}, bf16[4,192,128]{2,1,0:T(8,128)(2,1)S(1)}, u32[]{:S(2)}, u32[]{:S(2)}) collective-permute-start(bf16[4,192,128]{2,1,0:T(8,128)(2,1)S(1)} %collective-permute-done.18.refs_0_), channel_id=1, source_target_pairs={{0,4},{4,0},{8,12},{12,8},{16,20},{20,16},{24,28},{28,24},{1,5},{5... | collective-permute-start | bytes 589832 | tf_op jit(solution)/shard_map/ppermute | solution.py:88
  84.2 7.0 %collective-permute-start.32 = (bf16[2,192,128]{2,1,0:T(8,128)(2,1)S(1)}, bf16[2,192,128]{2,1,0:T(8,128)(2,1)S(1)}, u32[]{:S(2)}, u32[]{:S(2)}) collective-permute-start(bf16[2,192,128]{2,1,0:T(8,128)(2,1)S(1)} %get-tuple-element.76), channel_id=1, source_target_pairs={{0,8},{4,12},{8,0},{12,4},{16,24},{20,28},{24,16},{28,20},{1,9},{5... | collective-permute-start | bytes 294920 | tf_op jit(solution)/shard_map/ppermute | solution.py:88
  85.7 6.3 %collective-permute-start.33 = (bf16[2,192,128]{2,1,0:T(8,128)(2,1)S(1)}, bf16[2,192,128]{2,1,0:T(8,128)(2,1)S(1)}, u32[]{:S(2)}, u32[]{:S(2)}) collective-permute-start(bf16[2,192,128]{2,1,0:T(8,128)(2,1)S(1)} %get-tuple-element.77), channel_id=1, source_target_pairs={{0,16},{4,20},{8,24},{12,28},{16,0},{20,4},{24,8},{28,12},{1,17},{... | collective-permute-start | bytes 294920 | tf_op jit(solution)/shard_map/ppermute | solution.py:88
  86.8 6.3 %collective-permute-start.34 = (bf16[2,192,128]{2,1,0:T(8,128)(2,1)S(1)}, bf16[2,192,128]{2,1,0:T(8,128)(2,1)S(1)}, u32[]{:S(2)}, u32[]{:S(2)}) collective-permute-start(bf16[2,192,128]{2,1,0:T(8,128)(2,1)S(1)} %get-tuple-element.78), channel_id=1, source_target_pairs={{0,24},{4,28},{8,16},{12,20},{16,8},{20,12},{24,0},{28,4},{1,25},{... | collective-permute-start | bytes 294920 | tf_op jit(solution)/shard_map/ppermute | solution.py:88
  88.5 5.7 %collective-permute-start.26 = (bf16[2,192,128]{2,1,0:T(8,128)(2,1)S(1)}, bf16[2,192,128]{2,1,0:T(8,128)(2,1)S(1)}, u32[]{:S(2)}, u32[]{:S(2)}) collective-permute-start(bf16[2,192,128]{2,1,0:T(8,128)(2,1)S(1)} %get-tuple-element.70), channel_id=1, source_target_pairs={{0,8},{4,12},{8,0},{12,4},{16,24},{20,28},{24,16},{28,20},{1,9},{5... | collective-permute-start | bytes 294920 | tf_op jit(solution)/shard_map/ppermute | solution.py:88
  90.1 5.6 %collective-permute-start.27 = (bf16[2,192,128]{2,1,0:T(8,128)(2,1)S(1)}, bf16[2,192,128]{2,1,0:T(8,128)(2,1)S(1)}, u32[]{:S(2)}, u32[]{:S(2)}) collective-permute-start(bf16[2,192,128]{2,1,0:T(8,128)(2,1)S(1)} %get-tuple-element.71), channel_id=1, source_target_pairs={{0,16},{4,20},{8,24},{12,28},{16,0},{20,4},{24,8},{28,12},{1,17},{... | collective-permute-start | bytes 294920 | tf_op jit(solution)/shard_map/ppermute | solution.py:88
  91.2 5.5 %collective-permute-start.28 = (bf16[2,192,128]{2,1,0:T(8,128)(2,1)S(1)}, bf16[2,192,128]{2,1,0:T(8,128)(2,1)S(1)}, u32[]{:S(2)}, u32[]{:S(2)}) collective-permute-start(bf16[2,192,128]{2,1,0:T(8,128)(2,1)S(1)} %get-tuple-element.72), channel_id=1, source_target_pairs={{0,24},{4,28},{8,16},{12,20},{16,8},{20,12},{24,0},{28,4},{1,25},{... | collective-permute-start | bytes 294920 | tf_op jit(solution)/shard_map/ppermute | solution.py:88

commit v8 on v7

--- a/solution.py
+++ b/solution.py
@@ -362,32 +362,31 @@
     )(*[in_vmem(x) for x in tiles])
 
 
-def pick_kernel(count, order, *refs):
+def pick_kernel(sets, order, *refs):
+    count = sum(map(len, sets))
     kept, swapped, outs = refs[:count], refs[count : 2 * count], refs[2 * count :]
+    chips = len(outs) // len(sets)
     spot = lax.axis_index("expert")
     core = lax.rem(spot, CORES)
-    for flip, out in enumerate(outs):
+    for flip in range(chips):
         source = order[spot ^ (flip * CORES)]
         chip, here = source // CORES, lax.rem(source, CORES) == core
-
-        @pl.when(here)
-        def _():
-            for i in range(count):
-                out[i] = kept[i][chip]
-
-        @pl.when(jnp.logical_not(here))
-        def _():
-            for i in range(count):
-                out[i] = swapped[i][chip]
-
-
-def pick(order, kept, swapped):
+        for blocks, chosen in ((kept, here), (swapped, jnp.logical_not(here))):
+
+            @pl.when(chosen)
+            def _():
+                for n, flips in enumerate(sets):
+                    for i, k in enumerate(flips):
+                        outs[n * chips + flip][i] = blocks[k][chip]
+
+
+def pick(order, kept, swapped, sets):
     chips, *tile = kept[0].shape
-    count = len(kept)
-    return pl.pallas_call(
-        functools.partial(pick_kernel, count),
-        out_shape=[pltpu.VMEM((count, *tile), BF16)] * chips,
-        in_specs=[smem()] + [whole()] * (2 * count),
+    return pl.pallas_call(
+        functools.partial(pick_kernel, sets),
+        out_shape=[pltpu.VMEM((len(flips), *tile), BF16) for flips in sets for _ in range(chips)],
+        in_specs=[smem()] + [whole()] * (2 * len(kept)),
+        compiler_params=pltpu.CompilerParams(vmem_limit_bytes=VMEM_BYTES),
         name="pick",
     )(order, *[in_vmem(x) for x in [*kept, *swapped]])
 
@@ -460,9 +459,11 @@
             kept[k] = partner(x, "dp", k) if k else x
     swapped = {k: partner(x, "expert", 1) for k, x in kept.items()}
     sets = ((1, 0), (3, 2))
+    every = range(groups)
+    chosen = pick(placement, [kept[k] for k in every], [swapped[k] for k in every], sets)
     out = None
-    for flips in sets:
-        picked = pick(placement, [kept[k] for k in flips], [swapped[k] for k in flips])
+    for n, flips in enumerate(sets):
+        picked = chosen[n * planes : (n + 1) * planes]
         landed = [picked[0]] + [
             partner(picked[k], "expert", k * CORES) for k in range(1, planes)
         ]

time: 97.8 us -> 99.4 us (1.016)
  waiting for transfers between devices: 40.5 us -> 43 us
    ppermute x35, waiting for transfers between devices: 40.5 us -> 43 us  [partner(): return lax.ppermute(x, axis, [(i, i ^ flip) for i in range(size)])]
    unnamed x12 -> x14, local copies, waits for them, and re-layouts: 2.56 us -> 2.56 us
  transfers between devices with their start and end apart: 35 -> 35, of which waited for: 18 -> 18; matrix products, arithmetic and copies ran while one was open for 0% -> 0% of each run, Pallas kernels for 9% -> 7%
where the time goes in v8:
time: 99.4 us; the launch traced here: 99.2 us
  starting transfers between devices  43.2 us (43%)
  waiting for transfers between devices  43 us (43%)
  Pallas kernels  10.4 us (10%)
  local copies, waits for them, and re-layouts  2.56 us (3%)
    ppermute x35, starting transfers between devices, partner(): return lax.ppermute(x, axis, [(i, i ^ flip) for i in range(size)])  43.2 us
    ppermute x35, waiting for transfers between devices, partner(): return lax.ppermute(x, axis, [(i, i ^ flip) for i in range(size)])  43 us
    unnamed x14, local copies, waits for them, and re-layouts  2.56 us
    pallas_call x1, Pallas kernels, start_hidden(): pl.pallas_call(functools.partial(start_kernel, len(pieces), flips), out_s...  2.23 us
  transfers between devices with their start and end apart: 35, of which 18 were waited for; matrix products, arithmetic and copies ran while one was open for 0% of the time, Pallas kernels for 7%

profile of v8, /device:TPU:0, one launch (start us, length us, event | category | flops | bytes accessed | tf_op | source)
XLA Modules:
  0.0 99.2 jit_solution(14967952259756354801)
XLA Ops:
  0.0 1.0 pack_rows.1
  1.0 3.1 %collective-permute-start = (bf16[16,2688]{1,0:T(8,128)(2,1)S(1)}, bf16[16,2688]{1,0:T(8,128)(2,1)S(1)}, u32[]{:S(2)}, u32[]{:S(2)}) collective-permute-start(bf16[16,2688]{1,0:T(8,128)(2,1)S(1)} %get-tuple-element.45), channel_id=1, source_target_pairs={{0,1},{1,0},{2,3},{3,2},{4,5},{5,4},{6,7},{7,6},{8,9},{9,8},{10,11... | collective-permute-start | bytes 258056 | tf_op jit(solution)/shard_map/ppermute | solution.py:88
  4.0 2.6 %collective-permute-start.1 = (bf16[16,2688]{1,0:T(8,128)(2,1)S(1)}, bf16[16,2688]{1,0:T(8,128)(2,1)S(1)}, u32[]{:S(2)}, u32[]{:S(2)}) collective-permute-start(bf16[16,2688]{1,0:T(8,128)(2,1)S(1)} %get-tuple-element.46), channel_id=1, source_target_pairs={{0,2},{1,3},{2,0},{3,1},{4,6},{5,7},{6,4},{7,5},{8,10},{9,11},{10,... | collective-permute-start | bytes 258056 | tf_op jit(solution)/shard_map/ppermute | solution.py:88
  6.6 1.4 %copy-done = bf16[1,512,1536]{2,1,0:T(8,128)(2,1)S(1)} copy-done((bf16[1,512,1536]{2,1,0:T(8,128)(2,1)S(1)}, bf16[1,512,1536]{2,1,0:T(8,128)(2,1)}, u32[]{:S(2)}) %copy-start) | copy-done | bytes 1572888
  8.0 1.4 %pack_weights.1 = (bf16[512,384]{1,0:T(8,128)(2,1)S(1)}, bf16[512,384]{1,0:T(8,128)(2,1)S(1)}, bf16[512,384]{1,0:T(8,128)(2,1)}, bf16[512,384]{1,0:T(8,128)(2,1)S(1)}) custom-call(bf16[512,1536]{1,0:T(8,128)(2,1)S(1)} %bitcast.14), custom_call_target="tpu_custom_call" | custom-call | tf_op jit(solution)/shard_map/pack_weights/pallas_call | solution.py:166
  9.5 1.9 %collective-permute-start.10 = (bf16[512,384]{1,0:T(8,128)(2,1)}, bf16[512,384]{1,0:T(8,128)(2,1)}, u32[]{:S(2)}, u32[]{:S(2)}) collective-permute-start(bf16[512,384]{1,0:T(8,128)(2,1)} %get-tuple-element.50), channel_id=1, source_target_pairs={{0,2},{1,3},{2,0},{3,1},{4,6},{5,7},{6,4},{7,5},{8,10},{9,11},{10,... | collective-permute-start | bytes 1179656 | tf_op jit(solution)/shard_map/ppermute | solution.py:88
  11.4 1.1 %copy-done.3 = bf16[1,512,768]{2,1,0:T(8,128)(2,1)S(1)} copy-done((bf16[1,512,768]{2,1,0:T(8,128)(2,1)S(1)}, bf16[1,512,768]{2,1,0:T(8,128)(2,1)}, u32[]{:S(2)}) %copy-start.3) | copy-done | bytes 786456
  12.5 0.7 transposed.1
  13.2 8.9 %collective-permute-done.1.refs_2_ = bf16[16,2688]{1,0:T(8,128)(2,1)S(1)} collective-permute-done((bf16[16,2688]{1,0:T(8,128)(2,1)S(1)}, bf16[16,2688]{1,0:T(8,128)(2,1)S(1)}, u32[]{:S(2)}, u32[]{:S(2)}) %collective-permute-start.1) | collective-permute-done | bytes 86048 | tf_op jit(solution)/shard_map/ppermute | solution.py:88
  22.1 1.6 %collective-permute-start.3 = (bf16[64,2688]{1,0:T(8,128)(2,1)S(1)}, bf16[64,2688]{1,0:T(8,128)(2,1)S(1)}, u32[]{:S(2)}, u32[]{:S(2)}) collective-permute-start(bf16[64,2688]{1,0:T(8,128)(2,1)S(1)} %bitcast.8), channel_id=1, source_target_pairs={{0,8},{4,12},{8,0},{12,4},{16,24},{20,28},{24,16},{28,20},{1,9},{5... | collective-permute-start | bytes 1032200 | tf_op jit(solution)/shard_map/ppermute | solution.py:88
  23.7 1.5 %collective-permute-start.5 = (bf16[64,2688]{1,0:T(8,128)(2,1)S(1)}, bf16[64,2688]{1,0:T(8,128)(2,1)S(1)}, u32[]{:S(2)}, u32[]{:S(2)}) collective-permute-start(bf16[64,2688]{1,0:T(8,128)(2,1)S(1)} %bitcast.9), channel_id=1, source_target_pairs={{0,24},{4,28},{8,16},{12,20},{16,8},{20,12},{24,0},{28,4},{1,25},{... | collective-permute-start | bytes 1032200 | tf_op jit(solution)/shard_map/ppermute | solution.py:88
  25.7 3.8 %collective-permute-done.3.refs_1_ = bf16[64,2688]{1,0:T(8,128)(2,1)S(1)} collective-permute-done((bf16[64,2688]{1,0:T(8,128)(2,1)S(1)}, bf16[64,2688]{1,0:T(8,128)(2,1)S(1)}, u32[]{:S(2)}, u32[]{:S(2)}) %collective-permute-start.3) | collective-permute-done | bytes 344096 | tf_op jit(solution)/shard_map/ppermute | solution.py:88
  29.4 6.1 %collective-permute-start.11 = (bf16[512,384]{1,0:T(8,128)(2,1)}, bf16[512,384]{1,0:T(8,128)(2,1)S(1)}, u32[]{:S(2)}, u32[]{:S(2)}) collective-permute-start(bf16[512,384]{1,0:T(8,128)(2,1)} %copy-done.6), channel_id=1, source_target_pairs={{0,1},{1,0},{2,3},{3,2},{4,5},{5,4},{6,7},{7,6},{8,9},{9,8},{10,11... | collective-permute-start | bytes 1179656 | tf_op jit(solution)/shard_map/ppermute | solution.py:88
  35.6 2.6 %collective-permute-start.12 = (bf16[512,384]{1,0:T(8,128)(2,1)}, bf16[512,384]{1,0:T(8,128)(2,1)S(1)}, u32[]{:S(2)}, u32[]{:S(2)}) collective-permute-start(bf16[512,384]{1,0:T(8,128)(2,1)} %copy-done.5), channel_id=1, source_target_pairs={{0,3},{1,2},{2,1},{3,0},{4,7},{5,6},{6,5},{7,4},{8,11},{9,10},{10,... | collective-permute-start | bytes 1179656 | tf_op jit(solution)/shard_map/ppermute | solution.py:88
  38.8 1.1 %collective-permute-done.9.refs_7_ = bf16[64,2688]{1,0:T(8,128)(2,1)S(1)} collective-permute-done((bf16[64,2688]{1,0:T(8,128)(2,1)S(1)}, bf16[64,2688]{1,0:T(8,128)(2,1)S(1)}, u32[]{:S(2)}, u32[]{:S(2)}) %collective-permute-start.9) | collective-permute-done | bytes 344096 | tf_op jit(solution)/shard_map/ppermute | solution.py:88
  40.8 3.9 %collective-permute-done.11.refs_10_ = bf16[512,384]{1,0:T(8,128)(2,1)S(1)} collective-permute-done((bf16[512,384]{1,0:T(8,128)(2,1)}, bf16[512,384]{1,0:T(8,128)(2,1)S(1)}, u32[]{:S(2)}, u32[]{:S(2)}) %collective-permute-start.11) | collective-permute-done | bytes 393248 | tf_op jit(solution)/shard_map/ppermute | solution.py:88
  44.7 2.2 %start_hidden.1 = (f32[512,384]{1,0:T(8,128)S(1)}, bf16[512,512]{1,0:T(8,128)(2,1)S(1)}) custom-call(bf16[64,2688]{1,0:T(8,128)(2,1)S(1)} %bitcast.12, bf16[64,2688]{1,0:T(8,128)(2,1)S(1)} %collective-permute-done.3.refs_1_, bf16[64,2688]{1,0:T(8,128)(2,1)S(1)} %collective-permute-done.4.refs_2_, bf16[64,2688]{1,0:T(8,128)(2,1)S(1)} %collective-permute-done.5.refs_3_, ...), custom_call_target="tpu_custom_call" | custom-call | tf_op jit(solution)/shard_map/start_hidden/pallas_call | solution.py:229
  47.0 2.0 %collective-permute-done.12.refs_0_ = bf16[512,384]{1,0:T(8,128)(2,1)S(1)} collective-permute-done((bf16[512,384]{1,0:T(8,128)(2,1)}, bf16[512,384]{1,0:T(8,128)(2,1)S(1)}, u32[]{:S(2)}, u32[]{:S(2)}) %collective-permute-start.12) | collective-permute-done | bytes 393248 | tf_op jit(solution)/shard_map/ppermute | solution.py:88
  49.0 0.6 end_hidden.1.refs_0_
  49.8 2.9 %collective-permute-start.18 = (bf16[192,512]{1,0:T(8,128)(2,1)S(1)}, bf16[192,512]{1,0:T(8,128)(2,1)S(1)}, u32[]{:S(2)}, u32[]{:S(2)}) collective-permute-start(bf16[192,512]{1,0:T(8,128)(2,1)S(1)} %end_hidden.1.refs_0_), channel_id=1, source_target_pairs={{0,1},{1,0},{2,3},{3,2},{4,5},{5,4},{6,7},{7,6},{8,9},{9,8},{10,11... | collective-permute-start | bytes 589832 | tf_op jit(solution)/shard_map/ppermute | solution.py:88
  52.6 5.9 %collective-permute-done.13.refs_1_ = bf16[192,512]{1,0:T(8,128)(2,1)S(1)} collective-permute-done((bf16[192,512]{1,0:T(8,128)(2,1)S(1)}, bf16[192,512]{1,0:T(8,128)(2,1)S(1)}, u32[]{:S(2)}, u32[]{:S(2)}) %collective-permute-start.13) | collective-permute-done | bytes 196640 | tf_op jit(solution)/shard_map/ppermute | solution.py:88
  58.7 0.9 collective-permute-done.18.refs_0_
  59.6 0.9 update_tiles.3
  60.6 1.6 %collective-permute-start.19 = (bf16[2,192,128]{2,1,0:T(8,128)(2,1)S(1)}, bf16[2,192,128]{2,1,0:T(8,128)(2,1)S(1)}, u32[]{:S(2)}, u32[]{:S(2)}) collective-permute-start(bf16[2,192,128]{2,1,0:T(8,128)(2,1)S(1)} %get-tuple-element.65), channel_id=1, source_target_pairs={{0,8},{4,12},{8,0},{12,4},{16,24},{20,28},{24,16},{28,20},{1,9},{5... | collective-permute-start | bytes 294920 | tf_op jit(solution)/shard_map/ppermute | solution.py:88
  62.1 1.0 %collective-permute-start.20 = (bf16[2,192,128]{2,1,0:T(8,128)(2,1)S(1)}, bf16[2,192,128]{2,1,0:T(8,128)(2,1)S(1)}, u32[]{:S(2)}, u32[]{:S(2)}) collective-permute-start(bf16[2,192,128]{2,1,0:T(8,128)(2,1)S(1)} %get-tuple-element.66), channel_id=1, source_target_pairs={{0,16},{4,20},{8,24},{12,28},{16,0},{20,4},{24,8},{28,12},{1,17},{... | collective-permute-start | bytes 294920 | tf_op jit(solution)/shard_map/ppermute | solution.py:88
  63.1 1.0 %collective-permute-start.21 = (bf16[2,192,128]{2,1,0:T(8,128)(2,1)S(1)}, bf16[2,192,128]{2,1,0:T(8,128)(2,1)S(1)}, u32[]{:S(2)}, u32[]{:S(2)}) collective-permute-start(bf16[2,192,128]{2,1,0:T(8,128)(2,1)S(1)} %get-tuple-element.67), channel_id=1, source_target_pairs={{0,24},{4,28},{8,16},{12,20},{16,8},{20,12},{24,0},{28,4},{1,25},{... | collective-permute-start | bytes 294920 | tf_op jit(solution)/shard_map/ppermute | solution.py:88
  64.2 0.9 update_tiles.2
  65.1 1.6 %collective-permute-start.15 = (bf16[2,192,128]{2,1,0:T(8,128)(2,1)S(1)}, bf16[2,192,128]{2,1,0:T(8,128)(2,1)S(1)}, u32[]{:S(2)}, u32[]{:S(2)}) collective-permute-start(bf16[2,192,128]{2,1,0:T(8,128)(2,1)S(1)} %get-tuple-element.60), channel_id=1, source_target_pairs={{0,8},{4,12},{8,0},{12,4},{16,24},{20,28},{24,16},{28,20},{1,9},{5... | collective-permute-start | bytes 294920 | tf_op jit(solution)/shard_map/ppermute | solution.py:88
  66.7 1.5 %collective-permute-start.16 = (bf16[2,192,128]{2,1,0:T(8,128)(2,1)S(1)}, bf16[2,192,128]{2,1,0:T(8,128)(2,1)S(1)}, u32[]{:S(2)}, u32[]{:S(2)}) collective-permute-start(bf16[2,192,128]{2,1,0:T(8,128)(2,1)S(1)} %get-tuple-element.61), channel_id=1, source_target_pairs={{0,16},{4,20},{8,24},{12,28},{16,0},{20,4},{24,8},{28,12},{1,17},{... | collective-permute-start | bytes 294920 | tf_op jit(solution)/shard_map/ppermute | solution.py:88
  68.7 0.7 collective-permute-done.21.refs_3_
  69.4 1.2 %collective-permute-start.22 = (bf16[4,192,128]{2,1,0:T(8,128)(2,1)S(1)}, bf16[4,192,128]{2,1,0:T(8,128)(2,1)S(1)}, u32[]{:S(2)}, u32[]{:S(2)}) collective-permute-start(bf16[4,192,128]{2,1,0:T(8,128)(2,1)S(1)} %get-tuple-element.68), channel_id=1, source_target_pairs={{0,1},{1,0},{2,3},{3,2},{4,5},{5,4},{6,7},{7,6},{8,9},{9,8},{10,11... | collective-permute-start | bytes 589832 | tf_op jit(solution)/shard_map/ppermute | solution.py:88
  70.6 1.6 %collective-permute-start.23 = (bf16[4,192,128]{2,1,0:T(8,128)(2,1)S(1)}, bf16[4,192,128]{2,1,0:T(8,128)(2,1)S(1)}, u32[]{:S(2)}, u32[]{:S(2)}) collective-permute-start(bf16[4,192,128]{2,1,0:T(8,128)(2,1)S(1)} %get-tuple-element.69), channel_id=1, source_target_pairs={{0,2},{1,3},{2,0},{3,1},{4,6},{5,7},{6,4},{7,5},{8,10},{9,11},{10,... | collective-permute-start | bytes 589832 | tf_op jit(solution)/shard_map/ppermute | solution.py:88
  72.2 1.5 %collective-permute-done.17.refs_3_ = bf16[2,192,128]{2,1,0:T(8,128)(2,1)S(1)} collective-permute-done((bf16[2,192,128]{2,1,0:T(8,128)(2,1)S(1)}, bf16[2,192,128]{2,1,0:T(8,128)(2,1)S(1)}, u32[]{:S(2)}, u32[]{:S(2)}) %collective-permute-start.17) | collective-permute-done | bytes 98336 | tf_op jit(solution)/shard_map/ppermute | solution.py:88
  73.8 1.7 %collective-permute-start.24 = (bf16[4,192,128]{2,1,0:T(8,128)(2,1)S(1)}, bf16[4,192,128]{2,1,0:T(8,128)(2,1)S(1)}, u32[]{:S(2)}, u32[]{:S(2)}) collective-permute-start(bf16[4,192,128]{2,1,0:T(8,128)(2,1)S(1)} %get-tuple-element.70), channel_id=1, source_target_pairs={{0,3},{1,2},{2,1},{3,0},{4,7},{5,6},{6,5},{7,4},{8,11},{9,10},{10,... | collective-permute-start | bytes 589832 | tf_op jit(solution)/shard_map/ppermute | solution.py:88
  75.5 3.1 %collective-permute-done.22.refs_1_ = bf16[4,192,128]{2,1,0:T(8,128)(2,1)S(1)} collective-permute-done((bf16[4,192,128]{2,1,0:T(8,128)(2,1)S(1)}, bf16[4,192,128]{2,1,0:T(8,128)(2,1)S(1)}, u32[]{:S(2)}, u32[]{:S(2)}) %collective-permute-start.22) | collective-permute-done | bytes 196640 | tf_op jit(solution)/shard_map/ppermute | solution.py:88
  78.6 4.3 %collective-permute-done.23.refs_2_ = bf16[4,192,128]{2,1,0:T(8,128)(2,1)S(1)} collective-permute-done((bf16[4,192,128]{2,1,0:T(8,128)(2,1)S(1)}, bf16[4,192,128]{2,1,0:T(8,128)(2,1)S(1)}, u32[]{:S(2)}, u32[]{:S(2)}) %collective-permute-start.23) | collective-permute-done | bytes 196640 | tf_op jit(solution)/shard_map/ppermute | solution.py:88
  83.4 0.9 collective-permute-done.27.refs_6_
  84.6 0.7 pick.1
  85.3 1.5 %collective-permute-start.32 = (bf16[2,192,128]{2,1,0:T(8,128)(2,1)S(1)}, bf16[2,192,128]{2,1,0:T(8,128)(2,1)S(1)}, u32[]{:S(2)}, u32[]{:S(2)}) collective-permute-start(bf16[2,192,128]{2,1,0:T(8,128)(2,1)S(1)} %get-tuple-element.76), channel_id=1, source_target_pairs={{0,8},{4,12},{8,0},{12,4},{16,24},{20,28},{24,16},{28,20},{1,9},{5... | collective-permute-start | bytes 294920 | tf_op jit(solution)/shard_map/ppermute | solution.py:88
  86.8 0.5 collective-permute-start.29
  87.4 1.3 %collective-permute-start.33 = (bf16[2,192,128]{2,1,0:T(8,128)(2,1)S(1)}, bf16[2,192,128]{2,1,0:T(8,128)(2,1)S(1)}, u32[]{:S(2)}, u32[]{:S(2)}) collective-permute-start(bf16[2,192,128]{2,1,0:T(8,128)(2,1)S(1)} %get-tuple-element.77), channel_id=1, source_target_pairs={{0,16},{4,20},{8,24},{12,28},{16,0},{20,4},{24,8},{28,12},{1,17},{... | collective-permute-start | bytes 294920 | tf_op jit(solution)/shard_map/ppermute | solution.py:88
  88.7 1.7 %collective-permute-start.34 = (bf16[2,192,128]{2,1,0:T(8,128)(2,1)S(1)}, bf16[2,192,128]{2,1,0:T(8,128)(2,1)S(1)}, u32[]{:S(2)}, u32[]{:S(2)}) collective-permute-start(bf16[2,192,128]{2,1,0:T(8,128)(2,1)S(1)} %get-tuple-element.78), channel_id=1, source_target_pairs={{0,24},{4,28},{8,16},{12,20},{16,8},{20,12},{24,0},{28,4},{1,25},{... | collective-permute-start | bytes 294920 | tf_op jit(solution)/shard_map/ppermute | solution.py:88
  90.3 1.1 %collective-permute-start.30 = (bf16[2,192,128]{2,1,0:T(8,128)(2,1)S(1)}, bf16[2,192,128]{2,1,0:T(8,128)(2,1)S(1)}, u32[]{:S(2)}, u32[]{:S(2)}) collective-permute-start(bf16[2,192,128]{2,1,0:T(8,128)(2,1)S(1)} %get-tuple-element.73), channel_id=1, source_target_pairs={{0,16},{4,20},{8,24},{12,28},{16,0},{20,4},{24,8},{28,12},{1,17},{... | collective-permute-start | bytes 294920 | tf_op jit(solution)/shard_map/ppermute | solution.py:88
  91.4 1.6 %collective-permute-start.31 = (bf16[2,192,128]{2,1,0:T(8,128)(2,1)S(1)}, bf16[2,192,128]{2,1,0:T(8,128)(2,1)S(1)}, u32[]{:S(2)}, u32[]{:S(2)}) collective-permute-start(bf16[2,192,128]{2,1,0:T(8,128)(2,1)S(1)} %get-tuple-element.74), channel_id=1, source_target_pairs={{0,24},{4,28},{8,16},{12,20},{16,8},{20,12},{24,0},{28,4},{1,25},{... | collective-permute-start | bytes 294920 | tf_op jit(solution)/shard_map/ppermute | solution.py:88
  93.0 3.0 %collective-permute-done.34.refs_3_ = bf16[2,192,128]{2,1,0:T(8,128)(2,1)S(1)} collective-permute-done((bf16[2,192,128]{2,1,0:T(8,128)(2,1)S(1)}, bf16[2,192,128]{2,1,0:T(8,128)(2,1)S(1)}, u32[]{:S(2)}, u32[]{:S(2)}) %collective-permute-start.34) | collective-permute-done | bytes 98336 | tf_op jit(solution)/shard_map/ppermute | solution.py:88
  96.0 0.8 unpack.2.refs_4_
  96.8 1.5 %collective-permute-done.30.refs_2_ = bf16[2,192,128]{2,1,0:T(8,128)(2,1)S(1)} collective-permute-done((bf16[2,192,128]{2,1,0:T(8,128)(2,1)S(1)}, bf16[2,192,128]{2,1,0:T(8,128)(2,1)S(1)}, u32[]{:S(2)}, u32[]{:S(2)}) %collective-permute-start.30) | collective-permute-done | bytes 98336 | tf_op jit(solution)/shard_map/ppermute | solution.py:88
  98.4 0.8 unpack.3
  (50 shorter events, 3.8 us)
Async XLA Ops:
  1.0 8.5 %collective-permute-start = (bf16[16,2688]{1,0:T(8,128)(2,1)S(1)}, bf16[16,2688]{1,0:T(8,128)(2,1)S(1)}, u32[]{:S(2)}, u32[]{:S(2)}) collective-permute-start(bf16[16,2688]{1,0:T(8,128)(2,1)S(1)} %get-tuple-element.45), channel_id=1, source_target_pairs={{0,1},{1,0},{2,3},{3,2},{4,5},{5,4},{6,7},{7,6},{8,9},{9,8},{10,11... | collective-permute-start | bytes 258056 | tf_op jit(solution)/shard_map/ppermute | solution.py:88
  4.0 18.0 %collective-permute-start.1 = (bf16[16,2688]{1,0:T(8,128)(2,1)S(1)}, bf16[16,2688]{1,0:T(8,128)(2,1)S(1)}, u32[]{:S(2)}, u32[]{:S(2)}) collective-permute-start(bf16[16,2688]{1,0:T(8,128)(2,1)S(1)} %get-tuple-element.46), channel_id=1, source_target_pairs={{0,2},{1,3},{2,0},{3,1},{4,6},{5,7},{6,4},{7,5},{8,10},{9,11},{10,... | collective-permute-start | bytes 258056 | tf_op jit(solution)/shard_map/ppermute | solution.py:88
  6.6 15.4 %collective-permute-start.2 = (bf16[16,2688]{1,0:T(8,128)(2,1)S(1)}, bf16[16,2688]{1,0:T(8,128)(2,1)S(1)}, u32[]{:S(2)}, u32[]{:S(2)}) collective-permute-start(bf16[16,2688]{1,0:T(8,128)(2,1)S(1)} %get-tuple-element.47), channel_id=1, source_target_pairs={{0,3},{1,2},{2,1},{3,0},{4,7},{5,6},{6,5},{7,4},{8,11},{9,10},{10,... | collective-permute-start | bytes 258056 | tf_op jit(solution)/shard_map/ppermute | solution.py:88
  6.6 1.4 %copy-start = (bf16[1,512,1536]{2,1,0:T(8,128)(2,1)S(1)}, bf16[1,512,1536]{2,1,0:T(8,128)(2,1)}, u32[]{:S(2)}) copy-start(bf16[1,512,1536]{2,1,0:T(8,128)(2,1)} %param.13) | copy-start | bytes 4718596
  8.0 3.3 %copy-start.1 = (bf16[1,512,768]{2,1,0:T(8,128)(2,1)S(1)}, bf16[1,512,768]{2,1,0:T(8,128)(2,1)}, u32[]{:S(2)}) copy-start(bf16[1,512,768]{2,1,0:T(8,128)(2,1)} %param.14) | copy-start | bytes 2359300
  8.0 3.3 %copy-start.2 = (bf16[1,512,768]{2,1,0:T(8,128)(2,1)S(1)}, bf16[1,512,768]{2,1,0:T(8,128)(2,1)}, u32[]{:S(2)}) copy-start(bf16[1,512,768]{2,1,0:T(8,128)(2,1)} %param.15) | copy-start | bytes 2359300
  9.4 12.6 %copy-start.5 = (bf16[512,384]{1,0:T(8,128)(2,1)}, bf16[512,384]{1,0:T(8,128)(2,1)S(1)}, u32[]{:S(2)}) copy-start(bf16[512,384]{1,0:T(8,128)(2,1)S(1)} %get-tuple-element.56) | copy-start | bytes 1179652
  9.4 12.6 %copy-start.6 = (bf16[512,384]{1,0:T(8,128)(2,1)}, bf16[512,384]{1,0:T(8,128)(2,1)S(1)}, u32[]{:S(2)}) copy-start(bf16[512,384]{1,0:T(8,128)(2,1)S(1)} %get-tuple-element.52) | copy-start | bytes 1179652
  9.5 26.1 %collective-permute-start.10 = (bf16[512,384]{1,0:T(8,128)(2,1)}, bf16[512,384]{1,0:T(8,128)(2,1)}, u32[]{:S(2)}, u32[]{:S(2)}) collective-permute-start(bf16[512,384]{1,0:T(8,128)(2,1)} %get-tuple-element.50), channel_id=1, source_target_pairs={{0,2},{1,3},{2,0},{3,1},{4,6},{5,7},{6,4},{7,5},{8,10},{9,11},{10,... | collective-permute-start | bytes 1179656 | tf_op jit(solution)/shard_map/ppermute | solution.py:88
  11.4 1.1 %copy-start.3 = (bf16[1,512,768]{2,1,0:T(8,128)(2,1)S(1)}, bf16[1,512,768]{2,1,0:T(8,128)(2,1)}, u32[]{:S(2)}) copy-start(bf16[1,512,768]{2,1,0:T(8,128)(2,1)} %param.16) | copy-start | bytes 2359300
  22.1 7.3 %collective-permute-start.3 = (bf16[64,2688]{1,0:T(8,128)(2,1)S(1)}, bf16[64,2688]{1,0:T(8,128)(2,1)S(1)}, u32[]{:S(2)}, u32[]{:S(2)}) collective-permute-start(bf16[64,2688]{1,0:T(8,128)(2,1)S(1)} %bitcast.8), channel_id=1, source_target_pairs={{0,8},{4,12},{8,0},{12,4},{16,24},{20,28},{24,16},{28,20},{1,9},{5... | collective-permute-start | bytes 1032200 | tf_op jit(solution)/shard_map/ppermute | solution.py:88
  23.7 14.5 %collective-permute-start.5 = (bf16[64,2688]{1,0:T(8,128)(2,1)S(1)}, bf16[64,2688]{1,0:T(8,128)(2,1)S(1)}, u32[]{:S(2)}, u32[]{:S(2)}) collective-permute-start(bf16[64,2688]{1,0:T(8,128)(2,1)S(1)} %bitcast.9), channel_id=1, source_target_pairs={{0,24},{4,28},{8,16},{12,20},{16,8},{20,12},{24,0},{28,4},{1,25},{... | collective-permute-start | bytes 1032200 | tf_op jit(solution)/shard_map/ppermute | solution.py:88
  25.2 13.0 %collective-permute-start.4 = (bf16[64,2688]{1,0:T(8,128)(2,1)S(1)}, bf16[64,2688]{1,0:T(8,128)(2,1)S(1)}, u32[]{:S(2)}, u32[]{:S(2)}) collective-permute-start(bf16[64,2688]{1,0:T(8,128)(2,1)S(1)} %bitcast.10), channel_id=1, source_target_pairs={{0,16},{4,20},{8,24},{12,28},{16,0},{20,4},{24,8},{28,12},{1,17},{... | collective-permute-start | bytes 1032200 | tf_op jit(solution)/shard_map/ppermute | solution.py:88
  25.7 13.0 %collective-permute-start.6 = (bf16[64,2688]{1,0:T(8,128)(2,1)S(1)}, bf16[64,2688]{1,0:T(8,128)(2,1)S(1)}, u32[]{:S(2)}, u32[]{:S(2)}) collective-permute-start(bf16[64,2688]{1,0:T(8,128)(2,1)S(1)} %bitcast.11), channel_id=1, source_target_pairs={{0,4},{4,0},{8,12},{12,8},{16,20},{20,16},{24,28},{28,24},{1,5},{5... | collective-permute-start | bytes 1032200 | tf_op jit(solution)/shard_map/ppermute | solution.py:88
  29.4 15.3 %collective-permute-start.11 = (bf16[512,384]{1,0:T(8,128)(2,1)}, bf16[512,384]{1,0:T(8,128)(2,1)S(1)}, u32[]{:S(2)}, u32[]{:S(2)}) collective-permute-start(bf16[512,384]{1,0:T(8,128)(2,1)} %copy-done.6), channel_id=1, source_target_pairs={{0,1},{1,0},{2,3},{3,2},{4,5},{5,4},{6,7},{7,6},{8,9},{9,8},{10,11... | collective-permute-start | bytes 1179656 | tf_op jit(solution)/shard_map/ppermute | solution.py:88
  35.6 13.4 %collective-permute-start.12 = (bf16[512,384]{1,0:T(8,128)(2,1)}, bf16[512,384]{1,0:T(8,128)(2,1)S(1)}, u32[]{:S(2)}, u32[]{:S(2)}) collective-permute-start(bf16[512,384]{1,0:T(8,128)(2,1)} %copy-done.5), channel_id=1, source_target_pairs={{0,3},{1,2},{2,1},{3,0},{4,7},{5,6},{6,5},{7,4},{8,11},{9,10},{10,... | collective-permute-start | bytes 1179656 | tf_op jit(solution)/shard_map/ppermute | solution.py:88
  38.2 1.7 %collective-permute-start.9 = (bf16[64,2688]{1,0:T(8,128)(2,1)S(1)}, bf16[64,2688]{1,0:T(8,128)(2,1)S(1)}, u32[]{:S(2)}, u32[]{:S(2)}) collective-permute-start(bf16[64,2688]{1,0:T(8,128)(2,1)S(1)} %collective-permute-done.5.refs_3_), channel_id=1, source_target_pairs={{0,4},{4,0},{8,12},{12,8},{16,20},{20,16},{24,28},{28,24},{1,5},{5... | collective-permute-start | bytes 1032200 | tf_op jit(solution)/shard_map/ppermute | solution.py:88
  38.2 2.1 %collective-permute-start.8 = (bf16[64,2688]{1,0:T(8,128)(2,1)S(1)}, bf16[64,2688]{1,0:T(8,128)(2,1)S(1)}, u32[]{:S(2)}, u32[]{:S(2)}) collective-permute-start(bf16[64,2688]{1,0:T(8,128)(2,1)S(1)} %collective-permute-done.4.refs_2_), channel_id=1, source_target_pairs={{0,4},{4,0},{8,12},{12,8},{16,20},{20,16},{24,28},{28,24},{1,5},{5... | collective-permute-start | bytes 1032200 | tf_op jit(solution)/shard_map/ppermute | solution.py:88
  38.7 2.1 %collective-permute-start.7 = (bf16[64,2688]{1,0:T(8,128)(2,1)S(1)}, bf16[64,2688]{1,0:T(8,128)(2,1)S(1)}, u32[]{:S(2)}, u32[]{:S(2)}) collective-permute-start(bf16[64,2688]{1,0:T(8,128)(2,1)S(1)} %collective-permute-done.3.refs_1_), channel_id=1, source_target_pairs={{0,4},{4,0},{8,12},{12,8},{16,20},{20,16},{24,28},{28,24},{1,5},{5... | collective-permute-start | bytes 1032200 | tf_op jit(solution)/shard_map/ppermute | solution.py:88
  49.7 8.8 %collective-permute-start.13 = (bf16[192,512]{1,0:T(8,128)(2,1)S(1)}, bf16[192,512]{1,0:T(8,128)(2,1)S(1)}, u32[]{:S(2)}, u32[]{:S(2)}) collective-permute-start(bf16[192,512]{1,0:T(8,128)(2,1)S(1)} %end_hidden.1.refs_0_), channel_id=1, source_target_pairs={{0,2},{1,3},{2,0},{3,1},{4,6},{5,7},{6,4},{7,5},{8,10},{9,11},{10,... | collective-permute-start | bytes 589832 | tf_op jit(solution)/shard_map/ppermute | solution.py:88
  49.8 9.9 %collective-permute-start.18 = (bf16[192,512]{1,0:T(8,128)(2,1)S(1)}, bf16[192,512]{1,0:T(8,128)(2,1)S(1)}, u32[]{:S(2)}, u32[]{:S(2)}) collective-permute-start(bf16[192,512]{1,0:T(8,128)(2,1)S(1)} %end_hidden.1.refs_0_), channel_id=1, source_target_pairs={{0,1},{1,0},{2,3},{3,2},{4,5},{5,4},{6,7},{7,6},{8,9},{9,8},{10,11... | collective-permute-start | bytes 589832 | tf_op jit(solution)/shard_map/ppermute | solution.py:88
  58.5 5.7 %collective-permute-start.14 = (bf16[192,512]{1,0:T(8,128)(2,1)S(1)}, bf16[192,512]{1,0:T(8,128)(2,1)S(1)}, u32[]{:S(2)}, u32[]{:S(2)}) collective-permute-start(bf16[192,512]{1,0:T(8,128)(2,1)S(1)} %collective-permute-done.13.refs_1_), channel_id=1, source_target_pairs={{0,1},{1,0},{2,3},{3,2},{4,5},{5,4},{6,7},{7,6},{8,9},{9,8},{10,11... | collective-permute-start | bytes 589832 | tf_op jit(solution)/shard_map/ppermute | solution.py:88
  60.6 7.6 %collective-permute-start.19 = (bf16[2,192,128]{2,1,0:T(8,128)(2,1)S(1)}, bf16[2,192,128]{2,1,0:T(8,128)(2,1)S(1)}, u32[]{:S(2)}, u32[]{:S(2)}) collective-permute-start(bf16[2,192,128]{2,1,0:T(8,128)(2,1)S(1)} %get-tuple-element.65), channel_id=1, source_target_pairs={{0,8},{4,12},{8,0},{12,4},{16,24},{20,28},{24,16},{28,20},{1,9},{5... | collective-permute-start | bytes 294920 | tf_op jit(solution)/shard_map/ppermute | solution.py:88
  62.1 6.6 %collective-permute-start.20 = (bf16[2,192,128]{2,1,0:T(8,128)(2,1)S(1)}, bf16[2,192,128]{2,1,0:T(8,128)(2,1)S(1)}, u32[]{:S(2)}, u32[]{:S(2)}) collective-permute-start(bf16[2,192,128]{2,1,0:T(8,128)(2,1)S(1)} %get-tuple-element.66), channel_id=1, source_target_pairs={{0,16},{4,20},{8,24},{12,28},{16,0},{20,4},{24,8},{28,12},{1,17},{... | collective-permute-start | bytes 294920 | tf_op jit(solution)/shard_map/ppermute | solution.py:88
  63.1 21.5 %copy-start.4 = (s32[8]{0:T(128)S(1)}, s32[8]{0:T(128)}, u32[]{:S(2)}) copy-start(s32[8]{0:T(128)} %order.1) | copy-start | bytes 100
  63.1 6.3 %collective-permute-start.21 = (bf16[2,192,128]{2,1,0:T(8,128)(2,1)S(1)}, bf16[2,192,128]{2,1,0:T(8,128)(2,1)S(1)}, u32[]{:S(2)}, u32[]{:S(2)}) collective-permute-start(bf16[2,192,128]{2,1,0:T(8,128)(2,1)S(1)} %get-tuple-element.67), channel_id=1, source_target_pairs={{0,24},{4,28},{8,16},{12,20},{16,8},{20,12},{24,0},{28,4},{1,25},{... | collective-permute-start | bytes 294920 | tf_op jit(solution)/shard_map/ppermute | solution.py:88
  65.1 7.0 %collective-permute-start.15 = (bf16[2,192,128]{2,1,0:T(8,128)(2,1)S(1)}, bf16[2,192,128]{2,1,0:T(8,128)(2,1)S(1)}, u32[]{:S(2)}, u32[]{:S(2)}) collective-permute-start(bf16[2,192,128]{2,1,0:T(8,128)(2,1)S(1)} %get-tuple-element.60), channel_id=1, source_target_pairs={{0,8},{4,12},{8,0},{12,4},{16,24},{20,28},{24,16},{28,20},{1,9},{5... | collective-permute-start | bytes 294920 | tf_op jit(solution)/shard_map/ppermute | solution.py:88
  66.7 5.5 %collective-permute-start.16 = (bf16[2,192,128]{2,1,0:T(8,128)(2,1)S(1)}, bf16[2,192,128]{2,1,0:T(8,128)(2,1)S(1)}, u32[]{:S(2)}, u32[]{:S(2)}) collective-permute-start(bf16[2,192,128]{2,1,0:T(8,128)(2,1)S(1)} %get-tuple-element.61), channel_id=1, source_target_pairs={{0,16},{4,20},{8,24},{12,28},{16,0},{20,4},{24,8},{28,12},{1,17},{... | collective-permute-start | bytes 294920 | tf_op jit(solution)/shard_map/ppermute | solution.py:88
  68.2 5.5 %collective-permute-start.17 = (bf16[2,192,128]{2,1,0:T(8,128)(2,1)S(1)}, bf16[2,192,128]{2,1,0:T(8,128)(2,1)S(1)}, u32[]{:S(2)}, u32[]{:S(2)}) collective-permute-start(bf16[2,192,128]{2,1,0:T(8,128)(2,1)S(1)} %get-tuple-element.62), channel_id=1, source_target_pairs={{0,24},{4,28},{8,16},{12,20},{16,8},{20,12},{24,0},{28,4},{1,25},{... | collective-permute-start | bytes 294920 | tf_op jit(solution)/shard_map/ppermute | solution.py:88
  69.4 9.2 %collective-permute-start.22 = (bf16[4,192,128]{2,1,0:T(8,128)(2,1)S(1)}, bf16[4,192,128]{2,1,0:T(8,128)(2,1)S(1)}, u32[]{:S(2)}, u32[]{:S(2)}) collective-permute-start(bf16[4,192,128]{2,1,0:T(8,128)(2,1)S(1)} %get-tuple-element.68), channel_id=1, source_target_pairs={{0,1},{1,0},{2,3},{3,2},{4,5},{5,4},{6,7},{7,6},{8,9},{9,8},{10,11... | collective-permute-start | bytes 589832 | tf_op jit(solution)/shard_map/ppermute | solution.py:88
  70.6 12.3 %collective-permute-start.23 = (bf16[4,192,128]{2,1,0:T(8,128)(2,1)S(1)}, bf16[4,192,128]{2,1,0:T(8,128)(2,1)S(1)}, u32[]{:S(2)}, u32[]{:S(2)}) collective-permute-start(bf16[4,192,128]{2,1,0:T(8,128)(2,1)S(1)} %get-tuple-element.69), channel_id=1, source_target_pairs={{0,2},{1,3},{2,0},{3,1},{4,6},{5,7},{6,4},{7,5},{8,10},{9,11},{10,... | collective-permute-start | bytes 589832 | tf_op jit(solution)/shard_map/ppermute | solution.py:88
  73.8 9.1 %collective-permute-start.24 = (bf16[4,192,128]{2,1,0:T(8,128)(2,1)S(1)}, bf16[4,192,128]{2,1,0:T(8,128)(2,1)S(1)}, u32[]{:S(2)}, u32[]{:S(2)}) collective-permute-start(bf16[4,192,128]{2,1,0:T(8,128)(2,1)S(1)} %get-tuple-element.70), channel_id=1, source_target_pairs={{0,3},{1,2},{2,1},{3,0},{4,7},{5,6},{6,5},{7,4},{8,11},{9,10},{10,... | collective-permute-start | bytes 589832 | tf_op jit(solution)/shard_map/ppermute | solution.py:88
  75.5 8.9 %collective-permute-start.25 = (bf16[4,192,128]{2,1,0:T(8,128)(2,1)S(1)}, bf16[4,192,128]{2,1,0:T(8,128)(2,1)S(1)}, u32[]{:S(2)}, u32[]{:S(2)}) collective-permute-start(bf16[4,192,128]{2,1,0:T(8,128)(2,1)S(1)} %get-tuple-element.63.refs_0_), channel_id=1, source_target_pairs={{0,4},{4,0},{8,12},{12,8},{16,20},{20,16},{24,28},{28,24},{1,5},{5... | collective-permute-start | bytes 589832 | tf_op jit(solution)/shard_map/ppermute | solution.py:88
  78.6 4.8 %collective-permute-start.26 = (bf16[4,192,128]{2,1,0:T(8,128)(2,1)S(1)}, bf16[4,192,128]{2,1,0:T(8,128)(2,1)S(1)}, u32[]{:S(2)}, u32[]{:S(2)}) collective-permute-start(bf16[4,192,128]{2,1,0:T(8,128)(2,1)S(1)} %collective-permute-done.22.refs_1_), channel_id=1, source_target_pairs={{0,4},{4,0},{8,12},{12,8},{16,20},{20,16},{24,28},{28,24},{1,5},{5... | collective-permute-start | bytes 589832 | tf_op jit(solution)/shard_map/ppermute | solution.py:88
  82.9 1.4 %collective-permute-start.27 = (bf16[4,192,128]{2,1,0:T(8,128)(2,1)S(1)}, bf16[4,192,128]{2,1,0:T(8,128)(2,1)S(1)}, u32[]{:S(2)}, u32[]{:S(2)}) collective-permute-start(bf16[4,192,128]{2,1,0:T(8,128)(2,1)S(1)} %collective-permute-done.23.refs_2_), channel_id=1, source_target_pairs={{0,4},{4,0},{8,12},{12,8},{16,20},{20,16},{24,28},{28,24},{1,5},{5... | collective-permute-start | bytes 589832 | tf_op jit(solution)/shard_map/ppermute | solution.py:88
  82.9 1.7 %collective-permute-start.28 = (bf16[4,192,128]{2,1,0:T(8,128)(2,1)S(1)}, bf16[4,192,128]{2,1,0:T(8,128)(2,1)S(1)}, u32[]{:S(2)}, u32[]{:S(2)}) collective-permute-start(bf16[4,192,128]{2,1,0:T(8,128)(2,1)S(1)} %collective-permute-done.24.refs_3_), channel_id=1, source_target_pairs={{0,4},{4,0},{8,12},{12,8},{16,20},{20,16},{24,28},{28,24},{1,5},{5... | collective-permute-start | bytes 589832 | tf_op jit(solution)/shard_map/ppermute | solution.py:88
  85.3 6.1 %collective-permute-start.32 = (bf16[2,192,128]{2,1,0:T(8,128)(2,1)S(1)}, bf16[2,192,128]{2,1,0:T(8,128)(2,1)S(1)}, u32[]{:S(2)}, u32[]{:S(2)}) collective-permute-start(bf16[2,192,128]{2,1,0:T(8,128)(2,1)S(1)} %get-tuple-element.76), channel_id=1, source_target_pairs={{0,8},{4,12},{8,0},{12,4},{16,24},{20,28},{24,16},{28,20},{1,9},{5... | collective-permute-start | bytes 294920 | tf_op jit(solution)/shard_map/ppermute | solution.py:88
  86.8 10.0 %collective-permute-start.29 = (bf16[2,192,128]{2,1,0:T(8,128)(2,1)S(1)}, bf16[2,192,128]{2,1,0:T(8,128)(2,1)S(1)}, u32[]{:S(2)}, u32[]{:S(2)}) collective-permute-start(bf16[2,192,128]{2,1,0:T(8,128)(2,1)S(1)} %get-tuple-element.72), channel_id=1, source_target_pairs={{0,8},{4,12},{8,0},{12,4},{16,24},{20,28},{24,16},{28,20},{1,9},{5... | collective-permute-start | bytes 294920 | tf_op jit(solution)/shard_map/ppermute | solution.py:88
  87.4 5.6 %collective-permute-start.33 = (bf16[2,192,128]{2,1,0:T(8,128)(2,1)S(1)}, bf16[2,192,128]{2,1,0:T(8,128)(2,1)S(1)}, u32[]{:S(2)}, u32[]{:S(2)}) collective-permute-start(bf16[2,192,128]{2,1,0:T(8,128)(2,1)S(1)} %get-tuple-element.77), channel_id=1, source_target_pairs={{0,16},{4,20},{8,24},{12,28},{16,0},{20,4},{24,8},{28,12},{1,17},{... | collective-permute-start | bytes 294920 | tf_op jit(solution)/shard_map/ppermute | solution.py:88
  88.7 7.4 %collective-permute-start.34 = (bf16[2,192,128]{2,1,0:T(8,128)(2,1)S(1)}, bf16[2,192,128]{2,1,0:T(8,128)(2,1)S(1)}, u32[]{:S(2)}, u32[]{:S(2)}) collective-permute-start(bf16[2,192,128]{2,1,0:T(8,128)(2,1)S(1)} %get-tuple-element.78), channel_id=1, source_target_pairs={{0,24},{4,28},{8,16},{12,20},{16,8},{20,12},{24,0},{28,4},{1,25},{... | collective-permute-start | bytes 294920 | tf_op jit(solution)/shard_map/ppermute | solution.py:88
  90.3 8.0 %collective-permute-start.30 = (bf16[2,192,128]{2,1,0:T(8,128)(2,1)S(1)}, bf16[2,192,128]{2,1,0:T(8,128)(2,1)S(1)}, u32[]{:S(2)}, u32[]{:S(2)}) collective-permute-start(bf16[2,192,128]{2,1,0:T(8,128)(2,1)S(1)} %get-tuple-element.73), channel_id=1, source_target_pairs={{0,16},{4,20},{8,24},{12,28},{16,0},{20,4},{24,8},{28,12},{1,17},{... | collective-permute-start | bytes 294920 | tf_op jit(solution)/shard_map/ppermute | solution.py:88
  91.4 6.9 %collective-permute-start.31 = (bf16[2,192,128]{2,1,0:T(8,128)(2,1)S(1)}, bf16[2,192,128]{2,1,0:T(8,128)(2,1)S(1)}, u32[]{:S(2)}, u32[]{:S(2)}) collective-permute-start(bf16[2,192,128]{2,1,0:T(8,128)(2,1)S(1)} %get-tuple-element.74), channel_id=1, source_target_pairs={{0,24},{4,28},{8,16},{12,20},{16,8},{20,12},{24,0},{28,4},{1,25},{... | collective-permute-start | bytes 294920 | tf_op jit(solution)/shard_map/ppermute | solution.py:88
